TPU v7x, 32 devices: a whole 2x2x4 slice. The times are simulated.
32 devices in a mesh: section: 2 (over core), dp: 4 (over y, x), mp: 4 (over z).
Axes of the slice: x: 2, y: 2, z: 4, core: 2. Of those that a mesh axis runs over, the one named last changes fastest.
Arguments:
- segment_input: bfloat16 [2, 4, 256, 2048], P(None, 'dp', None, 'mp'), may hold values from -6 to 6
- out_grad: bfloat16 [2, 4, 256, 2048], P(None, 'dp', None, 'mp'), may hold values from -6 to 6
- pool_tokens: bfloat16 [16, 4, 128, 896], P('section', 'dp'), may hold values from -6 to 6
- neighbour_ids: int32 [2, 4, 4, 4], P(None, 'dp'), may hold values from 0 to 15, as said below
- neighbour_counts: int32 [2, 4, 4], P(None, 'dp'), may hold values from 1 to 4
- enc_gain: float32 [896], replicated, may hold values from 0.5 to 1.5
- enc_up: bfloat16 [896, 1024], P(None, 'mp'), may hold values from -0.1875 to 0.1875
- enc_down: bfloat16 [1024, 896], P(None, 'mp'), may hold values from -0.1875 to 0.1875
- norm_gain: float32 [2, 2048], P('section'), may hold values from 0.5 to 1.5
- w_query: bfloat16 [2, 2048, 1024], P('section', None, 'mp'), may hold values from -0.125 to 0.125
- w_key: bfloat16 [2, 896, 1024], P('section', None, 'mp'), may hold values from -0.1875 to 0.1875
- w_value: bfloat16 [2, 896, 1024], P('section', None, 'mp'), may hold values from -0.1875 to 0.1875
- w_out: bfloat16 [2, 1024, 2048], P('section', None, 'mp'), may hold values from -0.1875 to 0.1875
Outputs:
- grad_key: bfloat16 [2, 896, 1024], P('section', None, 'mp')
- grad_value: bfloat16 [2, 896, 1024], P('section', None, 'mp')
Inputs may be any that keep to these rules, and one draw needn't show every extreme that they name: `neighbour_ids`: the 4 slots of one stretch name distinct pool stretches.
All inputs are finite; a program needn't handle non-finite values.
Results may differ from a plain program's by a relative error of at most 0.025.
Values may be sent and summed in bfloat16 or wider, within the bound.
No kernel may reach another device: no remote copies, remote signals or barrier semaphores. Data moves between devices by JAX's collectives and lax.ppermute only.
A program may use at most 128 MiB of HBM per device.

v0:
```python
import jax
import jax.numpy as jnp
from jax import lax
from jax.sharding import PartitionSpec as P

HEAD = 128
NT = 128


EPSILON = 1e-05


def passed_along(value, axis, by):
    peers = lax.axis_size(axis)
    pairs = [(i, i + by) for i in range(peers) if 0 <= i + by < peers]
    return lax.ppermute(value, axis, pairs)


def rms_scale(values):
    return lax.rsqrt(jnp.mean(values * values, axis=-1, keepdims=True) + EPSILON)


def collect(tensor):
    return lax.all_gather(tensor, "mp", axis=1, tiled=True)


def collect_pair(first, second):
    return (
        lax.all_gather(first, "mp", axis=1, tiled=True),
        lax.all_gather(second, "mp", axis=1, tiled=True),
    )


def pass_on(tensor, offset):
    return passed_along(tensor, "section", offset)


def attend(queries, key_block, value_block, usable):
    scores = jnp.einsum("cqhe,ckhe->chqk", queries, key_block, preferred_element_type=jnp.float32)
    scores = jnp.where(usable[:, None, None, :], scores, -1e30)
    weights = jax.nn.softmax(scores, axis=-1)
    weights_bf = weights.astype(jnp.bfloat16)
    attended = jnp.einsum(
        "chqk,ckhe->cqhe", weights_bf, value_block, preferred_element_type=jnp.float32
    )
    return (weights, weights_bf, attended.astype(jnp.bfloat16))


def attend_back(queries, key_block, value_block, weights, weights_bf, grad_attended):
    grad_weights = jnp.einsum(
        "cqhe,ckhe->chqk", grad_attended, value_block, preferred_element_type=jnp.float32
    )
    grad_scores = weights * (grad_weights - jnp.sum(weights * grad_weights, axis=-1, keepdims=True))
    grad_values = jnp.einsum(
        "chqk,cqhe->ckhe", weights_bf, grad_attended, preferred_element_type=jnp.float32
    ).astype(jnp.bfloat16)
    grad_keys = jnp.einsum("chqk,cqhe->ckhe", grad_scores, queries.astype(jnp.float32)).astype(
        jnp.bfloat16
    )
    grad_queries = jnp.einsum("chqk,ckhe->cqhe", grad_scores, key_block.astype(jnp.float32))
    return (grad_keys, grad_values, grad_queries)


def front(rows_in, gain_full, query_cols, key_block, value_block, usable, head_count):
    rows_wide = rows_in.astype(jnp.float32)
    inv_rms = rms_scale(rows_wide)
    normed = (rows_wide * inv_rms * gain_full).astype(jnp.bfloat16)
    query_raw = jnp.dot(normed, query_cols, preferred_element_type=jnp.float32)
    queries = (query_raw * HEAD ** (-0.5)).astype(jnp.bfloat16)
    queries = queries.reshape(key_block.shape[0], -1, head_count, HEAD)
    weights, weights_bf, attended = attend(queries, key_block, value_block, usable)
    return (inv_rms, query_raw, queries, weights, weights_bf, attended)


def on_device(
    segment_input,
    out_grad,
    pool_tokens,
    neighbour_ids,
    neighbour_counts,
    enc_gain,
    enc_up,
    enc_down,
    norm_gain,
    w_query,
    w_key,
    w_value,
    w_out,
):
    model_count = lax.axis_size("mp")
    model_index = lax.axis_index("mp")
    segment_count = lax.axis_size("section")
    segment_index = lax.axis_index("section")
    micro_count = segment_input.shape[0]
    row_count = segment_input.shape[2]
    feat_count = segment_input.shape[3]
    width = feat_count * model_count
    head_count = w_query.shape[2] // HEAD
    tract_count = neighbour_ids.shape[2]
    key_span = neighbour_ids.shape[3] * NT
    raw_rows = pool_tokens[:, 0].reshape(-1, pool_tokens.shape[3])
    raw_wide = raw_rows.astype(jnp.float32)
    enc_normed = (raw_wide * rms_scale(raw_wide) * enc_gain).astype(jnp.bfloat16)
    hidden_part = jax.nn.gelu(
        jnp.dot(enc_normed, enc_up, preferred_element_type=jnp.float32)
    ).astype(jnp.bfloat16)
    hidden_full = collect(hidden_part)
    enc_feat = enc_down.shape[1]
    raw_slice = lax.dynamic_slice_in_dim(raw_wide, model_index * enc_feat, enc_feat, 1)
    encoded = (
        raw_slice + jnp.dot(hidden_full, enc_down, preferred_element_type=jnp.float32)
    ).astype(jnp.bfloat16)
    slot_ids = neighbour_ids[:, 0].reshape(-1)
    shard_rows = encoded.shape[0]
    token_index = jnp.arange(NT, dtype=jnp.int32)
    global_rows = ((slot_ids * NT)[:, None] + token_index[None, :]).reshape(-1)
    empty_pool = jnp.zeros((segment_count * shard_rows, enc_feat * model_count), jnp.bfloat16)
    portion = lax.all_gather(encoded, ("section", "mp"), axis=0, tiled=True)
    shard_total = portion.shape[0] // shard_rows

    def one_shard(position, whole_pool):
        shard_block = lax.dynamic_slice_in_dim(portion, position * shard_rows, shard_rows, 0)
        row_start = position // model_count * shard_rows
        col_start = position % model_count * enc_feat
        return lax.dynamic_update_slice(whole_pool, shard_block, (row_start, col_start))

    whole_pool = lax.fori_loop(0, shard_total, one_shard, empty_pool)
    neighbours = jnp.take(whole_pool, global_rows, axis=0)

    def project(weight):
        projected = jnp.dot(neighbours, weight[0], preferred_element_type=jnp.float32).astype(
            jnp.bfloat16
        )
        return projected.reshape(micro_count, tract_count, key_span, head_count, HEAD)

    key_all = project(w_key)
    value_all = project(w_value)
    span_index = jnp.arange(key_span, dtype=jnp.int32) // NT
    usable_all = span_index[None, None, :] < neighbour_counts[:, 0][:, :, None]
    query_cols = w_query[0]
    out_cols = w_out[0]
    query_rows, out_rows = (
        lax.all_to_all(query_cols, "mp", split_axis=0, concat_axis=1, tiled=True),
        lax.all_to_all(out_cols, "mp", split_axis=0, concat_axis=1, tiled=True),
    )
    gain_full = norm_gain[0]
    gain_own = lax.dynamic_slice_in_dim(gain_full, model_index * feat_count, feat_count, 0)
    inputs_own = segment_input[:, 0]
    grads_own = out_grad[:, 0]
    step_count = micro_count + segment_count - 1
    empty_share = jnp.zeros((row_count, feat_count), jnp.bfloat16)
    stored_start = jnp.zeros((micro_count, row_count, width), jnp.bfloat16)

    def forward_step(step, state):
        received, stored = state
        which = step - segment_index
        active = (which >= 0) & (which < micro_count)
        which = jnp.clip(which, 0, micro_count - 1)
        incoming = jnp.where(segment_index == 0, inputs_own[which], received)
        rows_full = collect(incoming)
        outputs = front(
            rows_full,
            gain_full,
            query_cols,
            key_all[which],
            value_all[which],
            usable_all[which],
            head_count,
        )
        attended = collect(outputs[5].reshape(row_count, -1))
        result = incoming.astype(jnp.float32) + jnp.dot(
            attended, out_cols, preferred_element_type=jnp.float32
        )
        stored = stored.at[which].set(jnp.where(active, rows_full, stored[which]))
        return (pass_on(result.astype(jnp.bfloat16), 1), stored)

    _, stored = lax.fori_loop(0, step_count, forward_step, (empty_share, stored_start))
    grad_start = jnp.zeros((micro_count, tract_count, key_span, head_count, HEAD), jnp.bfloat16)

    def backward_step(step, state):
        received, key_grads, value_grads = state
        which = step - (segment_count - 1 - segment_index)
        active = (which >= 0) & (which < micro_count)
        which = jnp.clip(which, 0, micro_count - 1)
        incoming = jnp.where(segment_index == segment_count - 1, grads_own[which], received)
        rows_full = stored[which]
        rows_own = lax.dynamic_slice_in_dim(rows_full, model_index * feat_count, feat_count, 1)
        key_block = key_all[which]
        value_block = value_all[which]
        inv_rms, query_raw, queries, weights, weights_bf, _ = front(
            rows_full, gain_full, query_cols, key_block, value_block, usable_all[which], head_count
        )
        grad_full = collect(incoming)
        grad_att = jnp.dot(grad_full, out_rows.T, preferred_element_type=jnp.float32).astype(
            jnp.bfloat16
        )
        grad_att = grad_att.reshape(queries.shape)
        grad_keys, grad_values, grad_queries = attend_back(
            queries, key_block, value_block, weights, weights_bf, grad_att
        )
        grad_scaled = (grad_queries * HEAD ** (-0.5)).reshape(row_count, -1).astype(jnp.bfloat16)
        part_total = jnp.sum(
            grad_scaled.astype(jnp.float32) * query_raw, axis=1, keepdims=True
        ).astype(jnp.bfloat16)
        scaled_full, totals = collect_pair(grad_scaled, part_total)
        row_total = jnp.sum(totals.astype(jnp.float32), axis=1, keepdims=True)
        grad_normed = jnp.dot(scaled_full, query_rows.T, preferred_element_type=jnp.float32)
        rows_wide = rows_own.astype(jnp.float32)
        grad_in = (
            incoming.astype(jnp.float32)
            + inv_rms * gain_own * grad_normed
            - rows_wide * inv_rms * inv_rms * row_total / width
        )
        key_grads = key_grads.at[which].set(jnp.where(active, grad_keys, key_grads[which]))
        value_grads = value_grads.at[which].set(jnp.where(active, grad_values, value_grads[which]))
        return (pass_on(grad_in.astype(jnp.bfloat16), -1), key_grads, value_grads)

    _, key_grads, value_grads = lax.fori_loop(
        0, step_count, backward_step, (empty_share, grad_start, grad_start)
    )
    contract = (((0,), (0,)), ((), ()))
    key_sum = lax.dot_general(
        neighbours,
        key_grads.reshape(-1, head_count * HEAD),
        contract,
        preferred_element_type=jnp.float32,
    )
    value_sum = lax.dot_general(
        neighbours,
        value_grads.reshape(-1, head_count * HEAD),
        contract,
        preferred_element_type=jnp.float32,
    )
    key_total, value_total = (
        lax.psum(key_sum.astype(jnp.bfloat16), "dp").astype(jnp.float32),
        lax.psum(value_sum.astype(jnp.bfloat16), "dp").astype(jnp.float32),
    )
    return (key_total.astype(jnp.bfloat16)[None], value_total.astype(jnp.bfloat16)[None])


def solution(mesh):
    placed = (
        P(None, "dp", None, "mp"),
        P(None, "dp", None, "mp"),
        P("section", "dp", None, None),
        P(None, "dp", None, None),
        P(None, "dp", None),
        P(),
        P(None, "mp"),
        P(None, "mp"),
        P("section", None),
        P("section", None, "mp"),
        P("section", None, "mp"),
        P("section", None, "mp"),
        P("section", None, "mp"),
    )
    return jax.shard_map(
        on_device,
        mesh=mesh,
        in_specs=placed,
        out_specs=(P("section", None, "mp"), P("section", None, "mp")),
        check_vma=False,
    )
```

profile of v0, /device:TPU:0, one launch (start us, length us, event | category | flops | bytes accessed | tf_op | source)
XLA Modules:
  0.0 749.0 jit_solution(12069792961373660321)
XLA Ops:
  16.3 49.0 %all-gather.8.cloned.1.call-done = bf16[1024,1024]{1,0:T(8,128)(2,1)} async-done(((bf16[1024,256]{1,0:T(8,128)(2,1)}), bf16[1024,1024]{1,0:T(8,128)(2,1)}) %all-gather.8.cloned.1.call-update) | async-done | bytes 2097168 | tf_op jit(solution)/shard_map/all_gather | solution.py:24
  72.5 49.9 %all-to-all-done = bf16[4,256,512]{2,1,0:T(8,128)(2,1)S(1)} async-done(((bf16[4,256,512]{2,1,0:T(8,128)(2,1)}), bf16[4,256,512]{2,1,0:T(8,128)(2,1)S(1)}, u32[]{:S(2)}, u32[]{:S(2)}) %all-to-all-start) | async-done | bytes 1048608 | tf_op jit(solution)/shard_map/all_to_all | solution.py:144
  130.0 19.7 %all-to-all-done.1 = bf16[4,512,256]{2,1,0:T(8,128)(2,1)S(1)} async-done(((bf16[4,512,256]{2,1,0:T(8,128)(2,1)}), bf16[4,512,256]{2,1,0:T(8,128)(2,1)S(1)}, u32[]{:S(2)}, u32[]{:S(2)}) %all-to-all-start.1) | async-done | bytes 1048608 | tf_op jit(solution)/shard_map/all_to_all | solution.py:143
  153.7 65.4 %while.54 = (s32[]{:T(128)}, bf16[2048,896]{1,0:T(8,128)(2,1)}, bf16[8192,224]{0,1:T(8,128)(2,1)}, s32[]{:T(128)}, s32[]{:T(128)}, /*index=5*/s32[]{:T(128)}, s3...) while((s32[]{:T(128)}, bf16[2048,896]{1,0:T(8,128)(2,1)}, ...), condition=%wide.region_2.3_spmd, body=%wide.region_1.2_spmd.sunk | while | flops 26 | bytes 2752914 | solution.py:127
  155.0 7.0 dynamic_update_slice.11
  163.2 7.7 %dynamic_update_slice.11 = bf16[2048,896]{1,0:T(8,128)(2,1)} dynamic-update-slice(bf16[2048,896]{1,0:T(8,128)(2,1)} %get-tuple-element.1273, bf16[1024,224]{1,0:T(8,128)(2,1)S(1)} %copy.148, s32[]{:T(128)S(6)} %select_n.309, s32[]{:T(128)S(6)} %select_n.311) | dynamic-update-slice | bytes 917508 | tf_op jit(solution)/shard_map/while/body/eval_jaxpr/dynamic_update_slice | solution.py:125
  172.2 7.7 %dynamic_update_slice.11 = bf16[2048,896]{1,0:T(8,128)(2,1)} dynamic-update-slice(bf16[2048,896]{1,0:T(8,128)(2,1)} %get-tuple-element.1273, bf16[1024,224]{1,0:T(8,128)(2,1)S(1)} %copy.148, s32[]{:T(128)S(6)} %select_n.309, s32[]{:T(128)S(6)} %select_n.311) | dynamic-update-slice | bytes 917508 | tf_op jit(solution)/shard_map/while/body/eval_jaxpr/dynamic_update_slice | solution.py:125
  181.2 7.0 dynamic_update_slice.11
  196.6 6.7 dynamic_update_slice.11
  204.7 6.7 dynamic_update_slice.11
  212.7 6.4 dynamic_update_slice.11
  219.2 22.4 %gather_fusion = bf16[4096,896]{1,0:T(8,128)(2,1)} fusion(bf16[2048,896]{1,0:T(8,128)(2,1)} %get-tuple-element.835, s32[4096]{0:T(1024)S(1)} %broadcast_clamp_fusion), kind=kCustom, calls=%fused_computation | custom fusion | bytes 14696448 | tf_op jit(solution)/shard_map/jit(_take)/gather | solution.py:128
  263.3 175.9 %while.55 = (s32[]{:T(128)}, bf16[256,512]{1,0:T(8,128)(2,1)S(1)}, bf16[2,256,2048]{2,1,0:T(8,128)(2,1)}, pred[]{:T(512)}, s32[]{:T(128)}, /*index=5*/bf16[2,256...) while((s32[]{:T(128)}, bf16[256,512]{1,0:T(8,128)(2,1)S(1)}, ...), condition=%wide.region_8.9_spmd, body=%wide.region_3.8_spmd.sunk | while | flops 677839616 | bytes 27550076 | solution.py:177
  266.1 28.1 %all-gather.12.cloned.1.call-done = bf16[256,2048]{1,0:T(8,128)(2,1)} async-done(((bf16[256,512]{1,0:T(8,128)(2,1)}), bf16[256,2048]{1,0:T(8,128)(2,1)}) %all-gather.12.cloned.1.call-update) | async-done | bytes 1048592 | tf_op jit(solution)/shard_map/while/body/eval_jaxpr/all_gather | solution.py:24
  301.6 15.5 %all_gather.62 = bf16[256,1024]{1,0:T(8,128)(2,1)S(1)} all-gather(bf16[256,256]{1,0:T(8,128)(2,1)S(1)} %bitcast.253), channel_id=1, replica_groups=mesh['section'=2,'dp'=4,'mp'=4] {'mp'}, dimensions={1}, use_global_device_ids=true | all-gather | bytes 655360 | tf_op jit(solution)/shard_map/while/body/eval_jaxpr/all_gather | solution.py:24
  325.0 27.8 %all-gather.12.cloned.1.call-done = bf16[256,2048]{1,0:T(8,128)(2,1)} async-done(((bf16[256,512]{1,0:T(8,128)(2,1)}), bf16[256,2048]{1,0:T(8,128)(2,1)}) %all-gather.12.cloned.1.call-update) | async-done | bytes 1048592 | tf_op jit(solution)/shard_map/while/body/eval_jaxpr/all_gather | solution.py:24
  360.1 15.6 %all_gather.62 = bf16[256,1024]{1,0:T(8,128)(2,1)S(1)} all-gather(bf16[256,256]{1,0:T(8,128)(2,1)S(1)} %bitcast.253), channel_id=1, replica_groups=mesh['section'=2,'dp'=4,'mp'=4] {'mp'}, dimensions={1}, use_global_device_ids=true | all-gather | bytes 655360 | tf_op jit(solution)/shard_map/while/body/eval_jaxpr/all_gather | solution.py:24
  383.6 27.8 %all-gather.12.cloned.1.call-done = bf16[256,2048]{1,0:T(8,128)(2,1)} async-done(((bf16[256,512]{1,0:T(8,128)(2,1)}), bf16[256,2048]{1,0:T(8,128)(2,1)}) %all-gather.12.cloned.1.call-update) | async-done | bytes 1048592 | tf_op jit(solution)/shard_map/while/body/eval_jaxpr/all_gather | solution.py:24
  418.7 15.5 %all_gather.62 = bf16[256,1024]{1,0:T(8,128)(2,1)S(1)} all-gather(bf16[256,256]{1,0:T(8,128)(2,1)S(1)} %bitcast.253), channel_id=1, replica_groups=mesh['section'=2,'dp'=4,'mp'=4] {'mp'}, dimensions={1}, use_global_device_ids=true | all-gather | bytes 655360 | tf_op jit(solution)/shard_map/while/body/eval_jaxpr/all_gather | solution.py:24
  444.1 230.6 %while.56 = (s32[]{:T(128)}, bf16[256,512]{1,0:T(8,128)(2,1)S(1)}, bf16[2,4,512,2,128]{4,3,2,1,0:T(2,128)(2,1)}, bf16[2,4,512,2,128]{4,3,2,1,0:T(2,128)(2,1)}, p...) while((s32[]{:T(128)}, bf16[256,512]{1,0:T(8,128)(2,1)S(1)}, ...), condition=%wide.region_17.18_spmd, body=%wide.region_9.17_spmd.sunk | while | flops 1153435392 | bytes 71749208 | solution.py:218
  459.3 15.5 %all-gather.14.cloned.1.call-done = bf16[256,2048]{1,0:T(8,128)(2,1)} async-done(((bf16[256,512]{1,0:T(8,128)(2,1)}), bf16[256,2048]{1,0:T(8,128)(2,1)}) %all-gather.14.cloned.1.call-update) | async-done | bytes 1048592 | tf_op jit(solution)/shard_map/while/body/eval_jaxpr/all_gather | solution.py:24
  480.1 15.6 %all_gather.64 = bf16[256,1024]{1,0:T(8,128)(2,1)S(1)} all-gather(bf16[256,256]{1,0:T(8,128)(2,1)S(1)} %bitcast.250), channel_id=1, replica_groups=mesh['section'=2,'dp'=4,'mp'=4] {'mp'}, dimensions={1}, use_global_device_ids=true | all-gather | bytes 655360 | tf_op jit(solution)/shard_map/while/body/eval_jaxpr/all_gather | solution.py:29
  495.8 9.8 %all-gather.2 = bf16[4,1,256]{2,1,0:T(2,128)(2,1)S(1)} all-gather(bf16[1,1,256]{2,1,0:T(2,128)(2,1)S(1)} %reshape.462), channel_id=1, replica_groups=mesh['section'=2,'dp'=4,'mp'=4] {'mp'}, dimensions={0}, use_global_device_ids=true | all-gather | bytes 2560 | tf_op jit(solution)/shard_map/while/body/eval_jaxpr/all_gather | solution.py:30
  536.6 14.8 %all-gather.14.cloned.1.call-done = bf16[256,2048]{1,0:T(8,128)(2,1)} async-done(((bf16[256,512]{1,0:T(8,128)(2,1)}), bf16[256,2048]{1,0:T(8,128)(2,1)}) %all-gather.14.cloned.1.call-update) | async-done | bytes 1048592 | tf_op jit(solution)/shard_map/while/body/eval_jaxpr/all_gather | solution.py:24
  556.7 15.5 %all_gather.64 = bf16[256,1024]{1,0:T(8,128)(2,1)S(1)} all-gather(bf16[256,256]{1,0:T(8,128)(2,1)S(1)} %bitcast.250), channel_id=1, replica_groups=mesh['section'=2,'dp'=4,'mp'=4] {'mp'}, dimensions={1}, use_global_device_ids=true | all-gather | bytes 655360 | tf_op jit(solution)/shard_map/while/body/eval_jaxpr/all_gather | solution.py:29
  572.2 9.9 %all-gather.2 = bf16[4,1,256]{2,1,0:T(2,128)(2,1)S(1)} all-gather(bf16[1,1,256]{2,1,0:T(2,128)(2,1)S(1)} %reshape.462), channel_id=1, replica_groups=mesh['section'=2,'dp'=4,'mp'=4] {'mp'}, dimensions={0}, use_global_device_ids=true | all-gather | bytes 2560 | tf_op jit(solution)/shard_map/while/body/eval_jaxpr/all_gather | solution.py:30
  613.2 14.9 %all-gather.14.cloned.1.call-done = bf16[256,2048]{1,0:T(8,128)(2,1)} async-done(((bf16[256,512]{1,0:T(8,128)(2,1)}), bf16[256,2048]{1,0:T(8,128)(2,1)}) %all-gather.14.cloned.1.call-update) | async-done | bytes 1048592 | tf_op jit(solution)/shard_map/while/body/eval_jaxpr/all_gather | solution.py:24
  633.3 15.5 %all_gather.64 = bf16[256,1024]{1,0:T(8,128)(2,1)S(1)} all-gather(bf16[256,256]{1,0:T(8,128)(2,1)S(1)} %bitcast.250), channel_id=1, replica_groups=mesh['section'=2,'dp'=4,'mp'=4] {'mp'}, dimensions={1}, use_global_device_ids=true | all-gather | bytes 655360 | tf_op jit(solution)/shard_map/while/body/eval_jaxpr/all_gather | solution.py:29
  648.9 9.9 %all-gather.2 = bf16[4,1,256]{2,1,0:T(2,128)(2,1)S(1)} all-gather(bf16[1,1,256]{2,1,0:T(2,128)(2,1)S(1)} %reshape.462), channel_id=1, replica_groups=mesh['section'=2,'dp'=4,'mp'=4] {'mp'}, dimensions={0}, use_global_device_ids=true | all-gather | bytes 2560 | tf_op jit(solution)/shard_map/while/body/eval_jaxpr/all_gather | solution.py:30
  674.7 7.4 fusion.102
  682.1 6.7 fusion.99
  688.9 50.0 %all-reduce.3.cloned.1.call-done = (bf16[1,896,256]{2,1,0:T(8,128)(2,1)}, bf16[1,896,256]{2,1,0:T(8,128)(2,1)}) async-done(((bf16[1,896,256]{2,1,0:T(8,128)(2,1)}, bf16[1,896,256]{2,1,0:T(8,128)(2,1)}), (bf16[1,896,256]{2,1,0:T(8,128)(2,1)}, bf16[1,896,256]{2,1,0:T(8,128)(2,1)})) %all-reduce.3.cloned.1.call-update) | async-done | bytes 917520 | tf_op jit(solution)/shard_map/psum | solution.py:235
  (284 shorter events, 227.8 us)
Async XLA Ops:
  7.2 234.4 %copy-start = (bf16[1,896,256]{2,1,0:T(8,128)(2,1)S(1)}, bf16[1,896,256]{2,1,0:T(8,128)(2,1)}, u32[]{:S(2)}) copy-start(bf16[1,896,256]{2,1,0:T(8,128)(2,1)} %param.35) | copy-start | bytes 1376260
  7.2 58.2 %all-gather.8.cloned.1.call-start = ((), (), s32[]{:S(2)}) async-start(), calls=%async_computation.2 | async-start | bytes 2621440 | tf_op jit(solution)/shard_map/all_gather | solution.py:24
  12.3 53.1 %copy-start.15 = (bf16[1024,224]{0,1:T(8,128)(2,1)S(1)}, bf16[1024,224]{0,1:T(8,128)(2,1)}, u32[]{:S(2)}) copy-start(bf16[1024,224]{0,1:T(8,128)(2,1)} %param.32) | copy-start | bytes 1376260
  16.3 135.3 %all-gather.10.cloned.1.call-start = ((), (), s32[]{:S(2)}) async-start(), calls=%async_computation.3 | async-start | bytes 4128768 | tf_op jit(solution)/shard_map/all_gather | solution.py:118
  68.8 57.4 %copy-start.13 = (f32[1,2048]{1,0:T(1,128)S(1)}, f32[1,2048]{1,0:T(1,128)}, u32[]{:S(2)}) copy-start(f32[1,2048]{1,0:T(1,128)} %param.33) | copy-start | bytes 24580
  68.8 57.4 %copy-start.12 = (s32[2,1,4]{2,1,0:T(1,128)S(1)}, s32[2,1,4]{2,1,0:T(1,128)}, u32[]{:S(2)}) copy-start(s32[2,1,4]{2,1,0:T(1,128)} %param.29) | copy-start | bytes 100
  68.8 53.7 %all-to-all-start = ((bf16[4,256,512]{2,1,0:T(8,128)(2,1)}), bf16[4,256,512]{2,1,0:T(8,128)(2,1)S(1)}, u32[]{:S(2)}, u32[]{:S(2)}) async-start(bf16[4,256,512]{2,1,0:T(8,128)(2,1)} %bitcast.38), calls=%async_computation | async-start | bytes 2097152 | tf_op jit(solution)/shard_map/all_to_all | solution.py:144
  122.5 27.2 %all-to-all-start.1 = ((bf16[4,512,256]{2,1,0:T(8,128)(2,1)}), bf16[4,512,256]{2,1,0:T(8,128)(2,1)S(1)}, u32[]{:S(2)}, u32[]{:S(2)}) async-start(bf16[4,512,256]{2,1,0:T(8,128)(2,1)} %bitcast.41), calls=%async_computation.1 | async-start | bytes 2097152 | tf_op jit(solution)/shard_map/all_to_all | solution.py:143
  263.3 31.0 %all-gather.12.cloned.1.call-start = ((), (), s32[]{:S(2)}) async-start(), calls=%async_computation.5 | async-start | bytes 1310720 | tf_op jit(solution)/shard_map/while/body/eval_jaxpr/all_gather | solution.py:24
  318.8 3.3 collective-permute-start
  322.1 30.7 %all-gather.12.cloned.1.call-start = ((), (), s32[]{:S(2)}) async-start(), calls=%async_computation.5 | async-start | bytes 1310720 | tf_op jit(solution)/shard_map/while/body/eval_jaxpr/all_gather | solution.py:24
  359.9 18.8 %copy-start.2 = (bf16[256,2048]{1,0:T(8,128)(2,1)S(1)}, bf16[256,2048]{1,0:T(8,128)(2,1)}, u32[]{:S(2)}) copy-start(bf16[256,2048]{1,0:T(8,128)(2,1)} %all-gather.12.cloned.1.call-done) | copy-start | bytes 3145732 | tf_op jit(solution)/shard_map/while
  377.4 3.3 collective-permute-start
  380.7 30.6 %all-gather.12.cloned.1.call-start = ((), (), s32[]{:S(2)}) async-start(), calls=%async_computation.5 | async-start | bytes 1310720 | tf_op jit(solution)/shard_map/while/body/eval_jaxpr/all_gather | solution.py:24
  435.9 3.3 collective-permute-start
  444.1 30.7 %all-gather.14.cloned.1.call-start = ((), (), s32[]{:S(2)}) async-start(), calls=%async_computation.6 | async-start | bytes 1310720 | tf_op jit(solution)/shard_map/while/body/eval_jaxpr/all_gather | solution.py:24
  478.9 26.8 %copy-start.6 = (bf16[256,512]{1,0:T(8,128)(2,1)S(1)}, bf16[256,512]{1,0:T(8,128)(2,1)}, u32[]{:S(2)}) copy-start(bf16[256,512]{1,0:T(8,128)(2,1)} %bitcast_select_fusion.7) | copy-start | bytes 786436 | tf_op jit(solution)/shard_map/while
  480.1 29.3 %copy-start.5 = (bf16[1,4,512,2,128]{2,4,3,1,0:T(8,128)(2,1)S(1)}, bf16[1,4,512,2,128]{2,4,3,1,0:T(8,128)(2,1)}, u32[]{:S(2)}) copy-start(bf16[1,4,512,2,128]{2,4,3,1,0:T(8,128)(2,1)} %copy.160) | copy-start | bytes 3145732 | tf_op jit(solution)/shard_map/while
  480.1 29.3 %copy-start.20 = (f32[4,2,64,512]{3,2,1,0:T(8,128)S(1)}, f32[4,2,64,512]{3,2,1,0:T(8,128)}, u32[]{:S(2)}) copy-start(f32[4,2,64,512]{3,2,1,0:T(8,128)} %copy-done.19) | copy-start | bytes 3145732 | tf_op jit(solution)/shard_map/while
  508.1 13.3 %collective-permute-start.1 = (bf16[256,512]{1,0:T(8,128)(2,1)}, bf16[256,512]{1,0:T(8,128)(2,1)S(1)}, u32[]{:S(2)}, u32[]{:S(2)}) collective-permute-start(bf16[256,512]{1,0:T(8,128)(2,1)} %fusion.196), channel_id=1, source_target_pairs={{16,0},{17,1},{18,2},{19,3},{20,4},{21,5},{22,6},{23,7},{24,8},{25... | collective-permute-start | bytes 786440 | tf_op jit(solution)/shard_map/while/body/eval_jaxpr/ppermute | solution.py:16
  521.4 29.9 %all-gather.14.cloned.1.call-start = ((), (), s32[]{:S(2)}) async-start(), calls=%async_computation.6 | async-start | bytes 1310720 | tf_op jit(solution)/shard_map/while/body/eval_jaxpr/all_gather | solution.py:24
  555.4 26.8 %copy-start.6 = (bf16[256,512]{1,0:T(8,128)(2,1)S(1)}, bf16[256,512]{1,0:T(8,128)(2,1)}, u32[]{:S(2)}) copy-start(bf16[256,512]{1,0:T(8,128)(2,1)} %bitcast_select_fusion.7) | copy-start | bytes 786436 | tf_op jit(solution)/shard_map/while
  556.6 29.4 %copy-start.5 = (bf16[1,4,512,2,128]{2,4,3,1,0:T(8,128)(2,1)S(1)}, bf16[1,4,512,2,128]{2,4,3,1,0:T(8,128)(2,1)}, u32[]{:S(2)}) copy-start(bf16[1,4,512,2,128]{2,4,3,1,0:T(8,128)(2,1)} %copy.160) | copy-start | bytes 3145732 | tf_op jit(solution)/shard_map/while
  556.7 29.4 %copy-start.20 = (f32[4,2,64,512]{3,2,1,0:T(8,128)S(1)}, f32[4,2,64,512]{3,2,1,0:T(8,128)}, u32[]{:S(2)}) copy-start(f32[4,2,64,512]{3,2,1,0:T(8,128)} %copy-done.19) | copy-start | bytes 3145732 | tf_op jit(solution)/shard_map/while
  584.7 13.3 %collective-permute-start.1 = (bf16[256,512]{1,0:T(8,128)(2,1)}, bf16[256,512]{1,0:T(8,128)(2,1)S(1)}, u32[]{:S(2)}, u32[]{:S(2)}) collective-permute-start(bf16[256,512]{1,0:T(8,128)(2,1)} %fusion.196), channel_id=1, source_target_pairs={{16,0},{17,1},{18,2},{19,3},{20,4},{21,5},{22,6},{23,7},{24,8},{25... | collective-permute-start | bytes 786440 | tf_op jit(solution)/shard_map/while/body/eval_jaxpr/ppermute | solution.py:16
  598.0 30.0 %all-gather.14.cloned.1.call-start = ((), (), s32[]{:S(2)}) async-start(), calls=%async_computation.6 | async-start | bytes 1310720 | tf_op jit(solution)/shard_map/while/body/eval_jaxpr/all_gather | solution.py:24
  632.1 26.8 %copy-start.6 = (bf16[256,512]{1,0:T(8,128)(2,1)S(1)}, bf16[256,512]{1,0:T(8,128)(2,1)}, u32[]{:S(2)}) copy-start(bf16[256,512]{1,0:T(8,128)(2,1)} %bitcast_select_fusion.7) | copy-start | bytes 786436 | tf_op jit(solution)/shard_map/while
  633.3 29.3 %copy-start.5 = (bf16[1,4,512,2,128]{2,4,3,1,0:T(8,128)(2,1)S(1)}, bf16[1,4,512,2,128]{2,4,3,1,0:T(8,128)(2,1)}, u32[]{:S(2)}) copy-start(bf16[1,4,512,2,128]{2,4,3,1,0:T(8,128)(2,1)} %copy.160) | copy-start | bytes 3145732 | tf_op jit(solution)/shard_map/while
  633.3 29.3 %copy-start.20 = (f32[4,2,64,512]{3,2,1,0:T(8,128)S(1)}, f32[4,2,64,512]{3,2,1,0:T(8,128)}, u32[]{:S(2)}) copy-start(f32[4,2,64,512]{3,2,1,0:T(8,128)} %copy-done.19) | copy-start | bytes 3145732 | tf_op jit(solution)/shard_map/while
  661.4 13.4 %collective-permute-start.1 = (bf16[256,512]{1,0:T(8,128)(2,1)}, bf16[256,512]{1,0:T(8,128)(2,1)S(1)}, u32[]{:S(2)}, u32[]{:S(2)}) collective-permute-start(bf16[256,512]{1,0:T(8,128)(2,1)} %fusion.196), channel_id=1, source_target_pairs={{16,0},{17,1},{18,2},{19,3},{20,4},{21,5},{22,6},{23,7},{24,8},{25... | collective-permute-start | bytes 786440 | tf_op jit(solution)/shard_map/while/body/eval_jaxpr/ppermute | solution.py:16
  674.7 64.1 %all-reduce.3.cloned.1.call-start = ((), (), s32[]{:S(2)}) async-start(), calls=%async_computation.4 | async-start | bytes 1835008 | tf_op jit(solution)/shard_map/psum | solution.py:235
  682.1 60.3 %copy-start.1 = (bf16[1,896,256]{2,1,0:T(8,128)(2,1)S(1)}, bf16[1,896,256]{2,1,0:T(8,128)(2,1)}, u32[]{:S(2)}) copy-start(bf16[1,896,256]{2,1,0:T(8,128)(2,1)} %param.35) | copy-start | bytes 1376260
  (20 other events, 127.4 us)
Sparse Core Ops, SparseCore 0:
  16.4 48.9 all-gather.7
  68.9 64.1 all-gather.9
  266.3 27.8 all-gather.11
  324.8 27.9 all-gather.11
  383.5 27.8 all-gather.11
  446.9 27.9 all-gather.13
  524.5 26.8 all-gather.13
  601.1 26.9 all-gather.13
  689.0 49.7 all-reduce.2
where the time goes:
time: 753 us; the launch traced here: 749 us
  waiting for transfers between devices  298 us (40%)
  local copies, waits for them, and re-layouts  169 us (22%)
  blocking collectives  123 us (16%)
  matrix products  100 us (13%)
  other arithmetic  29.3 us (4%)
  starting transfers between devices  15.1 us (2%)
  between operations  14 us (2%)
    all_gather x7, waiting for transfers between devices, collect(): return lax.all_gather(tensor, 'mp', axis=1, tiled=True)  178 us
    dynamic_update_slice x8, local copies, waits for them, and re-layouts, one_shard(): lax.dynamic_update_slice(whole_pool, shard_block, (row_start, col_start))  55.2 us
    psum x1, waiting for transfers between devices, on_device(): lax.psum(key_sum.astype(jnp.bfloat16), 'dp').astype(jnp.float32)  50 us
    all_to_all x1, waiting for transfers between devices, on_device(): lax.all_to_all(out_cols, 'mp', split_axis=0, concat_axis=1, tiled=True)  49.9 us
    all_gather x3, blocking collectives, collect(): return lax.all_gather(tensor, 'mp', axis=1, tiled=True)  46.6 us
    all_gather x3, blocking collectives, collect_pair(): lax.all_gather(first, 'mp', axis=1, tiled=True)  46.6 us
    all_gather x3, blocking collectives, collect_pair(): lax.all_gather(second, 'mp', axis=1, tiled=True)  29.6 us
    gather x1, local copies, waits for them, and re-layouts, on_device(): neighbours = jnp.take(whole_pool, global_rows, axis=0)  22.4 us
  transfers between devices with their start and end apart: 17, of which 10 were waited for; matrix products, arithmetic and copies ran while one was open for 13% of the time, Pallas kernels for 0%

commit v1 on v0

v1 whole, which is shorter than its diff:
```python
import functools

import jax
import jax.numpy as jnp
from jax import lax
from jax.experimental import pallas as pl
from jax.experimental.pallas import tpu as pltpu
from jax.sharding import PartitionSpec as P

HEAD = 128
NT = 128
EPSILON = 1e-05
SCALE = HEAD ** (-0.5)
PAD = 16
VMEM_LIMIT = 56 * 1024 * 1024

BF16 = jnp.bfloat16
F32 = jnp.float32
NN = (((1,), (0,)), ((), ()))
NTR = (((1,), (1,)), ((), ()))
TNR = (((0,), (0,)), ((), ()))


def mm(a, b, dims=NN):
    return lax.dot_general(a, b, dims, preferred_element_type=F32)


def xor_move(value, axis, by):
    count = lax.axis_size(axis)
    return lax.ppermute(value, axis, [(i, i ^ by) for i in range(count)])


def swap(value):
    return xor_move(value, "section", 1)


def after(value, *others):
    return lax.optimization_barrier((value,) + others)[0]


def vm():
    return pl.BlockSpec(memory_space=pltpu.VMEM)


def hbm():
    return pl.BlockSpec(memory_space=pl.ANY)


def smem():
    return pl.BlockSpec(memory_space=pltpu.SMEM)


def call(body, outs, specs, scratch=(), flops=0):
    nbytes = sum(o.size * o.dtype.itemsize for o in outs)
    return pl.pallas_call(
        body,
        out_shape=outs,
        in_specs=specs,
        out_specs=[vm() for _ in outs],
        scratch_shapes=list(scratch),
        compiler_params=pltpu.CompilerParams(vmem_limit_bytes=VMEM_LIMIT),
        cost_estimate=pl.CostEstimate(
            flops=flops, bytes_accessed=2 * nbytes, transcendentals=0
        ),
    )


def shape(dims, dtype=BF16):
    return jax.ShapeDtypeStruct(dims, dtype)


def to_row(column):
    rows = column.shape[0]
    here = lax.broadcasted_iota(jnp.int32, (rows, rows), 0)
    there = lax.broadcasted_iota(jnp.int32, (rows, rows), 1)
    return jnp.sum(jnp.where(here == there, column, 0.0), axis=0, keepdims=True)


def to_column(row):
    rows = row.shape[1]
    here = lax.broadcasted_iota(jnp.int32, (rows, rows), 0)
    there = lax.broadcasted_iota(jnp.int32, (rows, rows), 1)
    return jnp.sum(jnp.where(here == there, row, 0.0), axis=1, keepdims=True)


def load_pool(own, other, pool, sems):
    half = own.shape[0]
    s = lax.axis_index("section")
    copies = [
        pltpu.make_async_copy(own, pool.at[pl.ds(s * half, half)], sems.at[0]),
        pltpu.make_async_copy(other, pool.at[pl.ds((1 - s) * half, half)], sems.at[1]),
    ]
    for copy in copies:
        copy.start()
    return copies


def hidden_body(n, parts, gathered, *refs):
    pool_ref, gain_ref = refs[:2]
    if gathered:
        up, out_ref = refs[2:4]
    else:
        pieces, (out_ref, up, sems) = refs[2 : 2 + parts], refs[2 + parts :]
        s, g, m = (lax.axis_index(a) for a in ("section", "dp", "mp"))
        copies = []
        for i, piece in enumerate(pieces):
            half, dg = divmod(i, parts // 2)
            place = (s ^ half) * (parts // 2) + (g ^ dg)
            for dz in range(n):
                copies.append(
                    pltpu.make_async_copy(piece.at[dz], up.at[m ^ dz, place], sems.at[i * n + dz])
                )
        for copy in copies:
            copy.start()
        for copy in copies:
            copy.wait()
    rows, width = pool_ref.shape
    cols = up.shape[-1]
    chunk = 256

    def step(i, _):
        here = pl.ds(pl.multiple_of(i * chunk, chunk), chunk)
        wide = pool_ref[here, :].astype(F32)
        scale = lax.rsqrt(jnp.mean(wide * wide, axis=-1, keepdims=True) + EPSILON)
        normed = (wide * scale * gain_ref[...]).astype(BF16)
        for k in range(n):
            weight = up[k].reshape(width, cols)
            out_ref[here, k * cols : (k + 1) * cols] = jax.nn.gelu(mm(normed, weight)).astype(BF16)
        return 0

    lax.fori_loop(0, rows // chunk, step, 0)


def encoded_body(n, parts, gathered, *refs):
    pool_ref, hidden_ref, kv0_ref, kv1_ref = refs[:4]
    if gathered:
        down, enc_ref, out0_ref, out1_ref = refs[4:]
        weight = down[...]
    else:
        pieces = refs[4 : 4 + parts]
        enc_ref, out0_ref, out1_ref, down, sems = refs[4 + parts :]
        cols = pieces[0].shape[-1]
        s, g, m = (lax.axis_index(a) for a in ("section", "dp", "mp"))
        copies = []
        for i, piece in enumerate(pieces):
            half, dg = divmod(i, parts // 2)
            place = (s ^ half) * (parts // 2) + (g ^ dg)
            where = pl.ds(pl.multiple_of(place * cols, cols), cols)
            for dz in range(n):
                copies.append(
                    pltpu.make_async_copy(
                        piece.at[dz], down.at[m ^ dz, :, where], sems.at[i * n + dz]
                    )
                )
        for copy in copies:
            copy.start()
        for copy in copies:
            copy.wait()
    count, length, width = enc_ref.shape
    group = 2

    def step(i, _):
        here = pl.ds(pl.multiple_of(i * group * length, group * length), group * length)
        there = pl.ds(i * group, group)
        weight = down[...].reshape(width, hidden_ref.shape[1])
        enc = pool_ref[here, :].astype(F32) + mm(hidden_ref[here, :], weight, NTR)
        enc = enc.astype(BF16)
        enc_ref[there] = enc.reshape(group, length, width)
        out0_ref[there] = mm(enc, kv0_ref[...]).astype(BF16).reshape(group, length, -1)
        out1_ref[there] = mm(enc, kv1_ref[...]).astype(BF16).reshape(group, length, -1)
        return 0

    lax.fori_loop(0, count // group, step, 0)


def gather_slots(pool, ids_ref, micro, tract, slots, block):
    for k in range(slots):
        block[k * NT : (k + 1) * NT, :] = pool[ids_ref[micro, tract, k]]


def probabilities(queries, keys, used):
    scores = mm(queries, keys, NTR)
    lane = lax.broadcasted_iota(jnp.int32, scores.shape, 1)
    scores = jnp.where(lane < used * NT, scores, -1e30)
    powers = jnp.exp(scores - jnp.max(scores, axis=-1, keepdims=True))
    return powers / jnp.sum(powers, axis=-1, keepdims=True)


def first_layer_body(n, tracts, slots, *refs):
    ids_ref, counts_ref, gain_ref, wq_ref = refs[:4]
    pieces, (own, other) = refs[4 : 4 + n], refs[4 + n : 6 + n]
    att_ref, query_ref, probs_ref, pool, block, sems = refs[6 + n :]
    copies = load_pool(own, other, pool, sems)
    s, m = lax.axis_index("section"), lax.axis_index("mp")
    rows, feats = pieces[0].shape
    cols = wq_ref.shape[1]
    total = jnp.zeros((rows, 1), F32)
    for d in range(n):
        wide = pieces[d][...].astype(F32)
        total = total + jnp.sum(wide * wide, axis=-1, keepdims=True)
    scale = lax.rsqrt(total / (n * feats) + EPSILON)
    raw = jnp.zeros((rows, cols), F32)
    for d in range(n):
        source = m ^ d
        normed = (pieces[d][...].astype(F32) * scale * gain_ref[source]).astype(BF16)
        here = pl.ds(pl.multiple_of(source * feats, feats), feats)
        raw = raw + mm(normed, wq_ref[here, :])
    query_ref[...] = (raw * SCALE).astype(BF16)
    for copy in copies:
        copy.wait()
    length = rows // tracts
    heads = cols // HEAD
    for c in range(tracts):
        gather_slots(pool, ids_ref, s, c, slots, block)
        here = slice(c * length, (c + 1) * length)
        for h in range(heads):
            there = slice(h * HEAD, (h + 1) * HEAD)
            probs = probabilities(query_ref[here, there], block[:, there], counts_ref[s, c])
            probs_ref[c * heads + h] = probs
            vals = block[:, cols + h * HEAD : cols + (h + 1) * HEAD]
            att_ref[here, there] = mm(probs.astype(BF16), vals).astype(BF16)


def between_body(n, *refs):
    gain_ref, own_ref, wout_ref, wq_ref = refs[:4]
    pieces = refs[4 : 4 + n]
    rows_ref, messages = refs[4 + n], refs[5 + n :]
    m = lax.axis_index("mp")
    cols = pieces[0].shape[1]
    rows = own_ref.shape[0]
    wide = own_ref[...].astype(F32)
    for d in range(n):
        here = pl.ds(pl.multiple_of((m ^ d) * cols, cols), cols)
        wide = wide + mm(pieces[d][...], wout_ref[here, :])
    rounded = wide.astype(BF16)
    rows_ref[...] = rounded
    wide = rounded.astype(F32)
    square = to_row(jnp.sum(wide * wide, axis=-1, keepdims=True))
    high = square.astype(BF16).astype(F32)
    index = lax.broadcasted_iota(jnp.int32, (PAD, rows), 0)
    extra = jnp.where(index == 0, high, jnp.where(index == 1, square - high, 0.0)).astype(BF16)
    gained = (wide * gain_ref[m]).astype(BF16)
    for d in range(n):
        messages[d][:rows, :] = mm(gained, wq_ref[d]).astype(BF16)
        messages[d][rows:, :] = extra


def last_layer_body(n, width, tracts, slots, *refs):
    ids_ref, counts_ref = refs[:2]
    messages, grads = refs[2 : 2 + n], refs[2 + n : 2 + 2 * n]
    own, other, dkv_ref, out_ref, scale_ref, raw_ref, query_ref, att_ref, pool, block, sems = refs[
        2 + 2 * n :
    ]
    copies = load_pool(own, other, pool, sems)
    s = lax.axis_index("section")
    rows, cols = grads[0].shape
    raw = jnp.zeros((rows, cols), F32)
    square = jnp.zeros((1, rows), F32)
    grad = jnp.zeros((rows, cols), F32)
    for d in range(n):
        raw = raw + messages[d][:rows, :].astype(F32)
        extra = messages[d][rows:, :].astype(F32)
        square = square + extra[0:1, :] + extra[1:2, :]
        grad = grad + grads[d][...].astype(F32)
    scale = lax.rsqrt(to_column(square) / width + EPSILON)
    scale_ref[...] = jnp.broadcast_to(scale, scale_ref.shape)
    raw = raw * scale
    raw_ref[...] = raw
    query_ref[...] = (raw * SCALE).astype(BF16)
    att_ref[...] = grad.astype(BF16)
    for copy in copies:
        copy.wait()
    length = rows // tracts
    heads = cols // HEAD
    for c in range(tracts):
        gather_slots(pool, ids_ref, s, c, slots, block)
        here = slice(c * length, (c + 1) * length)
        slot_rows = slice(c * slots * NT, (c + 1) * slots * NT)
        for h in range(heads):
            there = slice(h * HEAD, (h + 1) * HEAD)
            beyond = slice(cols + h * HEAD, cols + (h + 1) * HEAD)
            queries, keys = query_ref[here, there], block[:, there]
            probs = probabilities(queries, keys, counts_ref[s, c])
            grad_att = att_ref[here, there]
            grad_probs = mm(grad_att, block[:, beyond], NTR)
            inner = jnp.sum(probs * grad_probs, axis=-1, keepdims=True)
            scores = (probs * (grad_probs - inner)).astype(BF16)
            dkv_ref[slot_rows, there] = mm(scores, queries, TNR).astype(BF16)
            dkv_ref[slot_rows, beyond] = mm(probs.astype(BF16), grad_att, TNR).astype(BF16)
            out_ref[here, there] = (mm(scores, keys) * SCALE).astype(BF16)
    part = jnp.sum(out_ref[:rows, :].astype(F32) * raw_ref[...], axis=-1, keepdims=True)
    index = lax.broadcasted_iota(jnp.int32, (PAD, rows), 0)
    out_ref[rows:, :] = jnp.where(index == 0, to_row(part), 0.0).astype(BF16)


def weight_grads(enc_ref, dkv_ref, key_ref, value_ref):
    cols = key_ref.shape[1]
    for r in range(0, enc_ref.shape[0], NT):
        total = mm(enc_ref[r : r + NT, :], dkv_ref[...])
        key_ref[r : r + NT, :] = total[:, :cols].astype(BF16)
        value_ref[r : r + NT, :] = total[:, cols:].astype(BF16)


def last_grads_body(tracts, slots, ids_ref, dkv_ref, own, other, enc_ref, key_ref, value_ref, pool, sems):
    copies = load_pool(own, other, pool, sems)
    s = lax.axis_index("section")
    for copy in copies:
        copy.wait()
    for c in range(tracts):
        for k in range(slots):
            place = (c * slots + k) * NT
            enc_ref[:, place : place + NT] = pool[ids_ref[s, c, k]].T
    weight_grads(enc_ref, dkv_ref, key_ref, value_ref)


def back_between_body(n, width, *refs):
    gain_ref, rows_ref, og_ref, scale_ref, wq_ref, wout_ref = refs[:6]
    pieces, messages = refs[6 : 6 + n], refs[6 + n :]
    s, m = lax.axis_index("section"), lax.axis_index("mp")
    rows, feats = rows_ref.shape
    cols = pieces[0].shape[1]
    normed = jnp.zeros((rows, feats), F32)
    total = jnp.zeros((1, rows), F32)
    for d in range(n):
        normed = normed + mm(pieces[d][:rows, :], wq_ref[d], NTR)
        total = total + pieces[d][rows:, :].astype(F32)[0:1, :]
    scale = scale_ref[:, 0:1]
    wide = rows_ref[...].astype(F32)
    grad = og_ref[s].astype(F32) + scale * gain_ref[m] * normed
    grad = grad - wide * (scale * scale * (to_column(total) / width))
    grad = grad.astype(BF16)
    for d in range(n):
        here = pl.ds(pl.multiple_of((m ^ d) * cols, cols), cols)
        messages[d][...] = mm(grad, wout_ref[here, :], NTR).astype(BF16)


def out_grad_body(n, *refs):
    og_ref, wout_ref = refs[:2]
    messages = refs[2:]
    s, m = lax.axis_index("section"), lax.axis_index("mp")
    cols = messages[0].shape[1]
    for d in range(n):
        here = pl.ds(pl.multiple_of((m ^ d) * cols, cols), cols)
        messages[d][...] = mm(og_ref[s], wout_ref[here, :], NTR).astype(BF16)


def first_back_body(n, tracts, slots, *refs):
    ids_ref, query_ref, probs_ref, enc_ref = refs[:4]
    grads = refs[4 : 4 + n]
    own, other, key_ref, value_ref, att_ref, dkv_ref, pool, block, sems = refs[4 + n :]
    copies = load_pool(own, other, pool, sems)
    s = lax.axis_index("section")
    rows, cols = query_ref.shape
    grad = jnp.zeros((rows, cols), F32)
    for d in range(n):
        grad = grad + grads[d][...].astype(F32)
    att_ref[...] = grad.astype(BF16)
    for copy in copies:
        copy.wait()
    length = rows // tracts
    heads = cols // HEAD
    for c in range(tracts):
        gather_slots(pool, ids_ref, s, c, slots, block)
        here = slice(c * length, (c + 1) * length)
        slot_rows = slice(c * slots * NT, (c + 1) * slots * NT)
        for h in range(heads):
            there = slice(h * HEAD, (h + 1) * HEAD)
            beyond = slice(cols + h * HEAD, cols + (h + 1) * HEAD)
            probs = probs_ref[c * heads + h]
            grad_att = att_ref[here, there]
            grad_probs = mm(grad_att, block[:, beyond], NTR)
            inner = jnp.sum(probs * grad_probs, axis=-1, keepdims=True)
            scores = (probs * (grad_probs - inner)).astype(BF16)
            dkv_ref[slot_rows, there] = mm(scores, query_ref[here, there], TNR).astype(BF16)
            dkv_ref[slot_rows, beyond] = mm(probs.astype(BF16), grad_att, TNR).astype(BF16)
    weight_grads(enc_ref, dkv_ref, key_ref, value_ref)


def along_mp(value, n):
    return [value] + [xor_move(value, "mp", d) for d in range(1, n)]


def scattered(messages):
    return [messages[0]] + [xor_move(messages[d], "mp", d) for d in range(1, len(messages))]


def over_dp(value, dp):
    if dp != 4:
        return lax.psum(value, "dp")
    half = value.shape[0] // 2
    parts = [value[:half], value[half:]]
    for order in ((1, 2), (2, 1)):
        moved = [xor_move(part, "dp", by) for part, by in zip(parts, order)]
        parts = [
            (a.astype(F32) + b.astype(F32)).astype(BF16) for a, b in zip(parts, moved)
        ]
    return jnp.concatenate(parts, axis=0)


def spread(along, dp):
    planes = [along] + [xor_move(along, "dp", d) for d in range(1, dp)]
    return planes + [swap(plane) for plane in planes]


def on_device(
    segment_input,
    out_grad,
    pool_tokens,
    neighbour_ids,
    neighbour_counts,
    enc_gain,
    enc_up,
    enc_down,
    norm_gain,
    w_query,
    w_key,
    w_value,
    w_out,
):
    n, dp = lax.axis_size("mp"), lax.axis_size("dp")
    s, g = lax.axis_index("section"), lax.axis_index("dp")
    m = lax.axis_index("mp")
    _, _, rows, feats = segment_input.shape
    width = n * feats
    cols = w_query.shape[2]
    half, _, length, enc_width = pool_tokens.shape
    tracts, slots = neighbour_ids.shape[2:]
    ids, counts = neighbour_ids[:, 0], neighbour_counts[:, 0]
    ff = enc_down.shape[0]
    first = s == 0

    def by_layer(own):
        other = swap(own)
        return jnp.where(first, own, other), jnp.where(first, other, own)

    down_t = enc_down.T
    parts = 2 * dp
    shares = (enc_width // n) % 16 == 0 and (enc_width // parts) % 16 == 0 and ff // parts == 128
    if shares:
        place = s * dp + g
        up_rows, down_cols = enc_width // parts, ff // parts
        up_piece = lax.dynamic_slice_in_dim(enc_up, place * up_rows, up_rows, 0)
        down_piece = lax.dynamic_slice_in_dim(down_t, place * down_cols, down_cols, 1)
        up_line = jnp.stack(along_mp(up_piece, n))
        down_piece = after(down_piece, up_line)
        down_line = jnp.stack(along_mp(down_piece, n))
        ups = spread(up_line, dp)
        downs = spread(down_line, dp)
        z_done = down_line
        up_scratch = [
            pltpu.VMEM((n, parts, up_rows, enc_up.shape[1]), BF16),
            pltpu.SemaphoreType.DMA((parts * n,)),
        ]
        down_scratch = [
            pltpu.VMEM((n, enc_width // n, ff), BF16),
            pltpu.SemaphoreType.DMA((parts * n,)),
        ]
        spec = [hbm()] * parts
    else:
        ups = [lax.all_gather(enc_up, "mp", axis=0)]
        downs = [lax.all_gather(down_t, "mp", axis=0, tiled=True)]
        z_done = enc_gain
        up_scratch = down_scratch = []
        spec = [vm()]

    wq0, wq1 = by_layer(w_query[0])
    wout0, wout1 = by_layer(w_out[0])
    kv0, kv1 = by_layer(jnp.concatenate([w_key[0], w_value[0]], axis=1))
    gain0, gain1 = by_layer(norm_gain.reshape(n, 1, feats))

    own_rows = lax.dynamic_index_in_dim(segment_input[:, 0], s, 0, keepdims=False)
    own_rows = after(own_rows, z_done)
    row_pieces = along_mp(own_rows, n)

    half_feats = feats // 2

    def query_share(d):
        start = (m ^ d) * feats + s * half_feats
        return lax.dynamic_slice_in_dim(wq1, start, half_feats, 0)

    shares_out = [query_share(d) for d in range(n)]
    shares_out = list(lax.optimization_barrier(tuple(shares_out) + tuple(row_pieces[1:])))[:n]
    mine = jnp.stack(scattered(shares_out))
    others = swap(mine)
    wq1_rows = jnp.where(
        first, jnp.concatenate([mine, others], 1), jnp.concatenate([others, mine], 1)
    )

    grad_messages = call(
        functools.partial(out_grad_body, n),
        [shape((rows, cols))] * n,
        [vm()] * 2,
        flops=2 * rows * width * cols,
    )(out_grad[:, 0], wout1)
    grad_messages = list(lax.optimization_barrier(tuple(grad_messages) + (mine,)))[:n]
    grad_pieces = scattered(grad_messages)

    pool_rows = pool_tokens[:, 0].reshape(half * length, enc_width)
    hidden = call(
        functools.partial(hidden_body, n, parts, not shares),
        [shape((half * length, ff))],
        [vm(), vm()] + spec,
        up_scratch,
        flops=2 * half * length * enc_width * ff,
    )(pool_rows, enc_gain[None, :], *ups)[0]
    enc_own, pool0_own, pool1_own = call(
        functools.partial(encoded_body, n, parts, not shares),
        [
            shape((half, length, enc_width)),
            shape((half, length, 2 * cols)),
            shape((half, length, 2 * cols)),
        ],
        [vm()] * 4 + spec,
        down_scratch,
        flops=4 * half * length * enc_width * ff,
    )(pool_rows, hidden, kv0, kv1, *downs)
    pool0_other = swap(pool0_own)
    pool1_other = swap(after(pool1_own, pool0_other))
    enc_other = swap(after(enc_own, pool0_other))
    pool_scratch = pltpu.VMEM((2 * half, length, 2 * cols), BF16)
    block_scratch = pltpu.VMEM((slots * NT, 2 * cols), BF16)
    pair = pltpu.SemaphoreType.DMA((2,))
    heads = cols // HEAD
    chunk = rows // tracts
    attention_flops = 2 * rows * slots * NT * cols

    att, query0, probs0 = call(
        functools.partial(first_layer_body, n, tracts, slots),
        [
            shape((rows, cols)),
            shape((rows, cols)),
            shape((tracts * heads, chunk, slots * NT), F32),
        ],
        [smem(), smem(), vm(), vm()] + [vm()] * n + [hbm(), hbm()],
        [pool_scratch, block_scratch, pair],
        flops=2 * rows * width * cols + 2 * attention_flops,
    )(ids, counts, gain0, wq0, *row_pieces, pool0_own, pool0_other)
    att_pieces = along_mp(att, n)
    rows1, *messages = call(
        functools.partial(between_body, n),
        [shape((rows, feats))] + [shape((rows + PAD, cols))] * n,
        [vm()] * (4 + n),
        flops=4 * rows * feats * n * cols,
    )(gain1, own_rows, wout0, wq1_rows, *att_pieces)
    query_pieces = scattered(messages)
    slot_rows = tracts * slots * NT
    dkv1, grad_query, scale1 = call(
        functools.partial(last_layer_body, n, width, tracts, slots),
        [shape((slot_rows, 2 * cols)), shape((rows + PAD, cols)), shape((rows, HEAD), F32)],
        [smem(), smem()] + [vm()] * (2 * n) + [hbm(), hbm()],
        [
            pltpu.VMEM((rows, cols), F32),
            pltpu.VMEM((rows, cols), BF16),
            pltpu.VMEM((rows, cols), BF16),
            pool_scratch,
            block_scratch,
            pair,
        ],
        flops=5 * attention_flops,
    )(ids, counts, *query_pieces, *grad_pieces, pool1_own, pool1_other)
    query_grads = along_mp(grad_query, n)
    enc_slots, key1, value1 = call(
        functools.partial(last_grads_body, tracts, slots),
        [shape((enc_width, slot_rows)), shape((enc_width, cols)), shape((enc_width, cols))],
        [smem(), vm(), hbm(), hbm()],
        [pltpu.VMEM((2 * half, length, enc_width), BF16), pair],
        flops=4 * enc_width * slot_rows * cols,
    )(ids, dkv1, enc_own, enc_other)
    messages = call(
        functools.partial(back_between_body, n, width),
        [shape((rows, cols))] * n,
        [vm()] * (6 + n),
        flops=4 * rows * feats * n * cols,
    )(gain1, rows1, out_grad[:, 0], scale1, wq1_rows, wout0, *query_grads)
    grad_pieces0 = scattered(messages)

    def over_cores(key_part, value_part):
        kept = jnp.where(first, key_part, value_part)
        other = swap(jnp.where(first, value_part, key_part))
        return (kept.astype(F32) + other.astype(F32)).astype(BF16)

    sum1 = over_dp(over_cores(key1, value1), dp)
    key0, value0 = call(
        functools.partial(first_back_body, n, tracts, slots),
        [shape((enc_width, cols)), shape((enc_width, cols))],
        [smem(), vm(), vm(), vm()] + [vm()] * n + [hbm(), hbm()],
        [
            pltpu.VMEM((rows, cols), BF16),
            pltpu.VMEM((slot_rows, 2 * cols), BF16),
            pool_scratch,
            block_scratch,
            pair,
        ],
        flops=3 * attention_flops + 4 * enc_width * slot_rows * cols,
    )(ids, query0, probs0, enc_slots, *grad_pieces0, pool0_own, pool0_other)
    sum0 = over_dp(over_cores(key0, value0), dp)
    received = swap(jnp.where(first, sum1, sum0))
    key_total = jnp.where(first, sum0, received)
    value_total = jnp.where(first, received, sum1)
    return (key_total[None], value_total[None])


def solution(mesh):
    placed = (
        P(None, "dp", None, "mp"),
        P(None, "dp", None, "mp"),
        P("section", "dp", None, None),
        P(None, "dp", None, None),
        P(None, "dp", None),
        P(),
        P(None, "mp"),
        P(None, "mp"),
        P("section", None),
        P("section", None, "mp"),
        P("section", None, "mp"),
        P("section", None, "mp"),
        P("section", None, "mp"),
    )
    return jax.shard_map(
        on_device,
        mesh=mesh,
        in_specs=placed,
        out_specs=(P("section", None, "mp"), P("section", None, "mp")),
        check_vma=False,
    )
```

time: 753 us -> 238 us (0.32)
  waiting for transfers between devices: 298 us -> 90.4 us
  local copies, waits for them, and re-layouts: 169 us -> 8.11 us
  blocking collectives: 123 us -> 0 us
  matrix products: 100 us -> 0 us
  Pallas kernels: 0 us -> 62.8 us
  starting transfers between devices: 15.1 us -> 58.6 us
  other arithmetic: 29.3 us -> 15.6 us
  between operations: 14 us -> 1.2 us
    all_gather x8 -> x0, waiting for transfers between devices: 178 us -> none  [the longest x7 178 us: collect(): return lax.all_gather(tensor, 'mp', axis=1, tiled=True)]
    all_gather x9 -> x0, blocking collectives: 123 us -> none  [the longest x3 46.6 us: collect(): return lax.all_gather(tensor, 'mp', axis=1, tiled=True)]
    ppermute x6 -> x60, waiting for transfers between devices: 0.02 us -> 90.4 us  [xor_move(): return lax.ppermute(value, axis, [(i, i ^ by) for i in range(count)])]
    dot_general x36 -> x0, matrix products: 89.1 us -> none  [the longest x6 12.7 us: front(): query_raw = jnp.dot(normed, query_cols, preferred_element_type=jnp.float32)]
    all_to_all x2 -> x0, waiting for transfers between devices: 69.6 us -> none  [the longest x1 49.9 us: on_device(): lax.all_to_all(out_cols, 'mp', split_axis=0, concat_axis=1, tiled=True)]
    pallas_call x0 -> x9, Pallas kernels: none -> 62.8 us  [the longest x1 11 us: on_device(): call(functools.partial(encoded_body, n, parts, not shares), [shape((half,...]
    dynamic_update_slice x8 -> x0, local copies, waits for them, and re-layouts: 55.2 us -> none  [one_shard(): lax.dynamic_update_slice(whole_pool, shard_block, (row_start, col_start))]
    ppermute x6 -> x60, starting transfers between devices: 7.76 us -> 58.6 us  [xor_move(): return lax.ppermute(value, axis, [(i, i ^ by) for i in range(count)])]
  transfers between devices with their start and end apart: 17 -> 60, of which waited for: 10 -> 24; matrix products, arithmetic and copies ran while one was open for 13% -> 7% of each run, Pallas kernels for 0% -> 27%
where the time goes in v1:
time: 238 us; the launch traced here: 237 us
  waiting for transfers between devices  90.4 us (38%)
  Pallas kernels  62.8 us (26%)
  starting transfers between devices  58.6 us (25%)
  other arithmetic  15.6 us (7%)
  local copies, waits for them, and re-layouts  8.11 us (3%)
    ppermute x60, waiting for transfers between devices, xor_move(): return lax.ppermute(value, axis, [(i, i ^ by) for i in range(count)])  90.4 us
    ppermute x60, starting transfers between devices, xor_move(): return lax.ppermute(value, axis, [(i, i ^ by) for i in range(count)])  58.6 us
    pallas_call x1, Pallas kernels, on_device(): call(functools.partial(encoded_body, n, parts, not shares), [shape((half,...  11 us
    pallas_call x1, Pallas kernels, on_device(): call(functools.partial(first_back_body, n, tracts, slots), [shape((enc_wi...  9.9 us
    pallas_call x1, Pallas kernels, on_device(): call(functools.partial(last_layer_body, n, width, tracts, slots), [shape(...  8.89 us
    pallas_call x1, Pallas kernels, on_device(): call(functools.partial(hidden_body, n, parts, not shares), [shape((half *...  8.41 us
    pallas_call x1, Pallas kernels, on_device(): call(functools.partial(last_grads_body, tracts, slots), [shape((enc_width...  7.83 us
    pallas_call x1, Pallas kernels, on_device(): call(functools.partial(first_layer_body, n, tracts, slots), [shape((rows,...  7.38 us
  transfers between devices with their start and end apart: 60, of which 24 were waited for; matrix products, arithmetic and copies ran while one was open for 7% of the time, Pallas kernels for 27%

profile of v1, /device:TPU:0, one launch (start us, length us, event | category | flops | bytes accessed | tf_op | source)
XLA Modules:
  0.0 236.7 jit_solution(11072695301253259355)
XLA Ops:
  2.2 4.0 %collective-permute-start.3 = (bf16[112,256]{1,0:T(8,128)(2,1)}, bf16[112,256]{1,0:T(8,128)(2,1)S(1)}, u32[]{:S(2)}, u32[]{:S(2)}) collective-permute-start(bf16[112,256]{1,0:T(8,128)(2,1)} %constant_dynamic-slice_fusion.4), channel_id=1, source_target_pairs={{0,2},{1,3},{2,0},{3,1},{4,6},{5,7},{6,4},{7,5},{8,10},{9,11},{10,... | collective-permute-start | bytes 172040 | tf_op jit(solution)/shard_map/ppermute | solution.py:30
  10.8 3.4 %collective-permute-done.4 = bf16[112,256]{1,0:T(8,128)(2,1)} collective-permute-done((bf16[112,256]{1,0:T(8,128)(2,1)}, bf16[112,256]{1,0:T(8,128)(2,1)}, u32[]{:S(2)}, u32[]{:S(2)}) %collective-permute-start.4) | collective-permute-done | bytes 57376 | tf_op jit(solution)/shard_map/ppermute | solution.py:30
  15.0 2.5 %collective-permute-start.13 = (bf16[4,112,256]{2,1,0:T(8,128)(2,1)S(1)}, bf16[4,112,256]{2,1,0:T(8,128)(2,1)S(1)}, u32[]{:S(2)}, u32[]{:S(2)}) collective-permute-start(bf16[4,112,256]{2,1,0:T(8,128)(2,1)S(1)} %pad_maximum_fusion.4.refs_2_), channel_id=1, source_target_pairs={{0,12},{4,8},{8,4},{12,0},{1,13},{5,9},{9,5},{13,1},{2,14},{6,10},... | collective-permute-start | bytes 688136 | tf_op jit(solution)/shard_map/ppermute | solution.py:30
  20.3 5.4 %collective-permute-done.7 = bf16[224,128]{1,0:T(8,128)(2,1)S(1)} collective-permute-done((bf16[224,128]{1,0:T(8,128)(2,1)S(1)}, bf16[224,128]{1,0:T(8,128)(2,1)S(1)}, u32[]{:S(2)}, u32[]{:S(2)}) %collective-permute-start.7) | collective-permute-done | bytes 57376 | tf_op jit(solution)/shard_map/ppermute | solution.py:30
  25.7 5.1 %collective-permute-done.6 = bf16[224,128]{1,0:T(8,128)(2,1)S(1)} collective-permute-done((bf16[224,128]{1,0:T(8,128)(2,1)S(1)}, bf16[224,128]{1,0:T(8,128)(2,1)S(1)}, u32[]{:S(2)}, u32[]{:S(2)}) %collective-permute-start.6) | collective-permute-done | bytes 57376 | tf_op jit(solution)/shard_map/ppermute | solution.py:30
  30.8 4.2 %collective-permute-done.5 = bf16[224,128]{1,0:T(8,128)(2,1)S(1)} collective-permute-done((bf16[224,128]{1,0:T(8,128)(2,1)S(1)}, bf16[224,128]{1,0:T(8,128)(2,1)S(1)}, u32[]{:S(2)}, u32[]{:S(2)}) %collective-permute-start.5) | collective-permute-done | bytes 57376 | tf_op jit(solution)/shard_map/ppermute | solution.py:30
  36.7 2.5 %collective-permute-start.21 = (bf16[4,224,128]{2,1,0:T(8,128)(2,1)}, bf16[4,224,128]{2,1,0:T(8,128)(2,1)}, u32[]{:S(2)}, u32[]{:S(2)}) collective-permute-start(bf16[4,224,128]{2,1,0:T(8,128)(2,1)} %pad_maximum_fusion.5.refs_4_), channel_id=1, source_target_pairs={{0,12},{4,8},{8,4},{12,0},{1,13},{5,9},{9,5},{13,1},{2,14},{6,10},... | collective-permute-start | bytes 688136 | tf_op jit(solution)/shard_map/ppermute | solution.py:30
  41.8 8.4 %shard_map.140.refs_1_ = bf16[1024,1024]{1,0:T(8,128)(2,1)} custom-call(bf16[1024,896]{1,0:T(8,128)(2,1)} %bitcast.63, f32[1,896]{1,0:T(1,128)} %broadcast_in_dim.9.refs_1_, bf16[4,112,256]{2,1,0:T(8,128)(2,1)} %copy-done.15, bf16[4,112,256]{2,1,0:T(8,128)(2,1)} %collective-permute-done.11.refs_3_, bf16[4,112,256]{2,1,0:T(8,128)(2,1)} %copy-done.31, ...), custom_call_target="tpu_custom_call" | custom-call | flops 1879048192 | bytes 4194304 | tf_op jit(solution)/shard_map/pallas_call | solution.py:499
  54.0 11.0 %shard_map.141 = (bf16[8,128,896]{2,1,0:T(8,128)(2,1)}, bf16[8,128,512]{2,1,0:T(8,128)(2,1)}, bf16[8,128,512]{2,1,0:T(8,128)(2,1)}) custom-call(bf16[1024,896]{1,0:T(8,128)(2,1)} %bitcast.64, bf16[1024,1024]{1,0:T(8,128)(2,1)} %shard_map.140.refs_1_, bf16[896,512]{1,0:T(8,128)(2,1)} %get-tuple-element.85.refs_2_, ...), custom_call_target="tpu_custom_call" | custom-call | flops 3758096384 | bytes 7864320 | tf_op jit(solution)/shard_map/pallas_call | solution.py:506
  67.2 2.9 %collective-permute-start.8 = (bf16[256,512]{1,0:T(8,128)(2,1)S(1)}, bf16[256,512]{1,0:T(8,128)(2,1)S(1)}, u32[]{:S(2)}, u32[]{:S(2)}) collective-permute-start(bf16[256,512]{1,0:T(8,128)(2,1)S(1)} %dynamic-slice_bitcast_fusion.refs_4_.refs_1_), channel_id=1, source_target_pairs={{0,1},{1,0},{2,3},{3,2},{4,5},{5,4},{6,7},{7,6},{8,9},{9,8},{10,11... | collective-permute-start | bytes 786440 | tf_op jit(solution)/shard_map/ppermute | solution.py:30
  72.6 4.2 %collective-permute-done.10.refs_7_ = bf16[256,512]{1,0:T(8,128)(2,1)S(1)} collective-permute-done((bf16[256,512]{1,0:T(8,128)(2,1)S(1)}, bf16[256,512]{1,0:T(8,128)(2,1)S(1)}, u32[]{:S(2)}, u32[]{:S(2)}) %collective-permute-start.10) | collective-permute-done | bytes 262176 | tf_op jit(solution)/shard_map/ppermute | solution.py:30
  76.8 13.9 %collective-permute-done.9.refs_6_ = bf16[256,512]{1,0:T(8,128)(2,1)S(1)} collective-permute-done((bf16[256,512]{1,0:T(8,128)(2,1)S(1)}, bf16[256,512]{1,0:T(8,128)(2,1)S(1)}, u32[]{:S(2)}, u32[]{:S(2)}) %collective-permute-start.9) | collective-permute-done | bytes 262176 | tf_op jit(solution)/shard_map/ppermute | solution.py:30
  95.1 2.4 %collective-permute-done.28 = bf16[256,256]{1,0:T(8,128)(2,1)S(1)} collective-permute-done((bf16[256,256]{1,0:T(8,128)(2,1)S(1)}, bf16[256,256]{1,0:T(8,128)(2,1)S(1)}, u32[]{:S(2)}, u32[]{:S(2)}) %collective-permute-start.28) | collective-permute-done | bytes 131104 | tf_op jit(solution)/shard_map/ppermute | solution.py:30
  97.5 6.1 %collective-permute-done.29 = bf16[256,256]{1,0:T(8,128)(2,1)S(1)} collective-permute-done((bf16[256,256]{1,0:T(8,128)(2,1)S(1)}, bf16[256,256]{1,0:T(8,128)(2,1)S(1)}, u32[]{:S(2)}, u32[]{:S(2)}) %collective-permute-start.29) | collective-permute-done | bytes 131104 | tf_op jit(solution)/shard_map/ppermute | solution.py:30
  106.3 7.4 %shard_map.142 = (bf16[256,256]{1,0:T(8,128)(2,1)}, bf16[256,256]{1,0:T(8,128)(2,1)}, f32[8,64,512]{2,1,0:T(8,128)}) custom-call(s32[2,4,4]{2,1,0:T(4,128)} %bitcast.55, s32[2,4]{1,0:T(2,128)} %bitcast.61, f32[4,1,512]{2,1,0:T(1,128)} %get-tuple-element.100.refs_2_, bf16[2048,256]{1,0:T(8,128)(2,1)} %get-tuple-element.82.refs_3_, ...), custom_call_target="tpu_custom_call" | custom-call | flops 402653184 | bytes 2621440 | tf_op jit(solution)/shard_map/pallas_call | solution.py:527
  118.1 2.7 %broadcast_select_fusion = (bf16[1024,512]{1,0:T(8,128)(2,1)}, bf16[1024,512]{1,0:T(8,128)(2,1)}) fusion(bf16[1024,512]{1,0:T(8,128)(2,1)} %collective-permute-done.27, pred[]{:T(512)S(6)} %eq.3, bf16[1,1024,512]{2,1,0:T(8,128)(2,1)S(1)} %copy-done.9), kind=kLoop, calls=%fused_computation.1 | loop fusion | flops 1048576 | bytes 4194305 | tf_op jit(solution)/shard_map/jit(_where)/select_n | solution.py:434
  120.8 2.6 %shard_map.144 = (bf16[256,256]{1,0:T(8,128)(2,1)}, bf16[256,256]{1,0:T(8,128)(2,1)}, bf16[256,256]{1,0:T(8,128)(2,1)}, bf16[256,256]{1,0:T(8,128)(2,1)}) custom-call(bf16[2,256,512]{2,1,0:T(8,128)(2,1)} %bitcast.34, bf16[1024,512]{1,0:T(8,128)(2,1)} %get-tuple-element.80.refs_1_), custom_call_target="tpu_custom_call" | custom-call | flops 268435456 | bytes 1048576 | tf_op jit(solution)/shard_map/pallas_call | solution.py:489
  123.4 4.2 %collective-permute-start.38 = (bf16[256,256]{1,0:T(8,128)(2,1)}, bf16[256,256]{1,0:T(8,128)(2,1)S(1)}, u32[]{:S(2)}, u32[]{:S(2)}) collective-permute-start(bf16[256,256]{1,0:T(8,128)(2,1)} %get-tuple-element.60), channel_id=1, source_target_pairs={{0,1},{1,0},{2,3},{3,2},{4,5},{5,4},{6,7},{7,6},{8,9},{9,8},{10,11... | collective-permute-start | bytes 393224 | tf_op jit(solution)/shard_map/ppermute | solution.py:30
  132.7 3.2 %shard_map.143 = (bf16[256,512]{1,0:T(8,128)(2,1)}, bf16[272,256]{1,0:T(8,128)(2,1)}, bf16[272,256]{1,0:T(8,128)(2,1)}, bf16[272,256]{1,0:T(8,128)(2,1)}, bf16[272,256]{1,0:T(8,128)(2,1)}) custom-call(f32[4,1,512]{2,1,0:T(1,128)} %get-tuple-element.101.refs_0_, bf16[256,512]{1,0:T(8,128)(2,1)} %copy-done.1, ...), custom_call_target="tpu_custom_call" | custom-call | flops 536870912 | bytes 1638400 | tf_op jit(solution)/shard_map/pallas_call | solution.py:539
  137.7 3.4 %collective-permute-done.39.refs_8_ = bf16[256,256]{1,0:T(8,128)(2,1)S(1)} collective-permute-done((bf16[256,256]{1,0:T(8,128)(2,1)}, bf16[256,256]{1,0:T(8,128)(2,1)S(1)}, u32[]{:S(2)}, u32[]{:S(2)}) %collective-permute-start.39) | collective-permute-done | bytes 131104 | tf_op jit(solution)/shard_map/ppermute | solution.py:30
  143.9 9.2 %collective-permute-done.36.refs_4_ = bf16[272,256]{1,0:T(8,128)(2,1)S(1)} collective-permute-done((bf16[272,256]{1,0:T(8,128)(2,1)}, bf16[272,256]{1,0:T(8,128)(2,1)S(1)}, u32[]{:S(2)}, u32[]{:S(2)}) %collective-permute-start.36) | collective-permute-done | bytes 139296 | tf_op jit(solution)/shard_map/ppermute | solution.py:30
  154.1 8.9 %shard_map.145 = (bf16[2048,512]{1,0:T(8,128)(2,1)}, bf16[272,256]{1,0:T(8,128)(2,1)}, f32[256,128]{1,0:T(8,128)}) custom-call(s32[2,4,4]{2,1,0:T(4,128)} %bitcast.56, s32[2,4]{1,0:T(2,128)} %bitcast.62, bf16[272,256]{1,0:T(8,128)(2,1)} %get-tuple-element.51.refs_2_, bf16[272,256]{1,0:T(8,128)(2,1)} %copy-done.19, bf16[272,256]{1,0:T(8,128)(2,1)} %copy-done.20, ...), custom_call_target="tpu_custom_call" | custom-call | flops 335544320 | bytes 4734976 | tf_op jit(solution)/shard_map/pallas_call | solution.py:547
  164.9 3.0 %collective-permute-start.44 = (bf16[272,256]{1,0:T(8,128)(2,1)}, bf16[272,256]{1,0:T(8,128)(2,1)S(1)}, u32[]{:S(2)}, u32[]{:S(2)}) collective-permute-start(bf16[272,256]{1,0:T(8,128)(2,1)} %get-tuple-element.71.refs_6_), channel_id=1, source_target_pairs={{0,2},{1,3},{2,0},{3,1},{4,6},{5,7},{6,4},{7,5},{8,10},{9,11},{10,... | collective-permute-start | bytes 417800 | tf_op jit(solution)/shard_map/ppermute | solution.py:30
  168.0 2.9 %collective-permute-done.45.refs_9_ = bf16[272,256]{1,0:T(8,128)(2,1)S(1)} collective-permute-done((bf16[272,256]{1,0:T(8,128)(2,1)}, bf16[272,256]{1,0:T(8,128)(2,1)S(1)}, u32[]{:S(2)}, u32[]{:S(2)}) %collective-permute-start.45) | collective-permute-done | bytes 139296 | tf_op jit(solution)/shard_map/ppermute | solution.py:30
  170.9 8.6 %collective-permute-done.44.refs_8_ = bf16[272,256]{1,0:T(8,128)(2,1)S(1)} collective-permute-done((bf16[272,256]{1,0:T(8,128)(2,1)}, bf16[272,256]{1,0:T(8,128)(2,1)S(1)}, u32[]{:S(2)}, u32[]{:S(2)}) %collective-permute-start.44) | collective-permute-done | bytes 139296 | tf_op jit(solution)/shard_map/ppermute | solution.py:30
  180.3 3.6 %shard_map.147 = (bf16[256,256]{1,0:T(8,128)(2,1)}, bf16[256,256]{1,0:T(8,128)(2,1)}, bf16[256,256]{1,0:T(8,128)(2,1)}, bf16[256,256]{1,0:T(8,128)(2,1)}) custom-call(f32[4,1,512]{2,1,0:T(1,128)} %get-tuple-element.101.refs_0_, bf16[256,512]{1,0:T(8,128)(2,1)} %get-tuple-element.69.refs_1_, bf16[2,256,512]{2,1,0:T(8,128)(2,1)} %bitcast.35, ...), custom_call_target="tpu_custom_call" | custom-call | flops 536870912 | bytes 1048576 | tf_op jit(solution)/shard_map/pallas_call | solution.py:569
  183.8 2.4 %collective-permute-start.47 = (bf16[256,256]{1,0:T(8,128)(2,1)}, bf16[256,256]{1,0:T(8,128)(2,1)S(1)}, u32[]{:S(2)}, u32[]{:S(2)}) collective-permute-start(bf16[256,256]{1,0:T(8,128)(2,1)} %get-tuple-element.74), channel_id=1, source_target_pairs={{0,2},{1,3},{2,0},{3,1},{4,6},{5,7},{6,4},{7,5},{8,10},{9,11},{10,... | collective-permute-start | bytes 393224 | tf_op jit(solution)/shard_map/ppermute | solution.py:30
  188.2 7.8 %shard_map.146 = (bf16[896,2048]{1,0:T(8,128)(2,1)}, bf16[896,256]{1,0:T(8,128)(2,1)}, bf16[896,256]{1,0:T(8,128)(2,1)}) custom-call(s32[2,4,4]{2,1,0:T(4,128)} %bitcast.57, bf16[2048,512]{1,0:T(8,128)(2,1)} %get-tuple-element.65.dkv_ref, bf16[8,128,896]{2,1,0:T(8,128)(2,1)} %get-tuple-element.67.own, bf16[8,128,896]{2,1,0:T(8,128)(2,1)} %collective-permute-done.42.other), custom_call_target="tpu_custom_call" | custom-call | flops 1879048192 | bytes 9175040 | tf_op jit(solution)/shard_map/pallas_call | solution.py:562
  198.0 9.9 %shard_map.148 = (bf16[896,256]{1,0:T(8,128)(2,1)}, bf16[896,256]{1,0:T(8,128)(2,1)}) custom-call(s32[2,4,4]{2,1,0:T(4,128)} %bitcast.58, bf16[256,256]{1,0:T(8,128)(2,1)} %get-tuple-element.44.refs_1_, f32[8,64,512]{2,1,0:T(8,128)} %get-tuple-element.45.refs_2_, bf16[896,2048]{1,0:T(8,128)(2,1)} %get-tuple-element.68.refs_3_, ...), custom_call_target="tpu_custom_call" | custom-call | flops 2080374784 | bytes 1835008 | tf_op jit(solution)/shard_map/pallas_call | solution.py:583
  214.3 4.1 %collective-permute-done.55 = bf16[448,256]{1,0:T(8,128)(2,1)S(1)} collective-permute-done((bf16[448,256]{1,0:T(8,128)(2,1)S(1)}, bf16[448,256]{1,0:T(8,128)(2,1)S(1)}, u32[]{:S(2)}, u32[]{:S(2)}) %collective-permute-start.55) | collective-permute-done | bytes 229408 | tf_op jit(solution)/shard_map/ppermute | solution.py:30
  226.9 2.8 %collective-permute-done.56 = bf16[448,256]{1,0:T(8,128)(2,1)S(1)} collective-permute-done((bf16[448,256]{1,0:T(8,128)(2,1)S(1)}, bf16[448,256]{1,0:T(8,128)(2,1)S(1)}, u32[]{:S(2)}, u32[]{:S(2)}) %collective-permute-start.56) | collective-permute-done | bytes 229408 | tf_op jit(solution)/shard_map/ppermute | solution.py:30
  229.9 3.5 %collective-permute-done.51 = bf16[448,256]{1,0:T(8,128)(2,1)S(1)} collective-permute-done((bf16[448,256]{1,0:T(8,128)(2,1)S(1)}, bf16[448,256]{1,0:T(8,128)(2,1)S(1)}, u32[]{:S(2)}, u32[]{:S(2)}) %collective-permute-start.51) | collective-permute-done | bytes 229408 | tf_op jit(solution)/shard_map/ppermute | solution.py:30
  (210 shorter events, 69.2 us)
Async XLA Ops:
  9.1 42.3 %collective-permute-start.18 = (bf16[896,512]{1,0:T(8,128)(2,1)S(1)}, bf16[896,512]{1,0:T(8,128)(2,1)S(1)}, u32[]{:S(2)}, u32[]{:S(2)}) collective-permute-start(bf16[896,512]{1,0:T(8,128)(2,1)S(1)} %pad_maximum_fusion), channel_id=1, source_target_pairs={{0,16},{16,0},{1,17},{17,1},{2,18},{18,2},{3,19},{19,3},{4,20},{20... | collective-permute-start | bytes 2752520 | tf_op jit(solution)/shard_map/ppermute | solution.py:30
  15.0 19.9 %collective-permute-start.13 = (bf16[4,112,256]{2,1,0:T(8,128)(2,1)S(1)}, bf16[4,112,256]{2,1,0:T(8,128)(2,1)S(1)}, u32[]{:S(2)}, u32[]{:S(2)}) collective-permute-start(bf16[4,112,256]{2,1,0:T(8,128)(2,1)S(1)} %pad_maximum_fusion.4.refs_2_), channel_id=1, source_target_pairs={{0,12},{4,8},{8,4},{12,0},{1,13},{5,9},{9,5},{13,1},{2,14},{6,10},... | collective-permute-start | bytes 688136 | tf_op jit(solution)/shard_map/ppermute | solution.py:30
  17.5 17.9 %collective-permute-start.12 = (bf16[4,112,256]{2,1,0:T(8,128)(2,1)S(1)}, bf16[4,112,256]{2,1,0:T(8,128)(2,1)S(1)}, u32[]{:S(2)}, u32[]{:S(2)}) collective-permute-start(bf16[4,112,256]{2,1,0:T(8,128)(2,1)S(1)} %pad_maximum_fusion.4.refs_2_), channel_id=1, source_target_pairs={{0,8},{4,12},{8,0},{12,4},{1,9},{5,13},{9,1},{13,5},{2,10},{6,14},... | collective-permute-start | bytes 688136 | tf_op jit(solution)/shard_map/ppermute | solution.py:30
  18.1 17.5 %collective-permute-start.11 = (bf16[4,112,256]{2,1,0:T(8,128)(2,1)S(1)}, bf16[4,112,256]{2,1,0:T(8,128)(2,1)}, u32[]{:S(2)}, u32[]{:S(2)}) collective-permute-start(bf16[4,112,256]{2,1,0:T(8,128)(2,1)S(1)} %pad_maximum_fusion.4.refs_2_), channel_id=1, source_target_pairs={{0,4},{4,0},{8,12},{12,8},{1,5},{5,1},{9,13},{13,9},{2,6},{6,2},{1... | collective-permute-start | bytes 688136 | tf_op jit(solution)/shard_map/ppermute | solution.py:30
  36.7 13.5 %collective-permute-start.21 = (bf16[4,224,128]{2,1,0:T(8,128)(2,1)}, bf16[4,224,128]{2,1,0:T(8,128)(2,1)}, u32[]{:S(2)}, u32[]{:S(2)}) collective-permute-start(bf16[4,224,128]{2,1,0:T(8,128)(2,1)} %pad_maximum_fusion.5.refs_4_), channel_id=1, source_target_pairs={{0,12},{4,8},{8,4},{12,0},{1,13},{5,9},{9,5},{13,1},{2,14},{6,10},... | collective-permute-start | bytes 688136 | tf_op jit(solution)/shard_map/ppermute | solution.py:30
  39.3 11.6 %collective-permute-start.20 = (bf16[4,224,128]{2,1,0:T(8,128)(2,1)}, bf16[4,224,128]{2,1,0:T(8,128)(2,1)}, u32[]{:S(2)}, u32[]{:S(2)}) collective-permute-start(bf16[4,224,128]{2,1,0:T(8,128)(2,1)} %pad_maximum_fusion.5.refs_4_), channel_id=1, source_target_pairs={{0,8},{4,12},{8,0},{12,4},{1,9},{5,13},{9,1},{13,5},{2,10},{6,14},... | collective-permute-start | bytes 688136 | tf_op jit(solution)/shard_map/ppermute | solution.py:30
  40.7 10.2 %collective-permute-start.19 = (bf16[4,224,128]{2,1,0:T(8,128)(2,1)}, bf16[4,224,128]{2,1,0:T(8,128)(2,1)}, u32[]{:S(2)}, u32[]{:S(2)}) collective-permute-start(bf16[4,224,128]{2,1,0:T(8,128)(2,1)} %pad_maximum_fusion.5.refs_4_), channel_id=1, source_target_pairs={{0,4},{4,0},{8,12},{12,8},{1,5},{5,1},{9,13},{13,9},{2,6},{6,2},{1... | collective-permute-start | bytes 688136 | tf_op jit(solution)/shard_map/ppermute | solution.py:30
  41.8 25.4 %collective-permute-start.1 = (bf16[2048,256]{1,0:T(8,128)(2,1)S(1)}, bf16[2048,256]{1,0:T(8,128)(2,1)}, u32[]{:S(2)}, u32[]{:S(2)}) collective-permute-start(bf16[2048,256]{1,0:T(8,128)(2,1)S(1)} %bitcast.42), channel_id=1, source_target_pairs={{0,16},{16,0},{1,17},{17,1},{2,18},{18,2},{3,19},{19,3},{4,20},{20... | collective-permute-start | bytes 3145736 | tf_op jit(solution)/shard_map/ppermute | solution.py:30
  65.5 50.0 %collective-permute-start.27 = (bf16[1024,512]{1,0:T(8,128)(2,1)S(1)}, bf16[1024,512]{1,0:T(8,128)(2,1)}, u32[]{:S(2)}, u32[]{:S(2)}) collective-permute-start(bf16[1024,512]{1,0:T(8,128)(2,1)S(1)} %bitcast.43), channel_id=1, source_target_pairs={{0,16},{16,0},{1,17},{17,1},{2,18},{18,2},{3,19},{19,3},{4,20},{20... | collective-permute-start | bytes 3145736 | tf_op jit(solution)/shard_map/ppermute | solution.py:30
  65.6 11.1 %collective-permute-start.10 = (bf16[256,512]{1,0:T(8,128)(2,1)S(1)}, bf16[256,512]{1,0:T(8,128)(2,1)S(1)}, u32[]{:S(2)}, u32[]{:S(2)}) collective-permute-start(bf16[256,512]{1,0:T(8,128)(2,1)S(1)} %dynamic-slice_bitcast_fusion.refs_4_.refs_1_), channel_id=1, source_target_pairs={{0,3},{1,2},{2,1},{3,0},{4,7},{5,6},{6,5},{7,4},{8,11},{9,10},{10,... | collective-permute-start | bytes 786440 | tf_op jit(solution)/shard_map/ppermute | solution.py:30
  66.5 24.1 %collective-permute-start.9 = (bf16[256,512]{1,0:T(8,128)(2,1)S(1)}, bf16[256,512]{1,0:T(8,128)(2,1)S(1)}, u32[]{:S(2)}, u32[]{:S(2)}) collective-permute-start(bf16[256,512]{1,0:T(8,128)(2,1)S(1)} %dynamic-slice_bitcast_fusion.refs_4_.refs_1_), channel_id=1, source_target_pairs={{0,2},{1,3},{2,0},{3,1},{4,6},{5,7},{6,4},{7,5},{8,10},{9,11},{10,... | collective-permute-start | bytes 786440 | tf_op jit(solution)/shard_map/ppermute | solution.py:30
  67.2 23.5 %collective-permute-start.8 = (bf16[256,512]{1,0:T(8,128)(2,1)S(1)}, bf16[256,512]{1,0:T(8,128)(2,1)S(1)}, u32[]{:S(2)}, u32[]{:S(2)}) collective-permute-start(bf16[256,512]{1,0:T(8,128)(2,1)S(1)} %dynamic-slice_bitcast_fusion.refs_4_.refs_1_), channel_id=1, source_target_pairs={{0,1},{1,0},{2,3},{3,2},{4,5},{5,4},{6,7},{7,6},{8,9},{9,8},{10,11... | collective-permute-start | bytes 786440 | tf_op jit(solution)/shard_map/ppermute | solution.py:30
  72.4 115.8 %collective-permute-start.42 = (bf16[8,128,896]{2,1,0:T(8,128)(2,1)}, bf16[8,128,896]{2,1,0:T(8,128)(2,1)}, u32[]{:S(2)}, u32[]{:S(2)}) collective-permute-start(bf16[8,128,896]{2,1,0:T(8,128)(2,1)} %get-tuple-element.67.own), channel_id=1, source_target_pairs={{0,16},{16,0},{1,17},{17,1},{2,18},{18,2},{3,19},{19,3},{4,20},{20... | collective-permute-start | bytes 5505032 | tf_op jit(solution)/shard_map/ppermute | solution.py:30
  90.7 12.9 %collective-permute-start.29 = (bf16[256,256]{1,0:T(8,128)(2,1)S(1)}, bf16[256,256]{1,0:T(8,128)(2,1)S(1)}, u32[]{:S(2)}, u32[]{:S(2)}) collective-permute-start(bf16[256,256]{1,0:T(8,128)(2,1)S(1)} %get-tuple-element.48), channel_id=1, source_target_pairs={{0,2},{1,3},{2,0},{3,1},{4,6},{5,7},{6,4},{7,5},{8,10},{9,11},{10,... | collective-permute-start | bytes 393224 | tf_op jit(solution)/shard_map/ppermute | solution.py:30
  93.0 10.6 %collective-permute-start.30 = (bf16[256,256]{1,0:T(8,128)(2,1)S(1)}, bf16[256,256]{1,0:T(8,128)(2,1)S(1)}, u32[]{:S(2)}, u32[]{:S(2)}) collective-permute-start(bf16[256,256]{1,0:T(8,128)(2,1)S(1)} %get-tuple-element.49), channel_id=1, source_target_pairs={{0,3},{1,2},{2,1},{3,0},{4,7},{5,6},{6,5},{7,4},{8,11},{9,10},{10,... | collective-permute-start | bytes 393224 | tf_op jit(solution)/shard_map/ppermute | solution.py:30
  103.7 13.7 %collective-permute-start.31 = (bf16[4,256,256]{2,1,0:T(8,128)(2,1)S(1)}, bf16[4,256,256]{2,1,0:T(8,128)(2,1)S(1)}, u32[]{:S(2)}, u32[]{:S(2)}) collective-permute-start(bf16[4,256,256]{2,1,0:T(8,128)(2,1)S(1)} %pad_maximum_fusion.1), channel_id=1, source_target_pairs={{0,16},{16,0},{1,17},{17,1},{2,18},{18,2},{3,19},{19,3},{4,20},{20... | collective-permute-start | bytes 1572872 | tf_op jit(solution)/shard_map/ppermute | solution.py:30
  104.3 48.8 %collective-permute-start.41 = (bf16[8,128,512]{2,1,0:T(8,128)(2,1)S(1)}, bf16[8,128,512]{2,1,0:T(8,128)(2,1)S(1)}, u32[]{:S(2)}, u32[]{:S(2)}) collective-permute-start(bf16[8,128,512]{2,1,0:T(8,128)(2,1)S(1)} %copy-done.10), channel_id=1, source_target_pairs={{0,16},{16,0},{1,17},{17,1},{2,18},{18,2},{3,19},{19,3},{4,20},{20... | collective-permute-start | bytes 3145736 | tf_op jit(solution)/shard_map/ppermute | solution.py:30
  115.5 14.1 %collective-permute-start.33 = (bf16[256,256]{1,0:T(8,128)(2,1)}, bf16[256,256]{1,0:T(8,128)(2,1)S(1)}, u32[]{:S(2)}, u32[]{:S(2)}) collective-permute-start(bf16[256,256]{1,0:T(8,128)(2,1)} %get-tuple-element.50.refs_4_), channel_id=1, source_target_pairs={{0,2},{1,3},{2,0},{3,1},{4,6},{5,7},{6,4},{7,5},{8,10},{9,11},{10,... | collective-permute-start | bytes 393224 | tf_op jit(solution)/shard_map/ppermute | solution.py:30
  117.4 12.2 %collective-permute-start.32 = (bf16[256,256]{1,0:T(8,128)(2,1)}, bf16[256,256]{1,0:T(8,128)(2,1)S(1)}, u32[]{:S(2)}, u32[]{:S(2)}) collective-permute-start(bf16[256,256]{1,0:T(8,128)(2,1)} %get-tuple-element.50.refs_4_), channel_id=1, source_target_pairs={{0,1},{1,0},{2,3},{3,2},{4,5},{5,4},{6,7},{7,6},{8,9},{9,8},{10,11... | collective-permute-start | bytes 393224 | tf_op jit(solution)/shard_map/ppermute | solution.py:30
  123.4 12.5 %collective-permute-start.38 = (bf16[256,256]{1,0:T(8,128)(2,1)}, bf16[256,256]{1,0:T(8,128)(2,1)S(1)}, u32[]{:S(2)}, u32[]{:S(2)}) collective-permute-start(bf16[256,256]{1,0:T(8,128)(2,1)} %get-tuple-element.60), channel_id=1, source_target_pairs={{0,1},{1,0},{2,3},{3,2},{4,5},{5,4},{6,7},{7,6},{8,9},{9,8},{10,11... | collective-permute-start | bytes 393224 | tf_op jit(solution)/shard_map/ppermute | solution.py:30
  129.6 11.4 %collective-permute-start.39 = (bf16[256,256]{1,0:T(8,128)(2,1)}, bf16[256,256]{1,0:T(8,128)(2,1)S(1)}, u32[]{:S(2)}, u32[]{:S(2)}) collective-permute-start(bf16[256,256]{1,0:T(8,128)(2,1)} %get-tuple-element.61), channel_id=1, source_target_pairs={{0,2},{1,3},{2,0},{3,1},{4,6},{5,7},{6,4},{7,5},{8,10},{9,11},{10,... | collective-permute-start | bytes 393224 | tf_op jit(solution)/shard_map/ppermute | solution.py:30
  129.6 11.4 %collective-permute-start.40 = (bf16[256,256]{1,0:T(8,128)(2,1)}, bf16[256,256]{1,0:T(8,128)(2,1)S(1)}, u32[]{:S(2)}, u32[]{:S(2)}) collective-permute-start(bf16[256,256]{1,0:T(8,128)(2,1)} %get-tuple-element.62), channel_id=1, source_target_pairs={{0,3},{1,2},{2,1},{3,0},{4,7},{5,6},{6,5},{7,4},{8,11},{9,10},{10,... | collective-permute-start | bytes 393224 | tf_op jit(solution)/shard_map/ppermute | solution.py:30
  141.1 12.0 %collective-permute-start.36 = (bf16[272,256]{1,0:T(8,128)(2,1)}, bf16[272,256]{1,0:T(8,128)(2,1)S(1)}, u32[]{:S(2)}, u32[]{:S(2)}) collective-permute-start(bf16[272,256]{1,0:T(8,128)(2,1)} %get-tuple-element.53), channel_id=1, source_target_pairs={{0,2},{1,3},{2,0},{3,1},{4,6},{5,7},{6,4},{7,5},{8,10},{9,11},{10,... | collective-permute-start | bytes 417800 | tf_op jit(solution)/shard_map/ppermute | solution.py:30
  141.1 12.0 %collective-permute-start.37 = (bf16[272,256]{1,0:T(8,128)(2,1)}, bf16[272,256]{1,0:T(8,128)(2,1)S(1)}, u32[]{:S(2)}, u32[]{:S(2)}) collective-permute-start(bf16[272,256]{1,0:T(8,128)(2,1)} %get-tuple-element.54), channel_id=1, source_target_pairs={{0,3},{1,2},{2,1},{3,0},{4,7},{5,6},{6,5},{7,4},{8,11},{9,10},{10,... | collective-permute-start | bytes 417800 | tf_op jit(solution)/shard_map/ppermute | solution.py:30
  164.9 14.6 %collective-permute-start.44 = (bf16[272,256]{1,0:T(8,128)(2,1)}, bf16[272,256]{1,0:T(8,128)(2,1)S(1)}, u32[]{:S(2)}, u32[]{:S(2)}) collective-permute-start(bf16[272,256]{1,0:T(8,128)(2,1)} %get-tuple-element.71.refs_6_), channel_id=1, source_target_pairs={{0,2},{1,3},{2,0},{3,1},{4,6},{5,7},{6,4},{7,5},{8,10},{9,11},{10,... | collective-permute-start | bytes 417800 | tf_op jit(solution)/shard_map/ppermute | solution.py:30
  168.0 11.6 %collective-permute-start.43 = (bf16[272,256]{1,0:T(8,128)(2,1)}, bf16[272,256]{1,0:T(8,128)(2,1)S(1)}, u32[]{:S(2)}, u32[]{:S(2)}) collective-permute-start(bf16[272,256]{1,0:T(8,128)(2,1)} %get-tuple-element.71.refs_6_), channel_id=1, source_target_pairs={{0,1},{1,0},{2,3},{3,2},{4,5},{5,4},{6,7},{7,6},{8,9},{9,8},{10,11... | collective-permute-start | bytes 417800 | tf_op jit(solution)/shard_map/ppermute | solution.py:30
  183.8 13.4 %collective-permute-start.46 = (bf16[256,256]{1,0:T(8,128)(2,1)}, bf16[256,256]{1,0:T(8,128)(2,1)S(1)}, u32[]{:S(2)}, u32[]{:S(2)}) collective-permute-start(bf16[256,256]{1,0:T(8,128)(2,1)} %get-tuple-element.73), channel_id=1, source_target_pairs={{0,1},{1,0},{2,3},{3,2},{4,5},{5,4},{6,7},{7,6},{8,9},{9,8},{10,11... | collective-permute-start | bytes 393224 | tf_op jit(solution)/shard_map/ppermute | solution.py:30
  183.8 13.4 %collective-permute-start.47 = (bf16[256,256]{1,0:T(8,128)(2,1)}, bf16[256,256]{1,0:T(8,128)(2,1)S(1)}, u32[]{:S(2)}, u32[]{:S(2)}) collective-permute-start(bf16[256,256]{1,0:T(8,128)(2,1)} %get-tuple-element.74), channel_id=1, source_target_pairs={{0,2},{1,3},{2,0},{3,1},{4,6},{5,7},{6,4},{7,5},{8,10},{9,11},{10,... | collective-permute-start | bytes 393224 | tf_op jit(solution)/shard_map/ppermute | solution.py:30
  186.2 11.1 %collective-permute-start.48 = (bf16[256,256]{1,0:T(8,128)(2,1)}, bf16[256,256]{1,0:T(8,128)(2,1)S(1)}, u32[]{:S(2)}, u32[]{:S(2)}) collective-permute-start(bf16[256,256]{1,0:T(8,128)(2,1)} %get-tuple-element.75), channel_id=1, source_target_pairs={{0,3},{1,2},{2,1},{3,0},{4,7},{5,6},{6,5},{7,4},{8,11},{9,10},{10,... | collective-permute-start | bytes 393224 | tf_op jit(solution)/shard_map/ppermute | solution.py:30
  197.1 12.5 %collective-permute-start.54 = (bf16[896,256]{1,0:T(8,128)(2,1)S(1)}, bf16[896,256]{1,0:T(8,128)(2,1)S(1)}, u32[]{:S(2)}, u32[]{:S(2)}) collective-permute-start(bf16[896,256]{1,0:T(8,128)(2,1)S(1)} %broadcast_select_fusion.7), channel_id=1, source_target_pairs={{0,16},{16,0},{1,17},{17,1},{2,18},{18,2},{3,19},{19,3},{4,20},{20... | collective-permute-start | bytes 1376264 | tf_op jit(solution)/shard_map/ppermute | solution.py:30
  213.0 10.3 %collective-permute-start.50 = (bf16[448,256]{1,0:T(8,128)(2,1)S(1)}, bf16[448,256]{1,0:T(8,128)(2,1)S(1)}, u32[]{:S(2)}, u32[]{:S(2)}) collective-permute-start(bf16[448,256]{1,0:T(8,128)(2,1)S(1)} %get-tuple-element.94), channel_id=1, source_target_pairs={{0,4},{4,0},{8,12},{12,8},{1,5},{5,1},{9,13},{13,9},{2,6},{6,2},{1... | collective-permute-start | bytes 688136 | tf_op jit(solution)/shard_map/ppermute | solution.py:30
  213.6 11.2 %collective-permute-start.52 = (bf16[448,256]{1,0:T(8,128)(2,1)S(1)}, bf16[448,256]{1,0:T(8,128)(2,1)S(1)}, u32[]{:S(2)}, u32[]{:S(2)}) collective-permute-start(bf16[448,256]{1,0:T(8,128)(2,1)S(1)} %get-tuple-element.95), channel_id=1, source_target_pairs={{0,8},{4,12},{8,0},{12,4},{1,9},{5,13},{9,1},{13,5},{2,10},{6,14},... | collective-permute-start | bytes 688136 | tf_op jit(solution)/shard_map/ppermute | solution.py:30
  (70 other events, 614.4 us)

commit v2 on v1

v2 whole, which is shorter than its diff:
```python
import functools

import jax
import jax.numpy as jnp
from jax import lax
from jax.experimental import pallas as pl
from jax.experimental.pallas import tpu as pltpu
from jax.sharding import PartitionSpec as P

HEAD = 128
NT = 128
EPSILON = 1e-05
SCALE = HEAD ** (-0.5)
PAD = 16
VMEM_LIMIT = 20 * 1024 * 1024
ENCODER_LIMIT = 32 * 1024 * 1024

BF16 = jnp.bfloat16
F32 = jnp.float32
NN = (((1,), (0,)), ((), ()))
NTR = (((1,), (1,)), ((), ()))
TNR = (((0,), (0,)), ((), ()))


def mm(a, b, dims=NN):
    return lax.dot_general(a, b, dims, preferred_element_type=F32)


def xor_move(value, axis, by):
    count = lax.axis_size(axis)
    return lax.ppermute(value, axis, [(i, i ^ by) for i in range(count)])


def swap(value):
    return xor_move(value, "section", 1)


def vm():
    return pl.BlockSpec(memory_space=pltpu.VMEM)


def hbm():
    return pl.BlockSpec(memory_space=pl.ANY)


def hbm_only():
    return pl.BlockSpec(memory_space=pltpu.HBM)


def smem():
    return pl.BlockSpec(memory_space=pltpu.SMEM)


def call(body, outs, specs, scratch=(), flops=0, limit=VMEM_LIMIT, deps=(), passing=()):
    count, more, kept, results = len(specs), len(deps), len(passing), len(outs)
    nbytes = sum(o.size * o.dtype.itemsize for o in outs)
    start = count + more + kept

    def kernel(*refs):
        body(*refs[:count], *refs[start : start + results], *refs[start + results + kept :])

    def run(*args):
        return pl.pallas_call(
            kernel,
            out_shape=list(outs) + [shape(x.shape, x.dtype) for x in passing],
            in_specs=list(specs) + [hbm()] * (more + kept),
            out_specs=[vm() for _ in outs] + [hbm()] * kept,
            scratch_shapes=list(scratch),
            input_output_aliases={count + more + i: results + i for i in range(kept)},
            compiler_params=pltpu.CompilerParams(vmem_limit_bytes=limit),
            cost_estimate=pl.CostEstimate(
                flops=flops // 1000, bytes_accessed=nbytes // 1000, transcendentals=0
            ),
        )(*args, *deps, *passing)

    return run


def shape(dims, dtype=BF16):
    return jax.ShapeDtypeStruct(dims, dtype)


def to_row(column):
    rows = column.shape[0]
    here = lax.broadcasted_iota(jnp.int32, (rows, rows), 0)
    there = lax.broadcasted_iota(jnp.int32, (rows, rows), 1)
    return jnp.sum(jnp.where(here == there, column, 0.0), axis=0, keepdims=True)


def to_column(row):
    rows = row.shape[1]
    here = lax.broadcasted_iota(jnp.int32, (rows, rows), 0)
    there = lax.broadcasted_iota(jnp.int32, (rows, rows), 1)
    return jnp.sum(jnp.where(here == there, row, 0.0), axis=1, keepdims=True)


def load_slots(own, other, ids_ref, tracts, slots, blocks, sems, start=0):
    half = own.shape[0]
    span = pl.ds(start, blocks.shape[1])
    s = lax.axis_index("section")
    waits = []
    for c in range(tracts):
        for k in range(slots):
            i = c * slots + k
            place = ids_ref[s, c, k]
            here = place // half == s
            target, sem = blocks.at[pl.ds(i * NT, NT)], sems.at[i]

            @pl.when(here)
            def _(target=target, sem=sem, place=place):
                pltpu.make_async_copy(own.at[place - s * half, :, span], target, sem).start()

            @pl.when(jnp.logical_not(here))
            def _(target=target, sem=sem, place=place):
                pltpu.make_async_copy(other.at[place - (1 - s) * half, :, span], target, sem).start()

            waits.append(pltpu.make_async_copy(own.at[0, :, span], target, sem))
    return waits


def of_layer(layer, own_ref, other_ref, *index):
    index = index or (Ellipsis,)
    own = lax.axis_index("section") == layer
    return jnp.where(own, own_ref[index], other_ref[index])


def pack(value, cols):
    rows, feats = value.shape
    if feats >= cols:
        return jnp.concatenate([value[:, i : i + cols] for i in range(0, feats, cols)], axis=0)
    share = rows * feats // cols
    return jnp.concatenate([value[i : i + share] for i in range(0, rows, share)], axis=1)


def unpack(value, rows, feats):
    cols = value.shape[1]
    if feats >= cols:
        return jnp.concatenate(
            [value[i : i + rows] for i in range(0, value.shape[0], rows)], axis=1
        )
    return jnp.concatenate([value[:, i : i + feats] for i in range(0, cols, feats)], axis=0)


def share_body(up_ref, down_ref, out_ref, sems):
    place = lax.axis_index("section") * lax.axis_size("dp") + lax.axis_index("dp")
    tall = out_ref.shape[0] // 2
    rows = pl.ds(pl.multiple_of(place * tall, tall), tall)
    cols = pl.ds(pl.multiple_of(place * HEAD, HEAD), HEAD)
    copies = [pltpu.make_async_copy(up_ref.at[rows], out_ref.at[pl.ds(0, tall)], sems.at[0])]
    for side in range(2):
        copies.append(
            pltpu.make_async_copy(
                down_ref.at[pl.ds(side * tall, tall), cols],
                out_ref.at[pl.ds(tall, tall), pl.ds(side * HEAD, HEAD)],
                sems.at[1 + side],
            )
        )
    for copy in copies:
        copy.start()
    for copy in copies:
        copy.wait()


def line_body(n, *refs):
    tall = refs[0].shape[0] // 2
    for d in range(n):
        refs[n][d] = refs[d][:tall, :]
        refs[n + 1][d] = refs[d][tall:, :]


def pair_body(*refs):
    for i in range(2):
        refs[4 + i][0] = refs[2 * i][...]
        refs[4 + i][1] = refs[2 * i + 1][...]


def gather_body(up, up1, up2, down, down2, down1, out_ref):
    for base, parts in ((0, (up, up1, up2)), (4, (down, down2, down1))):
        near = 1 if base == 0 else 2
        out_ref[base] = parts[0][...]
        out_ref[base + near] = parts[1][...]
        out_ref[base + 3 - near] = parts[2][0]
        out_ref[base + 3] = parts[2][1]


def shares_body(n, wq_own, wq_other, rows_ref, own_ref, *outs):
    s, m = lax.axis_index("section"), lax.axis_index("mp")
    own_ref[...] = pack(rows_ref[s], outs[0].shape[1])
    tall = outs[0].shape[0]
    for d in range(n):
        start = ((m ^ d) * 2 + s) * tall
        here = pl.ds(pl.multiple_of(start, tall), tall)
        outs[d][...] = of_layer(1, wq_own, wq_other, here, slice(None))


def projection_body(n, *refs):
    for d in range(n):
        refs[n][d] = refs[d][...]


def add_body(count, *refs):
    for i in range(count):
        total = refs[i][...].astype(F32) + refs[count + i][...].astype(F32)
        refs[2 * count + i][...] = total.astype(BF16)


def halves_body(kept_ref, other_ref, top_ref, bottom_ref):
    half = top_ref.shape[0]
    for i, out_ref in enumerate((top_ref, bottom_ref)):
        here = slice(i * half, (i + 1) * half)
        total = kept_ref[here, :].astype(F32) + other_ref[here, :].astype(F32)
        out_ref[...] = total.astype(BF16)


def norm_body(pool_ref, gain_ref, out_ref):
    wide = pool_ref[...].astype(F32)
    scale = lax.rsqrt(jnp.mean(wide * wide, axis=-1, keepdims=True) + EPSILON)
    out_ref[...] = (wide * scale * gain_ref[...]).astype(BF16)


def encoder_body(n, parts, gathered, *refs):
    pool_ref, normed_ref = refs[:2]
    pieces, (enc_ref, hidden, up, down, *sems) = refs[2:4], refs[4:]
    m = lax.axis_index("mp")
    if gathered:
        copies = [[pltpu.make_async_copy(pieces[i], (up, down)[i], sems[0].at[i])] for i in range(2)]
        downs = copies[1]
        ups = copies[:1] + [[]] * (n - 1)
        ups[0][0].start()
        downs[0].start()
    else:
        up_sems, down_sems = sems
        s, g = lax.axis_index("section"), lax.axis_index("dp")
        dp, tall, wide = parts // 2, pieces[0].shape[2], HEAD
        ups, downs = [[] for _ in range(n)], []
        for dz in range(n):
            for i in range(parts):
                half, dg = divmod(i, dp)
                place = (s ^ half) * dp + (g ^ dg)
                ups[dz].append(
                    pltpu.make_async_copy(
                        pieces[half].at[dg, dz], up.at[m ^ dz, place], up_sems.at[i * n + dz]
                    )
                )
                where = pl.ds(pl.multiple_of(place * wide, wide), wide)
                for side in range(2):
                    downs.append(
                        pltpu.make_async_copy(
                            pieces[half].at[dp + dg, dz, :, pl.ds(side * wide, wide)],
                            down.at[m ^ dz, pl.ds(side * tall, tall), where],
                            down_sems.at[(i * n + dz) * 2 + side],
                        )
                    )
            for copy in ups[dz]:
                copy.start()
        for copy in downs:
            copy.start()
    rows, width = normed_ref.shape
    cols = up.shape[-1]
    chunk = rows // 2
    for dz in range(n):
        for copy in ups[dz]:
            copy.wait()
        k = dz if gathered else m ^ dz
        there = pl.ds(pl.multiple_of(k * cols, cols), cols)
        weight = up[k].reshape(width, cols)
        for r in range(0, rows, chunk):
            product = mm(normed_ref[r : r + chunk, :], weight)
            hidden[r : r + chunk, there] = jax.nn.gelu(product).astype(BF16)
    for copy in downs:
        copy.wait()
    for r in range(0, rows, chunk):
        weight = down[...].reshape(width, hidden.shape[1])
        enc = pool_ref[r : r + chunk, :].astype(F32) + mm(hidden[r : r + chunk, :], weight, NTR)
        enc_ref[r : r + chunk, :] = enc.astype(BF16)


def projected_body(enc_ref, *refs):
    weights, (enc_kv_ref, out0_ref) = refs[:4], refs[4:]
    count, length, _ = enc_kv_ref.shape
    width, cols = weights[0].shape
    enc = enc_ref[...]
    enc_kv_ref[:, :, :width] = enc.reshape(count, length, width)
    for j in range(4):
        layer, kind = divmod(j, 2)
        weight = of_layer(layer, *weights[2 * kind : 2 * kind + 2])
        out = mm(enc, weight).astype(BF16).reshape(count, length, cols)
        if layer == 0:
            out0_ref[:, :, kind * cols : (kind + 1) * cols] = out
        else:
            start = width + kind * cols
            enc_kv_ref[:, :, start : start + cols] = out


def slot_slice(c, slots):
    return slice(c * slots * NT, (c + 1) * slots * NT)


def softmax_used(scores, used):
    lane = lax.broadcasted_iota(jnp.int32, scores.shape, scores.ndim - 1)
    scores = jnp.where(lane < used * NT, scores, -1e30)
    powers = jnp.exp(scores - jnp.max(scores, axis=-1, keepdims=True))
    return powers / jnp.sum(powers, axis=-1, keepdims=True)


def first_layer_body(
    n, tracts, slots, ids_ref, counts_ref, gain_own, gain_other, wq_own, wq_other, *refs
):
    *pieces, own, other, att_ref, query_ref, probs_ref, blocks, sems = refs
    waits = load_slots(own, other, ids_ref, tracts, slots, blocks, sems)
    s, m = lax.axis_index("section"), lax.axis_index("mp")
    rows, cols = att_ref.shape
    feats = gain_own.shape[-1]

    def piece(k):
        if len(pieces) == n or k < 2:
            return unpack(pieces[k][...], rows, feats).astype(F32)
        inner = jnp.logical_or(m == 1, m == 2)
        inside, outside = pieces[2 * k - 2 : 2 * k]
        return unpack(jnp.where(inner, inside[...], outside[...]), rows, feats).astype(F32)

    total = jnp.zeros((rows, 1), F32)
    for k in range(n):
        wide = piece(k)
        total = total + jnp.sum(wide * wide, axis=-1, keepdims=True)
    scale = lax.rsqrt(total / (n * feats) + EPSILON)
    raw = jnp.zeros((rows, cols), F32)
    for k in range(n):
        wide = piece(k)
        gain = of_layer(0, gain_own, gain_other, m ^ k)
        normed = (wide * scale * gain).astype(BF16)
        here = pl.ds(pl.multiple_of((m ^ k) * feats, feats), feats)
        raw = raw + mm(normed, of_layer(0, wq_own, wq_other, here, slice(None)))
    query_ref[...] = (raw * SCALE).astype(BF16)
    length = rows // tracts
    heads = cols // HEAD
    for copy in waits:
        copy.wait()
    for c in range(tracts):
        here, span = slice(c * length, (c + 1) * length), slot_slice(c, slots)
        for h in range(heads):
            there = slice(h * HEAD, (h + 1) * HEAD)
            probs_ref[c * heads + h] = mm(query_ref[here, there], blocks[span, there], NTR)
    for c in range(tracts):
        both = slice(c * heads, (c + 1) * heads)
        probs_ref[both] = softmax_used(probs_ref[both], counts_ref[s, c])
    for c in range(tracts):
        here, span = slice(c * length, (c + 1) * length), slot_slice(c, slots)
        for h in range(heads):
            there = slice(h * HEAD, (h + 1) * HEAD)
            beyond = slice(cols + h * HEAD, cols + (h + 1) * HEAD)
            probs = probs_ref[c * heads + h].astype(BF16)
            att_ref[here, there] = mm(probs, blocks[span, beyond]).astype(BF16)


def between_body(n, *refs):
    gain_own, gain_other, own_ref, wout_own, wout_other, wq_own, wq_other, og_ref = refs[:8]
    pieces = refs[8 : 8 + n]
    rows_ref, messages = refs[8 + n], refs[9 + n :]
    s, m = lax.axis_index("section"), lax.axis_index("mp")
    rows, cols = pieces[0].shape
    tall = wq_own.shape[1]
    feats = rows_ref.shape[1]
    wide = unpack(own_ref[...], rows, feats).astype(F32)
    for d in range(n):
        here = pl.ds(pl.multiple_of((m ^ d) * cols, cols), cols)
        wide = wide + mm(pieces[d][...], of_layer(0, wout_own, wout_other, here, slice(None)))
    rounded = wide.astype(BF16)
    rows_ref[...] = rounded
    wide = rounded.astype(F32)
    square = to_row(jnp.sum(wide * wide, axis=-1, keepdims=True))
    high = square.astype(BF16).astype(F32)
    index = lax.broadcasted_iota(jnp.int32, (PAD, rows), 0)
    extra = jnp.where(index == 0, high, jnp.where(index == 1, square - high, 0.0)).astype(BF16)
    gained = (wide * of_layer(1, gain_own, gain_other, m)).astype(BF16)
    for d in range(n):
        weight = jnp.concatenate([wq_own[d], wq_other[d]], axis=0)
        flipped = jnp.concatenate([wq_other[d], wq_own[d]], axis=0)
        messages[d][:rows, :] = mm(gained, jnp.where(s == 0, weight, flipped)).astype(BF16)
        messages[d][rows : rows + PAD, :] = extra
        here = pl.ds(pl.multiple_of((m ^ d) * cols, cols), cols)
        weight = of_layer(1, wout_own, wout_other, here, slice(None))
        messages[d][rows + PAD :, :] = mm(og_ref[s], weight, NTR).astype(BF16)


def score_grads(tracts, slots, heads, cols, att_ref, blocks, probs_ref, grads_ref, scores_ref, soft_ref):
    length = att_ref.shape[0] // tracts
    for c in range(tracts):
        here, span = slice(c * length, (c + 1) * length), slot_slice(c, slots)
        for h in range(heads):
            there = slice(h * HEAD, (h + 1) * HEAD)
            beyond = slice(cols + h * HEAD, cols + (h + 1) * HEAD)
            grads_ref[c * heads + h] = mm(att_ref[here, there], blocks[span, beyond], NTR)
    for c in range(tracts):
        both = slice(c * heads, (c + 1) * heads)
        probs, grads = probs_ref[both], grads_ref[both]
        inner = jnp.sum(probs * grads, axis=-1, keepdims=True)
        scores_ref[both] = (probs * (grads - inner)).astype(BF16)
        soft_ref[both] = probs.astype(BF16)


def slot_grads(tracts, slots, heads, cols, query_ref, att_ref, scores_ref, soft_ref, dkv_ref):
    length = att_ref.shape[0] // tracts
    for c in range(tracts):
        here, span = slice(c * length, (c + 1) * length), slot_slice(c, slots)
        for h in range(heads):
            there = slice(h * HEAD, (h + 1) * HEAD)
            beyond = slice(cols + h * HEAD, cols + (h + 1) * HEAD)
            dkv_ref[span, there] = mm(
                scores_ref[c * heads + h], query_ref[here, there], TNR
            ).astype(BF16)
            dkv_ref[span, beyond] = mm(
                soft_ref[c * heads + h], att_ref[here, there], TNR
            ).astype(BF16)


def last_layer_body(n, width, tracts, slots, *refs):
    ids_ref, counts_ref = refs[:2]
    messages = refs[2 : 2 + n]
    own, other, dkv_ref, out_ref, scale_ref = refs[2 + n : 7 + n]
    raw_ref, query_ref, att_ref, probs_ref, grads_ref, scores_ref, soft_ref, blocks, sems = refs[
        7 + n :
    ]
    waits = load_slots(own, other, ids_ref, tracts, slots, blocks, sems, own.shape[2] - blocks.shape[1])
    s = lax.axis_index("section")
    rows, cols = raw_ref.shape
    raw = jnp.zeros((rows, cols), F32)
    square = jnp.zeros((1, rows), F32)
    grad = jnp.zeros((rows, cols), F32)
    for d in range(n):
        raw = raw + messages[d][:rows, :].astype(F32)
        extra = messages[d][rows : rows + PAD, :].astype(F32)
        square = square + extra[0:1, :] + extra[1:2, :]
        grad = grad + messages[d][rows + PAD :, :].astype(F32)
    scale = lax.rsqrt(to_column(square) / width + EPSILON)
    scale_ref[...] = jnp.broadcast_to(scale, scale_ref.shape)
    raw = raw * scale
    raw_ref[...] = raw
    query_ref[...] = (raw * SCALE).astype(BF16)
    att_ref[...] = grad.astype(BF16)
    length = rows // tracts
    heads = cols // HEAD
    for copy in waits:
        copy.wait()
    for c in range(tracts):
        here, span = slice(c * length, (c + 1) * length), slot_slice(c, slots)
        for h in range(heads):
            there = slice(h * HEAD, (h + 1) * HEAD)
            probs_ref[c * heads + h] = mm(query_ref[here, there], blocks[span, there], NTR)
    for c in range(tracts):
        both = slice(c * heads, (c + 1) * heads)
        probs_ref[both] = softmax_used(probs_ref[both], counts_ref[s, c])
    score_grads(
        tracts, slots, heads, cols, att_ref, blocks, probs_ref, grads_ref, scores_ref, soft_ref
    )
    for c in range(tracts):
        here, span = slice(c * length, (c + 1) * length), slot_slice(c, slots)
        for h in range(heads):
            there = slice(h * HEAD, (h + 1) * HEAD)
            grad_query = mm(scores_ref[c * heads + h], blocks[span, there]) * SCALE
            out_ref[here, there] = grad_query.astype(BF16)
    part = jnp.sum(out_ref[:rows, :].astype(F32) * raw_ref[...], axis=-1, keepdims=True)
    index = lax.broadcasted_iota(jnp.int32, (PAD, rows), 0)
    out_ref[rows:, :] = jnp.where(index == 0, to_row(part), 0.0).astype(BF16)
    slot_grads(tracts, slots, heads, cols, query_ref, att_ref, scores_ref, soft_ref, dkv_ref)


def weight_grads(enc_ref, dkv_ref, kept_ref, sent_ref):
    cols = kept_ref.shape[1]
    first = lax.axis_index("section") == 0
    chunk = enc_ref.shape[0] // 2
    for r in range(0, enc_ref.shape[0], chunk):
        total = mm(enc_ref[r : r + chunk, :], dkv_ref[...])
        keys, values = total[:, :cols], total[:, cols:]
        kept_ref[r : r + chunk, :] = jnp.where(first, keys, values).astype(BF16)
        sent_ref[r : r + chunk, :] = jnp.where(first, values, keys).astype(BF16)


def last_grads_body(
    tracts, slots, ids_ref, dkv_ref, own, other, enc_ref, kept_ref, sent_ref, rows_ref, sems
):
    waits = load_slots(own, other, ids_ref, tracts, slots, rows_ref, sems)
    for i, copy in enumerate(waits):
        copy.wait()
        here = slice(i * NT, (i + 1) * NT)
        enc_ref[:, here] = rows_ref[here, :].T
    weight_grads(enc_ref, dkv_ref, kept_ref, sent_ref)


def back_between_body(n, width, *refs):
    gain_own, gain_other, rows_ref, og_ref, scale_ref, wq_own, wq_other = refs[:7]
    wout_own, wout_other = refs[7:9]
    pieces, messages = refs[9 : 9 + n], refs[9 + n :]
    s, m = lax.axis_index("section"), lax.axis_index("mp")
    rows, feats = rows_ref.shape
    cols = pieces[0].shape[1]
    normed = jnp.zeros((rows, feats), F32)
    total = jnp.zeros((1, rows), F32)
    for d in range(n):
        weight = jnp.concatenate([wq_own[d], wq_other[d]], axis=0)
        flipped = jnp.concatenate([wq_other[d], wq_own[d]], axis=0)
        normed = normed + mm(pieces[d][:rows, :], jnp.where(s == 0, weight, flipped), NTR)
        total = total + pieces[d][rows:, :].astype(F32)[0:1, :]
    scale = scale_ref[:, 0:1]
    wide = rows_ref[...].astype(F32)
    gain = of_layer(1, gain_own, gain_other, m)
    grad = og_ref[s].astype(F32) + scale * gain * normed
    grad = grad - wide * (scale * scale * (to_column(total) / width))
    grad = grad.astype(BF16)
    for d in range(n):
        here = pl.ds(pl.multiple_of((m ^ d) * cols, cols), cols)
        weight = of_layer(0, wout_own, wout_other, here, slice(None))
        messages[d][...] = mm(grad, weight, NTR).astype(BF16)


def first_back_body(n, tracts, slots, *refs):
    ids_ref, query_ref, probs_ref = refs[:3]
    grads = refs[3 : 3 + n]
    own, other, dkv_ref = refs[3 + n : 6 + n]
    att_ref, grads_ref, scores_ref, soft_ref, blocks, sems = refs[6 + n :]
    waits = load_slots(own, other, ids_ref, tracts, slots, blocks, sems)
    rows, cols = query_ref.shape
    grad = jnp.zeros((rows, cols), F32)
    for d in range(n):
        grad = grad + grads[d][...].astype(F32)
    att_ref[...] = grad.astype(BF16)
    heads = cols // HEAD
    for copy in waits:
        copy.wait()
    score_grads(
        tracts, slots, heads, cols, att_ref, blocks, probs_ref, grads_ref, scores_ref, soft_ref
    )
    slot_grads(tracts, slots, heads, cols, query_ref, att_ref, scores_ref, soft_ref, dkv_ref)


def along_mp(value, n):
    return [value] + [xor_move(value, "mp", d) for d in range(1, n)]


def scattered(messages):
    return [messages[0]] + [xor_move(messages[d], "mp", d) for d in range(1, len(messages))]


def on_device(
    segment_input,
    out_grad,
    pool_tokens,
    neighbour_ids,
    neighbour_counts,
    enc_gain,
    enc_up,
    enc_down,
    norm_gain,
    w_query,
    w_key,
    w_value,
    w_out,
):
    n, dp = lax.axis_size("mp"), lax.axis_size("dp")
    s = lax.axis_index("section")
    _, _, rows, feats = segment_input.shape
    width = n * feats
    cols = w_query.shape[2]
    half, _, length, enc_width = pool_tokens.shape
    tracts, slots = neighbour_ids.shape[2:]
    ids, counts = neighbour_ids[:, 0], neighbour_counts[:, 0]
    ff = enc_down.shape[0]
    first = s == 0
    gain = norm_gain.reshape(n, 1, feats)
    wq, wk, wv, wout = w_query[0], w_key[0], w_value[0], w_out[0]
    gains, wqs, wks, wvs, wouts = ((w, swap(w)) for w in (gain, wq, wk, wv, wout))

    def share_out(deps):
        return call(
            functools.partial(shares_body, n),
            [shape((rows * feats // cols, cols))] + [shape((feats // 2, cols))] * n,
            [vm()] * 3,
            deps=deps,
        )(*wqs, segment_input[:, 0])

    down_t = enc_down.T
    parts = 2 * dp
    up_rows, down_cols = enc_width // parts, ff // parts
    shares = up_rows % 16 == 0 and enc_width // n == 2 * up_rows and down_cols == HEAD
    shares = shares and enc_up.shape[1] == 2 * down_cols and dp == 4
    if shares:
        share = call(
            share_body,
            [shape((2 * up_rows, 2 * down_cols))],
            [hbm_only(), hbm_only()],
            [pltpu.SemaphoreType.DMA((3,))],
        )(enc_up, down_t)[0]
        line = along_mp(share, n)
        line_done = line[1:]
        piece = (n, up_rows, 2 * down_cols)
        up, down = call(
            functools.partial(line_body, n),
            [shape(piece)] * 2,
            [vm()] * n,
            deps=[wqs[1], wouts[1]],
        )(*line)
        own, *query_shares = share_out(line_done)
        inner, outer = [(1, 2), (2, 1)], [(1, 0), (2, 3)]
        up1, down2 = xor_move(up, "dp", 1), xor_move(down, "dp", 2)
        near, far_inner = xor_move(own, "mp", 1), lax.ppermute(own, "mp", inner)
        ups, downs = call(
            pair_body, [shape((2,) + piece)] * 2, [vm()] * 4, deps=[near, far_inner, wks[1]]
        )(up, up1, down, down2)
        up2, down1 = xor_move(ups, "dp", 2), xor_move(downs, "dp", 1)
        next_outer = lax.ppermute(far_inner, "mp", outer)
        next_inner = lax.ppermute(near, "mp", inner)
        gathered = call(
            gather_body,
            [shape((parts,) + piece)],
            [vm()] * 6,
            deps=[next_outer, next_inner, wvs[1]],
        )(up, up1, up2, down, down2, down1)[0]
        pieces = [gathered, swap(gathered)]
        far_outer = lax.ppermute(next_inner, "mp", outer)
        query_shares = scattered(query_shares)
        row_pieces = [own, near, next_inner, next_outer, far_inner, far_outer]
        before_projected = query_shares[1:] + [far_outer]
        scratch = [
            pltpu.VMEM((n, parts, up_rows, enc_up.shape[1]), BF16),
            pltpu.VMEM((n, enc_width // n, ff), BF16),
            pltpu.SemaphoreType.DMA((parts * n,)),
            pltpu.SemaphoreType.DMA((2 * parts * n,)),
        ]
    else:
        own, *query_shares = share_out([])
        row_pieces, query_shares = along_mp(own, n), scattered(query_shares)
        before_projected = []
        pieces = [
            lax.all_gather(enc_up, "mp", axis=0),
            lax.all_gather(down_t, "mp", axis=0, tiled=True),
        ]
        scratch = [
            pltpu.VMEM((n, enc_width, enc_up.shape[1]), BF16),
            pltpu.VMEM((enc_width, ff), BF16),
            pltpu.SemaphoreType.DMA((2,)),
        ]

    pool_rows = pool_tokens[:, 0].reshape(half * length, enc_width)
    normed = call(
        norm_body, [shape((half * length, enc_width))], [vm(), vm()], flops=half * length * enc_width
    )(pool_rows, enc_gain[None, :])[0]
    enc = call(
        functools.partial(encoder_body, n, parts, not shares),
        [shape((half * length, enc_width))],
        [vm()] * 4 if shares else [vm()] * 2 + [hbm()] * 2,
        [pltpu.VMEM((half * length, ff), BF16)] + scratch,
        flops=4 * half * length * enc_width * ff,
        limit=ENCODER_LIMIT if shares else 48 * 1024 * 1024,
    )(pool_rows, normed, *pieces)[0]
    enc_own, pool0_own = call(
        projected_body,
        [shape((half, length, enc_width + 2 * cols)), shape((half, length, 2 * cols))],
        [vm()] * 5,
        flops=8 * half * length * enc_width * cols,
        deps=before_projected,
    )(enc, *wks, *wvs)
    pool0_other = swap(pool0_own)
    projection = call(
        functools.partial(projection_body, n), [shape((n, feats // 2, cols))], [vm()] * n
    )(*query_shares)[0]
    projections = (projection, swap(projection))

    heads = cols // HEAD
    chunk = rows // tracts
    slot_rows = tracts * slots * NT
    blocks_scratch = pltpu.VMEM((slot_rows, 2 * cols), BF16)
    slot_sems = pltpu.SemaphoreType.DMA((tracts * slots,))
    wide_scores = pltpu.VMEM((tracts * heads, chunk, slots * NT), F32)
    bf_scores = pltpu.VMEM((tracts * heads, chunk, slots * NT), BF16)
    attention_flops = 2 * rows * slots * NT * cols

    att, query0, probs0, enc_own = call(
        functools.partial(first_layer_body, n, tracts, slots),
        [
            shape((rows, cols)),
            shape((rows, cols)),
            shape((tracts * heads, chunk, slots * NT), F32),
        ],
        [smem(), smem()] + [vm()] * (6 + len(row_pieces)),
        [blocks_scratch, slot_sems],
        flops=2 * rows * width * cols + 2 * attention_flops,
        passing=[enc_own],
    )(ids, counts, *gains, *wqs, *row_pieces, pool0_own, pool0_other)
    enc_other = swap(enc_own)
    att_pieces = along_mp(att, n)
    rows1, *messages = call(
        functools.partial(between_body, n),
        [shape((rows, feats))] + [shape((2 * rows + PAD, cols))] * n,
        [vm()] * (8 + n),
        flops=6 * rows * feats * n * cols,
        deps=[enc_other],
    )(*gains, own, *wouts, *projections, out_grad[:, 0], *att_pieces)
    query_pieces = scattered(messages)
    dkv1, grad_query, scale1 = call(
        functools.partial(last_layer_body, n, width, tracts, slots),
        [shape((slot_rows, 2 * cols)), shape((rows + PAD, cols)), shape((rows, HEAD), F32)],
        [smem(), smem()] + [vm()] * (n + 2),
        [
            pltpu.VMEM((rows, cols), F32),
            pltpu.VMEM((rows, cols), BF16),
            pltpu.VMEM((rows, cols), BF16),
            wide_scores,
            wide_scores,
            bf_scores,
            bf_scores,
            blocks_scratch,
            slot_sems,
        ],
        flops=5 * attention_flops,
    )(ids, counts, *query_pieces, enc_own, enc_other)
    query_grads = along_mp(grad_query, n)
    enc_slots, kept1, sent1 = call(
        functools.partial(last_grads_body, tracts, slots),
        [shape((enc_width, slot_rows)), shape((enc_width, cols)), shape((enc_width, cols))],
        [smem(), vm(), hbm(), hbm()],
        [pltpu.VMEM((slot_rows, enc_width), BF16), slot_sems],
        flops=4 * enc_width * slot_rows * cols,
    )(ids, dkv1, enc_own, enc_other)
    half_shape = shape((enc_width // 2, cols))
    *messages, kept1, sent1 = call(
        functools.partial(back_between_body, n, width),
        [shape((rows, cols))] * n,
        [vm()] * (9 + n),
        flops=4 * rows * feats * n * cols,
        passing=[kept1, sent1],
    )(*gains, rows1, out_grad[:, 0], scale1, *projections, *wouts, *query_grads)
    grad_pieces0 = scattered(messages)

    def over_dp(parts, order, deps=()):
        moved = [xor_move(part, "dp", by) for part, by in zip(parts, order)]
        return call(functools.partial(add_body, 2), [half_shape] * 2, [vm()] * 4, deps=deps)(
            *parts, *moved
        )

    def summed(kept, sent, deps=()):
        parts = call(halves_body, [half_shape] * 2, [vm()] * 2)(kept, swap(sent))
        if dp == 4:
            parts = over_dp(over_dp(parts, (1, 2), deps), (2, 1))
        else:
            parts = [lax.psum(part, "dp") for part in parts]
        return jnp.concatenate(parts, axis=0)

    sum1 = summed(kept1, sent1, grad_pieces0[1:])
    dkv0 = call(
        functools.partial(first_back_body, n, tracts, slots),
        [shape((slot_rows, 2 * cols))],
        [smem()] + [vm()] * (n + 4),
        [
            pltpu.VMEM((rows, cols), BF16),
            wide_scores,
            bf_scores,
            bf_scores,
            blocks_scratch,
            slot_sems,
        ],
        flops=3 * attention_flops,
    )(ids, query0, probs0, *grad_pieces0, pool0_own, pool0_other)[0]
    kept0, sent0 = call(
        weight_grads,
        [shape((enc_width, cols)), shape((enc_width, cols))],
        [vm()] * 2,
        flops=4 * enc_width * slot_rows * cols,
        deps=[sum1],
    )(enc_slots, dkv0)
    sum0 = summed(kept0, sent0)
    received = swap(jnp.where(first, sum1, sum0))
    key_total = jnp.where(first, sum0, received)
    value_total = jnp.where(first, received, sum1)
    return (key_total[None], value_total[None])


def solution(mesh):
    placed = (
        P(None, "dp", None, "mp"),
        P(None, "dp", None, "mp"),
        P("section", "dp", None, None),
        P(None, "dp", None, None),
        P(None, "dp", None),
        P(),
        P(None, "mp"),
        P(None, "mp"),
        P("section", None),
        P("section", None, "mp"),
        P("section", None, "mp"),
        P("section", None, "mp"),
        P("section", None, "mp"),
    )
    return jax.shard_map(
        on_device,
        mesh=mesh,
        in_specs=placed,
        out_specs=(P("section", None, "mp"), P("section", None, "mp")),
        check_vma=False,
    )
```

time: 238 us -> 185 us (0.78)
  Pallas kernels: 62.8 us -> 38.2 us
  other arithmetic: 15.6 us -> 1.04 us
  waiting for transfers between devices: 90.4 us -> 82.6 us
  local copies, waits for them, and re-layouts: 8.11 us -> 4.43 us
    pallas_call x9 -> x22, Pallas kernels: 62.8 us -> 38.2 us  [run(): pl.pallas_call(kernel, out_shape=list(outs) + [shape(x.shape, x.dtype) fo...]
    ppermute x60 -> x43, waiting for transfers between devices: 90.4 us -> 73.6 us  [xor_move(): return lax.ppermute(value, axis, [(i, i ^ by) for i in range(count)])]
    select_n x7 -> x0, other arithmetic: 10.7 us -> none  [the longest x4 7.29 us: by_layer(): return (jnp.where(first, own, other), jnp.where(first, other, own))]
    ppermute x0 -> x4, waiting for transfers between devices: none -> 8.98 us  [the longest x1 8.97 us: on_device(): next_outer = lax.ppermute(far_inner, 'mp', outer)]
    ppermute x60 -> x43, starting transfers between devices: 58.6 us -> 53.2 us  [xor_move(): return lax.ppermute(value, axis, [(i, i ^ by) for i in range(count)])]
    ppermute x0 -> x4, starting transfers between devices: none -> 4.05 us  [the longest x1 1.29 us: on_device(): next_outer = lax.ppermute(far_inner, 'mp', outer)]
    dynamic_slice x3 -> x0, local copies, waits for them, and re-layouts: 2.43 us -> none  [the longest x1 1.56 us: on_device(): up_piece = lax.dynamic_slice_in_dim(enc_up, place * up_rows, up_rows, 0)]
  transfers between devices with their start and end apart: 60 -> 47, of which waited for: 24 -> 23; matrix products, arithmetic and copies ran while one was open for 7% -> 0% of each run, Pallas kernels for 27% -> 12%
where the time goes in v2:
time: 185 us
  waiting for transfers between devices  82.6 us (45%)
  starting transfers between devices  57.3 us (31%)
  Pallas kernels  38.2 us (21%)
  local copies, waits for them, and re-layouts  4.43 us (2%)
    ppermute x43, waiting for transfers between devices, xor_move(): return lax.ppermute(value, axis, [(i, i ^ by) for i in range(count)])  73.6 us
    ppermute x43, starting transfers between devices, xor_move(): return lax.ppermute(value, axis, [(i, i ^ by) for i in range(count)])  53.2 us
    pallas_call x22, Pallas kernels, run(): pl.pallas_call(kernel, out_shape=list(outs) + [shape(x.shape, x.dtype) fo...  38.2 us
    ppermute x1, waiting for transfers between devices, on_device(): next_outer = lax.ppermute(far_inner, 'mp', outer)  8.97 us
    unnamed x30, local copies, waits for them, and re-layouts  4.39 us
  transfers between devices with their start and end apart: 47, of which 23 were waited for; matrix products, arithmetic and copies ran while one was open for 0% of the time, Pallas kernels for 12%

profile of v2, /device:TPU:0, one launch (start us, length us, event | category | flops | bytes accessed | tf_op | source)
XLA Modules:
  0.0 184.6 jit_solution(15522475281988021530)
XLA Ops:
  3.4 3.1 %collective-permute-start.2 = (bf16[224,256]{1,0:T(8,128)(2,1)S(1)}, bf16[224,256]{1,0:T(8,128)(2,1)S(1)}, u32[]{:S(2)}, u32[]{:S(2)}) collective-permute-start(bf16[224,256]{1,0:T(8,128)(2,1)S(1)} %shard_map.140.refs_0_), channel_id=1, source_target_pairs={{0,1},{1,0},{2,3},{3,2},{4,5},{5,4},{6,7},{7,6},{8,9},{9,8},{10,11... | collective-permute-start | bytes 344072 | tf_op jit(solution)/shard_map/ppermute | solution.py:31
  6.4 2.6 %collective-permute-start.3 = (bf16[224,256]{1,0:T(8,128)(2,1)S(1)}, bf16[224,256]{1,0:T(8,128)(2,1)S(1)}, u32[]{:S(2)}, u32[]{:S(2)}) collective-permute-start(bf16[224,256]{1,0:T(8,128)(2,1)S(1)} %shard_map.140.refs_0_), channel_id=1, source_target_pairs={{0,2},{1,3},{2,0},{3,1},{4,6},{5,7},{6,4},{7,5},{8,10},{9,11},{10,... | collective-permute-start | bytes 344072 | tf_op jit(solution)/shard_map/ppermute | solution.py:31
  9.8 4.8 %collective-permute-start.4 = (bf16[224,256]{1,0:T(8,128)(2,1)S(1)}, bf16[224,256]{1,0:T(8,128)(2,1)S(1)}, u32[]{:S(2)}, u32[]{:S(2)}) collective-permute-start(bf16[224,256]{1,0:T(8,128)(2,1)S(1)} %shard_map.140.refs_0_), channel_id=1, source_target_pairs={{0,3},{1,2},{2,1},{3,0},{4,7},{5,6},{6,5},{7,4},{8,11},{9,10},{10,... | collective-permute-start | bytes 344072 | tf_op jit(solution)/shard_map/ppermute | solution.py:31
  14.7 3.5 %collective-permute-done.3.refs_4_.refs_2_ = bf16[224,256]{1,0:T(8,128)(2,1)S(1)} collective-permute-done((bf16[224,256]{1,0:T(8,128)(2,1)S(1)}, bf16[224,256]{1,0:T(8,128)(2,1)S(1)}, u32[]{:S(2)}, u32[]{:S(2)}) %collective-permute-start.3) | collective-permute-done | bytes 114720 | tf_op jit(solution)/shard_map/ppermute | solution.py:31
  20.5 2.7 %collective-permute-start.10 = (bf16[512,256]{1,0:T(8,128)(2,1)S(1)}, bf16[512,256]{1,0:T(8,128)(2,1)S(1)}, u32[]{:S(2)}, u32[]{:S(2)}) collective-permute-start(bf16[512,256]{1,0:T(8,128)(2,1)S(1)} %get-tuple-element.48.refs_6_.refs_2_), channel_id=1, source_target_pairs={{0,1},{1,0},{2,3},{3,2},{4,5},{5,4},{6,7},{7,6},{8,9},{9,8},{10,11... | collective-permute-start | bytes 786440 | tf_op jit(solution)/shard_map/ppermute | solution.py:31
  27.1 3.9 %collective-permute-done.15.refs_1_ = bf16[4,112,256]{2,1,0:T(8,128)(2,1)S(1)} collective-permute-done((bf16[4,112,256]{2,1,0:T(8,128)(2,1)S(1)}, bf16[4,112,256]{2,1,0:T(8,128)(2,1)S(1)}, u32[]{:S(2)}, u32[]{:S(2)}) %collective-permute-start.15) | collective-permute-done | bytes 229408 | tf_op jit(solution)/shard_map/ppermute | solution.py:31
  36.5 9.0 %collective-permute-done.13.refs_6_.refs_9_ = bf16[512,256]{1,0:T(8,128)(2,1)S(1)} collective-permute-done((bf16[512,256]{1,0:T(8,128)(2,1)S(1)}, bf16[512,256]{1,0:T(8,128)(2,1)S(1)}, u32[]{:S(2)}, u32[]{:S(2)}) %collective-permute-start.13) | collective-permute-done | bytes 262176 | tf_op jit(solution)/shard_map/ppermute | solution.py:610
  47.0 2.7 %collective-permute-start.6 = (bf16[256,256]{1,0:T(8,128)(2,1)S(1)}, bf16[256,256]{1,0:T(8,128)(2,1)S(1)}, u32[]{:S(2)}, u32[]{:S(2)}) collective-permute-start(bf16[256,256]{1,0:T(8,128)(2,1)S(1)} %get-tuple-element.50), channel_id=1, source_target_pairs={{0,1},{1,0},{2,3},{3,2},{4,5},{5,4},{6,7},{7,6},{8,9},{9,8},{10,11... | collective-permute-start | bytes 393224 | tf_op jit(solution)/shard_map/ppermute | solution.py:31
  52.9 10.0 %shard_map.147.refs_0_ = bf16[1024,896]{1,0:T(8,128)(2,1)S(1)} custom-call(bf16[1024,896]{1,0:T(8,128)(2,1)S(1)} %bitcast.16, bf16[1024,896]{1,0:T(8,128)(2,1)S(1)} %shard_map.143.refs_1_, bf16[8,4,112,256]{3,2,1,0:T(8,128)(2,1)S(1)} %shard_map.146.refs_2_, bf16[8,4,112,256]{3,2,1,0:T(8,128)(2,1)S(1)} %collective-permute-done.21.refs_3_), custom_call_target="tpu_custom_call" | custom-call | flops 3758096 | bytes 1835 | tf_op jit(solution)/shard_map/pallas_call | solution.py:63
  64.7 2.4 %shard_map.148 = (bf16[8,128,1408]{2,1,0:T(8,128)(2,1)S(1)}, bf16[8,128,512]{2,1,0:T(8,128)(2,1)S(1)}) custom-call(bf16[1024,896]{1,0:T(8,128)(2,1)S(1)} %shard_map.147.refs_0_, bf16[896,256]{1,0:T(8,128)(2,1)S(1)} %bitcast.27, bf16[896,256]{1,0:T(8,128)(2,1)S(1)} %collective-permute-done.17.refs_6_.refs_2_, bf16[896,256]{1,0:T(8,128)(2,1)S(1)} %bitcast.29, ...), custom_call_target="tpu_custom_call" | custom-call | flops 1879048 | bytes 3932 | tf_op jit(solution)/shard_map/pallas_call | solution.py:63
  67.7 2.2 %collective-permute-done.refs_3_.refs_1_ = f32[4,1,512]{2,1,0:T(1,128)S(1)} collective-permute-done((f32[4,1,512]{2,1,0:T(1,128)S(1)}, f32[4,1,512]{2,1,0:T(1,128)S(1)}, u32[]{:S(2)}, u32[]{:S(2)}) %collective-permute-start) | collective-permute-done | bytes 8224 | tf_op jit(solution)/shard_map/ppermute | solution.py:31
  69.9 5.9 %shard_map.149 = (bf16[256,256]{1,0:T(8,128)(2,1)S(1)}, bf16[256,256]{1,0:T(8,128)(2,1)S(1)}, f32[8,64,512]{2,1,0:T(8,128)S(1)}, bf16[8,128,1408]{2,1,0:T(8,128)(2,1)S(1)}) custom-call(s32[2,4,4]{2,1,0:T(4,128)S(1)} %bitcast.35, s32[2,4]{1,0:T(2,128)S(1)} %bitcast.39, f32[4,1,512]{2,1,0:T(1,128)S(1)} %bitcast.32, ...), custom_call_target="tpu_custom_call", output_to_operand_aliasing={{3}: (14, {})} | custom-call | flops 402653 | bytes 1310 | tf_op jit(solution)/shard_map/pallas_call | solution.py:63
  76.8 2.6 %collective-permute-start.24 = (bf16[256,256]{1,0:T(8,128)(2,1)S(1)}, bf16[256,256]{1,0:T(8,128)(2,1)S(1)}, u32[]{:S(2)}, u32[]{:S(2)}) collective-permute-start(bf16[256,256]{1,0:T(8,128)(2,1)S(1)} %get-tuple-element.59.refs_8_), channel_id=1, source_target_pairs={{0,2},{1,3},{2,0},{3,1},{4,6},{5,7},{6,4},{7,5},{8,10},{9,11},{10,... | collective-permute-start | bytes 393224 | tf_op jit(solution)/shard_map/ppermute | solution.py:31
  82.0 2.3 %collective-permute-done.23.refs_9_ = bf16[256,256]{1,0:T(8,128)(2,1)S(1)} collective-permute-done((bf16[256,256]{1,0:T(8,128)(2,1)S(1)}, bf16[256,256]{1,0:T(8,128)(2,1)S(1)}, u32[]{:S(2)}, u32[]{:S(2)}) %collective-permute-start.23) | collective-permute-done | bytes 131104 | tf_op jit(solution)/shard_map/ppermute | solution.py:31
  84.2 5.5 %collective-permute-done.24.refs_10_ = bf16[256,256]{1,0:T(8,128)(2,1)S(1)} collective-permute-done((bf16[256,256]{1,0:T(8,128)(2,1)S(1)}, bf16[256,256]{1,0:T(8,128)(2,1)S(1)}, u32[]{:S(2)}, u32[]{:S(2)}) %collective-permute-start.24) | collective-permute-done | bytes 131104 | tf_op jit(solution)/shard_map/ppermute | solution.py:31
  90.9 2.4 %collective-permute-start.27 = (bf16[528,256]{1,0:T(8,128)(2,1)S(1)}, bf16[528,256]{1,0:T(8,128)(2,1)S(1)}, u32[]{:S(2)}, u32[]{:S(2)}) collective-permute-start(bf16[528,256]{1,0:T(8,128)(2,1)S(1)} %get-tuple-element.62), channel_id=1, source_target_pairs={{0,1},{1,0},{2,3},{3,2},{4,5},{5,4},{6,7},{7,6},{8,9},{9,8},{10,11... | collective-permute-start | bytes 811016 | tf_op jit(solution)/shard_map/ppermute | solution.py:31
  95.7 7.8 %collective-permute-done.27.refs_3_ = bf16[528,256]{1,0:T(8,128)(2,1)S(1)} collective-permute-done((bf16[528,256]{1,0:T(8,128)(2,1)S(1)}, bf16[528,256]{1,0:T(8,128)(2,1)S(1)}, u32[]{:S(2)}, u32[]{:S(2)}) %collective-permute-start.27) | collective-permute-done | bytes 270368 | tf_op jit(solution)/shard_map/ppermute | solution.py:31
  103.6 11.6 %collective-permute-done.28.refs_4_ = bf16[528,256]{1,0:T(8,128)(2,1)S(1)} collective-permute-done((bf16[528,256]{1,0:T(8,128)(2,1)S(1)}, bf16[528,256]{1,0:T(8,128)(2,1)S(1)}, u32[]{:S(2)}, u32[]{:S(2)}) %collective-permute-start.28) | collective-permute-done | bytes 270368 | tf_op jit(solution)/shard_map/ppermute | solution.py:31
  115.2 3.2 %shard_map.151 = (bf16[2048,512]{1,0:T(8,128)(2,1)S(1)}, bf16[272,256]{1,0:T(8,128)(2,1)S(1)}, f32[256,128]{1,0:T(8,128)S(1)}) custom-call(s32[2,4,4]{2,1,0:T(4,128)S(1)} %bitcast.36, s32[2,4]{1,0:T(2,128)S(1)} %bitcast.40, bf16[528,256]{1,0:T(8,128)(2,1)S(1)} %get-tuple-element.61.refs_2_, bf16[528,256]{1,0:T(8,128)(2,1)S(1)} %collective-permute-done.27.refs_3_, ...), custom_call_target="tpu_custom_call" | custom-call | flops 335544 | bytes 2367 | tf_op jit(solution)/shard_map/pallas_call | solution.py:63
  118.4 4.2 %collective-permute-start.30 = (bf16[272,256]{1,0:T(8,128)(2,1)S(1)}, bf16[272,256]{1,0:T(8,128)(2,1)S(1)}, u32[]{:S(2)}, u32[]{:S(2)}) collective-permute-start(bf16[272,256]{1,0:T(8,128)(2,1)S(1)} %get-tuple-element.71.refs_9_), channel_id=1, source_target_pairs={{0,1},{1,0},{2,3},{3,2},{4,5},{5,4},{6,7},{7,6},{8,9},{9,8},{10,11... | collective-permute-start | bytes 417800 | tf_op jit(solution)/shard_map/ppermute | solution.py:31
  125.0 5.4 %shard_map.152 = (bf16[896,2048]{1,0:T(8,128)(2,1)S(1)}, bf16[896,256]{1,0:T(8,128)(2,1)S(1)}, bf16[896,256]{1,0:T(8,128)(2,1)S(1)}) custom-call(s32[2,4,4]{2,1,0:T(4,128)S(1)} %bitcast.37, bf16[2048,512]{1,0:T(8,128)(2,1)S(1)} %get-tuple-element.65.refs_1_, bf16[8,128,1408]{2,1,0:T(8,128)(2,1)S(1)} %get-tuple-element.60.refs_6_.refs_2_, ...), custom_call_target="tpu_custom_call" | custom-call | flops 1879048 | bytes 4587 | tf_op jit(solution)/shard_map/pallas_call | solution.py:63
  130.5 3.7 %collective-permute-done.31.refs_11_ = bf16[272,256]{1,0:T(8,128)(2,1)S(1)} collective-permute-done((bf16[272,256]{1,0:T(8,128)(2,1)S(1)}, bf16[272,256]{1,0:T(8,128)(2,1)S(1)}, u32[]{:S(2)}, u32[]{:S(2)}) %collective-permute-start.31) | collective-permute-done | bytes 139296 | tf_op jit(solution)/shard_map/ppermute | solution.py:31
  135.1 1.8 collective-permute-done.36.refs_1_
  139.2 2.1 %collective-permute-start.33 = (bf16[256,256]{1,0:T(8,128)(2,1)S(1)}, bf16[256,256]{1,0:T(8,128)(2,1)S(1)}, u32[]{:S(2)}, u32[]{:S(2)}) collective-permute-start(bf16[256,256]{1,0:T(8,128)(2,1)S(1)} %get-tuple-element.75), channel_id=1, source_target_pairs={{0,1},{1,0},{2,3},{3,2},{4,5},{5,4},{6,7},{7,6},{8,9},{9,8},{10,11... | collective-permute-start | bytes 393224 | tf_op jit(solution)/shard_map/ppermute | solution.py:31
  143.6 2.2 %collective-permute-done.33.refs_4_ = bf16[256,256]{1,0:T(8,128)(2,1)S(1)} collective-permute-done((bf16[256,256]{1,0:T(8,128)(2,1)S(1)}, bf16[256,256]{1,0:T(8,128)(2,1)S(1)}, u32[]{:S(2)}, u32[]{:S(2)}) %collective-permute-start.33) | collective-permute-done | bytes 131104 | tf_op jit(solution)/shard_map/ppermute | solution.py:31
  145.8 8.0 %collective-permute-done.34.refs_5_ = bf16[256,256]{1,0:T(8,128)(2,1)S(1)} collective-permute-done((bf16[256,256]{1,0:T(8,128)(2,1)S(1)}, bf16[256,256]{1,0:T(8,128)(2,1)S(1)}, u32[]{:S(2)}, u32[]{:S(2)}) %collective-permute-start.34) | collective-permute-done | bytes 131104 | tf_op jit(solution)/shard_map/ppermute | solution.py:31
  156.1 5.4 %shard_map.154.refs_1_ = bf16[2048,512]{1,0:T(8,128)(2,1)S(1)} custom-call(s32[2,4,4]{2,1,0:T(4,128)S(1)} %bitcast.38, bf16[256,256]{1,0:T(8,128)(2,1)S(1)} %get-tuple-element.67.refs_1_, f32[8,64,512]{2,1,0:T(8,128)S(1)} %get-tuple-element.68.refs_2_, bf16[256,256]{1,0:T(8,128)(2,1)S(1)} %get-tuple-element.74.refs_3_, ...), custom_call_target="tpu_custom_call" | custom-call | flops 201326 | bytes 2097 | tf_op jit(solution)/shard_map/pallas_call | solution.py:63
  161.7 2.1 %shard_map.158 = (bf16[896,256]{1,0:T(8,128)(2,1)S(1)}, bf16[896,256]{1,0:T(8,128)(2,1)S(1)}) custom-call(bf16[896,2048]{1,0:T(8,128)(2,1)S(1)} %get-tuple-element.66.refs_0_, bf16[2048,512]{1,0:T(8,128)(2,1)S(1)} %shard_map.154.refs_1_, bf16[896,256]{1,0:T(8,128)(2,1)S(1)} %constant_dynamic-update-slice_fusion.refs_2_), custom_call_target="tpu_custom_call" | custom-call | flops 1879048 | bytes 917 | tf_op jit(solution)/shard_map/pallas_call | solution.py:63
  163.9 1.8 collective-permute-done.41.refs_1_
  167.7 5.8 %collective-permute-done.42.refs_2_ = bf16[448,256]{1,0:T(8,128)(2,1)S(1)} collective-permute-done((bf16[448,256]{1,0:T(8,128)(2,1)S(1)}, bf16[448,256]{1,0:T(8,128)(2,1)S(1)}, u32[]{:S(2)}, u32[]{:S(2)}) %collective-permute-start.42) | collective-permute-done | bytes 229408 | tf_op jit(solution)/shard_map/ppermute | solution.py:31
  175.9 5.4 %collective-permute-done.44.refs_2_ = bf16[448,256]{1,0:T(8,128)(2,1)S(1)} collective-permute-done((bf16[448,256]{1,0:T(8,128)(2,1)S(1)}, bf16[448,256]{1,0:T(8,128)(2,1)S(1)}, u32[]{:S(2)}, u32[]{:S(2)}) %collective-permute-start.44) | collective-permute-done | bytes 229408 | tf_op jit(solution)/shard_map/ppermute | solution.py:31
  181.8 1.8 collective-permute-done.46
  (119 shorter events, 45.7 us)
Async XLA Ops:
  0.6 17.6 %collective-permute-start.1 = (bf16[2048,256]{1,0:T(8,128)(2,1)}, bf16[2048,256]{1,0:T(8,128)(2,1)S(1)}, u32[]{:S(2)}, u32[]{:S(2)}) collective-permute-start(bf16[2048,256]{1,0:T(8,128)(2,1)} %bitcast.20), channel_id=1, source_target_pairs={{0,16},{16,0},{1,17},{17,1},{2,18},{18,2},{3,19},{19,3},{4,20},{20... | collective-permute-start | bytes 3145736 | tf_op jit(solution)/shard_map/ppermute | solution.py:31
  1.1 22.8 %collective-permute-start.5 = (bf16[1024,512]{1,0:T(8,128)(2,1)}, bf16[1024,512]{1,0:T(8,128)(2,1)S(1)}, u32[]{:S(2)}, u32[]{:S(2)}) collective-permute-start(bf16[1024,512]{1,0:T(8,128)(2,1)} %bitcast.17), channel_id=1, source_target_pairs={{0,16},{16,0},{1,17},{17,1},{2,18},{18,2},{3,19},{19,3},{4,20},{20... | collective-permute-start | bytes 3145736 | tf_op jit(solution)/shard_map/ppermute | solution.py:31
  6.4 20.6 %collective-permute-start.17 = (bf16[896,256]{1,0:T(8,128)(2,1)}, bf16[896,256]{1,0:T(8,128)(2,1)S(1)}, u32[]{:S(2)}, u32[]{:S(2)}) collective-permute-start(bf16[896,256]{1,0:T(8,128)(2,1)} %bitcast.26), channel_id=1, source_target_pairs={{0,16},{16,0},{1,17},{17,1},{2,18},{18,2},{3,19},{19,3},{4,20},{20... | collective-permute-start | bytes 1376264 | tf_op jit(solution)/shard_map/ppermute | solution.py:31
  6.4 11.8 %collective-permute-start.3 = (bf16[224,256]{1,0:T(8,128)(2,1)S(1)}, bf16[224,256]{1,0:T(8,128)(2,1)S(1)}, u32[]{:S(2)}, u32[]{:S(2)}) collective-permute-start(bf16[224,256]{1,0:T(8,128)(2,1)S(1)} %shard_map.140.refs_0_), channel_id=1, source_target_pairs={{0,2},{1,3},{2,0},{3,1},{4,6},{5,7},{6,4},{7,5},{8,10},{9,11},{10,... | collective-permute-start | bytes 344072 | tf_op jit(solution)/shard_map/ppermute | solution.py:31
  9.8 8.4 %collective-permute-start.4 = (bf16[224,256]{1,0:T(8,128)(2,1)S(1)}, bf16[224,256]{1,0:T(8,128)(2,1)S(1)}, u32[]{:S(2)}, u32[]{:S(2)}) collective-permute-start(bf16[224,256]{1,0:T(8,128)(2,1)S(1)} %shard_map.140.refs_0_), channel_id=1, source_target_pairs={{0,3},{1,2},{2,1},{3,0},{4,7},{5,6},{6,5},{7,4},{8,11},{9,10},{10,... | collective-permute-start | bytes 344072 | tf_op jit(solution)/shard_map/ppermute | solution.py:31
  20.5 11.7 %collective-permute-start.10 = (bf16[512,256]{1,0:T(8,128)(2,1)S(1)}, bf16[512,256]{1,0:T(8,128)(2,1)S(1)}, u32[]{:S(2)}, u32[]{:S(2)}) collective-permute-start(bf16[512,256]{1,0:T(8,128)(2,1)S(1)} %get-tuple-element.48.refs_6_.refs_2_), channel_id=1, source_target_pairs={{0,1},{1,0},{2,3},{3,2},{4,5},{5,4},{6,7},{7,6},{8,9},{9,8},{10,11... | collective-permute-start | bytes 786440 | tf_op jit(solution)/shard_map/ppermute | solution.py:31
  23.2 9.0 %collective-permute-start.12 = (bf16[512,256]{1,0:T(8,128)(2,1)S(1)}, bf16[512,256]{1,0:T(8,128)(2,1)S(1)}, u32[]{:S(2)}, u32[]{:S(2)}) collective-permute-start(bf16[512,256]{1,0:T(8,128)(2,1)S(1)} %get-tuple-element.48.refs_6_.refs_2_), channel_id=1, source_target_pairs={{1,2},{2,1},{5,6},{6,5},{9,10},{10,9},{13,14},{14,13},{17,18},{18,... | collective-permute-start | bytes 786440 | tf_op jit(solution)/shard_map/ppermute | solution.py:605
  27.1 9.5 %collective-permute-start.20 = (bf16[896,256]{1,0:T(8,128)(2,1)S(1)}, bf16[896,256]{1,0:T(8,128)(2,1)S(1)}, u32[]{:S(2)}, u32[]{:S(2)}) collective-permute-start(bf16[896,256]{1,0:T(8,128)(2,1)S(1)} %bitcast.28), channel_id=1, source_target_pairs={{0,16},{16,0},{1,17},{17,1},{2,18},{18,2},{3,19},{19,3},{4,20},{20... | collective-permute-start | bytes 1376264 | tf_op jit(solution)/shard_map/ppermute | solution.py:31
  32.3 13.2 %collective-permute-start.18 = (bf16[2,4,112,256]{3,2,1,0:T(8,128)(2,1)S(1)}, bf16[2,4,112,256]{3,2,1,0:T(8,128)(2,1)S(1)}, u32[]{:S(2)}, u32[]{:S(2)}) collective-permute-start(bf16[2,4,112,256]{3,2,1,0:T(8,128)(2,1)S(1)} %get-tuple-element.55), channel_id=1, source_target_pairs={{0,8},{4,12},{8,0},{12,4},{1,9},{5,13},{9,1},{13,5},{2,10},{6,14},... | collective-permute-start | bytes 1376264 | tf_op jit(solution)/shard_map/ppermute | solution.py:31
  33.9 11.6 %collective-permute-start.19 = (bf16[2,4,112,256]{3,2,1,0:T(8,128)(2,1)S(1)}, bf16[2,4,112,256]{3,2,1,0:T(8,128)(2,1)S(1)}, u32[]{:S(2)}, u32[]{:S(2)}) collective-permute-start(bf16[2,4,112,256]{3,2,1,0:T(8,128)(2,1)S(1)} %get-tuple-element.56), channel_id=1, source_target_pairs={{0,4},{4,0},{8,12},{12,8},{1,5},{5,1},{9,13},{13,9},{2,6},{6,2},{1... | collective-permute-start | bytes 1376264 | tf_op jit(solution)/shard_map/ppermute | solution.py:31
  35.2 10.3 %collective-permute-start.13 = (bf16[512,256]{1,0:T(8,128)(2,1)S(1)}, bf16[512,256]{1,0:T(8,128)(2,1)S(1)}, u32[]{:S(2)}, u32[]{:S(2)}) collective-permute-start(bf16[512,256]{1,0:T(8,128)(2,1)S(1)} %collective-permute-done.12.refs_5_.refs_10_), channel_id=1, source_target_pairs={{1,0},{2,3},{5,4},{6,7},{9,8},{10,11},{13,12},{14,15},{17,16},{18,... | collective-permute-start | bytes 786440 | tf_op jit(solution)/shard_map/ppermute | solution.py:610
  45.7 19.0 %collective-permute-start.14 = (bf16[512,256]{1,0:T(8,128)(2,1)S(1)}, bf16[512,256]{1,0:T(8,128)(2,1)S(1)}, u32[]{:S(2)}, u32[]{:S(2)}) collective-permute-start(bf16[512,256]{1,0:T(8,128)(2,1)S(1)} %collective-permute-done.11.refs_7_.refs_8_), channel_id=1, source_target_pairs={{1,0},{2,3},{5,4},{6,7},{9,8},{10,11},{13,12},{14,15},{17,16},{18,... | collective-permute-start | bytes 786440 | tf_op jit(solution)/shard_map/ppermute | solution.py:619
  47.0 17.7 %collective-permute-start.6 = (bf16[256,256]{1,0:T(8,128)(2,1)S(1)}, bf16[256,256]{1,0:T(8,128)(2,1)S(1)}, u32[]{:S(2)}, u32[]{:S(2)}) collective-permute-start(bf16[256,256]{1,0:T(8,128)(2,1)S(1)} %get-tuple-element.50), channel_id=1, source_target_pairs={{0,1},{1,0},{2,3},{3,2},{4,5},{5,4},{6,7},{7,6},{8,9},{9,8},{10,11... | collective-permute-start | bytes 393224 | tf_op jit(solution)/shard_map/ppermute | solution.py:31
  49.7 15.0 %collective-permute-start.7 = (bf16[256,256]{1,0:T(8,128)(2,1)S(1)}, bf16[256,256]{1,0:T(8,128)(2,1)S(1)}, u32[]{:S(2)}, u32[]{:S(2)}) collective-permute-start(bf16[256,256]{1,0:T(8,128)(2,1)S(1)} %get-tuple-element.51), channel_id=1, source_target_pairs={{0,2},{1,3},{2,0},{3,1},{4,6},{5,7},{6,4},{7,5},{8,10},{9,11},{10,... | collective-permute-start | bytes 393224 | tf_op jit(solution)/shard_map/ppermute | solution.py:31
  50.7 14.0 %collective-permute-start.8 = (bf16[256,256]{1,0:T(8,128)(2,1)S(1)}, bf16[256,256]{1,0:T(8,128)(2,1)S(1)}, u32[]{:S(2)}, u32[]{:S(2)}) collective-permute-start(bf16[256,256]{1,0:T(8,128)(2,1)S(1)} %get-tuple-element.52), channel_id=1, source_target_pairs={{0,3},{1,2},{2,1},{3,0},{4,7},{5,6},{6,5},{7,4},{8,11},{9,10},{10,... | collective-permute-start | bytes 393224 | tf_op jit(solution)/shard_map/ppermute | solution.py:31
  75.9 13.9 %collective-permute-start.26 = (bf16[8,128,1408]{2,1,0:T(8,128)(2,1)S(1)}, bf16[8,128,1408]{2,1,0:T(8,128)(2,1)S(1)}, u32[]{:S(2)}, u32[]{:S(2)}) collective-permute-start(bf16[8,128,1408]{2,1,0:T(8,128)(2,1)S(1)} %get-tuple-element.60.refs_6_.refs_2_), channel_id=1, source_target_pairs={{0,16},{16,0},{1,17},{17,1},{2,18},{18,2},{3,19},{19,3},{4,20},{20... | collective-permute-start | bytes 8650760 | tf_op jit(solution)/shard_map/ppermute | solution.py:31
  76.5 7.7 %collective-permute-start.23 = (bf16[256,256]{1,0:T(8,128)(2,1)S(1)}, bf16[256,256]{1,0:T(8,128)(2,1)S(1)}, u32[]{:S(2)}, u32[]{:S(2)}) collective-permute-start(bf16[256,256]{1,0:T(8,128)(2,1)S(1)} %get-tuple-element.59.refs_8_), channel_id=1, source_target_pairs={{0,1},{1,0},{2,3},{3,2},{4,5},{5,4},{6,7},{7,6},{8,9},{9,8},{10,11... | collective-permute-start | bytes 393224 | tf_op jit(solution)/shard_map/ppermute | solution.py:31
  76.8 12.9 %collective-permute-start.24 = (bf16[256,256]{1,0:T(8,128)(2,1)S(1)}, bf16[256,256]{1,0:T(8,128)(2,1)S(1)}, u32[]{:S(2)}, u32[]{:S(2)}) collective-permute-start(bf16[256,256]{1,0:T(8,128)(2,1)S(1)} %get-tuple-element.59.refs_8_), channel_id=1, source_target_pairs={{0,2},{1,3},{2,0},{3,1},{4,6},{5,7},{6,4},{7,5},{8,10},{9,11},{10,... | collective-permute-start | bytes 393224 | tf_op jit(solution)/shard_map/ppermute | solution.py:31
  79.5 10.3 %collective-permute-start.25 = (bf16[256,256]{1,0:T(8,128)(2,1)S(1)}, bf16[256,256]{1,0:T(8,128)(2,1)S(1)}, u32[]{:S(2)}, u32[]{:S(2)}) collective-permute-start(bf16[256,256]{1,0:T(8,128)(2,1)S(1)} %get-tuple-element.59.refs_8_), channel_id=1, source_target_pairs={{0,3},{1,2},{2,1},{3,0},{4,7},{5,6},{6,5},{7,4},{8,11},{9,10},{10,... | collective-permute-start | bytes 393224 | tf_op jit(solution)/shard_map/ppermute | solution.py:31
  90.9 12.7 %collective-permute-start.27 = (bf16[528,256]{1,0:T(8,128)(2,1)S(1)}, bf16[528,256]{1,0:T(8,128)(2,1)S(1)}, u32[]{:S(2)}, u32[]{:S(2)}) collective-permute-start(bf16[528,256]{1,0:T(8,128)(2,1)S(1)} %get-tuple-element.62), channel_id=1, source_target_pairs={{0,1},{1,0},{2,3},{3,2},{4,5},{5,4},{6,7},{7,6},{8,9},{9,8},{10,11... | collective-permute-start | bytes 811016 | tf_op jit(solution)/shard_map/ppermute | solution.py:31
  93.3 21.9 %collective-permute-start.28 = (bf16[528,256]{1,0:T(8,128)(2,1)S(1)}, bf16[528,256]{1,0:T(8,128)(2,1)S(1)}, u32[]{:S(2)}, u32[]{:S(2)}) collective-permute-start(bf16[528,256]{1,0:T(8,128)(2,1)S(1)} %get-tuple-element.63), channel_id=1, source_target_pairs={{0,2},{1,3},{2,0},{3,1},{4,6},{5,7},{6,4},{7,5},{8,10},{9,11},{10,... | collective-permute-start | bytes 811016 | tf_op jit(solution)/shard_map/ppermute | solution.py:31
  94.3 20.9 %collective-permute-start.29 = (bf16[528,256]{1,0:T(8,128)(2,1)S(1)}, bf16[528,256]{1,0:T(8,128)(2,1)S(1)}, u32[]{:S(2)}, u32[]{:S(2)}) collective-permute-start(bf16[528,256]{1,0:T(8,128)(2,1)S(1)} %get-tuple-element.64), channel_id=1, source_target_pairs={{0,3},{1,2},{2,1},{3,0},{4,7},{5,6},{6,5},{7,4},{8,11},{9,10},{10,... | collective-permute-start | bytes 811016 | tf_op jit(solution)/shard_map/ppermute | solution.py:31
  118.4 12.1 %collective-permute-start.30 = (bf16[272,256]{1,0:T(8,128)(2,1)S(1)}, bf16[272,256]{1,0:T(8,128)(2,1)S(1)}, u32[]{:S(2)}, u32[]{:S(2)}) collective-permute-start(bf16[272,256]{1,0:T(8,128)(2,1)S(1)} %get-tuple-element.71.refs_9_), channel_id=1, source_target_pairs={{0,1},{1,0},{2,3},{3,2},{4,5},{5,4},{6,7},{7,6},{8,9},{9,8},{10,11... | collective-permute-start | bytes 417800 | tf_op jit(solution)/shard_map/ppermute | solution.py:31
  122.6 11.5 %collective-permute-start.31 = (bf16[272,256]{1,0:T(8,128)(2,1)S(1)}, bf16[272,256]{1,0:T(8,128)(2,1)S(1)}, u32[]{:S(2)}, u32[]{:S(2)}) collective-permute-start(bf16[272,256]{1,0:T(8,128)(2,1)S(1)} %get-tuple-element.71.refs_9_), channel_id=1, source_target_pairs={{0,2},{1,3},{2,0},{3,1},{4,6},{5,7},{6,4},{7,5},{8,10},{9,11},{10,... | collective-permute-start | bytes 417800 | tf_op jit(solution)/shard_map/ppermute | solution.py:31
  123.6 10.5 %collective-permute-start.32 = (bf16[272,256]{1,0:T(8,128)(2,1)S(1)}, bf16[272,256]{1,0:T(8,128)(2,1)S(1)}, u32[]{:S(2)}, u32[]{:S(2)}) collective-permute-start(bf16[272,256]{1,0:T(8,128)(2,1)S(1)} %get-tuple-element.71.refs_9_), channel_id=1, source_target_pairs={{0,3},{1,2},{2,1},{3,0},{4,7},{5,6},{6,5},{7,4},{8,11},{9,10},{10,... | collective-permute-start | bytes 417800 | tf_op jit(solution)/shard_map/ppermute | solution.py:31
  137.0 16.8 %collective-permute-start.37 = (bf16[448,256]{1,0:T(8,128)(2,1)S(1)}, bf16[448,256]{1,0:T(8,128)(2,1)S(1)}, u32[]{:S(2)}, u32[]{:S(2)}) collective-permute-start(bf16[448,256]{1,0:T(8,128)(2,1)S(1)} %get-tuple-element.80.refs_0_), channel_id=1, source_target_pairs={{0,4},{4,0},{8,12},{12,8},{1,5},{5,1},{9,13},{13,9},{2,6},{6,2},{1... | collective-permute-start | bytes 688136 | tf_op jit(solution)/shard_map/ppermute | solution.py:31
  138.7 15.2 %collective-permute-start.38 = (bf16[448,256]{1,0:T(8,128)(2,1)S(1)}, bf16[448,256]{1,0:T(8,128)(2,1)S(1)}, u32[]{:S(2)}, u32[]{:S(2)}) collective-permute-start(bf16[448,256]{1,0:T(8,128)(2,1)S(1)} %get-tuple-element.81.refs_1_), channel_id=1, source_target_pairs={{0,8},{4,12},{8,0},{12,4},{1,9},{5,13},{9,1},{13,5},{2,10},{6,14},... | collective-permute-start | bytes 688136 | tf_op jit(solution)/shard_map/ppermute | solution.py:31
  141.2 12.6 %collective-permute-start.34 = (bf16[256,256]{1,0:T(8,128)(2,1)S(1)}, bf16[256,256]{1,0:T(8,128)(2,1)S(1)}, u32[]{:S(2)}, u32[]{:S(2)}) collective-permute-start(bf16[256,256]{1,0:T(8,128)(2,1)S(1)} %get-tuple-element.76), channel_id=1, source_target_pairs={{0,2},{1,3},{2,0},{3,1},{4,6},{5,7},{6,4},{7,5},{8,10},{9,11},{10,... | collective-permute-start | bytes 393224 | tf_op jit(solution)/shard_map/ppermute | solution.py:31
  142.0 11.8 %collective-permute-start.35 = (bf16[256,256]{1,0:T(8,128)(2,1)S(1)}, bf16[256,256]{1,0:T(8,128)(2,1)S(1)}, u32[]{:S(2)}, u32[]{:S(2)}) collective-permute-start(bf16[256,256]{1,0:T(8,128)(2,1)S(1)} %get-tuple-element.77), channel_id=1, source_target_pairs={{0,3},{1,2},{2,1},{3,0},{4,7},{5,6},{6,5},{7,4},{8,11},{9,10},{10,... | collective-permute-start | bytes 393224 | tf_op jit(solution)/shard_map/ppermute | solution.py:31
  153.9 7.5 %collective-permute-start.39 = (bf16[448,256]{1,0:T(8,128)(2,1)S(1)}, bf16[448,256]{1,0:T(8,128)(2,1)S(1)}, u32[]{:S(2)}, u32[]{:S(2)}) collective-permute-start(bf16[448,256]{1,0:T(8,128)(2,1)S(1)} %get-tuple-element.82.refs_0_), channel_id=1, source_target_pairs={{0,8},{4,12},{8,0},{12,4},{1,9},{5,13},{9,1},{13,5},{2,10},{6,14},... | collective-permute-start | bytes 688136 | tf_op jit(solution)/shard_map/ppermute | solution.py:31
  165.8 7.7 %collective-permute-start.42 = (bf16[448,256]{1,0:T(8,128)(2,1)S(1)}, bf16[448,256]{1,0:T(8,128)(2,1)S(1)}, u32[]{:S(2)}, u32[]{:S(2)}) collective-permute-start(bf16[448,256]{1,0:T(8,128)(2,1)S(1)} %get-tuple-element.88.refs_0_), channel_id=1, source_target_pairs={{0,4},{4,0},{8,12},{12,8},{1,5},{5,1},{9,13},{13,9},{2,6},{6,2},{1... | collective-permute-start | bytes 688136 | tf_op jit(solution)/shard_map/ppermute | solution.py:31
  167.2 7.4 %collective-permute-start.43 = (bf16[448,256]{1,0:T(8,128)(2,1)S(1)}, bf16[448,256]{1,0:T(8,128)(2,1)S(1)}, u32[]{:S(2)}, u32[]{:S(2)}) collective-permute-start(bf16[448,256]{1,0:T(8,128)(2,1)S(1)} %get-tuple-element.89.refs_1_), channel_id=1, source_target_pairs={{0,8},{4,12},{8,0},{12,4},{1,9},{5,13},{9,1},{13,5},{2,10},{6,14},... | collective-permute-start | bytes 688136 | tf_op jit(solution)/shard_map/ppermute | solution.py:31
  (29 other events, 195.9 us)

commit v3 on v2

--- a/solution.py
+++ b/solution.py
@@ -14,6 +14,7 @@
 PAD = 16
 VMEM_LIMIT = 20 * 1024 * 1024
 ENCODER_LIMIT = 32 * 1024 * 1024
+FIRST_LIMIT = 60 * 1024 * 1024
 
 BF16 = jnp.bfloat16
 F32 = jnp.float32
@@ -31,6 +32,10 @@
     return lax.ppermute(value, axis, [(i, i ^ by) for i in range(count)])
 
 
+def places(n):
+    return (0, 2, 3, 1) if n == 4 else tuple(range(n))
+
+
 def swap(value):
     return xor_move(value, "section", 1)
 
@@ -51,27 +56,29 @@
     return pl.BlockSpec(memory_space=pltpu.SMEM)
 
 
-def call(body, outs, specs, scratch=(), flops=0, limit=VMEM_LIMIT, deps=(), passing=()):
+def call(body, outs, specs, scratch=(), flops=0, limit=VMEM_LIMIT, first=(), deps=(), passing=()):
     count, more, kept, results = len(specs), len(deps), len(passing), len(outs)
     nbytes = sum(o.size * o.dtype.itemsize for o in outs)
-    start = count + more + kept
+    begin = len(first)
+    start = begin + count + more + kept
 
     def kernel(*refs):
-        body(*refs[:count], *refs[start : start + results], *refs[start + results + kept :])
+        given = refs[begin : begin + count]
+        body(*given, *refs[start : start + results], *refs[start + results + kept :])
 
     def run(*args):
         return pl.pallas_call(
             kernel,
             out_shape=list(outs) + [shape(x.shape, x.dtype) for x in passing],
-            in_specs=list(specs) + [hbm()] * (more + kept),
+            in_specs=[hbm()] * begin + list(specs) + [hbm()] * (more + kept),
             out_specs=[vm() for _ in outs] + [hbm()] * kept,
             scratch_shapes=list(scratch),
-            input_output_aliases={count + more + i: results + i for i in range(kept)},
+            input_output_aliases={begin + count + more + i: results + i for i in range(kept)},
             compiler_params=pltpu.CompilerParams(vmem_limit_bytes=limit),
             cost_estimate=pl.CostEstimate(
                 flops=flops // 1000, bytes_accessed=nbytes // 1000, transcendentals=0
             ),
-        )(*args, *deps, *passing)
+        )(*first, *args, *deps, *passing)
 
     return run
 
@@ -94,28 +101,25 @@
     return jnp.sum(jnp.where(here == there, row, 0.0), axis=1, keepdims=True)
 
 
-def load_slots(own, other, ids_ref, tracts, slots, blocks, sems, start=0):
+def slot_value(own, other, ids_ref, tract, slot, start, size):
     half = own.shape[0]
-    span = pl.ds(start, blocks.shape[1])
     s = lax.axis_index("section")
-    waits = []
+    place = ids_ref[s, tract, slot]
+    mine, theirs = place - s * half, place - (1 - s) * half
+    here = jnp.logical_and(mine >= 0, mine < half)
+    cols = slice(start, start + size)
+    return jnp.where(
+        here,
+        own[jnp.clip(mine, 0, half - 1), :, cols],
+        other[jnp.clip(theirs, 0, half - 1), :, cols],
+    )
+
+
+def fill_slots(own, other, ids_ref, tracts, slots, blocks, start=0):
     for c in range(tracts):
         for k in range(slots):
-            i = c * slots + k
-            place = ids_ref[s, c, k]
-            here = place // half == s
-            target, sem = blocks.at[pl.ds(i * NT, NT)], sems.at[i]
-
-            @pl.when(here)
-            def _(target=target, sem=sem, place=place):
-                pltpu.make_async_copy(own.at[place - s * half, :, span], target, sem).start()
-
-            @pl.when(jnp.logical_not(here))
-            def _(target=target, sem=sem, place=place):
-                pltpu.make_async_copy(other.at[place - (1 - s) * half, :, span], target, sem).start()
-
-            waits.append(pltpu.make_async_copy(own.at[0, :, span], target, sem))
-    return waits
+            here = slice((c * slots + k) * NT, (c * slots + k + 1) * NT)
+            blocks[here, :] = slot_value(own, other, ids_ref, c, k, start, blocks.shape[1])
 
 
 def of_layer(layer, own_ref, other_ref, *index):
@@ -141,61 +145,125 @@
     return jnp.concatenate([value[:, i : i + feats] for i in range(0, cols, feats)], axis=0)
 
 
-def share_body(up_ref, down_ref, out_ref, sems):
-    place = lax.axis_index("section") * lax.axis_size("dp") + lax.axis_index("dp")
-    tall = out_ref.shape[0] // 2
-    rows = pl.ds(pl.multiple_of(place * tall, tall), tall)
+def share_body(n, up_ref, down_ref, wq_own, wq_other, rows_ref, *refs):
+    outs, own_ref, sems = refs[:n], refs[n], refs[n + 1]
+    s, m = lax.axis_index("section"), lax.axis_index("mp")
+    place = s * lax.axis_size("dp") + lax.axis_index("dp")
+    parts = 2 * lax.axis_size("dp")
+    tall = up_ref.shape[0] // parts
+    share = wq_own.shape[0] // (n * parts)
+    rows = pl.ds(pl.multiple_of(place * tall, 16), tall)
     cols = pl.ds(pl.multiple_of(place * HEAD, HEAD), HEAD)
-    copies = [pltpu.make_async_copy(up_ref.at[rows], out_ref.at[pl.ds(0, tall)], sems.at[0])]
+    copies = [pltpu.make_async_copy(up_ref.at[rows], outs[0].at[pl.ds(0, tall)], sems.at[0])]
     for side in range(2):
         copies.append(
             pltpu.make_async_copy(
                 down_ref.at[pl.ds(side * tall, tall), cols],
-                out_ref.at[pl.ds(tall, tall), pl.ds(side * HEAD, HEAD)],
+                outs[0].at[pl.ds(tall, tall), pl.ds(side * HEAD, HEAD)],
                 sems.at[1 + side],
             )
         )
     for copy in copies:
         copy.start()
+    for i, d in enumerate(places(n)):
+        start = ((m ^ d) * parts + place) * share
+        here = pl.ds(pl.multiple_of(start, share), share)
+        target = outs[i].at[pl.ds(2 * tall, share)]
+        copies.append(pltpu.make_async_copy(wq_own.at[here], target, sems.at[3 + i]))
+
+        @pl.when(s == 1)
+        def _(here=here, target=target, i=i):
+            pltpu.make_async_copy(wq_own.at[here], target, sems.at[3 + i]).start()
+
+        @pl.when(s != 1)
+        def _(here=here, target=target, i=i):
+            pltpu.make_async_copy(wq_other.at[here], target, sems.at[3 + i]).start()
+
+    total, length = rows_ref.shape[1], own_ref.shape[1]
+    for i in range(own_ref.shape[0] // total):
+        source = rows_ref.at[s, :, pl.ds(i * length, length)]
+        target = own_ref.at[pl.ds(i * total, total)]
+        copies.append(pltpu.make_async_copy(source, target, sems.at[3 + n + i]))
+        copies[-1].start()
     for copy in copies:
         copy.wait()
-
-
-def line_body(n, *refs):
-    tall = refs[0].shape[0] // 2
-    for d in range(n):
-        refs[n][d] = refs[d][:tall, :]
-        refs[n + 1][d] = refs[d][tall:, :]
-
-
-def pair_body(*refs):
-    for i in range(2):
-        refs[4 + i][0] = refs[2 * i][...]
-        refs[4 + i][1] = refs[2 * i + 1][...]
-
-
-def gather_body(up, up1, up2, down, down2, down1, out_ref):
+    half = own_ref.shape[0] // 2
+    outs[n - 1][2 * tall + share :, :] = own_ref[:half, :]
+    for i in range(1, n):
+        outs[i][: 2 * tall, :] = outs[0][: 2 * tall, :]
+
+
+def line_body(n, tall, *refs):
+    half = (refs[0].shape[0] - 2 * tall) // 2
+    own_ref, far_ref = refs[n], refs[n + 1]
+    near_ref, message, kept_ref = refs[n + 4 :]
+    kept_ref[...] = own_ref[...]
+    near_ref[...] = refs[n - 1][2 * (tall + half) :, :]
+    rest = own_ref.shape[0] // 2
+    message[:rest, :] = own_ref[rest:, :]
+    message[rest:, :] = far_ref[...]
+    for i in range(1, n):
+        for j in range(2):
+            start = 2 * tall + j * half
+            refs[n + 2 + j][i - 1, :tall] = refs[i][j * tall : (j + 1) * tall, :]
+            refs[n + 2 + j][i - 1, tall:] = refs[i][start : start + half, :]
+
+
+def pair_body(up, up1, down, down2, near1, moved, far2, far3, ups, downs, message, near):
+    for here, there, out_ref in ((up, up1, ups), (down, down2, downs)):
+        out_ref[0] = here[...]
+        out_ref[1] = there[...]
+    first, rest, rows = near.shape[0], near1.shape[0], far2.shape[0]
+    near[:rest, :] = near1[...]
+    near[rest:, :] = moved[:rest, :]
+    message[:first, :] = near[...]
+    for i, far in enumerate((far3, far2)):
+        start = rest + i * rows
+        total = moved[start : start + rows, :].astype(F32) + far[...].astype(F32)
+        message[first + i * rows : first + (i + 1) * rows, :] = total.astype(BF16)
+
+
+def gather_body(
+    up, up1, up2, down, down2, down1, moved, close, key_ref, value_ref,
+    out_ref, next_ref, grad_ref, key_out, value_out,
+):
+    key_out[...] = key_ref[...]
+    value_out[...] = value_ref[...]
     for base, parts in ((0, (up, up1, up2)), (4, (down, down2, down1))):
         near = 1 if base == 0 else 2
         out_ref[base] = parts[0][...]
         out_ref[base + near] = parts[1][...]
         out_ref[base + 3 - near] = parts[2][0]
         out_ref[base + 3] = parts[2][1]
-
-
-def shares_body(n, wq_own, wq_other, rows_ref, own_ref, *outs):
+    first, rows = next_ref.shape[0], grad_ref.shape[0]
+    next_ref[...] = moved[:first, :]
+    total = moved[first + rows :, :].astype(F32) + close[...].astype(F32)
+    grad_ref[...] = total.astype(BF16)
+
+
+def rows_body(cols, rows_ref, own_ref):
+    own_ref[...] = pack(rows_ref[lax.axis_index("section")], cols)
+
+
+def query_shares_body(n, wq_own, wq_other, *outs):
+    m = lax.axis_index("mp")
+    tall = outs[0].shape[0]
+    for i, d in enumerate(places(n)):
+        here = pl.ds(pl.multiple_of((m ^ d) * tall, tall), tall)
+        outs[i][...] = of_layer(1, wq_own, wq_other, here, slice(None))
+
+
+def out_grads_body(n, og_ref, wout_own, wout_other, *outs):
     s, m = lax.axis_index("section"), lax.axis_index("mp")
-    own_ref[...] = pack(rows_ref[s], outs[0].shape[1])
-    tall = outs[0].shape[0]
-    for d in range(n):
-        start = ((m ^ d) * 2 + s) * tall
-        here = pl.ds(pl.multiple_of(start, tall), tall)
-        outs[d][...] = of_layer(1, wq_own, wq_other, here, slice(None))
-
-
-def projection_body(n, *refs):
-    for d in range(n):
-        refs[n][d] = refs[d][...]
+    cols = outs[0].shape[1]
+    rows = og_ref.shape[1]
+    for i, d in enumerate(places(n)):
+        here = pl.ds(pl.multiple_of((m ^ d) * cols, cols), cols)
+        weight = of_layer(1, wout_own, wout_other, here, slice(None))
+        outs[i][...] = mm(og_ref[s], weight, NTR).astype(BF16)
+    for i, out_ref in enumerate(outs[1:3]):
+        if len(outs) > n:
+            outs[n][i * rows : (i + 1) * rows, :] = out_ref[...]
 
 
 def add_body(count, *refs):
@@ -220,7 +288,11 @@
 
 def encoder_body(n, parts, gathered, *refs):
     pool_ref, normed_ref = refs[:2]
-    pieces, (enc_ref, hidden, up, down, *sems) = refs[2:4], refs[4:]
+    if gathered:
+        pieces, (enc_ref, hidden, up, down, *sems) = refs[2:4], refs[4:]
+    else:
+        pieces, (enc_ref, wq_ref, hidden, up, down) = refs[2:4], refs[8:]
+        up_ref, down_ref, wq_own, wq_other = refs[4:8]
     m = lax.axis_index("mp")
     if gathered:
         copies = [[pltpu.make_async_copy(pieces[i], (up, down)[i], sems[0].at[i])] for i in range(2)]
@@ -229,32 +301,28 @@
         ups[0][0].start()
         downs[0].start()
     else:
-        up_sems, down_sems = sems
         s, g = lax.axis_index("section"), lax.axis_index("dp")
-        dp, tall, wide = parts // 2, pieces[0].shape[2], HEAD
+        dp, tall, wide = parts // 2, up.shape[2], HEAD
+        share = pieces[0].shape[2] - tall
         ups, downs = [[] for _ in range(n)], []
-        for dz in range(n):
+        up[m] = up_ref[...].reshape(up.shape[1:])
+        down[m] = down_ref[...]
+        here = pl.ds(pl.multiple_of(m * wq_ref.shape[1], wq_ref.shape[1]), wq_ref.shape[1])
+        wq_ref[0] = of_layer(1, wq_own, wq_other, here, slice(None))
+        for j, dz in enumerate(places(n)[1:]):
             for i in range(parts):
                 half, dg = divmod(i, dp)
                 place = (s ^ half) * dp + (g ^ dg)
-                ups[dz].append(
-                    pltpu.make_async_copy(
-                        pieces[half].at[dg, dz], up.at[m ^ dz, place], up_sems.at[i * n + dz]
-                    )
-                )
+                for k in range(2):
+                    start = pl.multiple_of((2 * place + k) * share, share)
+                    wq_ref[j + 1, pl.ds(start, share)] = pieces[half][k * dp + dg, j, tall:]
+                up[m ^ dz, place] = pieces[half][dg, j, :tall]
                 where = pl.ds(pl.multiple_of(place * wide, wide), wide)
                 for side in range(2):
-                    downs.append(
-                        pltpu.make_async_copy(
-                            pieces[half].at[dp + dg, dz, :, pl.ds(side * wide, wide)],
-                            down.at[m ^ dz, pl.ds(side * tall, tall), where],
-                            down_sems.at[(i * n + dz) * 2 + side],
-                        )
-                    )
-            for copy in ups[dz]:
-                copy.start()
-        for copy in downs:
-            copy.start()
+                    rows_of = slice(side * tall, (side + 1) * tall)
+                    down[m ^ dz, rows_of, where] = pieces[half][
+                        dp + dg, j, :tall, side * wide : (side + 1) * wide
+                    ]
     rows, width = normed_ref.shape
     cols = up.shape[-1]
     chunk = rows // 2
@@ -306,10 +374,10 @@
 def first_layer_body(
     n, tracts, slots, ids_ref, counts_ref, gain_own, gain_other, wq_own, wq_other, *refs
 ):
-    *pieces, own, other, att_ref, query_ref, probs_ref, blocks, sems = refs
-    waits = load_slots(own, other, ids_ref, tracts, slots, blocks, sems)
+    *pieces, own, other, att_ref, query_ref, probs_ref, blocks = refs
+    fill_slots(own, other, ids_ref, tracts, slots, blocks)
     s, m = lax.axis_index("section"), lax.axis_index("mp")
-    rows, cols = att_ref.shape
+    rows, cols = query_ref.shape
     feats = gain_own.shape[-1]
 
     def piece(k):
@@ -334,8 +402,6 @@
     query_ref[...] = (raw * SCALE).astype(BF16)
     length = rows // tracts
     heads = cols // HEAD
-    for copy in waits:
-        copy.wait()
     for c in range(tracts):
         here, span = slice(c * length, (c + 1) * length), slot_slice(c, slots)
         for h in range(heads):
@@ -354,17 +420,16 @@
 
 
 def between_body(n, *refs):
-    gain_own, gain_other, own_ref, wout_own, wout_other, wq_own, wq_other, og_ref = refs[:8]
-    pieces = refs[8 : 8 + n]
-    rows_ref, messages = refs[8 + n], refs[9 + n :]
-    s, m = lax.axis_index("section"), lax.axis_index("mp")
+    gain_own, gain_other, own_ref, wout_own, wout_other, wq_ref = refs[:6]
+    pieces = refs[6 : 6 + n]
+    rows_ref, messages = refs[6 + n], refs[7 + n :]
+    m = lax.axis_index("mp")
     rows, cols = pieces[0].shape
-    tall = wq_own.shape[1]
     feats = rows_ref.shape[1]
     wide = unpack(own_ref[...], rows, feats).astype(F32)
-    for d in range(n):
+    for i, d in enumerate(places(n)):
         here = pl.ds(pl.multiple_of((m ^ d) * cols, cols), cols)
-        wide = wide + mm(pieces[d][...], of_layer(0, wout_own, wout_other, here, slice(None)))
+        wide = wide + mm(pieces[i][...], of_layer(0, wout_own, wout_other, here, slice(None)))
     rounded = wide.astype(BF16)
     rows_ref[...] = rounded
     wide = rounded.astype(F32)
@@ -373,23 +438,18 @@
     index = lax.broadcasted_iota(jnp.int32, (PAD, rows), 0)
     extra = jnp.where(index == 0, high, jnp.where(index == 1, square - high, 0.0)).astype(BF16)
     gained = (wide * of_layer(1, gain_own, gain_other, m)).astype(BF16)
-    for d in range(n):
-        weight = jnp.concatenate([wq_own[d], wq_other[d]], axis=0)
-        flipped = jnp.concatenate([wq_other[d], wq_own[d]], axis=0)
-        messages[d][:rows, :] = mm(gained, jnp.where(s == 0, weight, flipped)).astype(BF16)
-        messages[d][rows : rows + PAD, :] = extra
-        here = pl.ds(pl.multiple_of((m ^ d) * cols, cols), cols)
-        weight = of_layer(1, wout_own, wout_other, here, slice(None))
-        messages[d][rows + PAD :, :] = mm(og_ref[s], weight, NTR).astype(BF16)
-
-
-def score_grads(tracts, slots, heads, cols, att_ref, blocks, probs_ref, grads_ref, scores_ref, soft_ref):
+    for i in range(n):
+        messages[i][:rows, :] = mm(gained, wq_ref[i]).astype(BF16)
+        messages[i][rows:, :] = extra
+
+
+def score_grads(tracts, slots, heads, start, att_ref, blocks, probs_ref, grads_ref, scores_ref, soft_ref):
     length = att_ref.shape[0] // tracts
     for c in range(tracts):
         here, span = slice(c * length, (c + 1) * length), slot_slice(c, slots)
         for h in range(heads):
             there = slice(h * HEAD, (h + 1) * HEAD)
-            beyond = slice(cols + h * HEAD, cols + (h + 1) * HEAD)
+            beyond = slice(start + h * HEAD, start + (h + 1) * HEAD)
             grads_ref[c * heads + h] = mm(att_ref[here, there], blocks[span, beyond], NTR)
     for c in range(tracts):
         both = slice(c * heads, (c + 1) * heads)
@@ -416,12 +476,10 @@
 
 def last_layer_body(n, width, tracts, slots, *refs):
     ids_ref, counts_ref = refs[:2]
-    messages = refs[2 : 2 + n]
-    own, other, dkv_ref, out_ref, scale_ref = refs[2 + n : 7 + n]
-    raw_ref, query_ref, att_ref, probs_ref, grads_ref, scores_ref, soft_ref, blocks, sems = refs[
-        7 + n :
-    ]
-    waits = load_slots(own, other, ids_ref, tracts, slots, blocks, sems, own.shape[2] - blocks.shape[1])
+    messages, grads = refs[2 : 2 + n], refs[2 + n : -13]
+    own, other, dkv_ref, out_ref, scale_ref = refs[-13:-8]
+    raw_ref, query_ref, att_ref, probs_ref, grads_ref, scores_ref, soft_ref, blocks = refs[-8:]
+    fill_slots(own, other, ids_ref, tracts, slots, blocks, own.shape[2] - blocks.shape[1])
     s = lax.axis_index("section")
     rows, cols = raw_ref.shape
     raw = jnp.zeros((rows, cols), F32)
@@ -429,9 +487,11 @@
     grad = jnp.zeros((rows, cols), F32)
     for d in range(n):
         raw = raw + messages[d][:rows, :].astype(F32)
-        extra = messages[d][rows : rows + PAD, :].astype(F32)
+        extra = messages[d][rows:, :].astype(F32)
         square = square + extra[0:1, :] + extra[1:2, :]
-        grad = grad + messages[d][rows + PAD :, :].astype(F32)
+    for part in grads:
+        start = max(part.shape[0] - 2 * rows, 0)
+        grad = grad + part[start : start + rows, :].astype(F32)
     scale = lax.rsqrt(to_column(square) / width + EPSILON)
     scale_ref[...] = jnp.broadcast_to(scale, scale_ref.shape)
     raw = raw * scale
@@ -440,8 +500,6 @@
     att_ref[...] = grad.astype(BF16)
     length = rows // tracts
     heads = cols // HEAD
-    for copy in waits:
-        copy.wait()
     for c in range(tracts):
         here, span = slice(c * length, (c + 1) * length), slot_slice(c, slots)
         for h in range(heads):
@@ -476,30 +534,34 @@
         sent_ref[r : r + chunk, :] = jnp.where(first, values, keys).astype(BF16)
 
 
+def part_grads_body(keep, enc_ref, dkv_ref, out_ref):
+    cols = out_ref.shape[1]
+    kind = lax.axis_index("section") if keep else 1 - lax.axis_index("section")
+    here = pl.ds(pl.multiple_of(kind * cols, cols), cols)
+    out_ref[...] = mm(enc_ref[...], dkv_ref[:, here]).astype(BF16)
+
+
 def last_grads_body(
-    tracts, slots, ids_ref, dkv_ref, own, other, enc_ref, kept_ref, sent_ref, rows_ref, sems
+    tracts, slots, ids_ref, dkv_ref, own, other, enc_ref, kept_ref, sent_ref
 ):
-    waits = load_slots(own, other, ids_ref, tracts, slots, rows_ref, sems)
-    for i, copy in enumerate(waits):
-        copy.wait()
-        here = slice(i * NT, (i + 1) * NT)
-        enc_ref[:, here] = rows_ref[here, :].T
+    for c in range(tracts):
+        for k in range(slots):
+            here = slice((c * slots + k) * NT, (c * slots + k + 1) * NT)
+            enc_ref[:, here] = slot_value(own, other, ids_ref, c, k, 0, enc_ref.shape[0]).T
     weight_grads(enc_ref, dkv_ref, kept_ref, sent_ref)
 
 
 def back_between_body(n, width, *refs):
-    gain_own, gain_other, rows_ref, og_ref, scale_ref, wq_own, wq_other = refs[:7]
-    wout_own, wout_other = refs[7:9]
-    pieces, messages = refs[9 : 9 + n], refs[9 + n :]
+    gain_own, gain_other, rows_ref, og_ref, scale_ref, wq_ref = refs[:6]
+    wout_own, wout_other = refs[6:8]
+    pieces, messages = refs[8 : 8 + n], refs[8 + n :]
     s, m = lax.axis_index("section"), lax.axis_index("mp")
     rows, feats = rows_ref.shape
     cols = pieces[0].shape[1]
     normed = jnp.zeros((rows, feats), F32)
     total = jnp.zeros((1, rows), F32)
     for d in range(n):
-        weight = jnp.concatenate([wq_own[d], wq_other[d]], axis=0)
-        flipped = jnp.concatenate([wq_other[d], wq_own[d]], axis=0)
-        normed = normed + mm(pieces[d][:rows, :], jnp.where(s == 0, weight, flipped), NTR)
+        normed = normed + mm(pieces[d][:rows, :], wq_ref[d], NTR)
         total = total + pieces[d][rows:, :].astype(F32)[0:1, :]
     scale = scale_ref[:, 0:1]
     wide = rows_ref[...].astype(F32)
@@ -507,38 +569,37 @@
     grad = og_ref[s].astype(F32) + scale * gain * normed
     grad = grad - wide * (scale * scale * (to_column(total) / width))
     grad = grad.astype(BF16)
-    for d in range(n):
+    for i, d in enumerate(places(n)):
         here = pl.ds(pl.multiple_of((m ^ d) * cols, cols), cols)
         weight = of_layer(0, wout_own, wout_other, here, slice(None))
-        messages[d][...] = mm(grad, weight, NTR).astype(BF16)
+        messages[i][...] = mm(grad, weight, NTR).astype(BF16)
 
 
 def first_back_body(n, tracts, slots, *refs):
     ids_ref, query_ref, probs_ref = refs[:3]
     grads = refs[3 : 3 + n]
     own, other, dkv_ref = refs[3 + n : 6 + n]
-    att_ref, grads_ref, scores_ref, soft_ref, blocks, sems = refs[6 + n :]
-    waits = load_slots(own, other, ids_ref, tracts, slots, blocks, sems)
+    att_ref, grads_ref, scores_ref, soft_ref, blocks = refs[6 + n :]
+    fill_slots(own, other, ids_ref, tracts, slots, blocks, query_ref.shape[1])
     rows, cols = query_ref.shape
     grad = jnp.zeros((rows, cols), F32)
     for d in range(n):
         grad = grad + grads[d][...].astype(F32)
     att_ref[...] = grad.astype(BF16)
     heads = cols // HEAD
-    for copy in waits:
-        copy.wait()
     score_grads(
-        tracts, slots, heads, cols, att_ref, blocks, probs_ref, grads_ref, scores_ref, soft_ref
+        tracts, slots, heads, 0, att_ref, blocks, probs_ref, grads_ref, scores_ref, soft_ref
     )
     slot_grads(tracts, slots, heads, cols, query_ref, att_ref, scores_ref, soft_ref, dkv_ref)
 
 
 def along_mp(value, n):
-    return [value] + [xor_move(value, "mp", d) for d in range(1, n)]
+    return [value] + [xor_move(value, "mp", d) for d in places(n)[1:]]
 
 
 def scattered(messages):
-    return [messages[0]] + [xor_move(messages[d], "mp", d) for d in range(1, len(messages))]
+    order = places(len(messages))
+    return [messages[0]] + [xor_move(messages[i], "mp", order[i]) for i in range(1, len(messages))]
 
 
 def on_device(
@@ -568,67 +629,85 @@
     first = s == 0
     gain = norm_gain.reshape(n, 1, feats)
     wq, wk, wv, wout = w_query[0], w_key[0], w_value[0], w_out[0]
-    gains, wqs, wks, wvs, wouts = ((w, swap(w)) for w in (gain, wq, wk, wv, wout))
-
-    def share_out(deps):
-        return call(
-            functools.partial(shares_body, n),
-            [shape((rows * feats // cols, cols))] + [shape((feats // 2, cols))] * n,
-            [vm()] * 3,
-            deps=deps,
-        )(*wqs, segment_input[:, 0])
+    gains, wqs, wouts = ((w, swap(w)) for w in (gain, wq, wout))
 
     down_t = enc_down.T
     parts = 2 * dp
     up_rows, down_cols = enc_width // parts, ff // parts
     shares = up_rows % 16 == 0 and enc_width // n == 2 * up_rows and down_cols == HEAD
-    shares = shares and enc_up.shape[1] == 2 * down_cols and dp == 4
+    shares = shares and enc_up.shape[1] == 2 * down_cols and dp == 4 and n == 4
+    shares = shares and feats % (32 * parts) == 0 and cols == enc_up.shape[1]
     if shares:
-        share = call(
-            share_body,
-            [shape((2 * up_rows, 2 * down_cols))],
-            [hbm_only(), hbm_only()],
-            [pltpu.SemaphoreType.DMA((3,))],
-        )(enc_up, down_t)[0]
-        line = along_mp(share, n)
-        line_done = line[1:]
-        piece = (n, up_rows, 2 * down_cols)
-        up, down = call(
-            functools.partial(line_body, n),
-            [shape(piece)] * 2,
-            [vm()] * n,
-            deps=[wqs[1], wouts[1]],
-        )(*line)
-        own, *query_shares = share_out(line_done)
+        own_shape = shape((rows * feats // cols, cols))
+        messages = [shape((2 * up_rows + feats // parts, 2 * down_cols))] * (n - 1)
+        rest = own_shape.shape[0] // 2
+        longer = shape((messages[0].shape[0] + rest, cols))
+        *messages, own = call(
+            functools.partial(share_body, n),
+            messages + [longer, own_shape],
+            [hbm()] * 5,
+            [pltpu.SemaphoreType.DMA((3 + n + feats // cols,))],
+            limit=FIRST_LIMIT,
+        )(enc_up, down_t, *wqs, segment_input[:, 0])
+        line = scattered(messages)
+        *grads, far_grads = call(
+            functools.partial(out_grads_body, n),
+            [shape((rows, cols))] * n + [shape((2 * rows, cols))],
+            [vm()] * 3,
+            flops=2 * rows * width * cols,
+        )(out_grad[:, 0], *wouts)
+        piece = (n - 1, up_rows + feats // (2 * parts), 2 * down_cols)
+        up, down, near, message, own = call(
+            functools.partial(line_body, n, up_rows),
+            [shape(piece)] * 2
+            + [shape((rest, cols)), shape((rest + 2 * rows, cols)), own_shape],
+            [vm()] * (n + 2),
+        )(*line, own, far_grads)
         inner, outer = [(1, 2), (2, 1)], [(1, 0), (2, 3)]
         up1, down2 = xor_move(up, "dp", 1), xor_move(down, "dp", 2)
-        near, far_inner = xor_move(own, "mp", 1), lax.ppermute(own, "mp", inner)
-        ups, downs = call(
-            pair_body, [shape((2,) + piece)] * 2, [vm()] * 4, deps=[near, far_inner, wks[1]]
-        )(up, up1, down, down2)
+        far_inner = lax.ppermute(own, "mp", inner)
+        message = xor_move(message, "mp", 1)
+        ups, downs, message, near = call(
+            pair_body,
+            [shape((2,) + piece)] * 2 + [shape((own_shape.shape[0] + 2 * rows, cols)), own_shape],
+            [vm()] * 8,
+            deps=[far_inner],
+        )(up, up1, down, down2, near, message, grads[1], grads[2])
         up2, down1 = xor_move(ups, "dp", 2), xor_move(downs, "dp", 1)
         next_outer = lax.ppermute(far_inner, "mp", outer)
-        next_inner = lax.ppermute(near, "mp", inner)
-        gathered = call(
+        message = lax.ppermute(message, "mp", inner)
+        gathered, next_inner, close, wk, wv = call(
             gather_body,
-            [shape((parts,) + piece)],
-            [vm()] * 6,
-            deps=[next_outer, next_inner, wvs[1]],
-        )(up, up1, up2, down, down2, down1)[0]
-        pieces = [gathered, swap(gathered)]
+            [shape((parts,) + piece), own_shape, shape((rows, cols))]
+            + [shape((enc_width, cols))] * 2,
+            [vm()] * 10,
+            deps=[next_outer],
+        )(up, up1, up2, down, down2, down1, message, grads[3], wk, wv)
+        pieces = [gathered, swap(gathered), enc_up, down_t, *wqs]
         far_outer = lax.ppermute(next_inner, "mp", outer)
-        query_shares = scattered(query_shares)
+        close = xor_move(close, "mp", 1)
+        grad_parts = [grads[0], message, close]
         row_pieces = [own, near, next_inner, next_outer, far_inner, far_outer]
-        before_projected = query_shares[1:] + [far_outer]
+        before_projected = [far_outer, close]
         scratch = [
             pltpu.VMEM((n, parts, up_rows, enc_up.shape[1]), BF16),
             pltpu.VMEM((n, enc_width // n, ff), BF16),
-            pltpu.SemaphoreType.DMA((parts * n,)),
-            pltpu.SemaphoreType.DMA((2 * parts * n,)),
         ]
     else:
-        own, *query_shares = share_out([])
-        row_pieces, query_shares = along_mp(own, n), scattered(query_shares)
+        own = call(
+            functools.partial(rows_body, cols), [shape((rows * feats // cols, cols))], [vm()]
+        )(segment_input[:, 0])[0]
+        grad_parts = call(
+            functools.partial(out_grads_body, n),
+            [shape((rows, cols))] * n,
+            [vm()] * 3,
+            flops=2 * rows * width * cols,
+        )(out_grad[:, 0], *wouts)
+        row_pieces, grad_parts = along_mp(own, n), scattered(grad_parts)
+        query_shares = call(
+            functools.partial(query_shares_body, n), [shape((feats, cols))] * n, [vm()] * 2
+        )(*wqs)
+        projection = jnp.stack(scattered(query_shares))
         before_projected = []
         pieces = [
             lax.all_gather(enc_up, "mp", axis=0),
@@ -640,18 +719,23 @@
             pltpu.SemaphoreType.DMA((2,)),
         ]
 
+    wks, wvs = (wk, swap(wk)), (wv, swap(wv))
+
     pool_rows = pool_tokens[:, 0].reshape(half * length, enc_width)
     normed = call(
         norm_body, [shape((half * length, enc_width))], [vm(), vm()], flops=half * length * enc_width
     )(pool_rows, enc_gain[None, :])[0]
-    enc = call(
+    encoded = call(
         functools.partial(encoder_body, n, parts, not shares),
-        [shape((half * length, enc_width))],
-        [vm()] * 4 if shares else [vm()] * 2 + [hbm()] * 2,
+        [shape((half * length, enc_width))] + [shape((n, feats, cols))] * shares,
+        [vm()] * 8 if shares else [vm()] * 2 + [hbm()] * 2,
         [pltpu.VMEM((half * length, ff), BF16)] + scratch,
         flops=4 * half * length * enc_width * ff,
         limit=ENCODER_LIMIT if shares else 48 * 1024 * 1024,
-    )(pool_rows, normed, *pieces)[0]
+    )(pool_rows, normed, *pieces)
+    enc = encoded[0]
+    if shares:
+        projection = encoded[1]
     enc_own, pool0_own = call(
         projected_body,
         [shape((half, length, enc_width + 2 * cols)), shape((half, length, 2 * cols))],
@@ -660,16 +744,11 @@
         deps=before_projected,
     )(enc, *wks, *wvs)
     pool0_other = swap(pool0_own)
-    projection = call(
-        functools.partial(projection_body, n), [shape((n, feats // 2, cols))], [vm()] * n
-    )(*query_shares)[0]
-    projections = (projection, swap(projection))
-
     heads = cols // HEAD
     chunk = rows // tracts
     slot_rows = tracts * slots * NT
     blocks_scratch = pltpu.VMEM((slot_rows, 2 * cols), BF16)
-    slot_sems = pltpu.SemaphoreType.DMA((tracts * slots,))
+    part_scratch = pltpu.VMEM((slot_rows, cols), BF16)
     wide_scores = pltpu.VMEM((tracts * heads, chunk, slots * NT), F32)
     bf_scores = pltpu.VMEM((tracts * heads, chunk, slots * NT), BF16)
     attention_flops = 2 * rows * slots * NT * cols
@@ -682,7 +761,7 @@
             shape((tracts * heads, chunk, slots * NT), F32),
         ],
         [smem(), smem()] + [vm()] * (6 + len(row_pieces)),
-        [blocks_scratch, slot_sems],
+        [blocks_scratch],
         flops=2 * rows * width * cols + 2 * attention_flops,
         passing=[enc_own],
     )(ids, counts, *gains, *wqs, *row_pieces, pool0_own, pool0_other)
@@ -690,16 +769,16 @@
     att_pieces = along_mp(att, n)
     rows1, *messages = call(
         functools.partial(between_body, n),
-        [shape((rows, feats))] + [shape((2 * rows + PAD, cols))] * n,
-        [vm()] * (8 + n),
-        flops=6 * rows * feats * n * cols,
+        [shape((rows, feats))] + [shape((rows + PAD, cols))] * n,
+        [vm()] * (6 + n),
+        flops=4 * rows * feats * n * cols,
         deps=[enc_other],
-    )(*gains, own, *wouts, *projections, out_grad[:, 0], *att_pieces)
+    )(*gains, own, *wouts, projection, *att_pieces)
     query_pieces = scattered(messages)
     dkv1, grad_query, scale1 = call(
         functools.partial(last_layer_body, n, width, tracts, slots),
         [shape((slot_rows, 2 * cols)), shape((rows + PAD, cols)), shape((rows, HEAD), F32)],
-        [smem(), smem()] + [vm()] * (n + 2),
+        [smem(), smem()] + [vm()] * (n + len(grad_parts) + 2),
         [
             pltpu.VMEM((rows, cols), F32),
             pltpu.VMEM((rows, cols), BF16),
@@ -709,31 +788,29 @@
             bf_scores,
             bf_scores,
             blocks_scratch,
-            slot_sems,
         ],
         flops=5 * attention_flops,
-    )(ids, counts, *query_pieces, enc_own, enc_other)
+    )(ids, counts, *query_pieces, *grad_parts, enc_own, enc_other)
     query_grads = along_mp(grad_query, n)
     enc_slots, kept1, sent1 = call(
         functools.partial(last_grads_body, tracts, slots),
         [shape((enc_width, slot_rows)), shape((enc_width, cols)), shape((enc_width, cols))],
-        [smem(), vm(), hbm(), hbm()],
-        [pltpu.VMEM((slot_rows, enc_width), BF16), slot_sems],
+        [smem(), vm(), vm(), vm()],
         flops=4 * enc_width * slot_rows * cols,
     )(ids, dkv1, enc_own, enc_other)
     half_shape = shape((enc_width // 2, cols))
     *messages, kept1, sent1 = call(
         functools.partial(back_between_body, n, width),
         [shape((rows, cols))] * n,
-        [vm()] * (9 + n),
+        [vm()] * (8 + n),
         flops=4 * rows * feats * n * cols,
         passing=[kept1, sent1],
-    )(*gains, rows1, out_grad[:, 0], scale1, *projections, *wouts, *query_grads)
+    )(*gains, rows1, out_grad[:, 0], scale1, projection, *wouts, *query_grads)
     grad_pieces0 = scattered(messages)
 
     def over_dp(parts, order, deps=()):
         moved = [xor_move(part, "dp", by) for part, by in zip(parts, order)]
-        return call(functools.partial(add_body, 2), [half_shape] * 2, [vm()] * 4, deps=deps)(
+        return call(functools.partial(add_body, 2), [half_shape] * 2, [vm()] * 4, first=deps)(
             *parts, *moved
         )
 
@@ -755,18 +832,20 @@
             wide_scores,
             bf_scores,
             bf_scores,
-            blocks_scratch,
-            slot_sems,
+            part_scratch,
         ],
         flops=3 * attention_flops,
     )(ids, query0, probs0, *grad_pieces0, pool0_own, pool0_other)[0]
-    kept0, sent0 = call(
-        weight_grads,
-        [shape((enc_width, cols)), shape((enc_width, cols))],
-        [vm()] * 2,
-        flops=4 * enc_width * slot_rows * cols,
-        deps=[sum1],
-    )(enc_slots, dkv0)
+    sent0, kept0 = (
+        call(
+            functools.partial(part_grads_body, keep),
+            [shape((enc_width, cols))],
+            [vm()] * 2,
+            flops=2 * enc_width * slot_rows * cols,
+            deps=[] if keep else [sum1],
+        )(enc_slots, dkv0)[0]
+        for keep in (False, True)
+    )
     sum0 = summed(kept0, sent0)
     received = swap(jnp.where(first, sum1, sum0))
     key_total = jnp.where(first, sum0, received)

time: 185 us -> 163 us (0.88)
  Pallas kernels: 38.2 us -> 26.9 us
  starting transfers between devices: 57.3 us -> 48 us
  local copies, waits for them, and re-layouts: 4.43 us -> 1.15 us
  waiting for transfers between devices: 82.6 us -> 84.9 us
    pallas_call x22, Pallas kernels: 38.2 us -> 26.9 us  [run(): pl.pallas_call(kernel, out_shape=list(outs) + [shape(x.shape, x.dtype) fo...]
    ppermute x43 -> x40, starting transfers between devices: 53.2 us -> 43.7 us  [xor_move(): return lax.ppermute(value, axis, [(i, i ^ by) for i in range(count)])]
    ppermute x43 -> x40, waiting for transfers between devices: 73.6 us -> 76.9 us  [xor_move(): return lax.ppermute(value, axis, [(i, i ^ by) for i in range(count)])]
    unnamed x30 -> x34, local copies, waits for them, and re-layouts: 4.39 us -> 1.12 us
  transfers between devices with their start and end apart: 47 -> 44, of which waited for: 23 -> 26; matrix products, arithmetic and copies ran while one was open for 0% -> 0% of each run, Pallas kernels for 12% -> 9%
where the time goes in v3:
time: 163 us
  waiting for transfers between devices  84.9 us (52%)
  starting transfers between devices  48 us (29%)
  Pallas kernels  26.9 us (17%)
    ppermute x40, waiting for transfers between devices, xor_move(): return lax.ppermute(value, axis, [(i, i ^ by) for i in range(count)])  76.9 us
    ppermute x40, starting transfers between devices, xor_move(): return lax.ppermute(value, axis, [(i, i ^ by) for i in range(count)])  43.7 us
    pallas_call x22, Pallas kernels, run(): pl.pallas_call(kernel, out_shape=list(outs) + [shape(x.shape, x.dtype) fo...  26.9 us
    ppermute x1, waiting for transfers between devices, on_device(): next_outer = lax.ppermute(far_inner, 'mp', outer)  7.92 us
  transfers between devices with their start and end apart: 44, of which 26 were waited for; matrix products, arithmetic and copies ran while one was open for 0% of the time, Pallas kernels for 9%

profile of v3, /device:TPU:0, one launch (start us, length us, event | category | flops | bytes accessed | tf_op | source)
XLA Modules:
  0.0 163.1 jit_solution(9852466683914265854)
XLA Ops:
  1.2 2.4 %collective-permute-done.1.refs_3_.refs_7_.refs_5_ = bf16[2048,256]{1,0:T(8,128)(2,1)S(1)} collective-permute-done((bf16[2048,256]{1,0:T(8,128)(2,1)}, bf16[2048,256]{1,0:T(8,128)(2,1)S(1)}, u32[]{:S(2)}, u32[]{:S(2)}) %collective-permute-start.1) | collective-permute-done | bytes 1048608 | tf_op jit(solution)/shard_map/ppermute | solution.py:32
  4.7 2.1 %shard_map.140 = (bf16[288,256]{1,0:T(8,128)(2,1)}, bf16[288,256]{1,0:T(8,128)(2,1)}, bf16[288,256]{1,0:T(8,128)(2,1)}, bf16[544,256]{1,0:T(8,128)(2,1)}, bf16[512,256]{1,0:T(8,128)(2,1)}) custom-call(bf16[896,256]{1,0:T(8,128)(2,1)} %refs_4_.1, bf16[224,1024]{1,0:T(8,128)(2,1)} %bitcast.27, bf16[2048,256]{1,0:T(8,128)(2,1)} %bitcast.16, ...), custom_call_target="tpu_custom_call" | custom-call | bytes 983 | tf_op jit(solution)/shard_map/pallas_call | solution.py:70
  6.8 3.0 %collective-permute-start.4 = (bf16[544,256]{1,0:T(8,128)(2,1)}, bf16[544,256]{1,0:T(8,128)(2,1)S(1)}, u32[]{:S(2)}, u32[]{:S(2)}) collective-permute-start(bf16[544,256]{1,0:T(8,128)(2,1)} %get-tuple-element.66), channel_id=1, source_target_pairs={{0,1},{1,0},{2,3},{3,2},{4,5},{5,4},{6,7},{7,6},{8,9},{9,8},{10,11... | collective-permute-start | bytes 835592 | tf_op jit(solution)/shard_map/ppermute | solution.py:32
  9.8 2.6 %collective-permute-start.2 = (bf16[288,256]{1,0:T(8,128)(2,1)}, bf16[288,256]{1,0:T(8,128)(2,1)S(1)}, u32[]{:S(2)}, u32[]{:S(2)}) collective-permute-start(bf16[288,256]{1,0:T(8,128)(2,1)} %get-tuple-element.64), channel_id=1, source_target_pairs={{0,2},{1,3},{2,0},{3,1},{4,6},{5,7},{6,4},{7,5},{8,10},{9,11},{10,... | collective-permute-start | bytes 442376 | tf_op jit(solution)/shard_map/ppermute | solution.py:32
  13.0 7.4 %collective-permute-done.2.refs_1_ = bf16[288,256]{1,0:T(8,128)(2,1)S(1)} collective-permute-done((bf16[288,256]{1,0:T(8,128)(2,1)}, bf16[288,256]{1,0:T(8,128)(2,1)S(1)}, u32[]{:S(2)}, u32[]{:S(2)}) %collective-permute-start.2) | collective-permute-done | bytes 147488 | tf_op jit(solution)/shard_map/ppermute | solution.py:32
  20.4 5.2 %collective-permute-done.3.refs_2_ = bf16[288,256]{1,0:T(8,128)(2,1)S(1)} collective-permute-done((bf16[288,256]{1,0:T(8,128)(2,1)}, bf16[288,256]{1,0:T(8,128)(2,1)S(1)}, u32[]{:S(2)}, u32[]{:S(2)}) %collective-permute-start.3) | collective-permute-done | bytes 147488 | tf_op jit(solution)/shard_map/ppermute | solution.py:32
  30.6 2.9 %collective-permute-done.6.refs_1_ = bf16[3,144,256]{2,1,0:T(8,128)(2,1)S(1)} collective-permute-done((bf16[3,144,256]{2,1,0:T(8,128)(2,1)S(1)}, bf16[3,144,256]{2,1,0:T(8,128)(2,1)S(1)}, u32[]{:S(2)}, u32[]{:S(2)}) %collective-permute-start.6) | collective-permute-done | bytes 221216 | tf_op jit(solution)/shard_map/ppermute | solution.py:32
  41.5 7.9 %collective-permute-done.13.refs_10_.refs_9_ = bf16[512,256]{1,0:T(8,128)(2,1)S(1)} collective-permute-done((bf16[512,256]{1,0:T(8,128)(2,1)S(1)}, bf16[512,256]{1,0:T(8,128)(2,1)S(1)}, u32[]{:S(2)}, u32[]{:S(2)}) %collective-permute-start.13) | collective-permute-done | bytes 262176 | tf_op jit(solution)/shard_map/ppermute | solution.py:677
  51.9 2.8 %collective-permute-start.18 = (bf16[256,256]{1,0:T(8,128)(2,1)S(1)}, bf16[256,256]{1,0:T(8,128)(2,1)S(1)}, u32[]{:S(2)}, u32[]{:S(2)}) collective-permute-start(bf16[256,256]{1,0:T(8,128)(2,1)S(1)} %get-tuple-element.87), channel_id=1, source_target_pairs={{0,1},{1,0},{2,3},{3,2},{4,5},{5,4},{6,7},{7,6},{8,9},{9,8},{10,11... | collective-permute-start | bytes 393224 | tf_op jit(solution)/shard_map/ppermute | solution.py:32
  55.5 5.8 %shard_map.146 = (bf16[1024,896]{1,0:T(8,128)(2,1)S(1)}, bf16[4,512,256]{2,1,0:T(8,128)(2,1)S(1)}) custom-call(bf16[1024,896]{1,0:T(8,128)(2,1)S(1)} %bitcast.24, bf16[1024,896]{1,0:T(8,128)(2,1)S(1)} %shard_map.143.refs_1_, bf16[8,3,144,256]{3,2,1,0:T(8,128)(2,1)S(1)} %get-tuple-element.80.refs_2_, ...), custom_call_target="tpu_custom_call" | custom-call | flops 3758096 | bytes 2883 | tf_op jit(solution)/shard_map/pallas_call | solution.py:70
  61.4 2.7 %collective-permute-done.18.refs_6_.refs_8_ = bf16[256,256]{1,0:T(8,128)(2,1)S(1)} collective-permute-done((bf16[256,256]{1,0:T(8,128)(2,1)S(1)}, bf16[256,256]{1,0:T(8,128)(2,1)S(1)}, u32[]{:S(2)}, u32[]{:S(2)}) %collective-permute-start.18) | collective-permute-done | bytes 131104 | tf_op jit(solution)/shard_map/ppermute | solution.py:32
  64.1 2.4 %shard_map.147 = (bf16[8,128,1408]{2,1,0:T(8,128)(2,1)S(1)}, bf16[8,128,512]{2,1,0:T(8,128)(2,1)S(1)}) custom-call(bf16[1024,896]{1,0:T(8,128)(2,1)S(1)} %get-tuple-element.84.refs_0_, bf16[896,256]{1,0:T(8,128)(2,1)S(1)} %get-tuple-element.85.refs_1_, bf16[896,256]{1,0:T(8,128)(2,1)S(1)} %collective-permute-done.16.refs_2_, ...), custom_call_target="tpu_custom_call" | custom-call | flops 1879048 | bytes 3932 | tf_op jit(solution)/shard_map/pallas_call | solution.py:70
  67.0 2.2 %collective-permute-done.refs_3_.refs_1_ = f32[4,1,512]{2,1,0:T(1,128)S(1)} collective-permute-done((f32[4,1,512]{2,1,0:T(1,128)S(1)}, f32[4,1,512]{2,1,0:T(1,128)S(1)}, u32[]{:S(2)}, u32[]{:S(2)}) %collective-permute-start) | collective-permute-done | bytes 8224 | tf_op jit(solution)/shard_map/ppermute | solution.py:32
  69.2 2.6 %shard_map.148 = (bf16[256,256]{1,0:T(8,128)(2,1)S(1)}, bf16[256,256]{1,0:T(8,128)(2,1)S(1)}, f32[8,64,512]{2,1,0:T(8,128)S(1)}, bf16[8,128,1408]{2,1,0:T(8,128)(2,1)S(1)}) custom-call(s32[2,4,4]{2,1,0:T(4,128)S(1)} %bitcast.35, s32[2,4]{1,0:T(2,128)S(1)} %bitcast.39, f32[4,1,512]{2,1,0:T(1,128)S(1)} %bitcast.32, ...), custom_call_target="tpu_custom_call", output_to_operand_aliasing={{3}: (14, {})} | custom-call | flops 402653 | bytes 1310 | tf_op jit(solution)/shard_map/pallas_call | solution.py:70
  72.0 1.9 %collective-permute-start.21 = (bf16[256,256]{1,0:T(8,128)(2,1)S(1)}, bf16[256,256]{1,0:T(8,128)(2,1)S(1)}, u32[]{:S(2)}, u32[]{:S(2)}) collective-permute-start(bf16[256,256]{1,0:T(8,128)(2,1)S(1)} %get-tuple-element.90.refs_6_), channel_id=1, source_target_pairs={{0,3},{1,2},{2,1},{3,0},{4,7},{5,6},{6,5},{7,4},{8,11},{9,10},{10,... | collective-permute-start | bytes 393224 | tf_op jit(solution)/shard_map/ppermute | solution.py:32
  75.5 7.9 %collective-permute-done.20.refs_7_ = bf16[256,256]{1,0:T(8,128)(2,1)S(1)} collective-permute-done((bf16[256,256]{1,0:T(8,128)(2,1)S(1)}, bf16[256,256]{1,0:T(8,128)(2,1)S(1)}, u32[]{:S(2)}, u32[]{:S(2)}) %collective-permute-start.20) | collective-permute-done | bytes 131104 | tf_op jit(solution)/shard_map/ppermute | solution.py:32
  85.5 2.8 %collective-permute-start.24 = (bf16[272,256]{1,0:T(8,128)(2,1)S(1)}, bf16[272,256]{1,0:T(8,128)(2,1)S(1)}, u32[]{:S(2)}, u32[]{:S(2)}) collective-permute-start(bf16[272,256]{1,0:T(8,128)(2,1)S(1)} %get-tuple-element.93), channel_id=1, source_target_pairs={{0,2},{1,3},{2,0},{3,1},{4,6},{5,7},{6,4},{7,5},{8,10},{9,11},{10,... | collective-permute-start | bytes 417800 | tf_op jit(solution)/shard_map/ppermute | solution.py:32
  90.0 9.1 %collective-permute-done.24.refs_3_ = bf16[272,256]{1,0:T(8,128)(2,1)S(1)} collective-permute-done((bf16[272,256]{1,0:T(8,128)(2,1)S(1)}, bf16[272,256]{1,0:T(8,128)(2,1)S(1)}, u32[]{:S(2)}, u32[]{:S(2)}) %collective-permute-start.24) | collective-permute-done | bytes 139296 | tf_op jit(solution)/shard_map/ppermute | solution.py:32
  99.6 2.7 %shard_map.150 = (bf16[2048,512]{1,0:T(8,128)(2,1)S(1)}, bf16[272,256]{1,0:T(8,128)(2,1)S(1)}, f32[256,128]{1,0:T(8,128)S(1)}) custom-call(s32[2,4,4]{2,1,0:T(4,128)S(1)} %bitcast.36, s32[2,4]{1,0:T(2,128)S(1)} %bitcast.40, bf16[272,256]{1,0:T(8,128)(2,1)S(1)} %get-tuple-element.92.refs_2_, bf16[272,256]{1,0:T(8,128)(2,1)S(1)} %collective-permute-done.24.refs_3_, ...), custom_call_target="tpu_custom_call" | custom-call | flops 335544 | bytes 2367 | tf_op jit(solution)/shard_map/pallas_call | solution.py:70
  102.2 2.5 %collective-permute-start.27 = (bf16[272,256]{1,0:T(8,128)(2,1)S(1)}, bf16[272,256]{1,0:T(8,128)(2,1)S(1)}, u32[]{:S(2)}, u32[]{:S(2)}) collective-permute-start(bf16[272,256]{1,0:T(8,128)(2,1)S(1)} %get-tuple-element.103.refs_8_), channel_id=1, source_target_pairs={{0,2},{1,3},{2,0},{3,1},{4,6},{5,7},{6,4},{7,5},{8,10},{9,11},{10,... | collective-permute-start | bytes 417800 | tf_op jit(solution)/shard_map/ppermute | solution.py:32
  104.7 2.2 %collective-permute-start.28 = (bf16[272,256]{1,0:T(8,128)(2,1)S(1)}, bf16[272,256]{1,0:T(8,128)(2,1)S(1)}, u32[]{:S(2)}, u32[]{:S(2)}) collective-permute-start(bf16[272,256]{1,0:T(8,128)(2,1)S(1)} %get-tuple-element.103.refs_8_), channel_id=1, source_target_pairs={{0,3},{1,2},{2,1},{3,0},{4,7},{5,6},{6,5},{7,4},{8,11},{9,10},{10,... | collective-permute-start | bytes 417800 | tf_op jit(solution)/shard_map/ppermute | solution.py:32
  106.9 3.1 %shard_map.151 = (bf16[896,2048]{1,0:T(8,128)(2,1)S(1)}, bf16[896,256]{1,0:T(8,128)(2,1)S(1)}, bf16[896,256]{1,0:T(8,128)(2,1)S(1)}) custom-call(s32[2,4,4]{2,1,0:T(4,128)S(1)} %bitcast.37, bf16[2048,512]{1,0:T(8,128)(2,1)S(1)} %get-tuple-element.97.refs_1_, bf16[8,128,1408]{2,1,0:T(8,128)(2,1)S(1)} %get-tuple-element.91.refs_9_.refs_2_, ...), custom_call_target="tpu_custom_call" | custom-call | flops 1879048 | bytes 4587 | tf_op jit(solution)/shard_map/pallas_call | solution.py:70
  110.0 5.0 %collective-permute-done.27.refs_9_ = bf16[272,256]{1,0:T(8,128)(2,1)S(1)} collective-permute-done((bf16[272,256]{1,0:T(8,128)(2,1)S(1)}, bf16[272,256]{1,0:T(8,128)(2,1)S(1)}, u32[]{:S(2)}, u32[]{:S(2)}) %collective-permute-start.27) | collective-permute-done | bytes 139296 | tf_op jit(solution)/shard_map/ppermute | solution.py:32
  116.6 1.8 %collective-permute-done.33.refs_1_ = bf16[896,256]{1,0:T(8,128)(2,1)S(1)} collective-permute-done((bf16[896,256]{1,0:T(8,128)(2,1)S(1)}, bf16[896,256]{1,0:T(8,128)(2,1)S(1)}, u32[]{:S(2)}, u32[]{:S(2)}) %collective-permute-start.33) | collective-permute-done | bytes 458784 | tf_op jit(solution)/shard_map/ppermute | solution.py:32
  120.8 1.9 %collective-permute-start.30 = (bf16[256,256]{1,0:T(8,128)(2,1)S(1)}, bf16[256,256]{1,0:T(8,128)(2,1)S(1)}, u32[]{:S(2)}, u32[]{:S(2)}) collective-permute-start(bf16[256,256]{1,0:T(8,128)(2,1)S(1)} %get-tuple-element.107), channel_id=1, source_target_pairs={{0,2},{1,3},{2,0},{3,1},{4,6},{5,7},{6,4},{7,5},{8,10},{9,11},{10,... | collective-permute-start | bytes 393224 | tf_op jit(solution)/shard_map/ppermute | solution.py:32
  122.8 2.6 %collective-permute-start.31 = (bf16[256,256]{1,0:T(8,128)(2,1)S(1)}, bf16[256,256]{1,0:T(8,128)(2,1)S(1)}, u32[]{:S(2)}, u32[]{:S(2)}) collective-permute-start(bf16[256,256]{1,0:T(8,128)(2,1)S(1)} %get-tuple-element.108), channel_id=1, source_target_pairs={{0,3},{1,2},{2,1},{3,0},{4,7},{5,6},{6,5},{7,4},{8,11},{9,10},{10,... | collective-permute-start | bytes 393224 | tf_op jit(solution)/shard_map/ppermute | solution.py:32
  125.4 8.3 %collective-permute-done.30.refs_4_.refs_0_ = bf16[256,256]{1,0:T(8,128)(2,1)S(1)} collective-permute-done((bf16[256,256]{1,0:T(8,128)(2,1)S(1)}, bf16[256,256]{1,0:T(8,128)(2,1)S(1)}, u32[]{:S(2)}, u32[]{:S(2)}) %collective-permute-start.30) | collective-permute-done | bytes 131104 | tf_op jit(solution)/shard_map/ppermute | solution.py:32
  135.7 2.0 %shard_map.153.refs_1_ = bf16[2048,512]{1,0:T(8,128)(2,1)S(1)} custom-call(s32[2,4,4]{2,1,0:T(4,128)S(1)} %bitcast.38, bf16[256,256]{1,0:T(8,128)(2,1)S(1)} %get-tuple-element.99.refs_1_, f32[8,64,512]{2,1,0:T(8,128)S(1)} %get-tuple-element.100.refs_2_, bf16[256,256]{1,0:T(8,128)(2,1)S(1)} %get-tuple-element.106.refs_3_, ...), custom_call_target="tpu_custom_call" | custom-call | flops 201326 | bytes 2097 | tf_op jit(solution)/shard_map/pallas_call | solution.py:70
  137.7 2.4 %collective-permute-done.36.refs_2_ = bf16[448,256]{1,0:T(8,128)(2,1)S(1)} collective-permute-done((bf16[448,256]{1,0:T(8,128)(2,1)S(1)}, bf16[448,256]{1,0:T(8,128)(2,1)S(1)}, u32[]{:S(2)}, u32[]{:S(2)}) %collective-permute-start.36) | collective-permute-done | bytes 229408 | tf_op jit(solution)/shard_map/ppermute | solution.py:32
  146.3 5.6 %collective-permute-done.39.refs_2_ = bf16[448,256]{1,0:T(8,128)(2,1)S(1)} collective-permute-done((bf16[448,256]{1,0:T(8,128)(2,1)S(1)}, bf16[448,256]{1,0:T(8,128)(2,1)S(1)}, u32[]{:S(2)}, u32[]{:S(2)}) %collective-permute-start.39) | collective-permute-done | bytes 229408 | tf_op jit(solution)/shard_map/ppermute | solution.py:32
  155.1 4.0 %collective-permute-done.41.refs_2_ = bf16[448,256]{1,0:T(8,128)(2,1)S(1)} collective-permute-done((bf16[448,256]{1,0:T(8,128)(2,1)S(1)}, bf16[448,256]{1,0:T(8,128)(2,1)S(1)}, u32[]{:S(2)}, u32[]{:S(2)}) %collective-permute-start.41) | collective-permute-done | bytes 229408 | tf_op jit(solution)/shard_map/ppermute | solution.py:32
  160.3 1.8 %collective-permute-done.43 = bf16[896,256]{1,0:T(8,128)(2,1)S(1)} collective-permute-done((bf16[896,256]{1,0:T(8,128)(2,1)S(1)}, bf16[896,256]{1,0:T(8,128)(2,1)S(1)}, u32[]{:S(2)}, u32[]{:S(2)}) %collective-permute-start.43) | collective-permute-done | bytes 458784 | tf_op jit(solution)/shard_map/ppermute | solution.py:32
  (117 shorter events, 42.3 us)
Async XLA Ops:
  1.2 11.3 %collective-permute-start.5 = (bf16[1024,512]{1,0:T(8,128)(2,1)}, bf16[1024,512]{1,0:T(8,128)(2,1)S(1)}, u32[]{:S(2)}, u32[]{:S(2)}) collective-permute-start(bf16[1024,512]{1,0:T(8,128)(2,1)} %bitcast.19), channel_id=1, source_target_pairs={{0,16},{16,0},{1,17},{17,1},{2,18},{18,2},{3,19},{19,3},{4,20},{20... | collective-permute-start | bytes 3145736 | tf_op jit(solution)/shard_map/ppermute | solution.py:32
  6.8 18.8 %collective-permute-start.4 = (bf16[544,256]{1,0:T(8,128)(2,1)}, bf16[544,256]{1,0:T(8,128)(2,1)S(1)}, u32[]{:S(2)}, u32[]{:S(2)}) collective-permute-start(bf16[544,256]{1,0:T(8,128)(2,1)} %get-tuple-element.66), channel_id=1, source_target_pairs={{0,1},{1,0},{2,3},{3,2},{4,5},{5,4},{6,7},{7,6},{8,9},{9,8},{10,11... | collective-permute-start | bytes 835592 | tf_op jit(solution)/shard_map/ppermute | solution.py:32
  9.8 10.5 %collective-permute-start.2 = (bf16[288,256]{1,0:T(8,128)(2,1)}, bf16[288,256]{1,0:T(8,128)(2,1)S(1)}, u32[]{:S(2)}, u32[]{:S(2)}) collective-permute-start(bf16[288,256]{1,0:T(8,128)(2,1)} %get-tuple-element.64), channel_id=1, source_target_pairs={{0,2},{1,3},{2,0},{3,1},{4,6},{5,7},{6,4},{7,5},{8,10},{9,11},{10,... | collective-permute-start | bytes 442376 | tf_op jit(solution)/shard_map/ppermute | solution.py:32
  12.4 13.2 %collective-permute-start.3 = (bf16[288,256]{1,0:T(8,128)(2,1)}, bf16[288,256]{1,0:T(8,128)(2,1)S(1)}, u32[]{:S(2)}, u32[]{:S(2)}) collective-permute-start(bf16[288,256]{1,0:T(8,128)(2,1)} %get-tuple-element.65), channel_id=1, source_target_pairs={{0,3},{1,2},{2,1},{3,0},{4,7},{5,6},{6,5},{7,4},{8,11},{9,10},{10,... | collective-permute-start | bytes 442376 | tf_op jit(solution)/shard_map/ppermute | solution.py:32
  25.7 10.3 %collective-permute-start.8 = (bf16[768,256]{1,0:T(8,128)(2,1)S(1)}, bf16[768,256]{1,0:T(8,128)(2,1)S(1)}, u32[]{:S(2)}, u32[]{:S(2)}) collective-permute-start(bf16[768,256]{1,0:T(8,128)(2,1)S(1)} %get-tuple-element.73), channel_id=1, source_target_pairs={{0,1},{1,0},{2,3},{3,2},{4,5},{5,4},{6,7},{7,6},{8,9},{9,8},{10,11... | collective-permute-start | bytes 1179656 | tf_op jit(solution)/shard_map/ppermute | solution.py:32
  26.8 8.2 %collective-permute-start.9 = (bf16[512,256]{1,0:T(8,128)(2,1)S(1)}, bf16[512,256]{1,0:T(8,128)(2,1)S(1)}, u32[]{:S(2)}, u32[]{:S(2)}) collective-permute-start(bf16[512,256]{1,0:T(8,128)(2,1)S(1)} %get-tuple-element.69.refs_6_.refs_2_), channel_id=1, source_target_pairs={{1,2},{2,1},{5,6},{6,5},{9,10},{10,9},{13,14},{14,13},{17,18},{18,... | collective-permute-start | bytes 786440 | tf_op jit(solution)/shard_map/ppermute | solution.py:668
  36.3 13.1 %collective-permute-start.12 = (bf16[1024,256]{1,0:T(8,128)(2,1)S(1)}, bf16[1024,256]{1,0:T(8,128)(2,1)S(1)}, u32[]{:S(2)}, u32[]{:S(2)}) collective-permute-start(bf16[1024,256]{1,0:T(8,128)(2,1)S(1)} %get-tuple-element.78), channel_id=1, source_target_pairs={{1,2},{2,1},{5,6},{6,5},{9,10},{10,9},{13,14},{14,13},{17,18},{18,... | collective-permute-start | bytes 1572872 | tf_op jit(solution)/shard_map/ppermute | solution.py:678
  37.1 12.3 %collective-permute-start.10 = (bf16[2,3,144,256]{3,2,1,0:T(8,128)(2,1)S(1)}, bf16[2,3,144,256]{3,2,1,0:T(8,128)(2,1)S(1)}, u32[]{:S(2)}, u32[]{:S(2)}) collective-permute-start(bf16[2,3,144,256]{3,2,1,0:T(8,128)(2,1)S(1)} %get-tuple-element.76), channel_id=1, source_target_pairs={{0,8},{4,12},{8,0},{12,4},{1,9},{5,13},{9,1},{13,5},{2,10},{6,14},... | collective-permute-start | bytes 1327112 | tf_op jit(solution)/shard_map/ppermute | solution.py:32
  38.7 10.7 %collective-permute-start.11 = (bf16[2,3,144,256]{3,2,1,0:T(8,128)(2,1)S(1)}, bf16[2,3,144,256]{3,2,1,0:T(8,128)(2,1)S(1)}, u32[]{:S(2)}, u32[]{:S(2)}) collective-permute-start(bf16[2,3,144,256]{3,2,1,0:T(8,128)(2,1)S(1)} %get-tuple-element.77), channel_id=1, source_target_pairs={{0,4},{4,0},{8,12},{12,8},{1,5},{5,1},{9,13},{13,9},{2,6},{6,2},{1... | collective-permute-start | bytes 1327112 | tf_op jit(solution)/shard_map/ppermute | solution.py:32
  40.2 9.2 %collective-permute-start.13 = (bf16[512,256]{1,0:T(8,128)(2,1)S(1)}, bf16[512,256]{1,0:T(8,128)(2,1)S(1)}, u32[]{:S(2)}, u32[]{:S(2)}) collective-permute-start(bf16[512,256]{1,0:T(8,128)(2,1)S(1)} %collective-permute-done.9.refs_8_.refs_10_), channel_id=1, source_target_pairs={{1,0},{2,3},{5,4},{6,7},{9,8},{10,11},{13,12},{14,15},{17,16},{18,... | collective-permute-start | bytes 786440 | tf_op jit(solution)/shard_map/ppermute | solution.py:677
  49.8 14.3 %collective-permute-start.16 = (bf16[896,256]{1,0:T(8,128)(2,1)S(1)}, bf16[896,256]{1,0:T(8,128)(2,1)S(1)}, u32[]{:S(2)}, u32[]{:S(2)}) collective-permute-start(bf16[896,256]{1,0:T(8,128)(2,1)S(1)} %get-tuple-element.85.refs_1_), channel_id=1, source_target_pairs={{0,16},{16,0},{1,17},{17,1},{2,18},{18,2},{3,19},{19,3},{4,20},{20... | collective-permute-start | bytes 1376264 | tf_op jit(solution)/shard_map/ppermute | solution.py:32
  50.3 13.8 %collective-permute-start.17 = (bf16[896,256]{1,0:T(8,128)(2,1)S(1)}, bf16[896,256]{1,0:T(8,128)(2,1)S(1)}, u32[]{:S(2)}, u32[]{:S(2)}) collective-permute-start(bf16[896,256]{1,0:T(8,128)(2,1)S(1)} %get-tuple-element.86.refs_3_), channel_id=1, source_target_pairs={{0,16},{16,0},{1,17},{17,1},{2,18},{18,2},{3,19},{19,3},{4,20},{20... | collective-permute-start | bytes 1376264 | tf_op jit(solution)/shard_map/ppermute | solution.py:32
  50.3 13.7 %collective-permute-start.15 = (bf16[512,256]{1,0:T(8,128)(2,1)S(1)}, bf16[512,256]{1,0:T(8,128)(2,1)S(1)}, u32[]{:S(2)}, u32[]{:S(2)}) collective-permute-start(bf16[512,256]{1,0:T(8,128)(2,1)S(1)} %get-tuple-element.83.refs_8_), channel_id=1, source_target_pairs={{1,0},{2,3},{5,4},{6,7},{9,8},{10,11},{13,12},{14,15},{17,16},{18,... | collective-permute-start | bytes 786440 | tf_op jit(solution)/shard_map/ppermute | solution.py:687
  51.9 12.1 %collective-permute-start.18 = (bf16[256,256]{1,0:T(8,128)(2,1)S(1)}, bf16[256,256]{1,0:T(8,128)(2,1)S(1)}, u32[]{:S(2)}, u32[]{:S(2)}) collective-permute-start(bf16[256,256]{1,0:T(8,128)(2,1)S(1)} %get-tuple-element.87), channel_id=1, source_target_pairs={{0,1},{1,0},{2,3},{3,2},{4,5},{5,4},{6,7},{7,6},{8,9},{9,8},{10,11... | collective-permute-start | bytes 393224 | tf_op jit(solution)/shard_map/ppermute | solution.py:32
  71.8 12.9 %collective-permute-start.23 = (bf16[8,128,1408]{2,1,0:T(8,128)(2,1)S(1)}, bf16[8,128,1408]{2,1,0:T(8,128)(2,1)S(1)}, u32[]{:S(2)}, u32[]{:S(2)}) collective-permute-start(bf16[8,128,1408]{2,1,0:T(8,128)(2,1)S(1)} %get-tuple-element.91.refs_9_.refs_2_), channel_id=1, source_target_pairs={{0,16},{16,0},{1,17},{17,1},{2,18},{18,2},{3,19},{19,3},{4,20},{20... | collective-permute-start | bytes 8650760 | tf_op jit(solution)/shard_map/ppermute | solution.py:32
  72.0 11.4 %collective-permute-start.20 = (bf16[256,256]{1,0:T(8,128)(2,1)S(1)}, bf16[256,256]{1,0:T(8,128)(2,1)S(1)}, u32[]{:S(2)}, u32[]{:S(2)}) collective-permute-start(bf16[256,256]{1,0:T(8,128)(2,1)S(1)} %get-tuple-element.90.refs_6_), channel_id=1, source_target_pairs={{0,2},{1,3},{2,0},{3,1},{4,6},{5,7},{6,4},{7,5},{8,10},{9,11},{10,... | collective-permute-start | bytes 393224 | tf_op jit(solution)/shard_map/ppermute | solution.py:32
  72.0 11.4 %collective-permute-start.21 = (bf16[256,256]{1,0:T(8,128)(2,1)S(1)}, bf16[256,256]{1,0:T(8,128)(2,1)S(1)}, u32[]{:S(2)}, u32[]{:S(2)}) collective-permute-start(bf16[256,256]{1,0:T(8,128)(2,1)S(1)} %get-tuple-element.90.refs_6_), channel_id=1, source_target_pairs={{0,3},{1,2},{2,1},{3,0},{4,7},{5,6},{6,5},{7,4},{8,11},{9,10},{10,... | collective-permute-start | bytes 393224 | tf_op jit(solution)/shard_map/ppermute | solution.py:32
  73.9 10.8 %collective-permute-start.22 = (bf16[256,256]{1,0:T(8,128)(2,1)S(1)}, bf16[256,256]{1,0:T(8,128)(2,1)S(1)}, u32[]{:S(2)}, u32[]{:S(2)}) collective-permute-start(bf16[256,256]{1,0:T(8,128)(2,1)S(1)} %get-tuple-element.90.refs_6_), channel_id=1, source_target_pairs={{0,1},{1,0},{2,3},{3,2},{4,5},{5,4},{6,7},{7,6},{8,9},{9,8},{10,11... | collective-permute-start | bytes 393224 | tf_op jit(solution)/shard_map/ppermute | solution.py:32
  85.5 13.5 %collective-permute-start.24 = (bf16[272,256]{1,0:T(8,128)(2,1)S(1)}, bf16[272,256]{1,0:T(8,128)(2,1)S(1)}, u32[]{:S(2)}, u32[]{:S(2)}) collective-permute-start(bf16[272,256]{1,0:T(8,128)(2,1)S(1)} %get-tuple-element.93), channel_id=1, source_target_pairs={{0,2},{1,3},{2,0},{3,1},{4,6},{5,7},{6,4},{7,5},{8,10},{9,11},{10,... | collective-permute-start | bytes 417800 | tf_op jit(solution)/shard_map/ppermute | solution.py:32
  88.3 10.7 %collective-permute-start.25 = (bf16[272,256]{1,0:T(8,128)(2,1)S(1)}, bf16[272,256]{1,0:T(8,128)(2,1)S(1)}, u32[]{:S(2)}, u32[]{:S(2)}) collective-permute-start(bf16[272,256]{1,0:T(8,128)(2,1)S(1)} %get-tuple-element.94), channel_id=1, source_target_pairs={{0,3},{1,2},{2,1},{3,0},{4,7},{5,6},{6,5},{7,4},{8,11},{9,10},{10,... | collective-permute-start | bytes 417800 | tf_op jit(solution)/shard_map/ppermute | solution.py:32
  90.0 9.6 %collective-permute-start.26 = (bf16[272,256]{1,0:T(8,128)(2,1)S(1)}, bf16[272,256]{1,0:T(8,128)(2,1)S(1)}, u32[]{:S(2)}, u32[]{:S(2)}) collective-permute-start(bf16[272,256]{1,0:T(8,128)(2,1)S(1)} %get-tuple-element.95), channel_id=1, source_target_pairs={{0,1},{1,0},{2,3},{3,2},{4,5},{5,4},{6,7},{7,6},{8,9},{9,8},{10,11... | collective-permute-start | bytes 417800 | tf_op jit(solution)/shard_map/ppermute | solution.py:32
  102.2 12.7 %collective-permute-start.27 = (bf16[272,256]{1,0:T(8,128)(2,1)S(1)}, bf16[272,256]{1,0:T(8,128)(2,1)S(1)}, u32[]{:S(2)}, u32[]{:S(2)}) collective-permute-start(bf16[272,256]{1,0:T(8,128)(2,1)S(1)} %get-tuple-element.103.refs_8_), channel_id=1, source_target_pairs={{0,2},{1,3},{2,0},{3,1},{4,6},{5,7},{6,4},{7,5},{8,10},{9,11},{10,... | collective-permute-start | bytes 417800 | tf_op jit(solution)/shard_map/ppermute | solution.py:32
  104.7 10.3 %collective-permute-start.28 = (bf16[272,256]{1,0:T(8,128)(2,1)S(1)}, bf16[272,256]{1,0:T(8,128)(2,1)S(1)}, u32[]{:S(2)}, u32[]{:S(2)}) collective-permute-start(bf16[272,256]{1,0:T(8,128)(2,1)S(1)} %get-tuple-element.103.refs_8_), channel_id=1, source_target_pairs={{0,3},{1,2},{2,1},{3,0},{4,7},{5,6},{6,5},{7,4},{8,11},{9,10},{10,... | collective-permute-start | bytes 417800 | tf_op jit(solution)/shard_map/ppermute | solution.py:32
  106.9 8.7 %collective-permute-start.29 = (bf16[272,256]{1,0:T(8,128)(2,1)S(1)}, bf16[272,256]{1,0:T(8,128)(2,1)S(1)}, u32[]{:S(2)}, u32[]{:S(2)}) collective-permute-start(bf16[272,256]{1,0:T(8,128)(2,1)S(1)} %get-tuple-element.103.refs_8_), channel_id=1, source_target_pairs={{0,1},{1,0},{2,3},{3,2},{4,5},{5,4},{6,7},{7,6},{8,9},{9,8},{10,11... | collective-permute-start | bytes 417800 | tf_op jit(solution)/shard_map/ppermute | solution.py:32
  118.5 15.4 %collective-permute-start.34 = (bf16[448,256]{1,0:T(8,128)(2,1)S(1)}, bf16[448,256]{1,0:T(8,128)(2,1)S(1)}, u32[]{:S(2)}, u32[]{:S(2)}) collective-permute-start(bf16[448,256]{1,0:T(8,128)(2,1)S(1)} %get-tuple-element.112.refs_3_), channel_id=1, source_target_pairs={{0,4},{4,0},{8,12},{12,8},{1,5},{5,1},{9,13},{13,9},{2,6},{6,2},{1... | collective-permute-start | bytes 688136 | tf_op jit(solution)/shard_map/ppermute | solution.py:32
  119.8 14.1 %collective-permute-start.35 = (bf16[448,256]{1,0:T(8,128)(2,1)S(1)}, bf16[448,256]{1,0:T(8,128)(2,1)S(1)}, u32[]{:S(2)}, u32[]{:S(2)}) collective-permute-start(bf16[448,256]{1,0:T(8,128)(2,1)S(1)} %get-tuple-element.113.refs_4_), channel_id=1, source_target_pairs={{0,8},{4,12},{8,0},{12,4},{1,9},{5,13},{9,1},{13,5},{2,10},{6,14},... | collective-permute-start | bytes 688136 | tf_op jit(solution)/shard_map/ppermute | solution.py:32
  120.8 12.9 %collective-permute-start.30 = (bf16[256,256]{1,0:T(8,128)(2,1)S(1)}, bf16[256,256]{1,0:T(8,128)(2,1)S(1)}, u32[]{:S(2)}, u32[]{:S(2)}) collective-permute-start(bf16[256,256]{1,0:T(8,128)(2,1)S(1)} %get-tuple-element.107), channel_id=1, source_target_pairs={{0,2},{1,3},{2,0},{3,1},{4,6},{5,7},{6,4},{7,5},{8,10},{9,11},{10,... | collective-permute-start | bytes 393224 | tf_op jit(solution)/shard_map/ppermute | solution.py:32
  122.8 11.0 %collective-permute-start.31 = (bf16[256,256]{1,0:T(8,128)(2,1)S(1)}, bf16[256,256]{1,0:T(8,128)(2,1)S(1)}, u32[]{:S(2)}, u32[]{:S(2)}) collective-permute-start(bf16[256,256]{1,0:T(8,128)(2,1)S(1)} %get-tuple-element.108), channel_id=1, source_target_pairs={{0,3},{1,2},{2,1},{3,0},{4,7},{5,6},{6,5},{7,4},{8,11},{9,10},{10,... | collective-permute-start | bytes 393224 | tf_op jit(solution)/shard_map/ppermute | solution.py:32
  125.4 8.5 %collective-permute-start.32 = (bf16[256,256]{1,0:T(8,128)(2,1)S(1)}, bf16[256,256]{1,0:T(8,128)(2,1)S(1)}, u32[]{:S(2)}, u32[]{:S(2)}) collective-permute-start(bf16[256,256]{1,0:T(8,128)(2,1)S(1)} %get-tuple-element.109), channel_id=1, source_target_pairs={{0,1},{1,0},{2,3},{3,2},{4,5},{5,4},{6,7},{7,6},{8,9},{9,8},{10,11... | collective-permute-start | bytes 393224 | tf_op jit(solution)/shard_map/ppermute | solution.py:32
  144.2 7.7 %collective-permute-start.39 = (bf16[448,256]{1,0:T(8,128)(2,1)S(1)}, bf16[448,256]{1,0:T(8,128)(2,1)S(1)}, u32[]{:S(2)}, u32[]{:S(2)}) collective-permute-start(bf16[448,256]{1,0:T(8,128)(2,1)S(1)} %get-tuple-element.118.refs_0_), channel_id=1, source_target_pairs={{0,4},{4,0},{8,12},{12,8},{1,5},{5,1},{9,13},{13,9},{2,6},{6,2},{1... | collective-permute-start | bytes 688136 | tf_op jit(solution)/shard_map/ppermute | solution.py:32
  145.0 7.4 %collective-permute-start.40 = (bf16[448,256]{1,0:T(8,128)(2,1)S(1)}, bf16[448,256]{1,0:T(8,128)(2,1)S(1)}, u32[]{:S(2)}, u32[]{:S(2)}) collective-permute-start(bf16[448,256]{1,0:T(8,128)(2,1)S(1)} %get-tuple-element.119.refs_1_), channel_id=1, source_target_pairs={{0,8},{4,12},{8,0},{12,4},{1,9},{5,13},{9,1},{13,5},{2,10},{6,14},... | collective-permute-start | bytes 688136 | tf_op jit(solution)/shard_map/ppermute | solution.py:32
  152.5 6.6 %collective-permute-start.41 = (bf16[448,256]{1,0:T(8,128)(2,1)S(1)}, bf16[448,256]{1,0:T(8,128)(2,1)S(1)}, u32[]{:S(2)}, u32[]{:S(2)}) collective-permute-start(bf16[448,256]{1,0:T(8,128)(2,1)S(1)} %get-tuple-element.120.refs_0_), channel_id=1, source_target_pairs={{0,8},{4,12},{8,0},{12,4},{1,9},{5,13},{9,1},{13,5},{2,10},{6,14},... | collective-permute-start | bytes 688136 | tf_op jit(solution)/shard_map/ppermute | solution.py:32
  (28 other events, 266.7 us)

commit v4 on v3

--- a/solution.py
+++ b/solution.py
@@ -225,20 +225,22 @@
 
 def gather_body(
     up, up1, up2, down, down2, down1, moved, close, key_ref, value_ref,
-    out_ref, next_ref, grad_ref, key_out, value_out,
+    out_ref, next_ref, message, weight_ref,
 ):
-    key_out[...] = key_ref[...]
-    value_out[...] = value_ref[...]
+    tall = key_ref.shape[0]
+    weight_ref[:tall, :] = key_ref[...]
+    weight_ref[tall:, :] = value_ref[...]
     for base, parts in ((0, (up, up1, up2)), (4, (down, down2, down1))):
         near = 1 if base == 0 else 2
         out_ref[base] = parts[0][...]
         out_ref[base + near] = parts[1][...]
         out_ref[base + 3 - near] = parts[2][0]
         out_ref[base + 3] = parts[2][1]
-    first, rows = next_ref.shape[0], grad_ref.shape[0]
+    first, rows = next_ref.shape[0], close.shape[0]
     next_ref[...] = moved[:first, :]
+    message[:first, :] = moved[:first, :]
     total = moved[first + rows :, :].astype(F32) + close[...].astype(F32)
-    grad_ref[...] = total.astype(BF16)
+    message[first:, :] = total.astype(BF16)
 
 
 def rows_body(cols, rows_ref, own_ref):
@@ -272,10 +274,11 @@
         refs[2 * count + i][...] = total.astype(BF16)
 
 
-def halves_body(kept_ref, other_ref, top_ref, bottom_ref):
-    half = top_ref.shape[0]
-    for i, out_ref in enumerate((top_ref, bottom_ref)):
-        here = slice(i * half, (i + 1) * half)
+def pieces_body(kept_ref, other_ref, *outs):
+    start = 0
+    for out_ref in outs:
+        here = slice(start, start + out_ref.shape[0])
+        start += out_ref.shape[0]
         total = kept_ref[here, :].astype(F32) + other_ref[here, :].astype(F32)
         out_ref[...] = total.astype(BF16)
 
@@ -325,7 +328,7 @@
                     ]
     rows, width = normed_ref.shape
     cols = up.shape[-1]
-    chunk = rows // 2
+    chunk = rows // 4
     for dz in range(n):
         for copy in ups[dz]:
             copy.wait()
@@ -343,21 +346,17 @@
         enc_ref[r : r + chunk, :] = enc.astype(BF16)
 
 
-def projected_body(enc_ref, *refs):
-    weights, (enc_kv_ref, out0_ref) = refs[:4], refs[4:]
-    count, length, _ = enc_kv_ref.shape
-    width, cols = weights[0].shape
+def projected_body(layer, enc_ref, wkv_own, wkv_other, out_ref):
+    count, length, total = out_ref.shape
+    cols, width = wkv_own.shape[1], wkv_own.shape[0] // 2
     enc = enc_ref[...]
-    enc_kv_ref[:, :, :width] = enc.reshape(count, length, width)
-    for j in range(4):
-        layer, kind = divmod(j, 2)
-        weight = of_layer(layer, *weights[2 * kind : 2 * kind + 2])
+    start = total - 2 * cols
+    if start:
+        out_ref[:, :, :start] = enc.reshape(count, length, width)
+    for kind in range(2):
+        weight = of_layer(layer, wkv_own, wkv_other, slice(kind * width, (kind + 1) * width))
         out = mm(enc, weight).astype(BF16).reshape(count, length, cols)
-        if layer == 0:
-            out0_ref[:, :, kind * cols : (kind + 1) * cols] = out
-        else:
-            start = width + kind * cols
-            enc_kv_ref[:, :, start : start + cols] = out
+        out_ref[:, :, start + kind * cols : start + (kind + 1) * cols] = out
 
 
 def slot_slice(c, slots):
@@ -371,12 +370,9 @@
     return powers / jnp.sum(powers, axis=-1, keepdims=True)
 
 
-def first_layer_body(
-    n, tracts, slots, ids_ref, counts_ref, gain_own, gain_other, wq_own, wq_other, *refs
-):
-    *pieces, own, other, att_ref, query_ref, probs_ref, blocks = refs
-    fill_slots(own, other, ids_ref, tracts, slots, blocks)
-    s, m = lax.axis_index("section"), lax.axis_index("mp")
+def query_body(n, gain_own, gain_other, wq_own, wq_other, *refs):
+    pieces, query_ref = refs[:-1], refs[-1]
+    m = lax.axis_index("mp")
     rows, cols = query_ref.shape
     feats = gain_own.shape[-1]
 
@@ -385,7 +381,9 @@
             return unpack(pieces[k][...], rows, feats).astype(F32)
         inner = jnp.logical_or(m == 1, m == 2)
         inside, outside = pieces[2 * k - 2 : 2 * k]
-        return unpack(jnp.where(inner, inside[...], outside[...]), rows, feats).astype(F32)
+        here = slice(0, rows * feats // cols)
+        value = jnp.where(inner, inside[here, :], outside[here, :])
+        return unpack(value, rows, feats).astype(F32)
 
     total = jnp.zeros((rows, 1), F32)
     for k in range(n):
@@ -394,14 +392,16 @@
     scale = lax.rsqrt(total / (n * feats) + EPSILON)
     raw = jnp.zeros((rows, cols), F32)
     for k in range(n):
-        wide = piece(k)
         gain = of_layer(0, gain_own, gain_other, m ^ k)
-        normed = (wide * scale * gain).astype(BF16)
+        normed = (piece(k) * scale * gain).astype(BF16)
         here = pl.ds(pl.multiple_of((m ^ k) * feats, feats), feats)
         raw = raw + mm(normed, of_layer(0, wq_own, wq_other, here, slice(None)))
     query_ref[...] = (raw * SCALE).astype(BF16)
-    length = rows // tracts
-    heads = cols // HEAD
+
+
+def scores_of(tracts, slots, heads, query_ref, counts_ref, blocks, probs_ref):
+    s = lax.axis_index("section")
+    length = query_ref.shape[0] // tracts
     for c in range(tracts):
         here, span = slice(c * length, (c + 1) * length), slot_slice(c, slots)
         for h in range(heads):
@@ -410,6 +410,15 @@
     for c in range(tracts):
         both = slice(c * heads, (c + 1) * heads)
         probs_ref[both] = softmax_used(probs_ref[both], counts_ref[s, c])
+
+
+def first_layer_body(
+    tracts, slots, ids_ref, counts_ref, query_ref, own, other, att_ref, probs_ref, blocks
+):
+    fill_slots(own, other, ids_ref, tracts, slots, blocks)
+    rows, cols = query_ref.shape
+    heads, length = cols // HEAD, rows // tracts
+    scores_of(tracts, slots, heads, query_ref, counts_ref, blocks, probs_ref)
     for c in range(tracts):
         here, span = slice(c * length, (c + 1) * length), slot_slice(c, slots)
         for h in range(heads):
@@ -443,14 +452,18 @@
         messages[i][rows:, :] = extra
 
 
-def score_grads(tracts, slots, heads, start, att_ref, blocks, probs_ref, grads_ref, scores_ref, soft_ref):
-    length = att_ref.shape[0] // tracts
+def prob_grads(tracts, slots, heads, att_ref, blocks, grads_ref):
+    rows, cols = att_ref.shape
+    length = rows // tracts
     for c in range(tracts):
         here, span = slice(c * length, (c + 1) * length), slot_slice(c, slots)
         for h in range(heads):
             there = slice(h * HEAD, (h + 1) * HEAD)
-            beyond = slice(start + h * HEAD, start + (h + 1) * HEAD)
+            beyond = slice(cols + h * HEAD, cols + (h + 1) * HEAD)
             grads_ref[c * heads + h] = mm(att_ref[here, there], blocks[span, beyond], NTR)
+
+
+def score_grads(tracts, heads, probs_ref, grads_ref, scores_ref, soft_ref):
     for c in range(tracts):
         both = slice(c * heads, (c + 1) * heads)
         probs, grads = probs_ref[both], grads_ref[both]
@@ -474,43 +487,37 @@
             ).astype(BF16)
 
 
-def last_layer_body(n, width, tracts, slots, *refs):
-    ids_ref, counts_ref = refs[:2]
-    messages, grads = refs[2 : 2 + n], refs[2 + n : -13]
-    own, other, dkv_ref, out_ref, scale_ref = refs[-13:-8]
-    raw_ref, query_ref, att_ref, probs_ref, grads_ref, scores_ref, soft_ref, blocks = refs[-8:]
+def last_values_body(tracts, slots, ids_ref, *refs):
+    grads, (own, other, blocks, att_ref, grads_ref) = refs[:-5], refs[-5:]
     fill_slots(own, other, ids_ref, tracts, slots, blocks, own.shape[2] - blocks.shape[1])
-    s = lax.axis_index("section")
+    rows, cols = att_ref.shape
+    grad = jnp.zeros((rows, cols), F32)
+    for part in grads:
+        start = grads[1].shape[0] - 2 * rows if part.shape[0] > rows else 0
+        grad = grad + part[start : start + rows, :].astype(F32)
+    att_ref[...] = grad.astype(BF16)
+    prob_grads(tracts, slots, cols // HEAD, att_ref, blocks, grads_ref)
+
+
+def last_layer_body(n, width, tracts, slots, counts_ref, *refs):
+    messages, (blocks, grads_ref) = refs[:n], refs[n : n + 2]
+    out_ref, scale_ref, query_ref, scores_ref, soft_ref, raw_ref, probs_ref = refs[n + 2 :]
     rows, cols = raw_ref.shape
     raw = jnp.zeros((rows, cols), F32)
     square = jnp.zeros((1, rows), F32)
-    grad = jnp.zeros((rows, cols), F32)
     for d in range(n):
         raw = raw + messages[d][:rows, :].astype(F32)
         extra = messages[d][rows:, :].astype(F32)
         square = square + extra[0:1, :] + extra[1:2, :]
-    for part in grads:
-        start = max(part.shape[0] - 2 * rows, 0)
-        grad = grad + part[start : start + rows, :].astype(F32)
     scale = lax.rsqrt(to_column(square) / width + EPSILON)
     scale_ref[...] = jnp.broadcast_to(scale, scale_ref.shape)
     raw = raw * scale
     raw_ref[...] = raw
     query_ref[...] = (raw * SCALE).astype(BF16)
-    att_ref[...] = grad.astype(BF16)
     length = rows // tracts
     heads = cols // HEAD
-    for c in range(tracts):
-        here, span = slice(c * length, (c + 1) * length), slot_slice(c, slots)
-        for h in range(heads):
-            there = slice(h * HEAD, (h + 1) * HEAD)
-            probs_ref[c * heads + h] = mm(query_ref[here, there], blocks[span, there], NTR)
-    for c in range(tracts):
-        both = slice(c * heads, (c + 1) * heads)
-        probs_ref[both] = softmax_used(probs_ref[both], counts_ref[s, c])
-    score_grads(
-        tracts, slots, heads, cols, att_ref, blocks, probs_ref, grads_ref, scores_ref, soft_ref
-    )
+    scores_of(tracts, slots, heads, query_ref, counts_ref, blocks, probs_ref)
+    score_grads(tracts, heads, probs_ref, grads_ref, scores_ref, soft_ref)
     for c in range(tracts):
         here, span = slice(c * length, (c + 1) * length), slot_slice(c, slots)
         for h in range(heads):
@@ -520,7 +527,13 @@
     part = jnp.sum(out_ref[:rows, :].astype(F32) * raw_ref[...], axis=-1, keepdims=True)
     index = lax.broadcasted_iota(jnp.int32, (PAD, rows), 0)
     out_ref[rows:, :] = jnp.where(index == 0, to_row(part), 0.0).astype(BF16)
-    slot_grads(tracts, slots, heads, cols, query_ref, att_ref, scores_ref, soft_ref, dkv_ref)
+
+
+def last_slots_body(tracts, slots, query_ref, att_ref, scores_ref, soft_ref, dkv_ref):
+    cols = query_ref.shape[1]
+    slot_grads(
+        tracts, slots, cols // HEAD, cols, query_ref, att_ref, scores_ref, soft_ref, dkv_ref
+    )
 
 
 def weight_grads(enc_ref, dkv_ref, kept_ref, sent_ref):
@@ -575,21 +588,16 @@
         messages[i][...] = mm(grad, weight, NTR).astype(BF16)
 
 
-def first_back_body(n, tracts, slots, *refs):
-    ids_ref, query_ref, probs_ref = refs[:3]
-    grads = refs[3 : 3 + n]
-    own, other, dkv_ref = refs[3 + n : 6 + n]
-    att_ref, grads_ref, scores_ref, soft_ref, blocks = refs[6 + n :]
-    fill_slots(own, other, ids_ref, tracts, slots, blocks, query_ref.shape[1])
+def first_back_body(n, tracts, slots, query_ref, probs_ref, blocks, *refs):
+    grads, (dkv_ref, att_ref, grads_ref, scores_ref, soft_ref) = refs[:n], refs[n:]
     rows, cols = query_ref.shape
     grad = jnp.zeros((rows, cols), F32)
     for d in range(n):
         grad = grad + grads[d][...].astype(F32)
     att_ref[...] = grad.astype(BF16)
     heads = cols // HEAD
-    score_grads(
-        tracts, slots, heads, 0, att_ref, blocks, probs_ref, grads_ref, scores_ref, soft_ref
-    )
+    prob_grads(tracts, slots, heads, att_ref, blocks, grads_ref)
+    score_grads(tracts, heads, probs_ref, grads_ref, scores_ref, soft_ref)
     slot_grads(tracts, slots, heads, cols, query_ref, att_ref, scores_ref, soft_ref, dkv_ref)
 
 
@@ -631,6 +639,10 @@
     wq, wk, wv, wout = w_query[0], w_key[0], w_value[0], w_out[0]
     gains, wqs, wouts = ((w, swap(w)) for w in (gain, wq, wout))
 
+    pool_rows = pool_tokens[:, 0].reshape(half * length, enc_width)
+    normed = call(
+        norm_body, [shape((half * length, enc_width))], [vm(), vm()], flops=half * length * enc_width
+    )(pool_rows, enc_gain[None, :])[0]
     down_t = enc_down.T
     parts = 2 * dp
     up_rows, down_cols = enc_width // parts, ff // parts
@@ -662,6 +674,7 @@
             [shape(piece)] * 2
             + [shape((rest, cols)), shape((rest + 2 * rows, cols)), own_shape],
             [vm()] * (n + 2),
+            deps=[gains[1]],
         )(*line, own, far_grads)
         inner, outer = [(1, 2), (2, 1)], [(1, 0), (2, 3)]
         up1, down2 = xor_move(up, "dp", 1), xor_move(down, "dp", 2)
@@ -676,19 +689,18 @@
         up2, down1 = xor_move(ups, "dp", 2), xor_move(downs, "dp", 1)
         next_outer = lax.ppermute(far_inner, "mp", outer)
         message = lax.ppermute(message, "mp", inner)
-        gathered, next_inner, close, wk, wv = call(
+        last = shape((own_shape.shape[0] + rows, cols))
+        gathered, next_inner, close, wkv = call(
             gather_body,
-            [shape((parts,) + piece), own_shape, shape((rows, cols))]
-            + [shape((enc_width, cols))] * 2,
+            [shape((parts,) + piece), own_shape, last, shape((2 * enc_width, cols))],
             [vm()] * 10,
-            deps=[next_outer],
+            deps=[next_outer, normed],
         )(up, up1, up2, down, down2, down1, message, grads[3], wk, wv)
         pieces = [gathered, swap(gathered), enc_up, down_t, *wqs]
-        far_outer = lax.ppermute(next_inner, "mp", outer)
         close = xor_move(close, "mp", 1)
         grad_parts = [grads[0], message, close]
-        row_pieces = [own, near, next_inner, next_outer, far_inner, far_outer]
-        before_projected = [far_outer, close]
+        row_pieces = [own, near, next_inner, next_outer, far_inner, close]
+        before_projected = [close]
         scratch = [
             pltpu.VMEM((n, parts, up_rows, enc_up.shape[1]), BF16),
             pltpu.VMEM((n, enc_width // n, ff), BF16),
@@ -703,11 +715,12 @@
             [vm()] * 3,
             flops=2 * rows * width * cols,
         )(out_grad[:, 0], *wouts)
-        row_pieces, grad_parts = along_mp(own, n), scattered(grad_parts)
+        row_pieces, grad_parts = along_mp(own, n), scattered(list(grad_parts))
         query_shares = call(
             functools.partial(query_shares_body, n), [shape((feats, cols))] * n, [vm()] * 2
         )(*wqs)
         projection = jnp.stack(scattered(query_shares))
+        wkv = jnp.concatenate([wk, wv], axis=0)
         before_projected = []
         pieces = [
             lax.all_gather(enc_up, "mp", axis=0),
@@ -719,12 +732,8 @@
             pltpu.SemaphoreType.DMA((2,)),
         ]
 
-    wks, wvs = (wk, swap(wk)), (wv, swap(wv))
-
-    pool_rows = pool_tokens[:, 0].reshape(half * length, enc_width)
-    normed = call(
-        norm_body, [shape((half * length, enc_width))], [vm(), vm()], flops=half * length * enc_width
-    )(pool_rows, enc_gain[None, :])[0]
+    wkvs = (wkv, swap(wkv))
+
     encoded = call(
         functools.partial(encoder_body, n, parts, not shares),
         [shape((half * length, enc_width))] + [shape((n, feats, cols))] * shares,
@@ -736,35 +745,40 @@
     enc = encoded[0]
     if shares:
         projection = encoded[1]
-    enc_own, pool0_own = call(
-        projected_body,
-        [shape((half, length, enc_width + 2 * cols)), shape((half, length, 2 * cols))],
-        [vm()] * 5,
-        flops=8 * half * length * enc_width * cols,
-        deps=before_projected,
-    )(enc, *wks, *wvs)
+    pool0_own, enc_own = (
+        call(
+            functools.partial(projected_body, layer),
+            [shape((half, length, layer * enc_width + 2 * cols))],
+            [vm()] * 3,
+            flops=4 * half * length * enc_width * cols,
+            deps=before_projected,
+        )(enc, *wkvs)[0]
+        for layer in (0, 1)
+    )
     pool0_other = swap(pool0_own)
     heads = cols // HEAD
     chunk = rows // tracts
     slot_rows = tracts * slots * NT
-    blocks_scratch = pltpu.VMEM((slot_rows, 2 * cols), BF16)
-    part_scratch = pltpu.VMEM((slot_rows, cols), BF16)
     wide_scores = pltpu.VMEM((tracts * heads, chunk, slots * NT), F32)
     bf_scores = pltpu.VMEM((tracts * heads, chunk, slots * NT), BF16)
     attention_flops = 2 * rows * slots * NT * cols
 
-    att, query0, probs0, enc_own = call(
-        functools.partial(first_layer_body, n, tracts, slots),
-        [
-            shape((rows, cols)),
-            shape((rows, cols)),
-            shape((tracts * heads, chunk, slots * NT), F32),
-        ],
-        [smem(), smem()] + [vm()] * (6 + len(row_pieces)),
-        [blocks_scratch],
-        flops=2 * rows * width * cols + 2 * attention_flops,
+    wide_shape = shape((tracts * heads, chunk, slots * NT), F32)
+    block_shape = shape((slot_rows, 2 * cols))
+    query0 = call(
+        functools.partial(query_body, n),
+        [shape((rows, cols))],
+        [vm()] * (4 + len(row_pieces)),
+        flops=2 * rows * width * cols,
+        deps=[pool0_own],
+    )(*gains, *wqs, *row_pieces)[0]
+    att, probs0, blocks0, enc_own = call(
+        functools.partial(first_layer_body, tracts, slots),
+        [shape((rows, cols)), wide_shape, block_shape],
+        [smem(), smem()] + [vm()] * 3,
+        flops=2 * attention_flops,
         passing=[enc_own],
-    )(ids, counts, *gains, *wqs, *row_pieces, pool0_own, pool0_other)
+    )(ids, counts, query0, pool0_own, pool0_other)
     enc_other = swap(enc_own)
     att_pieces = along_mp(att, n)
     rows1, *messages = call(
@@ -775,22 +789,26 @@
         deps=[enc_other],
     )(*gains, own, *wouts, projection, *att_pieces)
     query_pieces = scattered(messages)
-    dkv1, grad_query, scale1 = call(
+    bf_shape = shape((tracts * heads, chunk, slots * NT))
+    blocks1, att1, prob_grads1 = call(
+        functools.partial(last_values_body, tracts, slots),
+        [block_shape, shape((rows, cols)), wide_shape],
+        [smem()] + [vm()] * (len(grad_parts) + 2),
+        flops=attention_flops,
+    )(ids, *grad_parts, enc_own, enc_other)
+    grad_query, scale1, query1, *soft1 = call(
         functools.partial(last_layer_body, n, width, tracts, slots),
-        [shape((slot_rows, 2 * cols)), shape((rows + PAD, cols)), shape((rows, HEAD), F32)],
-        [smem(), smem()] + [vm()] * (n + len(grad_parts) + 2),
-        [
-            pltpu.VMEM((rows, cols), F32),
-            pltpu.VMEM((rows, cols), BF16),
-            pltpu.VMEM((rows, cols), BF16),
-            wide_scores,
-            wide_scores,
-            bf_scores,
-            bf_scores,
-            blocks_scratch,
-        ],
-        flops=5 * attention_flops,
-    )(ids, counts, *query_pieces, *grad_parts, enc_own, enc_other)
+        [shape((rows + PAD, cols)), shape((rows, HEAD), F32), shape((rows, cols))] + [bf_shape] * 2,
+        [smem()] + [vm()] * (n + 2),
+        [pltpu.VMEM((rows, cols), F32), wide_scores],
+        flops=3 * attention_flops,
+    )(counts, *query_pieces, blocks1, prob_grads1)
+    dkv1 = call(
+        functools.partial(last_slots_body, tracts, slots),
+        [shape((slot_rows, 2 * cols))],
+        [vm()] * 4,
+        flops=2 * attention_flops,
+    )(query1, att1, *soft1)[0]
     query_grads = along_mp(grad_query, n)
     enc_slots, kept1, sent1 = call(
         functools.partial(last_grads_body, tracts, slots),
@@ -798,7 +816,6 @@
         [smem(), vm(), vm(), vm()],
         flops=4 * enc_width * slot_rows * cols,
     )(ids, dkv1, enc_own, enc_other)
-    half_shape = shape((enc_width // 2, cols))
     *messages, kept1, sent1 = call(
         functools.partial(back_between_body, n, width),
         [shape((rows, cols))] * n,
@@ -808,45 +825,56 @@
     )(*gains, rows1, out_grad[:, 0], scale1, projection, *wouts, *query_grads)
     grad_pieces0 = scattered(messages)
 
-    def over_dp(parts, order, deps=()):
-        moved = [xor_move(part, "dp", by) for part, by in zip(parts, order)]
-        return call(functools.partial(add_body, 2), [half_shape] * 2, [vm()] * 4, first=deps)(
-            *parts, *moved
-        )
-
-    def summed(kept, sent, deps=()):
-        parts = call(halves_body, [half_shape] * 2, [vm()] * 2)(kept, swap(sent))
-        if dp == 4:
-            parts = over_dp(over_dp(parts, (1, 2), deps), (2, 1))
-        else:
-            parts = [lax.psum(part, "dp") for part in parts]
-        return jnp.concatenate(parts, axis=0)
-
-    sum1 = summed(kept1, sent1, grad_pieces0[1:])
+    def over_dp(parts, order):
+        size = len(parts)
+        moved = [None] * size
+        for by in sorted(set(order)):
+            members = [i for i in range(size) if order[i] == by]
+            if len(members) == 1:
+                moved[members[0]] = xor_move(parts[members[0]], "dp", by)
+                continue
+            message = xor_move(jnp.concatenate([parts[i] for i in members], axis=0), "dp", by)
+            start = 0
+            for i in members:
+                moved[i] = lax.slice_in_dim(message, start, start + parts[i].shape[0])
+                start += parts[i].shape[0]
+        shapes = [shape(part.shape) for part in parts]
+        return call(functools.partial(add_body, size), shapes, [vm()] * (2 * size))(*parts, *moved)
+
+    def pieces_of(kept, sent, sizes):
+        parts = [shape((size, cols)) for size in sizes]
+        return call(pieces_body, parts, [vm()] * 2)(kept, swap(sent))
+
+    size = enc_width // 2
+    early = size // 2 + 16 if size % 32 == 0 else size // 2
+    ax, bx, ay, by = pieces_of(kept1, sent1, [early, size - early] * 2)
+    if dp == 4:
+        ax, ay = over_dp([ax, ay], (1, 2))
     dkv0 = call(
         functools.partial(first_back_body, n, tracts, slots),
         [shape((slot_rows, 2 * cols))],
-        [smem()] + [vm()] * (n + 4),
-        [
-            pltpu.VMEM((rows, cols), BF16),
-            wide_scores,
-            bf_scores,
-            bf_scores,
-            part_scratch,
-        ],
+        [vm()] * (n + 3),
+        [pltpu.VMEM((rows, cols), BF16), wide_scores, bf_scores, bf_scores],
         flops=3 * attention_flops,
-    )(ids, query0, probs0, *grad_pieces0, pool0_own, pool0_other)[0]
+    )(query0, probs0, blocks0, *grad_pieces0)[0]
     sent0, kept0 = (
         call(
             functools.partial(part_grads_body, keep),
             [shape((enc_width, cols))],
             [vm()] * 2,
             flops=2 * enc_width * slot_rows * cols,
-            deps=[] if keep else [sum1],
+            deps=[] if keep else [ax, ay],
         )(enc_slots, dkv0)[0]
         for keep in (False, True)
     )
-    sum0 = summed(kept0, sent0)
+    top, bottom = pieces_of(kept0, sent0, [size] * 2)
+    if dp == 4:
+        top, bottom, ax, ay, bx, by = over_dp([top, bottom, ax, ay, bx, by], (1, 2, 2, 1, 1, 2))
+        top, bottom, bx, by = over_dp([top, bottom, bx, by], (2, 1, 2, 1))
+    else:
+        top, bottom, ax, ay, bx, by = lax.psum((top, bottom, ax, ay, bx, by), "dp")
+    sum0 = jnp.concatenate([top, bottom], axis=0)
+    sum1 = jnp.concatenate([ax, bx, ay, by], axis=0)
     received = swap(jnp.where(first, sum1, sum0))
     key_total = jnp.where(first, sum0, received)
     value_total = jnp.where(first, received, sum1)

time: 163 us -> 157 us (0.963)
  starting transfers between devices: 48 us -> 44.1 us
  waiting for transfers between devices: 84.9 us -> 82.6 us
    ppermute x40 -> x37, starting transfers between devices: 43.7 us -> 41.3 us  [xor_move(): return lax.ppermute(value, axis, [(i, i ^ by) for i in range(count)])]
    ppermute x40 -> x37, waiting for transfers between devices: 76.9 us -> 75.5 us  [xor_move(): return lax.ppermute(value, axis, [(i, i ^ by) for i in range(count)])]
    pallas_call x22 -> x25, Pallas kernels: 26.9 us -> 26.8 us  [run(): pl.pallas_call(kernel, out_shape=list(outs) + [shape(x.shape, x.dtype) fo...]
  transfers between devices with their start and end apart: 44 -> 40, of which waited for: 26 -> 25; matrix products, arithmetic and copies ran while one was open for 0% -> 0% of each run, Pallas kernels for 9% -> 12%
where the time goes in v4:
time: 157 us
  waiting for transfers between devices  82.6 us (53%)
  starting transfers between devices  44.1 us (28%)
  Pallas kernels  26.8 us (17%)
    ppermute x37, waiting for transfers between devices, xor_move(): return lax.ppermute(value, axis, [(i, i ^ by) for i in range(count)])  75.5 us
    ppermute x37, starting transfers between devices, xor_move(): return lax.ppermute(value, axis, [(i, i ^ by) for i in range(count)])  41.3 us
    pallas_call x25, Pallas kernels, run(): pl.pallas_call(kernel, out_shape=list(outs) + [shape(x.shape, x.dtype) fo...  26.8 us
    ppermute x1, waiting for transfers between devices, on_device(): next_outer = lax.ppermute(far_inner, 'mp', outer)  7.18 us
  transfers between devices with their start and end apart: 40, of which 25 were waited for; matrix products, arithmetic and copies ran while one was open for 0% of the time, Pallas kernels for 12%

profile of v4, /device:TPU:0, one launch (start us, length us, event | category | flops | bytes accessed | tf_op | source)
XLA Modules:
  0.0 157.3 jit_solution(3545307792029444822)
XLA Ops:
  1.3 2.4 %collective-permute-done.1.refs_3_.refs_7_ = bf16[2048,256]{1,0:T(8,128)(2,1)S(1)} collective-permute-done((bf16[2048,256]{1,0:T(8,128)(2,1)}, bf16[2048,256]{1,0:T(8,128)(2,1)S(1)}, u32[]{:S(2)}, u32[]{:S(2)}) %collective-permute-start.1) | collective-permute-done | bytes 1048608 | tf_op jit(solution)/shard_map/ppermute | solution.py:32
  4.7 2.1 %shard_map.140 = (bf16[288,256]{1,0:T(8,128)(2,1)}, bf16[288,256]{1,0:T(8,128)(2,1)}, bf16[288,256]{1,0:T(8,128)(2,1)}, bf16[544,256]{1,0:T(8,128)(2,1)}, bf16[512,256]{1,0:T(8,128)(2,1)}) custom-call(bf16[896,256]{1,0:T(8,128)(2,1)} %refs_4_.1, bf16[224,1024]{1,0:T(8,128)(2,1)} %bitcast.27, bf16[2048,256]{1,0:T(8,128)(2,1)} %bitcast.16, ...), custom_call_target="tpu_custom_call" | custom-call | bytes 983 | tf_op jit(solution)/shard_map/pallas_call | solution.py:70
  6.9 3.0 %collective-permute-start.4 = (bf16[544,256]{1,0:T(8,128)(2,1)}, bf16[544,256]{1,0:T(8,128)(2,1)S(1)}, u32[]{:S(2)}, u32[]{:S(2)}) collective-permute-start(bf16[544,256]{1,0:T(8,128)(2,1)} %get-tuple-element.74), channel_id=1, source_target_pairs={{0,1},{1,0},{2,3},{3,2},{4,5},{5,4},{6,7},{7,6},{8,9},{9,8},{10,11... | collective-permute-start | bytes 835592 | tf_op jit(solution)/shard_map/ppermute | solution.py:32
  9.9 2.6 %collective-permute-start.2 = (bf16[288,256]{1,0:T(8,128)(2,1)}, bf16[288,256]{1,0:T(8,128)(2,1)S(1)}, u32[]{:S(2)}, u32[]{:S(2)}) collective-permute-start(bf16[288,256]{1,0:T(8,128)(2,1)} %get-tuple-element.72), channel_id=1, source_target_pairs={{0,2},{1,3},{2,0},{3,1},{4,6},{5,7},{6,4},{7,5},{8,10},{9,11},{10,... | collective-permute-start | bytes 442376 | tf_op jit(solution)/shard_map/ppermute | solution.py:32
  13.6 6.8 %collective-permute-done.2.refs_1_ = bf16[288,256]{1,0:T(8,128)(2,1)S(1)} collective-permute-done((bf16[288,256]{1,0:T(8,128)(2,1)}, bf16[288,256]{1,0:T(8,128)(2,1)S(1)}, u32[]{:S(2)}, u32[]{:S(2)}) %collective-permute-start.2) | collective-permute-done | bytes 147488 | tf_op jit(solution)/shard_map/ppermute | solution.py:32
  20.4 5.2 %collective-permute-done.3.refs_2_ = bf16[288,256]{1,0:T(8,128)(2,1)S(1)} collective-permute-done((bf16[288,256]{1,0:T(8,128)(2,1)}, bf16[288,256]{1,0:T(8,128)(2,1)S(1)}, u32[]{:S(2)}, u32[]{:S(2)}) %collective-permute-start.3) | collective-permute-done | bytes 147488 | tf_op jit(solution)/shard_map/ppermute | solution.py:32
  27.5 1.6 collective-permute-start.6
  29.1 1.5 collective-permute-start.7
  30.6 2.9 %collective-permute-done.6.refs_1_ = bf16[3,144,256]{2,1,0:T(8,128)(2,1)S(1)} collective-permute-done((bf16[3,144,256]{2,1,0:T(8,128)(2,1)S(1)}, bf16[3,144,256]{2,1,0:T(8,128)(2,1)S(1)}, u32[]{:S(2)}, u32[]{:S(2)}) %collective-permute-start.6) | collective-permute-done | bytes 221216 | tf_op jit(solution)/shard_map/ppermute | solution.py:32
  37.1 1.6 %collective-permute-start.10 = (bf16[2,3,144,256]{3,2,1,0:T(8,128)(2,1)S(1)}, bf16[2,3,144,256]{3,2,1,0:T(8,128)(2,1)S(1)}, u32[]{:S(2)}, u32[]{:S(2)}) collective-permute-start(bf16[2,3,144,256]{3,2,1,0:T(8,128)(2,1)S(1)} %get-tuple-element.84), channel_id=1, source_target_pairs={{0,8},{4,12},{8,0},{12,4},{1,9},{5,13},{9,1},{13,5},{2,10},{6,14},... | collective-permute-start | bytes 1327112 | tf_op jit(solution)/shard_map/ppermute | solution.py:32
  42.2 7.2 %collective-permute-done.13.refs_10_.refs_7_ = bf16[512,256]{1,0:T(8,128)(2,1)S(1)} collective-permute-done((bf16[512,256]{1,0:T(8,128)(2,1)S(1)}, bf16[512,256]{1,0:T(8,128)(2,1)S(1)}, u32[]{:S(2)}, u32[]{:S(2)}) %collective-permute-start.13) | collective-permute-done | bytes 262176 | tf_op jit(solution)/shard_map/ppermute | solution.py:690
  50.3 2.7 %collective-permute-start.15 = (bf16[768,256]{1,0:T(8,128)(2,1)S(1)}, bf16[768,256]{1,0:T(8,128)(2,1)S(1)}, u32[]{:S(2)}, u32[]{:S(2)}) collective-permute-start(bf16[768,256]{1,0:T(8,128)(2,1)S(1)} %get-tuple-element.92), channel_id=1, source_target_pairs={{0,1},{1,0},{2,3},{3,2},{4,5},{5,4},{6,7},{7,6},{8,9},{9,8},{10,11... | collective-permute-start | bytes 1179656 | tf_op jit(solution)/shard_map/ppermute | solution.py:32
  53.5 5.6 %shard_map.146 = (bf16[1024,896]{1,0:T(8,128)(2,1)S(1)}, bf16[4,512,256]{2,1,0:T(8,128)(2,1)S(1)}) custom-call(bf16[1024,896]{1,0:T(8,128)(2,1)S(1)} %bitcast.24, bf16[1024,896]{1,0:T(8,128)(2,1)S(1)} %shard_map.143.refs_11_.refs_1_, bf16[8,3,144,256]{3,2,1,0:T(8,128)(2,1)S(1)} %get-tuple-element.88.refs_2_, ...), custom_call_target="tpu_custom_call" | custom-call | flops 3758096 | bytes 2883 | tf_op jit(solution)/shard_map/pallas_call | solution.py:70
  59.1 3.3 %collective-permute-done.15.refs_3_.refs_9_ = bf16[768,256]{1,0:T(8,128)(2,1)S(1)} collective-permute-done((bf16[768,256]{1,0:T(8,128)(2,1)S(1)}, bf16[768,256]{1,0:T(8,128)(2,1)S(1)}, u32[]{:S(2)}, u32[]{:S(2)}) %collective-permute-start.15) | collective-permute-done | bytes 393248 | tf_op jit(solution)/shard_map/ppermute | solution.py:32
  66.4 1.6 %shard_map.150 = (bf16[256,256]{1,0:T(8,128)(2,1)S(1)}, f32[8,64,512]{2,1,0:T(8,128)S(1)}, bf16[2048,512]{1,0:T(8,128)(2,1)S(1)}, bf16[8,128,1408]{2,1,0:T(8,128)(2,1)S(1)}) custom-call(s32[2,4,4]{2,1,0:T(4,128)S(1)} %bitcast.35, s32[2,4]{1,0:T(2,128)S(1)} %bitcast.38, ...), custom_call_target="tpu_custom_call", output_to_operand_aliasing={{3}: (5, {})} | custom-call | flops 134217 | bytes 3276 | tf_op jit(solution)/shard_map/pallas_call | solution.py:70
  68.3 1.9 %collective-permute-start.18 = (bf16[256,256]{1,0:T(8,128)(2,1)S(1)}, bf16[256,256]{1,0:T(8,128)(2,1)S(1)}, u32[]{:S(2)}, u32[]{:S(2)}) collective-permute-start(bf16[256,256]{1,0:T(8,128)(2,1)S(1)} %get-tuple-element.95.refs_6_), channel_id=1, source_target_pairs={{0,2},{1,3},{2,0},{3,1},{4,6},{5,7},{6,4},{7,5},{8,10},{9,11},{10,... | collective-permute-start | bytes 393224 | tf_op jit(solution)/shard_map/ppermute | solution.py:32
  70.1 2.2 %collective-permute-start.19 = (bf16[256,256]{1,0:T(8,128)(2,1)S(1)}, bf16[256,256]{1,0:T(8,128)(2,1)S(1)}, u32[]{:S(2)}, u32[]{:S(2)}) collective-permute-start(bf16[256,256]{1,0:T(8,128)(2,1)S(1)} %get-tuple-element.95.refs_6_), channel_id=1, source_target_pairs={{0,3},{1,2},{2,1},{3,0},{4,7},{5,6},{6,5},{7,4},{8,11},{9,10},{10,... | collective-permute-start | bytes 393224 | tf_op jit(solution)/shard_map/ppermute | solution.py:32
  72.4 8.8 %collective-permute-done.18.refs_7_ = bf16[256,256]{1,0:T(8,128)(2,1)S(1)} collective-permute-done((bf16[256,256]{1,0:T(8,128)(2,1)S(1)}, bf16[256,256]{1,0:T(8,128)(2,1)S(1)}, u32[]{:S(2)}, u32[]{:S(2)}) %collective-permute-start.18) | collective-permute-done | bytes 131104 | tf_op jit(solution)/shard_map/ppermute | solution.py:32
  82.7 2.2 %collective-permute-start.22 = (bf16[272,256]{1,0:T(8,128)(2,1)S(1)}, bf16[272,256]{1,0:T(8,128)(2,1)S(1)}, u32[]{:S(2)}, u32[]{:S(2)}) collective-permute-start(bf16[272,256]{1,0:T(8,128)(2,1)S(1)} %get-tuple-element.98), channel_id=1, source_target_pairs={{0,2},{1,3},{2,0},{3,1},{4,6},{5,7},{6,4},{7,5},{8,10},{9,11},{10,... | collective-permute-start | bytes 417800 | tf_op jit(solution)/shard_map/ppermute | solution.py:32
  85.0 2.2 %collective-permute-start.23 = (bf16[272,256]{1,0:T(8,128)(2,1)S(1)}, bf16[272,256]{1,0:T(8,128)(2,1)S(1)}, u32[]{:S(2)}, u32[]{:S(2)}) collective-permute-start(bf16[272,256]{1,0:T(8,128)(2,1)S(1)} %get-tuple-element.99), channel_id=1, source_target_pairs={{0,3},{1,2},{2,1},{3,0},{4,7},{5,6},{6,5},{7,4},{8,11},{9,10},{10,... | collective-permute-start | bytes 417800 | tf_op jit(solution)/shard_map/ppermute | solution.py:32
  88.5 7.4 %collective-permute-done.22.refs_2_ = bf16[272,256]{1,0:T(8,128)(2,1)S(1)} collective-permute-done((bf16[272,256]{1,0:T(8,128)(2,1)S(1)}, bf16[272,256]{1,0:T(8,128)(2,1)S(1)}, u32[]{:S(2)}, u32[]{:S(2)}) %collective-permute-start.22) | collective-permute-done | bytes 139296 | tf_op jit(solution)/shard_map/ppermute | solution.py:32
  96.2 1.8 %shard_map.153 = (bf16[272,256]{1,0:T(8,128)(2,1)S(1)}, f32[256,128]{1,0:T(8,128)S(1)}, bf16[256,256]{1,0:T(8,128)(2,1)S(1)}, bf16[8,64,512]{2,1,0:T(8,128)(2,1)S(1)}, bf16[8,64,512]{2,1,0:T(8,128)(2,1)S(1)}) custom-call(s32[2,4]{1,0:T(2,128)S(1)} %bitcast.39, bf16[272,256]{1,0:T(8,128)(2,1)S(1)} %get-tuple-element.97.refs_1_, ...), custom_call_target="tpu_custom_call" | custom-call | flops 201326 | bytes 1449 | tf_op jit(solution)/shard_map/pallas_call | solution.py:70
  98.0 2.5 %collective-permute-start.25 = (bf16[272,256]{1,0:T(8,128)(2,1)S(1)}, bf16[272,256]{1,0:T(8,128)(2,1)S(1)}, u32[]{:S(2)}, u32[]{:S(2)}) collective-permute-start(bf16[272,256]{1,0:T(8,128)(2,1)S(1)} %get-tuple-element.113.refs_8_), channel_id=1, source_target_pairs={{0,2},{1,3},{2,0},{3,1},{4,6},{5,7},{6,4},{7,5},{8,10},{9,11},{10,... | collective-permute-start | bytes 417800 | tf_op jit(solution)/shard_map/ppermute | solution.py:32
  100.5 1.6 %collective-permute-start.26 = (bf16[272,256]{1,0:T(8,128)(2,1)S(1)}, bf16[272,256]{1,0:T(8,128)(2,1)S(1)}, u32[]{:S(2)}, u32[]{:S(2)}) collective-permute-start(bf16[272,256]{1,0:T(8,128)(2,1)S(1)} %get-tuple-element.113.refs_8_), channel_id=1, source_target_pairs={{0,3},{1,2},{2,1},{3,0},{4,7},{5,6},{6,5},{7,4},{8,11},{9,10},{10,... | collective-permute-start | bytes 417800 | tf_op jit(solution)/shard_map/ppermute | solution.py:32
  103.1 2.8 %shard_map.155 = (bf16[896,2048]{1,0:T(8,128)(2,1)S(1)}, bf16[896,256]{1,0:T(8,128)(2,1)S(1)}, bf16[896,256]{1,0:T(8,128)(2,1)S(1)}) custom-call(s32[2,4,4]{2,1,0:T(4,128)S(1)} %bitcast.37, bf16[2048,512]{1,0:T(8,128)(2,1)S(1)} %shard_map.154.refs_1_, bf16[8,128,1408]{2,1,0:T(8,128)(2,1)S(1)} %get-tuple-element.96.refs_4_.refs_2_, ...), custom_call_target="tpu_custom_call" | custom-call | flops 1879048 | bytes 4587 | tf_op jit(solution)/shard_map/pallas_call | solution.py:70
  105.8 4.3 %collective-permute-done.25.refs_9_ = bf16[272,256]{1,0:T(8,128)(2,1)S(1)} collective-permute-done((bf16[272,256]{1,0:T(8,128)(2,1)S(1)}, bf16[272,256]{1,0:T(8,128)(2,1)S(1)}, u32[]{:S(2)}, u32[]{:S(2)}) %collective-permute-start.25) | collective-permute-done | bytes 139296 | tf_op jit(solution)/shard_map/ppermute | solution.py:32
  111.5 2.0 %collective-permute-start.28 = (bf16[256,256]{1,0:T(8,128)(2,1)S(1)}, bf16[256,256]{1,0:T(8,128)(2,1)S(1)}, u32[]{:S(2)}, u32[]{:S(2)}) collective-permute-start(bf16[256,256]{1,0:T(8,128)(2,1)S(1)} %get-tuple-element.117), channel_id=1, source_target_pairs={{0,2},{1,3},{2,0},{3,1},{4,6},{5,7},{6,4},{7,5},{8,10},{9,11},{10,... | collective-permute-start | bytes 393224 | tf_op jit(solution)/shard_map/ppermute | solution.py:32
  113.5 2.6 %collective-permute-start.29 = (bf16[256,256]{1,0:T(8,128)(2,1)S(1)}, bf16[256,256]{1,0:T(8,128)(2,1)S(1)}, u32[]{:S(2)}, u32[]{:S(2)}) collective-permute-start(bf16[256,256]{1,0:T(8,128)(2,1)S(1)} %get-tuple-element.118), channel_id=1, source_target_pairs={{0,3},{1,2},{2,1},{3,0},{4,7},{5,6},{6,5},{7,4},{8,11},{9,10},{10,... | collective-permute-start | bytes 393224 | tf_op jit(solution)/shard_map/ppermute | solution.py:32
  118.2 6.3 %collective-permute-done.28.refs_4_ = bf16[256,256]{1,0:T(8,128)(2,1)S(1)} collective-permute-done((bf16[256,256]{1,0:T(8,128)(2,1)S(1)}, bf16[256,256]{1,0:T(8,128)(2,1)S(1)}, u32[]{:S(2)}, u32[]{:S(2)}) %collective-permute-start.28) | collective-permute-done | bytes 131104 | tf_op jit(solution)/shard_map/ppermute | solution.py:32
  132.8 9.7 %collective-permute-done.36 = bf16[896,256]{1,0:T(8,128)(2,1)S(1)} collective-permute-done((bf16[896,256]{1,0:T(8,128)(2,1)S(1)}, bf16[896,256]{1,0:T(8,128)(2,1)S(1)}, u32[]{:S(2)}, u32[]{:S(2)}) %collective-permute-start.36) | collective-permute-done | bytes 458784 | tf_op jit(solution)/shard_map/ppermute | solution.py:32
  146.0 6.8 %collective-permute-done.38 = bf16[656,256]{1,0:T(8,128)(2,1)S(1)} collective-permute-done((bf16[656,256]{1,0:T(8,128)(2,1)S(1)}, bf16[656,256]{1,0:T(8,128)(2,1)S(1)}, u32[]{:S(2)}, u32[]{:S(2)}) %collective-permute-start.38) | collective-permute-done | bytes 335904 | tf_op jit(solution)/shard_map/ppermute | solution.py:32
  154.5 1.8 %collective-permute-done.39 = bf16[896,256]{1,0:T(8,128)(2,1)S(1)} collective-permute-done((bf16[896,256]{1,0:T(8,128)(2,1)S(1)}, bf16[896,256]{1,0:T(8,128)(2,1)S(1)}, u32[]{:S(2)}, u32[]{:S(2)}) %collective-permute-start.39) | collective-permute-done | bytes 458784 | tf_op jit(solution)/shard_map/ppermute | solution.py:32
  (128 shorter events, 38.9 us)
Async XLA Ops:
  1.2 11.3 %collective-permute-start.5 = (bf16[1024,512]{1,0:T(8,128)(2,1)}, bf16[1024,512]{1,0:T(8,128)(2,1)S(1)}, u32[]{:S(2)}, u32[]{:S(2)}) collective-permute-start(bf16[1024,512]{1,0:T(8,128)(2,1)} %bitcast.19), channel_id=1, source_target_pairs={{0,16},{16,0},{1,17},{17,1},{2,18},{18,2},{3,19},{19,3},{4,20},{20... | collective-permute-start | bytes 3145736 | tf_op jit(solution)/shard_map/ppermute | solution.py:32
  6.9 18.8 %collective-permute-start.4 = (bf16[544,256]{1,0:T(8,128)(2,1)}, bf16[544,256]{1,0:T(8,128)(2,1)S(1)}, u32[]{:S(2)}, u32[]{:S(2)}) collective-permute-start(bf16[544,256]{1,0:T(8,128)(2,1)} %get-tuple-element.74), channel_id=1, source_target_pairs={{0,1},{1,0},{2,3},{3,2},{4,5},{5,4},{6,7},{7,6},{8,9},{9,8},{10,11... | collective-permute-start | bytes 835592 | tf_op jit(solution)/shard_map/ppermute | solution.py:32
  9.9 10.5 %collective-permute-start.2 = (bf16[288,256]{1,0:T(8,128)(2,1)}, bf16[288,256]{1,0:T(8,128)(2,1)S(1)}, u32[]{:S(2)}, u32[]{:S(2)}) collective-permute-start(bf16[288,256]{1,0:T(8,128)(2,1)} %get-tuple-element.72), channel_id=1, source_target_pairs={{0,2},{1,3},{2,0},{3,1},{4,6},{5,7},{6,4},{7,5},{8,10},{9,11},{10,... | collective-permute-start | bytes 442376 | tf_op jit(solution)/shard_map/ppermute | solution.py:32
  12.5 13.2 %collective-permute-start.3 = (bf16[288,256]{1,0:T(8,128)(2,1)}, bf16[288,256]{1,0:T(8,128)(2,1)S(1)}, u32[]{:S(2)}, u32[]{:S(2)}) collective-permute-start(bf16[288,256]{1,0:T(8,128)(2,1)} %get-tuple-element.73), channel_id=1, source_target_pairs={{0,3},{1,2},{2,1},{3,0},{4,7},{5,6},{6,5},{7,4},{8,11},{9,10},{10,... | collective-permute-start | bytes 442376 | tf_op jit(solution)/shard_map/ppermute | solution.py:32
  25.8 10.3 %collective-permute-start.8 = (bf16[768,256]{1,0:T(8,128)(2,1)S(1)}, bf16[768,256]{1,0:T(8,128)(2,1)S(1)}, u32[]{:S(2)}, u32[]{:S(2)}) collective-permute-start(bf16[768,256]{1,0:T(8,128)(2,1)S(1)} %get-tuple-element.81), channel_id=1, source_target_pairs={{0,1},{1,0},{2,3},{3,2},{4,5},{5,4},{6,7},{7,6},{8,9},{9,8},{10,11... | collective-permute-start | bytes 1179656 | tf_op jit(solution)/shard_map/ppermute | solution.py:32
  26.9 8.2 %collective-permute-start.9 = (bf16[512,256]{1,0:T(8,128)(2,1)S(1)}, bf16[512,256]{1,0:T(8,128)(2,1)S(1)}, u32[]{:S(2)}, u32[]{:S(2)}) collective-permute-start(bf16[512,256]{1,0:T(8,128)(2,1)S(1)} %get-tuple-element.77.refs_4_.refs_2_), channel_id=1, source_target_pairs={{1,2},{2,1},{5,6},{6,5},{9,10},{10,9},{13,14},{14,13},{17,18},{18,... | collective-permute-start | bytes 786440 | tf_op jit(solution)/shard_map/ppermute | solution.py:681
  27.5 6.0 %collective-permute-start.6 = (bf16[3,144,256]{2,1,0:T(8,128)(2,1)S(1)}, bf16[3,144,256]{2,1,0:T(8,128)(2,1)S(1)}, u32[]{:S(2)}, u32[]{:S(2)}) collective-permute-start(bf16[3,144,256]{2,1,0:T(8,128)(2,1)S(1)} %get-tuple-element.78.refs_0_), channel_id=1, source_target_pairs={{0,4},{4,0},{8,12},{12,8},{1,5},{5,1},{9,13},{13,9},{2,6},{6,2},{1... | collective-permute-start | bytes 663560 | tf_op jit(solution)/shard_map/ppermute | solution.py:32
  36.3 13.1 %collective-permute-start.12 = (bf16[1024,256]{1,0:T(8,128)(2,1)S(1)}, bf16[1024,256]{1,0:T(8,128)(2,1)S(1)}, u32[]{:S(2)}, u32[]{:S(2)}) collective-permute-start(bf16[1024,256]{1,0:T(8,128)(2,1)S(1)} %get-tuple-element.86), channel_id=1, source_target_pairs={{1,2},{2,1},{5,6},{6,5},{9,10},{10,9},{13,14},{14,13},{17,18},{18,... | collective-permute-start | bytes 1572872 | tf_op jit(solution)/shard_map/ppermute | solution.py:691
  37.1 12.3 %collective-permute-start.10 = (bf16[2,3,144,256]{3,2,1,0:T(8,128)(2,1)S(1)}, bf16[2,3,144,256]{3,2,1,0:T(8,128)(2,1)S(1)}, u32[]{:S(2)}, u32[]{:S(2)}) collective-permute-start(bf16[2,3,144,256]{3,2,1,0:T(8,128)(2,1)S(1)} %get-tuple-element.84), channel_id=1, source_target_pairs={{0,8},{4,12},{8,0},{12,4},{1,9},{5,13},{9,1},{13,5},{2,10},{6,14},... | collective-permute-start | bytes 1327112 | tf_op jit(solution)/shard_map/ppermute | solution.py:32
  38.7 10.7 %collective-permute-start.11 = (bf16[2,3,144,256]{3,2,1,0:T(8,128)(2,1)S(1)}, bf16[2,3,144,256]{3,2,1,0:T(8,128)(2,1)S(1)}, u32[]{:S(2)}, u32[]{:S(2)}) collective-permute-start(bf16[2,3,144,256]{3,2,1,0:T(8,128)(2,1)S(1)} %get-tuple-element.85), channel_id=1, source_target_pairs={{0,4},{4,0},{8,12},{12,8},{1,5},{5,1},{9,13},{13,9},{2,6},{6,2},{1... | collective-permute-start | bytes 1327112 | tf_op jit(solution)/shard_map/ppermute | solution.py:32
  40.2 9.2 %collective-permute-start.13 = (bf16[512,256]{1,0:T(8,128)(2,1)S(1)}, bf16[512,256]{1,0:T(8,128)(2,1)S(1)}, u32[]{:S(2)}, u32[]{:S(2)}) collective-permute-start(bf16[512,256]{1,0:T(8,128)(2,1)S(1)} %collective-permute-done.9.refs_8_), channel_id=1, source_target_pairs={{1,0},{2,3},{5,4},{6,7},{9,8},{10,11},{13,12},{14,15},{17,16},{18,... | collective-permute-start | bytes 786440 | tf_op jit(solution)/shard_map/ppermute | solution.py:690
  49.8 12.6 %collective-permute-start.16 = (bf16[1792,256]{1,0:T(8,128)(2,1)S(1)}, bf16[1792,256]{1,0:T(8,128)(2,1)S(1)}, u32[]{:S(2)}, u32[]{:S(2)}) collective-permute-start(bf16[1792,256]{1,0:T(8,128)(2,1)S(1)} %get-tuple-element.94.refs_1_), channel_id=1, source_target_pairs={{0,16},{16,0},{1,17},{17,1},{2,18},{18,2},{3,19},{19,3},{4,20},{20... | collective-permute-start | bytes 2752520 | tf_op jit(solution)/shard_map/ppermute | solution.py:32
  50.3 12.1 %collective-permute-start.15 = (bf16[768,256]{1,0:T(8,128)(2,1)S(1)}, bf16[768,256]{1,0:T(8,128)(2,1)S(1)}, u32[]{:S(2)}, u32[]{:S(2)}) collective-permute-start(bf16[768,256]{1,0:T(8,128)(2,1)S(1)} %get-tuple-element.92), channel_id=1, source_target_pairs={{0,1},{1,0},{2,3},{3,2},{4,5},{5,4},{6,7},{7,6},{8,9},{9,8},{10,11... | collective-permute-start | bytes 1179656 | tf_op jit(solution)/shard_map/ppermute | solution.py:32
  68.1 13.9 %collective-permute-start.21 = (bf16[8,128,1408]{2,1,0:T(8,128)(2,1)S(1)}, bf16[8,128,1408]{2,1,0:T(8,128)(2,1)S(1)}, u32[]{:S(2)}, u32[]{:S(2)}) collective-permute-start(bf16[8,128,1408]{2,1,0:T(8,128)(2,1)S(1)} %get-tuple-element.96.refs_4_.refs_2_), channel_id=1, source_target_pairs={{0,16},{16,0},{1,17},{17,1},{2,18},{18,2},{3,19},{19,3},{4,20},{20... | collective-permute-start | bytes 8650760 | tf_op jit(solution)/shard_map/ppermute | solution.py:32
  68.3 12.9 %collective-permute-start.18 = (bf16[256,256]{1,0:T(8,128)(2,1)S(1)}, bf16[256,256]{1,0:T(8,128)(2,1)S(1)}, u32[]{:S(2)}, u32[]{:S(2)}) collective-permute-start(bf16[256,256]{1,0:T(8,128)(2,1)S(1)} %get-tuple-element.95.refs_6_), channel_id=1, source_target_pairs={{0,2},{1,3},{2,0},{3,1},{4,6},{5,7},{6,4},{7,5},{8,10},{9,11},{10,... | collective-permute-start | bytes 393224 | tf_op jit(solution)/shard_map/ppermute | solution.py:32
  70.1 11.0 %collective-permute-start.19 = (bf16[256,256]{1,0:T(8,128)(2,1)S(1)}, bf16[256,256]{1,0:T(8,128)(2,1)S(1)}, u32[]{:S(2)}, u32[]{:S(2)}) collective-permute-start(bf16[256,256]{1,0:T(8,128)(2,1)S(1)} %get-tuple-element.95.refs_6_), channel_id=1, source_target_pairs={{0,3},{1,2},{2,1},{3,0},{4,7},{5,6},{6,5},{7,4},{8,11},{9,10},{10,... | collective-permute-start | bytes 393224 | tf_op jit(solution)/shard_map/ppermute | solution.py:32
  72.4 9.5 %collective-permute-start.20 = (bf16[256,256]{1,0:T(8,128)(2,1)S(1)}, bf16[256,256]{1,0:T(8,128)(2,1)S(1)}, u32[]{:S(2)}, u32[]{:S(2)}) collective-permute-start(bf16[256,256]{1,0:T(8,128)(2,1)S(1)} %get-tuple-element.95.refs_6_), channel_id=1, source_target_pairs={{0,1},{1,0},{2,3},{3,2},{4,5},{5,4},{6,7},{7,6},{8,9},{9,8},{10,11... | collective-permute-start | bytes 393224 | tf_op jit(solution)/shard_map/ppermute | solution.py:32
  82.7 13.1 %collective-permute-start.22 = (bf16[272,256]{1,0:T(8,128)(2,1)S(1)}, bf16[272,256]{1,0:T(8,128)(2,1)S(1)}, u32[]{:S(2)}, u32[]{:S(2)}) collective-permute-start(bf16[272,256]{1,0:T(8,128)(2,1)S(1)} %get-tuple-element.98), channel_id=1, source_target_pairs={{0,2},{1,3},{2,0},{3,1},{4,6},{5,7},{6,4},{7,5},{8,10},{9,11},{10,... | collective-permute-start | bytes 417800 | tf_op jit(solution)/shard_map/ppermute | solution.py:32
  85.0 10.9 %collective-permute-start.23 = (bf16[272,256]{1,0:T(8,128)(2,1)S(1)}, bf16[272,256]{1,0:T(8,128)(2,1)S(1)}, u32[]{:S(2)}, u32[]{:S(2)}) collective-permute-start(bf16[272,256]{1,0:T(8,128)(2,1)S(1)} %get-tuple-element.99), channel_id=1, source_target_pairs={{0,3},{1,2},{2,1},{3,0},{4,7},{5,6},{6,5},{7,4},{8,11},{9,10},{10,... | collective-permute-start | bytes 417800 | tf_op jit(solution)/shard_map/ppermute | solution.py:32
  87.2 9.0 %collective-permute-start.24 = (bf16[272,256]{1,0:T(8,128)(2,1)S(1)}, bf16[272,256]{1,0:T(8,128)(2,1)S(1)}, u32[]{:S(2)}, u32[]{:S(2)}) collective-permute-start(bf16[272,256]{1,0:T(8,128)(2,1)S(1)} %get-tuple-element.100), channel_id=1, source_target_pairs={{0,1},{1,0},{2,3},{3,2},{4,5},{5,4},{6,7},{7,6},{8,9},{9,8},{10,11... | collective-permute-start | bytes 417800 | tf_op jit(solution)/shard_map/ppermute | solution.py:32
  98.0 12.1 %collective-permute-start.25 = (bf16[272,256]{1,0:T(8,128)(2,1)S(1)}, bf16[272,256]{1,0:T(8,128)(2,1)S(1)}, u32[]{:S(2)}, u32[]{:S(2)}) collective-permute-start(bf16[272,256]{1,0:T(8,128)(2,1)S(1)} %get-tuple-element.113.refs_8_), channel_id=1, source_target_pairs={{0,2},{1,3},{2,0},{3,1},{4,6},{5,7},{6,4},{7,5},{8,10},{9,11},{10,... | collective-permute-start | bytes 417800 | tf_op jit(solution)/shard_map/ppermute | solution.py:32
  100.5 9.6 %collective-permute-start.26 = (bf16[272,256]{1,0:T(8,128)(2,1)S(1)}, bf16[272,256]{1,0:T(8,128)(2,1)S(1)}, u32[]{:S(2)}, u32[]{:S(2)}) collective-permute-start(bf16[272,256]{1,0:T(8,128)(2,1)S(1)} %get-tuple-element.113.refs_8_), channel_id=1, source_target_pairs={{0,3},{1,2},{2,1},{3,0},{4,7},{5,6},{6,5},{7,4},{8,11},{9,10},{10,... | collective-permute-start | bytes 417800 | tf_op jit(solution)/shard_map/ppermute | solution.py:32
  102.1 8.5 %collective-permute-start.27 = (bf16[272,256]{1,0:T(8,128)(2,1)S(1)}, bf16[272,256]{1,0:T(8,128)(2,1)S(1)}, u32[]{:S(2)}, u32[]{:S(2)}) collective-permute-start(bf16[272,256]{1,0:T(8,128)(2,1)S(1)} %get-tuple-element.113.refs_8_), channel_id=1, source_target_pairs={{0,1},{1,0},{2,3},{3,2},{4,5},{5,4},{6,7},{7,6},{8,9},{9,8},{10,11... | collective-permute-start | bytes 417800 | tf_op jit(solution)/shard_map/ppermute | solution.py:32
  111.5 12.9 %collective-permute-start.28 = (bf16[256,256]{1,0:T(8,128)(2,1)S(1)}, bf16[256,256]{1,0:T(8,128)(2,1)S(1)}, u32[]{:S(2)}, u32[]{:S(2)}) collective-permute-start(bf16[256,256]{1,0:T(8,128)(2,1)S(1)} %get-tuple-element.117), channel_id=1, source_target_pairs={{0,2},{1,3},{2,0},{3,1},{4,6},{5,7},{6,4},{7,5},{8,10},{9,11},{10,... | collective-permute-start | bytes 393224 | tf_op jit(solution)/shard_map/ppermute | solution.py:32
  113.5 10.9 %collective-permute-start.29 = (bf16[256,256]{1,0:T(8,128)(2,1)S(1)}, bf16[256,256]{1,0:T(8,128)(2,1)S(1)}, u32[]{:S(2)}, u32[]{:S(2)}) collective-permute-start(bf16[256,256]{1,0:T(8,128)(2,1)S(1)} %get-tuple-element.118), channel_id=1, source_target_pairs={{0,3},{1,2},{2,1},{3,0},{4,7},{5,6},{6,5},{7,4},{8,11},{9,10},{10,... | collective-permute-start | bytes 393224 | tf_op jit(solution)/shard_map/ppermute | solution.py:32
  116.2 9.1 %collective-permute-start.30 = (bf16[256,256]{1,0:T(8,128)(2,1)S(1)}, bf16[256,256]{1,0:T(8,128)(2,1)S(1)}, u32[]{:S(2)}, u32[]{:S(2)}) collective-permute-start(bf16[256,256]{1,0:T(8,128)(2,1)S(1)} %get-tuple-element.119), channel_id=1, source_target_pairs={{0,1},{1,0},{2,3},{3,2},{4,5},{5,4},{6,7},{7,6},{8,9},{9,8},{10,11... | collective-permute-start | bytes 393224 | tf_op jit(solution)/shard_map/ppermute | solution.py:32
  116.3 10.3 %collective-permute-start.32 = (bf16[240,256]{1,0:T(8,128)(2,1)S(1)}, bf16[240,256]{1,0:T(8,128)(2,1)S(1)}, u32[]{:S(2)}, u32[]{:S(2)}) collective-permute-start(bf16[240,256]{1,0:T(8,128)(2,1)S(1)} %get-tuple-element.122.refs_0_), channel_id=1, source_target_pairs={{0,4},{4,0},{8,12},{12,8},{1,5},{5,1},{9,13},{13,9},{2,6},{6,2},{1... | collective-permute-start | bytes 368648 | tf_op jit(solution)/shard_map/ppermute | solution.py:32
  117.6 9.0 %collective-permute-start.33 = (bf16[240,256]{1,0:T(8,128)(2,1)S(1)}, bf16[240,256]{1,0:T(8,128)(2,1)S(1)}, u32[]{:S(2)}, u32[]{:S(2)}) collective-permute-start(bf16[240,256]{1,0:T(8,128)(2,1)S(1)} %get-tuple-element.123.refs_1_), channel_id=1, source_target_pairs={{0,8},{4,12},{8,0},{12,4},{1,9},{5,13},{9,1},{13,5},{2,10},{6,14},... | collective-permute-start | bytes 368648 | tf_op jit(solution)/shard_map/ppermute | solution.py:32
  129.8 12.6 %collective-permute-start.36 = (bf16[896,256]{1,0:T(8,128)(2,1)S(1)}, bf16[896,256]{1,0:T(8,128)(2,1)S(1)}, u32[]{:S(2)}, u32[]{:S(2)}) collective-permute-start(bf16[896,256]{1,0:T(8,128)(2,1)S(1)} %pad_maximum_fusion.1), channel_id=1, source_target_pairs={{0,8},{4,12},{8,0},{12,4},{1,9},{5,13},{9,1},{13,5},{2,10},{6,14},... | collective-permute-start | bytes 1376264 | tf_op jit(solution)/shard_map/ppermute | solution.py:32
  131.4 12.3 %collective-permute-start.35 = (bf16[896,256]{1,0:T(8,128)(2,1)S(1)}, bf16[896,256]{1,0:T(8,128)(2,1)S(1)}, u32[]{:S(2)}, u32[]{:S(2)}) collective-permute-start(bf16[896,256]{1,0:T(8,128)(2,1)S(1)} %pad_maximum_fusion), channel_id=1, source_target_pairs={{0,4},{4,0},{8,12},{12,8},{1,5},{5,1},{9,13},{13,9},{2,6},{6,2},{1... | collective-permute-start | bytes 1376264 | tf_op jit(solution)/shard_map/ppermute | solution.py:32
  144.0 8.8 %collective-permute-start.38 = (bf16[656,256]{1,0:T(8,128)(2,1)S(1)}, bf16[656,256]{1,0:T(8,128)(2,1)S(1)}, u32[]{:S(2)}, u32[]{:S(2)}) collective-permute-start(bf16[656,256]{1,0:T(8,128)(2,1)S(1)} %pad_maximum_fusion.3), channel_id=1, source_target_pairs={{0,4},{4,0},{8,12},{12,8},{1,5},{5,1},{9,13},{13,9},{2,6},{6,2},{1... | collective-permute-start | bytes 1007624 | tf_op jit(solution)/shard_map/ppermute | solution.py:32
  145.5 8.6 %collective-permute-start.37 = (bf16[656,256]{1,0:T(8,128)(2,1)S(1)}, bf16[656,256]{1,0:T(8,128)(2,1)S(1)}, u32[]{:S(2)}, u32[]{:S(2)}) collective-permute-start(bf16[656,256]{1,0:T(8,128)(2,1)S(1)} %pad_maximum_fusion.2), channel_id=1, source_target_pairs={{0,8},{4,12},{8,0},{12,4},{1,9},{5,13},{9,1},{13,5},{2,10},{6,14},... | collective-permute-start | bytes 1007624 | tf_op jit(solution)/shard_map/ppermute | solution.py:32
  (24 other events, 202.7 us)

commit v5 on v4

--- a/solution.py
+++ b/solution.py
@@ -196,12 +196,15 @@
 def line_body(n, tall, *refs):
     half = (refs[0].shape[0] - 2 * tall) // 2
     own_ref, far_ref = refs[n], refs[n + 1]
-    near_ref, message, kept_ref = refs[n + 4 :]
-    kept_ref[...] = own_ref[...]
+    near_ref, message, inner_ref = refs[n + 4 :]
+    size = own_ref.shape[0]
+    inner_ref[:size, :] = own_ref[...]
+    inner_ref[size:, :] = refs[n - 1][2 * (tall + half) :, :]
     near_ref[...] = refs[n - 1][2 * (tall + half) :, :]
     rest = own_ref.shape[0] // 2
     message[:rest, :] = own_ref[rest:, :]
-    message[rest:, :] = far_ref[...]
+    message[rest:-PAD, :] = far_ref[...]
+    message[-PAD:, :] = jnp.zeros((PAD, message.shape[1]), BF16)
     for i in range(1, n):
         for j in range(2):
             start = 2 * tall + j * half
@@ -213,19 +216,19 @@
     for here, there, out_ref in ((up, up1, ups), (down, down2, downs)):
         out_ref[0] = here[...]
         out_ref[1] = there[...]
-    first, rest, rows = near.shape[0], near1.shape[0], far2.shape[0]
+    rest, rows = near1.shape[0], far2.shape[0]
     near[:rest, :] = near1[...]
     near[rest:, :] = moved[:rest, :]
-    message[:first, :] = near[...]
+    message[:rest, :] = moved[:rest, :]
     for i, far in enumerate((far3, far2)):
         start = rest + i * rows
         total = moved[start : start + rows, :].astype(F32) + far[...].astype(F32)
-        message[first + i * rows : first + (i + 1) * rows, :] = total.astype(BF16)
+        message[start : start + rows, :] = total.astype(BF16)
 
 
 def gather_body(
     up, up1, up2, down, down2, down1, moved, close, key_ref, value_ref,
-    out_ref, next_ref, message, weight_ref,
+    out_ref, message, weight_ref,
 ):
     tall = key_ref.shape[0]
     weight_ref[:tall, :] = key_ref[...]
@@ -236,11 +239,11 @@
         out_ref[base + near] = parts[1][...]
         out_ref[base + 3 - near] = parts[2][0]
         out_ref[base + 3] = parts[2][1]
-    first, rows = next_ref.shape[0], close.shape[0]
-    next_ref[...] = moved[:first, :]
-    message[:first, :] = moved[:first, :]
-    total = moved[first + rows :, :].astype(F32) + close[...].astype(F32)
-    message[first:, :] = total.astype(BF16)
+    rows = close.shape[0]
+    rest = message.shape[0] - rows
+    message[:rest, :] = moved[:rest, :]
+    total = moved[rest + rows :, :].astype(F32) + close[...].astype(F32)
+    message[rest:, :] = total.astype(BF16)
 
 
 def rows_body(cols, rows_ref, own_ref):
@@ -379,10 +382,16 @@
     def piece(k):
         if len(pieces) == n or k < 2:
             return unpack(pieces[k][...], rows, feats).astype(F32)
+        far_inner, next_outer, late_inner, late_outer = (ref[...] for ref in pieces[2:])
+        size = rows * feats // cols
+        rest = size // 2
         inner = jnp.logical_or(m == 1, m == 2)
-        inside, outside = pieces[2 * k - 2 : 2 * k]
-        here = slice(0, rows * feats // cols)
-        value = jnp.where(inner, inside[here, :], outside[here, :])
+        if k == 2:
+            inside = jnp.concatenate([far_inner[size:], late_inner[:rest]], axis=0)
+            value = jnp.where(inner, inside, next_outer[:size])
+        else:
+            outside = jnp.concatenate([next_outer[size:], late_outer[:rest]], axis=0)
+            value = jnp.where(inner, far_inner[:size], outside)
         return unpack(value, rows, feats).astype(F32)
 
     total = jnp.zeros((rows, 1), F32)
@@ -669,37 +678,36 @@
             flops=2 * rows * width * cols,
         )(out_grad[:, 0], *wouts)
         piece = (n - 1, up_rows + feats // (2 * parts), 2 * down_cols)
-        up, down, near, message, own = call(
+        up, down, near, message, inner_rows = call(
             functools.partial(line_body, n, up_rows),
             [shape(piece)] * 2
-            + [shape((rest, cols)), shape((rest + 2 * rows, cols)), own_shape],
+            + [shape((rest + size, cols)) for size in (0, 2 * rows + PAD, own_shape.shape[0])],
             [vm()] * (n + 2),
             deps=[gains[1]],
         )(*line, own, far_grads)
         inner, outer = [(1, 2), (2, 1)], [(1, 0), (2, 3)]
         up1, down2 = xor_move(up, "dp", 1), xor_move(down, "dp", 2)
-        far_inner = lax.ppermute(own, "mp", inner)
+        far_inner = lax.ppermute(inner_rows, "mp", inner)
         message = xor_move(message, "mp", 1)
         ups, downs, message, near = call(
             pair_body,
-            [shape((2,) + piece)] * 2 + [shape((own_shape.shape[0] + 2 * rows, cols)), own_shape],
+            [shape((2,) + piece)] * 2 + [shape((rest + 2 * rows, cols)), own_shape],
             [vm()] * 8,
             deps=[far_inner],
         )(up, up1, down, down2, near, message, grads[1], grads[2])
         up2, down1 = xor_move(ups, "dp", 2), xor_move(downs, "dp", 1)
         next_outer = lax.ppermute(far_inner, "mp", outer)
         message = lax.ppermute(message, "mp", inner)
-        last = shape((own_shape.shape[0] + rows, cols))
-        gathered, next_inner, close, wkv = call(
+        gathered, close, wkv = call(
             gather_body,
-            [shape((parts,) + piece), own_shape, last, shape((2 * enc_width, cols))],
+            [shape((parts,) + piece), shape((rest + rows, cols)), shape((2 * enc_width, cols))],
             [vm()] * 10,
             deps=[next_outer, normed],
         )(up, up1, up2, down, down2, down1, message, grads[3], wk, wv)
         pieces = [gathered, swap(gathered), enc_up, down_t, *wqs]
         close = xor_move(close, "mp", 1)
         grad_parts = [grads[0], message, close]
-        row_pieces = [own, near, next_inner, next_outer, far_inner, close]
+        row_pieces = [own, near, far_inner, next_outer, message, close]
         before_projected = [close]
         scratch = [
             pltpu.VMEM((n, parts, up_rows, enc_up.shape[1]), BF16),

time: 157 us -> 156 us (level)
    ppermute x37, waiting for transfers between devices: 75.5 us -> 73.8 us  [xor_move(): return lax.ppermute(value, axis, [(i, i ^ by) for i in range(count)])]
    ppermute x1, waiting for transfers between devices: 7.18 us -> 8.76 us  [on_device(): next_outer = lax.ppermute(far_inner, 'mp', outer)]
  transfers between devices with their start and end apart: 40 -> 40, of which waited for: 25 -> 24; matrix products, arithmetic and copies ran while one was open for 0% -> 0% of each run, Pallas kernels for 12% -> 12%
where the time goes in v5:
time: 156 us
  waiting for transfers between devices  82.6 us (53%)
  starting transfers between devices  42.8 us (27%)
  Pallas kernels  26.8 us (17%)
    ppermute x37, waiting for transfers between devices, xor_move(): return lax.ppermute(value, axis, [(i, i ^ by) for i in range(count)])  73.8 us
    ppermute x37, starting transfers between devices, xor_move(): return lax.ppermute(value, axis, [(i, i ^ by) for i in range(count)])  40.1 us
    pallas_call x25, Pallas kernels, run(): pl.pallas_call(kernel, out_shape=list(outs) + [shape(x.shape, x.dtype) fo...  26.8 us
    ppermute x1, waiting for transfers between devices, on_device(): next_outer = lax.ppermute(far_inner, 'mp', outer)  8.76 us
  transfers between devices with their start and end apart: 40, of which 24 were waited for; matrix products, arithmetic and copies ran while one was open for 0% of the time, Pallas kernels for 12%

profile of v5, /device:TPU:0, one launch (start us, length us, event | category | flops | bytes accessed | tf_op | source)
XLA Modules:
  0.0 155.8 jit_solution(4868356342433906590)
XLA Ops:
  1.3 2.4 %collective-permute-done.1.refs_3_.refs_7_ = bf16[2048,256]{1,0:T(8,128)(2,1)S(1)} collective-permute-done((bf16[2048,256]{1,0:T(8,128)(2,1)}, bf16[2048,256]{1,0:T(8,128)(2,1)S(1)}, u32[]{:S(2)}, u32[]{:S(2)}) %collective-permute-start.1) | collective-permute-done | bytes 1048608 | tf_op jit(solution)/shard_map/ppermute | solution.py:32
  4.7 2.1 %shard_map.140 = (bf16[288,256]{1,0:T(8,128)(2,1)}, bf16[288,256]{1,0:T(8,128)(2,1)}, bf16[288,256]{1,0:T(8,128)(2,1)}, bf16[544,256]{1,0:T(8,128)(2,1)}, bf16[512,256]{1,0:T(8,128)(2,1)}) custom-call(bf16[896,256]{1,0:T(8,128)(2,1)} %refs_4_.1, bf16[224,1024]{1,0:T(8,128)(2,1)} %bitcast.27, bf16[2048,256]{1,0:T(8,128)(2,1)} %bitcast.16, ...), custom_call_target="tpu_custom_call" | custom-call | bytes 983 | tf_op jit(solution)/shard_map/pallas_call | solution.py:70
  6.9 3.0 %collective-permute-start.5 = (bf16[544,256]{1,0:T(8,128)(2,1)}, bf16[544,256]{1,0:T(8,128)(2,1)S(1)}, u32[]{:S(2)}, u32[]{:S(2)}) collective-permute-start(bf16[544,256]{1,0:T(8,128)(2,1)} %get-tuple-element.74), channel_id=1, source_target_pairs={{0,1},{1,0},{2,3},{3,2},{4,5},{5,4},{6,7},{7,6},{8,9},{9,8},{10,11... | collective-permute-start | bytes 835592 | tf_op jit(solution)/shard_map/ppermute | solution.py:32
  9.9 2.6 %collective-permute-start.3 = (bf16[288,256]{1,0:T(8,128)(2,1)}, bf16[288,256]{1,0:T(8,128)(2,1)S(1)}, u32[]{:S(2)}, u32[]{:S(2)}) collective-permute-start(bf16[288,256]{1,0:T(8,128)(2,1)} %get-tuple-element.72), channel_id=1, source_target_pairs={{0,2},{1,3},{2,0},{3,1},{4,6},{5,7},{6,4},{7,5},{8,10},{9,11},{10,... | collective-permute-start | bytes 442376 | tf_op jit(solution)/shard_map/ppermute | solution.py:32
  13.6 6.8 %collective-permute-done.3.refs_1_ = bf16[288,256]{1,0:T(8,128)(2,1)S(1)} collective-permute-done((bf16[288,256]{1,0:T(8,128)(2,1)}, bf16[288,256]{1,0:T(8,128)(2,1)S(1)}, u32[]{:S(2)}, u32[]{:S(2)}) %collective-permute-start.3) | collective-permute-done | bytes 147488 | tf_op jit(solution)/shard_map/ppermute | solution.py:32
  20.4 5.2 %collective-permute-done.4.refs_2_ = bf16[288,256]{1,0:T(8,128)(2,1)S(1)} collective-permute-done((bf16[288,256]{1,0:T(8,128)(2,1)}, bf16[288,256]{1,0:T(8,128)(2,1)S(1)}, u32[]{:S(2)}, u32[]{:S(2)}) %collective-permute-start.4) | collective-permute-done | bytes 147488 | tf_op jit(solution)/shard_map/ppermute | solution.py:32
  27.5 1.6 collective-permute-start.6
  29.1 1.5 collective-permute-start.7
  30.6 2.9 %collective-permute-done.6.refs_1_ = bf16[3,144,256]{2,1,0:T(8,128)(2,1)S(1)} collective-permute-done((bf16[3,144,256]{2,1,0:T(8,128)(2,1)S(1)}, bf16[3,144,256]{2,1,0:T(8,128)(2,1)S(1)}, u32[]{:S(2)}, u32[]{:S(2)}) %collective-permute-start.6) | collective-permute-done | bytes 221216 | tf_op jit(solution)/shard_map/ppermute | solution.py:32
  36.4 1.6 %collective-permute-start.10 = (bf16[2,3,144,256]{3,2,1,0:T(8,128)(2,1)S(1)}, bf16[2,3,144,256]{3,2,1,0:T(8,128)(2,1)S(1)}, u32[]{:S(2)}, u32[]{:S(2)}) collective-permute-start(bf16[2,3,144,256]{3,2,1,0:T(8,128)(2,1)S(1)} %get-tuple-element.83), channel_id=1, source_target_pairs={{0,8},{4,12},{8,0},{12,4},{1,9},{5,13},{9,1},{13,5},{2,10},{6,14},... | collective-permute-start | bytes 1327112 | tf_op jit(solution)/shard_map/ppermute | solution.py:32
  38.0 1.5 collective-permute-start.11
  42.2 8.8 %collective-permute-done.13.refs_10_.refs_7_ = bf16[768,256]{1,0:T(8,128)(2,1)S(1)} collective-permute-done((bf16[768,256]{1,0:T(8,128)(2,1)S(1)}, bf16[768,256]{1,0:T(8,128)(2,1)S(1)}, u32[]{:S(2)}, u32[]{:S(2)}) %collective-permute-start.13) | collective-permute-done | bytes 393248 | tf_op jit(solution)/shard_map/ppermute | solution.py:699
  51.9 3.7 %collective-permute-start.15 = (bf16[512,256]{1,0:T(8,128)(2,1)S(1)}, bf16[512,256]{1,0:T(8,128)(2,1)S(1)}, u32[]{:S(2)}, u32[]{:S(2)}) collective-permute-start(bf16[512,256]{1,0:T(8,128)(2,1)S(1)} %get-tuple-element.90), channel_id=1, source_target_pairs={{0,1},{1,0},{2,3},{3,2},{4,5},{5,4},{6,7},{7,6},{8,9},{9,8},{10,11... | collective-permute-start | bytes 786440 | tf_op jit(solution)/shard_map/ppermute | solution.py:32
  55.6 5.6 %shard_map.146 = (bf16[1024,896]{1,0:T(8,128)(2,1)S(1)}, bf16[4,512,256]{2,1,0:T(8,128)(2,1)S(1)}) custom-call(bf16[1024,896]{1,0:T(8,128)(2,1)S(1)} %bitcast.24, bf16[1024,896]{1,0:T(8,128)(2,1)S(1)} %shard_map.141.refs_11_.refs_1_, bf16[8,3,144,256]{3,2,1,0:T(8,128)(2,1)S(1)} %get-tuple-element.87.refs_2_, ...), custom_call_target="tpu_custom_call" | custom-call | flops 3758096 | bytes 2883 | tf_op jit(solution)/shard_map/pallas_call | solution.py:70
  66.1 1.6 %shard_map.150 = (bf16[256,256]{1,0:T(8,128)(2,1)S(1)}, f32[8,64,512]{2,1,0:T(8,128)S(1)}, bf16[2048,512]{1,0:T(8,128)(2,1)S(1)}, bf16[8,128,1408]{2,1,0:T(8,128)(2,1)S(1)}) custom-call(s32[2,4,4]{2,1,0:T(4,128)S(1)} %bitcast.35, s32[2,4]{1,0:T(2,128)S(1)} %bitcast.38, ...), custom_call_target="tpu_custom_call", output_to_operand_aliasing={{3}: (5, {})} | custom-call | flops 134217 | bytes 3276 | tf_op jit(solution)/shard_map/pallas_call | solution.py:70
  67.9 2.4 %collective-permute-start.18 = (bf16[256,256]{1,0:T(8,128)(2,1)S(1)}, bf16[256,256]{1,0:T(8,128)(2,1)S(1)}, u32[]{:S(2)}, u32[]{:S(2)}) collective-permute-start(bf16[256,256]{1,0:T(8,128)(2,1)S(1)} %get-tuple-element.93.refs_6_), channel_id=1, source_target_pairs={{0,2},{1,3},{2,0},{3,1},{4,6},{5,7},{6,4},{7,5},{8,10},{9,11},{10,... | collective-permute-start | bytes 393224 | tf_op jit(solution)/shard_map/ppermute | solution.py:32
  70.3 2.2 %collective-permute-start.19 = (bf16[256,256]{1,0:T(8,128)(2,1)S(1)}, bf16[256,256]{1,0:T(8,128)(2,1)S(1)}, u32[]{:S(2)}, u32[]{:S(2)}) collective-permute-start(bf16[256,256]{1,0:T(8,128)(2,1)S(1)} %get-tuple-element.93.refs_6_), channel_id=1, source_target_pairs={{0,3},{1,2},{2,1},{3,0},{4,7},{5,6},{6,5},{7,4},{8,11},{9,10},{10,... | collective-permute-start | bytes 393224 | tf_op jit(solution)/shard_map/ppermute | solution.py:32
  72.6 8.3 %collective-permute-done.18.refs_7_ = bf16[256,256]{1,0:T(8,128)(2,1)S(1)} collective-permute-done((bf16[256,256]{1,0:T(8,128)(2,1)S(1)}, bf16[256,256]{1,0:T(8,128)(2,1)S(1)}, u32[]{:S(2)}, u32[]{:S(2)}) %collective-permute-start.18) | collective-permute-done | bytes 131104 | tf_op jit(solution)/shard_map/ppermute | solution.py:32
  82.4 2.6 %collective-permute-start.22 = (bf16[272,256]{1,0:T(8,128)(2,1)S(1)}, bf16[272,256]{1,0:T(8,128)(2,1)S(1)}, u32[]{:S(2)}, u32[]{:S(2)}) collective-permute-start(bf16[272,256]{1,0:T(8,128)(2,1)S(1)} %get-tuple-element.96), channel_id=1, source_target_pairs={{0,2},{1,3},{2,0},{3,1},{4,6},{5,7},{6,4},{7,5},{8,10},{9,11},{10,... | collective-permute-start | bytes 417800 | tf_op jit(solution)/shard_map/ppermute | solution.py:32
  85.0 1.9 %collective-permute-start.23 = (bf16[272,256]{1,0:T(8,128)(2,1)S(1)}, bf16[272,256]{1,0:T(8,128)(2,1)S(1)}, u32[]{:S(2)}, u32[]{:S(2)}) collective-permute-start(bf16[272,256]{1,0:T(8,128)(2,1)S(1)} %get-tuple-element.97), channel_id=1, source_target_pairs={{0,3},{1,2},{2,1},{3,0},{4,7},{5,6},{6,5},{7,4},{8,11},{9,10},{10,... | collective-permute-start | bytes 417800 | tf_op jit(solution)/shard_map/ppermute | solution.py:32
  88.1 7.8 %collective-permute-done.22.refs_2_ = bf16[272,256]{1,0:T(8,128)(2,1)S(1)} collective-permute-done((bf16[272,256]{1,0:T(8,128)(2,1)S(1)}, bf16[272,256]{1,0:T(8,128)(2,1)S(1)}, u32[]{:S(2)}, u32[]{:S(2)}) %collective-permute-start.22) | collective-permute-done | bytes 139296 | tf_op jit(solution)/shard_map/ppermute | solution.py:32
  96.0 1.8 %shard_map.153 = (bf16[272,256]{1,0:T(8,128)(2,1)S(1)}, f32[256,128]{1,0:T(8,128)S(1)}, bf16[256,256]{1,0:T(8,128)(2,1)S(1)}, bf16[8,64,512]{2,1,0:T(8,128)(2,1)S(1)}, bf16[8,64,512]{2,1,0:T(8,128)(2,1)S(1)}) custom-call(s32[2,4]{1,0:T(2,128)S(1)} %bitcast.39, bf16[272,256]{1,0:T(8,128)(2,1)S(1)} %get-tuple-element.95.refs_1_, ...), custom_call_target="tpu_custom_call" | custom-call | flops 201326 | bytes 1449 | tf_op jit(solution)/shard_map/pallas_call | solution.py:70
  97.8 2.4 %collective-permute-start.25 = (bf16[272,256]{1,0:T(8,128)(2,1)S(1)}, bf16[272,256]{1,0:T(8,128)(2,1)S(1)}, u32[]{:S(2)}, u32[]{:S(2)}) collective-permute-start(bf16[272,256]{1,0:T(8,128)(2,1)S(1)} %get-tuple-element.111.refs_8_), channel_id=1, source_target_pairs={{0,2},{1,3},{2,0},{3,1},{4,6},{5,7},{6,4},{7,5},{8,10},{9,11},{10,... | collective-permute-start | bytes 417800 | tf_op jit(solution)/shard_map/ppermute | solution.py:32
  100.2 2.2 %collective-permute-start.26 = (bf16[272,256]{1,0:T(8,128)(2,1)S(1)}, bf16[272,256]{1,0:T(8,128)(2,1)S(1)}, u32[]{:S(2)}, u32[]{:S(2)}) collective-permute-start(bf16[272,256]{1,0:T(8,128)(2,1)S(1)} %get-tuple-element.111.refs_8_), channel_id=1, source_target_pairs={{0,3},{1,2},{2,1},{3,0},{4,7},{5,6},{6,5},{7,4},{8,11},{9,10},{10,... | collective-permute-start | bytes 417800 | tf_op jit(solution)/shard_map/ppermute | solution.py:32
  103.4 2.8 %shard_map.155 = (bf16[896,2048]{1,0:T(8,128)(2,1)S(1)}, bf16[896,256]{1,0:T(8,128)(2,1)S(1)}, bf16[896,256]{1,0:T(8,128)(2,1)S(1)}) custom-call(s32[2,4,4]{2,1,0:T(4,128)S(1)} %bitcast.37, bf16[2048,512]{1,0:T(8,128)(2,1)S(1)} %shard_map.154.refs_1_, bf16[8,128,1408]{2,1,0:T(8,128)(2,1)S(1)} %get-tuple-element.94.refs_4_.refs_2_, ...), custom_call_target="tpu_custom_call" | custom-call | flops 1879048 | bytes 4587 | tf_op jit(solution)/shard_map/pallas_call | solution.py:70
  106.1 3.9 %collective-permute-done.25.refs_9_ = bf16[272,256]{1,0:T(8,128)(2,1)S(1)} collective-permute-done((bf16[272,256]{1,0:T(8,128)(2,1)S(1)}, bf16[272,256]{1,0:T(8,128)(2,1)S(1)}, u32[]{:S(2)}, u32[]{:S(2)}) %collective-permute-start.25) | collective-permute-done | bytes 139296 | tf_op jit(solution)/shard_map/ppermute | solution.py:32
  111.7 2.5 %collective-permute-start.28 = (bf16[256,256]{1,0:T(8,128)(2,1)S(1)}, bf16[256,256]{1,0:T(8,128)(2,1)S(1)}, u32[]{:S(2)}, u32[]{:S(2)}) collective-permute-start(bf16[256,256]{1,0:T(8,128)(2,1)S(1)} %get-tuple-element.115), channel_id=1, source_target_pairs={{0,2},{1,3},{2,0},{3,1},{4,6},{5,7},{6,4},{7,5},{8,10},{9,11},{10,... | collective-permute-start | bytes 393224 | tf_op jit(solution)/shard_map/ppermute | solution.py:32
  116.6 8.0 %collective-permute-done.28.refs_4_ = bf16[256,256]{1,0:T(8,128)(2,1)S(1)} collective-permute-done((bf16[256,256]{1,0:T(8,128)(2,1)S(1)}, bf16[256,256]{1,0:T(8,128)(2,1)S(1)}, u32[]{:S(2)}, u32[]{:S(2)}) %collective-permute-start.28) | collective-permute-done | bytes 131104 | tf_op jit(solution)/shard_map/ppermute | solution.py:32
  131.3 11.4 %collective-permute-done.36 = bf16[896,256]{1,0:T(8,128)(2,1)S(1)} collective-permute-done((bf16[896,256]{1,0:T(8,128)(2,1)S(1)}, bf16[896,256]{1,0:T(8,128)(2,1)S(1)}, u32[]{:S(2)}, u32[]{:S(2)}) %collective-permute-start.36) | collective-permute-done | bytes 458784 | tf_op jit(solution)/shard_map/ppermute | solution.py:32
  144.0 1.6 collective-permute-start.37
  145.5 6.7 %collective-permute-done.38 = bf16[656,256]{1,0:T(8,128)(2,1)S(1)} collective-permute-done((bf16[656,256]{1,0:T(8,128)(2,1)S(1)}, bf16[656,256]{1,0:T(8,128)(2,1)S(1)}, u32[]{:S(2)}, u32[]{:S(2)}) %collective-permute-start.38) | collective-permute-done | bytes 335904 | tf_op jit(solution)/shard_map/ppermute | solution.py:32
  153.0 1.8 %collective-permute-done.39 = bf16[896,256]{1,0:T(8,128)(2,1)S(1)} collective-permute-done((bf16[896,256]{1,0:T(8,128)(2,1)S(1)}, bf16[896,256]{1,0:T(8,128)(2,1)S(1)}, u32[]{:S(2)}, u32[]{:S(2)}) %collective-permute-start.39) | collective-permute-done | bytes 458784 | tf_op jit(solution)/shard_map/ppermute | solution.py:32
  (128 shorter events, 33.7 us)
Async XLA Ops:
  1.2 11.3 %collective-permute-start.2 = (bf16[1024,512]{1,0:T(8,128)(2,1)}, bf16[1024,512]{1,0:T(8,128)(2,1)S(1)}, u32[]{:S(2)}, u32[]{:S(2)}) collective-permute-start(bf16[1024,512]{1,0:T(8,128)(2,1)} %bitcast.19), channel_id=1, source_target_pairs={{0,16},{16,0},{1,17},{17,1},{2,18},{18,2},{3,19},{19,3},{4,20},{20... | collective-permute-start | bytes 3145736 | tf_op jit(solution)/shard_map/ppermute | solution.py:32
  6.9 18.8 %collective-permute-start.5 = (bf16[544,256]{1,0:T(8,128)(2,1)}, bf16[544,256]{1,0:T(8,128)(2,1)S(1)}, u32[]{:S(2)}, u32[]{:S(2)}) collective-permute-start(bf16[544,256]{1,0:T(8,128)(2,1)} %get-tuple-element.74), channel_id=1, source_target_pairs={{0,1},{1,0},{2,3},{3,2},{4,5},{5,4},{6,7},{7,6},{8,9},{9,8},{10,11... | collective-permute-start | bytes 835592 | tf_op jit(solution)/shard_map/ppermute | solution.py:32
  9.9 10.5 %collective-permute-start.3 = (bf16[288,256]{1,0:T(8,128)(2,1)}, bf16[288,256]{1,0:T(8,128)(2,1)S(1)}, u32[]{:S(2)}, u32[]{:S(2)}) collective-permute-start(bf16[288,256]{1,0:T(8,128)(2,1)} %get-tuple-element.72), channel_id=1, source_target_pairs={{0,2},{1,3},{2,0},{3,1},{4,6},{5,7},{6,4},{7,5},{8,10},{9,11},{10,... | collective-permute-start | bytes 442376 | tf_op jit(solution)/shard_map/ppermute | solution.py:32
  12.5 13.2 %collective-permute-start.4 = (bf16[288,256]{1,0:T(8,128)(2,1)}, bf16[288,256]{1,0:T(8,128)(2,1)S(1)}, u32[]{:S(2)}, u32[]{:S(2)}) collective-permute-start(bf16[288,256]{1,0:T(8,128)(2,1)} %get-tuple-element.73), channel_id=1, source_target_pairs={{0,3},{1,2},{2,1},{3,0},{4,7},{5,6},{6,5},{7,4},{8,11},{9,10},{10,... | collective-permute-start | bytes 442376 | tf_op jit(solution)/shard_map/ppermute | solution.py:32
  25.8 10.5 %collective-permute-start.8 = (bf16[784,256]{1,0:T(8,128)(2,1)S(1)}, bf16[784,256]{1,0:T(8,128)(2,1)S(1)}, u32[]{:S(2)}, u32[]{:S(2)}) collective-permute-start(bf16[784,256]{1,0:T(8,128)(2,1)S(1)} %get-tuple-element.79), channel_id=1, source_target_pairs={{0,1},{1,0},{2,3},{3,2},{4,5},{5,4},{6,7},{7,6},{8,9},{9,8},{10,11... | collective-permute-start | bytes 1204232 | tf_op jit(solution)/shard_map/ppermute | solution.py:32
  26.9 8.2 %collective-permute-start.9 = (bf16[768,256]{1,0:T(8,128)(2,1)S(1)}, bf16[768,256]{1,0:T(8,128)(2,1)S(1)}, u32[]{:S(2)}, u32[]{:S(2)}) collective-permute-start(bf16[768,256]{1,0:T(8,128)(2,1)S(1)} %get-tuple-element.82), channel_id=1, source_target_pairs={{1,2},{2,1},{5,6},{6,5},{9,10},{10,9},{13,14},{14,13},{17,18},{18,... | collective-permute-start | bytes 1179656 | tf_op jit(solution)/shard_map/ppermute | solution.py:690
  27.5 6.0 %collective-permute-start.6 = (bf16[3,144,256]{2,1,0:T(8,128)(2,1)S(1)}, bf16[3,144,256]{2,1,0:T(8,128)(2,1)S(1)}, u32[]{:S(2)}, u32[]{:S(2)}) collective-permute-start(bf16[3,144,256]{2,1,0:T(8,128)(2,1)S(1)} %get-tuple-element.76.refs_0_), channel_id=1, source_target_pairs={{0,4},{4,0},{8,12},{12,8},{1,5},{5,1},{9,13},{13,9},{2,6},{6,2},{1... | collective-permute-start | bytes 663560 | tf_op jit(solution)/shard_map/ppermute | solution.py:32
  36.4 14.6 %collective-permute-start.10 = (bf16[2,3,144,256]{3,2,1,0:T(8,128)(2,1)S(1)}, bf16[2,3,144,256]{3,2,1,0:T(8,128)(2,1)S(1)}, u32[]{:S(2)}, u32[]{:S(2)}) collective-permute-start(bf16[2,3,144,256]{3,2,1,0:T(8,128)(2,1)S(1)} %get-tuple-element.83), channel_id=1, source_target_pairs={{0,8},{4,12},{8,0},{12,4},{1,9},{5,13},{9,1},{13,5},{2,10},{6,14},... | collective-permute-start | bytes 1327112 | tf_op jit(solution)/shard_map/ppermute | solution.py:32
  38.0 13.0 %collective-permute-start.11 = (bf16[2,3,144,256]{3,2,1,0:T(8,128)(2,1)S(1)}, bf16[2,3,144,256]{3,2,1,0:T(8,128)(2,1)S(1)}, u32[]{:S(2)}, u32[]{:S(2)}) collective-permute-start(bf16[2,3,144,256]{3,2,1,0:T(8,128)(2,1)S(1)} %get-tuple-element.84), channel_id=1, source_target_pairs={{0,4},{4,0},{8,12},{12,8},{1,5},{5,1},{9,13},{13,9},{2,6},{6,2},{1... | collective-permute-start | bytes 1327112 | tf_op jit(solution)/shard_map/ppermute | solution.py:32
  39.5 11.5 %collective-permute-start.13 = (bf16[768,256]{1,0:T(8,128)(2,1)S(1)}, bf16[768,256]{1,0:T(8,128)(2,1)S(1)}, u32[]{:S(2)}, u32[]{:S(2)}) collective-permute-start(bf16[768,256]{1,0:T(8,128)(2,1)S(1)} %collective-permute-done.9.refs_8_.refs_6_), channel_id=1, source_target_pairs={{1,0},{2,3},{5,4},{6,7},{9,8},{10,11},{13,12},{14,15},{17,16},{18,... | collective-permute-start | bytes 1179656 | tf_op jit(solution)/shard_map/ppermute | solution.py:699
  40.8 10.2 %collective-permute-start.12 = (bf16[768,256]{1,0:T(8,128)(2,1)S(1)}, bf16[768,256]{1,0:T(8,128)(2,1)S(1)}, u32[]{:S(2)}, u32[]{:S(2)}) collective-permute-start(bf16[768,256]{1,0:T(8,128)(2,1)S(1)} %get-tuple-element.85), channel_id=1, source_target_pairs={{1,2},{2,1},{5,6},{6,5},{9,10},{10,9},{13,14},{14,13},{17,18},{18,... | collective-permute-start | bytes 1179656 | tf_op jit(solution)/shard_map/ppermute | solution.py:700
  51.4 10.7 %collective-permute-start.16 = (bf16[1792,256]{1,0:T(8,128)(2,1)S(1)}, bf16[1792,256]{1,0:T(8,128)(2,1)S(1)}, u32[]{:S(2)}, u32[]{:S(2)}) collective-permute-start(bf16[1792,256]{1,0:T(8,128)(2,1)S(1)} %get-tuple-element.92.refs_1_), channel_id=1, source_target_pairs={{0,16},{16,0},{1,17},{17,1},{2,18},{18,2},{3,19},{19,3},{4,20},{20... | collective-permute-start | bytes 2752520 | tf_op jit(solution)/shard_map/ppermute | solution.py:32
  51.9 10.2 %collective-permute-start.15 = (bf16[512,256]{1,0:T(8,128)(2,1)S(1)}, bf16[512,256]{1,0:T(8,128)(2,1)S(1)}, u32[]{:S(2)}, u32[]{:S(2)}) collective-permute-start(bf16[512,256]{1,0:T(8,128)(2,1)S(1)} %get-tuple-element.90), channel_id=1, source_target_pairs={{0,1},{1,0},{2,3},{3,2},{4,5},{5,4},{6,7},{7,6},{8,9},{9,8},{10,11... | collective-permute-start | bytes 786440 | tf_op jit(solution)/shard_map/ppermute | solution.py:32
  67.7 13.9 %collective-permute-start.21 = (bf16[8,128,1408]{2,1,0:T(8,128)(2,1)S(1)}, bf16[8,128,1408]{2,1,0:T(8,128)(2,1)S(1)}, u32[]{:S(2)}, u32[]{:S(2)}) collective-permute-start(bf16[8,128,1408]{2,1,0:T(8,128)(2,1)S(1)} %get-tuple-element.94.refs_4_.refs_2_), channel_id=1, source_target_pairs={{0,16},{16,0},{1,17},{17,1},{2,18},{18,2},{3,19},{19,3},{4,20},{20... | collective-permute-start | bytes 8650760 | tf_op jit(solution)/shard_map/ppermute | solution.py:32
  67.9 12.9 %collective-permute-start.18 = (bf16[256,256]{1,0:T(8,128)(2,1)S(1)}, bf16[256,256]{1,0:T(8,128)(2,1)S(1)}, u32[]{:S(2)}, u32[]{:S(2)}) collective-permute-start(bf16[256,256]{1,0:T(8,128)(2,1)S(1)} %get-tuple-element.93.refs_6_), channel_id=1, source_target_pairs={{0,2},{1,3},{2,0},{3,1},{4,6},{5,7},{6,4},{7,5},{8,10},{9,11},{10,... | collective-permute-start | bytes 393224 | tf_op jit(solution)/shard_map/ppermute | solution.py:32
  70.3 10.5 %collective-permute-start.19 = (bf16[256,256]{1,0:T(8,128)(2,1)S(1)}, bf16[256,256]{1,0:T(8,128)(2,1)S(1)}, u32[]{:S(2)}, u32[]{:S(2)}) collective-permute-start(bf16[256,256]{1,0:T(8,128)(2,1)S(1)} %get-tuple-element.93.refs_6_), channel_id=1, source_target_pairs={{0,3},{1,2},{2,1},{3,0},{4,7},{5,6},{6,5},{7,4},{8,11},{9,10},{10,... | collective-permute-start | bytes 393224 | tf_op jit(solution)/shard_map/ppermute | solution.py:32
  72.6 9.0 %collective-permute-start.20 = (bf16[256,256]{1,0:T(8,128)(2,1)S(1)}, bf16[256,256]{1,0:T(8,128)(2,1)S(1)}, u32[]{:S(2)}, u32[]{:S(2)}) collective-permute-start(bf16[256,256]{1,0:T(8,128)(2,1)S(1)} %get-tuple-element.93.refs_6_), channel_id=1, source_target_pairs={{0,1},{1,0},{2,3},{3,2},{4,5},{5,4},{6,7},{7,6},{8,9},{9,8},{10,11... | collective-permute-start | bytes 393224 | tf_op jit(solution)/shard_map/ppermute | solution.py:32
  82.4 13.5 %collective-permute-start.22 = (bf16[272,256]{1,0:T(8,128)(2,1)S(1)}, bf16[272,256]{1,0:T(8,128)(2,1)S(1)}, u32[]{:S(2)}, u32[]{:S(2)}) collective-permute-start(bf16[272,256]{1,0:T(8,128)(2,1)S(1)} %get-tuple-element.96), channel_id=1, source_target_pairs={{0,2},{1,3},{2,0},{3,1},{4,6},{5,7},{6,4},{7,5},{8,10},{9,11},{10,... | collective-permute-start | bytes 417800 | tf_op jit(solution)/shard_map/ppermute | solution.py:32
  85.0 10.9 %collective-permute-start.23 = (bf16[272,256]{1,0:T(8,128)(2,1)S(1)}, bf16[272,256]{1,0:T(8,128)(2,1)S(1)}, u32[]{:S(2)}, u32[]{:S(2)}) collective-permute-start(bf16[272,256]{1,0:T(8,128)(2,1)S(1)} %get-tuple-element.97), channel_id=1, source_target_pairs={{0,3},{1,2},{2,1},{3,0},{4,7},{5,6},{6,5},{7,4},{8,11},{9,10},{10,... | collective-permute-start | bytes 417800 | tf_op jit(solution)/shard_map/ppermute | solution.py:32
  86.9 9.1 %collective-permute-start.24 = (bf16[272,256]{1,0:T(8,128)(2,1)S(1)}, bf16[272,256]{1,0:T(8,128)(2,1)S(1)}, u32[]{:S(2)}, u32[]{:S(2)}) collective-permute-start(bf16[272,256]{1,0:T(8,128)(2,1)S(1)} %get-tuple-element.98), channel_id=1, source_target_pairs={{0,1},{1,0},{2,3},{3,2},{4,5},{5,4},{6,7},{7,6},{8,9},{9,8},{10,11... | collective-permute-start | bytes 417800 | tf_op jit(solution)/shard_map/ppermute | solution.py:32
  97.8 12.2 %collective-permute-start.25 = (bf16[272,256]{1,0:T(8,128)(2,1)S(1)}, bf16[272,256]{1,0:T(8,128)(2,1)S(1)}, u32[]{:S(2)}, u32[]{:S(2)}) collective-permute-start(bf16[272,256]{1,0:T(8,128)(2,1)S(1)} %get-tuple-element.111.refs_8_), channel_id=1, source_target_pairs={{0,2},{1,3},{2,0},{3,1},{4,6},{5,7},{6,4},{7,5},{8,10},{9,11},{10,... | collective-permute-start | bytes 417800 | tf_op jit(solution)/shard_map/ppermute | solution.py:32
  100.2 9.8 %collective-permute-start.26 = (bf16[272,256]{1,0:T(8,128)(2,1)S(1)}, bf16[272,256]{1,0:T(8,128)(2,1)S(1)}, u32[]{:S(2)}, u32[]{:S(2)}) collective-permute-start(bf16[272,256]{1,0:T(8,128)(2,1)S(1)} %get-tuple-element.111.refs_8_), channel_id=1, source_target_pairs={{0,3},{1,2},{2,1},{3,0},{4,7},{5,6},{6,5},{7,4},{8,11},{9,10},{10,... | collective-permute-start | bytes 417800 | tf_op jit(solution)/shard_map/ppermute | solution.py:32
  102.4 8.3 %collective-permute-start.27 = (bf16[272,256]{1,0:T(8,128)(2,1)S(1)}, bf16[272,256]{1,0:T(8,128)(2,1)S(1)}, u32[]{:S(2)}, u32[]{:S(2)}) collective-permute-start(bf16[272,256]{1,0:T(8,128)(2,1)S(1)} %get-tuple-element.111.refs_8_), channel_id=1, source_target_pairs={{0,1},{1,0},{2,3},{3,2},{4,5},{5,4},{6,7},{7,6},{8,9},{9,8},{10,11... | collective-permute-start | bytes 417800 | tf_op jit(solution)/shard_map/ppermute | solution.py:32
  111.7 12.9 %collective-permute-start.28 = (bf16[256,256]{1,0:T(8,128)(2,1)S(1)}, bf16[256,256]{1,0:T(8,128)(2,1)S(1)}, u32[]{:S(2)}, u32[]{:S(2)}) collective-permute-start(bf16[256,256]{1,0:T(8,128)(2,1)S(1)} %get-tuple-element.115), channel_id=1, source_target_pairs={{0,2},{1,3},{2,0},{3,1},{4,6},{5,7},{6,4},{7,5},{8,10},{9,11},{10,... | collective-permute-start | bytes 393224 | tf_op jit(solution)/shard_map/ppermute | solution.py:32
  114.2 10.4 %collective-permute-start.29 = (bf16[256,256]{1,0:T(8,128)(2,1)S(1)}, bf16[256,256]{1,0:T(8,128)(2,1)S(1)}, u32[]{:S(2)}, u32[]{:S(2)}) collective-permute-start(bf16[256,256]{1,0:T(8,128)(2,1)S(1)} %get-tuple-element.116), channel_id=1, source_target_pairs={{0,3},{1,2},{2,1},{3,0},{4,7},{5,6},{6,5},{7,4},{8,11},{9,10},{10,... | collective-permute-start | bytes 393224 | tf_op jit(solution)/shard_map/ppermute | solution.py:32
  115.4 10.1 %collective-permute-start.30 = (bf16[256,256]{1,0:T(8,128)(2,1)S(1)}, bf16[256,256]{1,0:T(8,128)(2,1)S(1)}, u32[]{:S(2)}, u32[]{:S(2)}) collective-permute-start(bf16[256,256]{1,0:T(8,128)(2,1)S(1)} %get-tuple-element.117), channel_id=1, source_target_pairs={{0,1},{1,0},{2,3},{3,2},{4,5},{5,4},{6,7},{7,6},{8,9},{9,8},{10,11... | collective-permute-start | bytes 393224 | tf_op jit(solution)/shard_map/ppermute | solution.py:32
  115.5 11.3 %collective-permute-start.32 = (bf16[240,256]{1,0:T(8,128)(2,1)S(1)}, bf16[240,256]{1,0:T(8,128)(2,1)S(1)}, u32[]{:S(2)}, u32[]{:S(2)}) collective-permute-start(bf16[240,256]{1,0:T(8,128)(2,1)S(1)} %get-tuple-element.120.refs_0_), channel_id=1, source_target_pairs={{0,4},{4,0},{8,12},{12,8},{1,5},{5,1},{9,13},{13,9},{2,6},{6,2},{1... | collective-permute-start | bytes 368648 | tf_op jit(solution)/shard_map/ppermute | solution.py:32
  116.1 10.7 %collective-permute-start.33 = (bf16[240,256]{1,0:T(8,128)(2,1)S(1)}, bf16[240,256]{1,0:T(8,128)(2,1)S(1)}, u32[]{:S(2)}, u32[]{:S(2)}) collective-permute-start(bf16[240,256]{1,0:T(8,128)(2,1)S(1)} %get-tuple-element.121.refs_1_), channel_id=1, source_target_pairs={{0,8},{4,12},{8,0},{12,4},{1,9},{5,13},{9,1},{13,5},{2,10},{6,14},... | collective-permute-start | bytes 368648 | tf_op jit(solution)/shard_map/ppermute | solution.py:32
  130.1 12.6 %collective-permute-start.36 = (bf16[896,256]{1,0:T(8,128)(2,1)S(1)}, bf16[896,256]{1,0:T(8,128)(2,1)S(1)}, u32[]{:S(2)}, u32[]{:S(2)}) collective-permute-start(bf16[896,256]{1,0:T(8,128)(2,1)S(1)} %pad_maximum_fusion.1), channel_id=1, source_target_pairs={{0,8},{4,12},{8,0},{12,4},{1,9},{5,13},{9,1},{13,5},{2,10},{6,14},... | collective-permute-start | bytes 1376264 | tf_op jit(solution)/shard_map/ppermute | solution.py:32
  130.7 12.3 %collective-permute-start.35 = (bf16[896,256]{1,0:T(8,128)(2,1)S(1)}, bf16[896,256]{1,0:T(8,128)(2,1)S(1)}, u32[]{:S(2)}, u32[]{:S(2)}) collective-permute-start(bf16[896,256]{1,0:T(8,128)(2,1)S(1)} %pad_maximum_fusion), channel_id=1, source_target_pairs={{0,4},{4,0},{8,12},{12,8},{1,5},{5,1},{9,13},{13,9},{2,6},{6,2},{1... | collective-permute-start | bytes 1376264 | tf_op jit(solution)/shard_map/ppermute | solution.py:32
  143.3 8.9 %collective-permute-start.38 = (bf16[656,256]{1,0:T(8,128)(2,1)S(1)}, bf16[656,256]{1,0:T(8,128)(2,1)S(1)}, u32[]{:S(2)}, u32[]{:S(2)}) collective-permute-start(bf16[656,256]{1,0:T(8,128)(2,1)S(1)} %pad_maximum_fusion.3), channel_id=1, source_target_pairs={{0,4},{4,0},{8,12},{12,8},{1,5},{5,1},{9,13},{13,9},{2,6},{6,2},{1... | collective-permute-start | bytes 1007624 | tf_op jit(solution)/shard_map/ppermute | solution.py:32
  144.0 8.6 %collective-permute-start.37 = (bf16[656,256]{1,0:T(8,128)(2,1)S(1)}, bf16[656,256]{1,0:T(8,128)(2,1)S(1)}, u32[]{:S(2)}, u32[]{:S(2)}) collective-permute-start(bf16[656,256]{1,0:T(8,128)(2,1)S(1)} %pad_maximum_fusion.2), channel_id=1, source_target_pairs={{0,8},{4,12},{8,0},{12,4},{1,9},{5,13},{9,1},{13,5},{2,10},{6,14},... | collective-permute-start | bytes 1007624 | tf_op jit(solution)/shard_map/ppermute | solution.py:32
  (24 other events, 207.1 us)

commit v6 on v5

--- a/solution.py
+++ b/solution.py
@@ -145,52 +145,31 @@
     return jnp.concatenate([value[:, i : i + feats] for i in range(0, cols, feats)], axis=0)
 
 
-def share_body(n, up_ref, down_ref, wq_own, wq_other, rows_ref, *refs):
-    outs, own_ref, sems = refs[:n], refs[n], refs[n + 1]
+def share_body(up_ref, down_ref, rows_ref, out_ref, own_ref):
+    s = lax.axis_index("section")
+    place = s * lax.axis_size("dp") + lax.axis_index("dp")
+    tall = out_ref.shape[0] // 2
+    cols = pl.ds(pl.multiple_of(place * HEAD, HEAD), HEAD)
+    out_ref[:tall, :] = up_ref[pl.ds(pl.multiple_of(place * tall, 16), tall), :]
+    for side in range(2):
+        there = slice(side * HEAD, (side + 1) * HEAD)
+        out_ref[tall:, there] = down_ref[side * tall : (side + 1) * tall, cols]
+    own_ref[...] = pack(rows_ref[s], own_ref.shape[1])
+
+
+def messages_body(n, share_ref, own_ref, wq_own, wq_other, *outs):
     s, m = lax.axis_index("section"), lax.axis_index("mp")
     place = s * lax.axis_size("dp") + lax.axis_index("dp")
     parts = 2 * lax.axis_size("dp")
-    tall = up_ref.shape[0] // parts
+    above = share_ref.shape[0]
     share = wq_own.shape[0] // (n * parts)
-    rows = pl.ds(pl.multiple_of(place * tall, 16), tall)
-    cols = pl.ds(pl.multiple_of(place * HEAD, HEAD), HEAD)
-    copies = [pltpu.make_async_copy(up_ref.at[rows], outs[0].at[pl.ds(0, tall)], sems.at[0])]
-    for side in range(2):
-        copies.append(
-            pltpu.make_async_copy(
-                down_ref.at[pl.ds(side * tall, tall), cols],
-                outs[0].at[pl.ds(tall, tall), pl.ds(side * HEAD, HEAD)],
-                sems.at[1 + side],
-            )
-        )
-    for copy in copies:
-        copy.start()
     for i, d in enumerate(places(n)):
+        outs[i][:above, :] = share_ref[...]
         start = ((m ^ d) * parts + place) * share
         here = pl.ds(pl.multiple_of(start, share), share)
-        target = outs[i].at[pl.ds(2 * tall, share)]
-        copies.append(pltpu.make_async_copy(wq_own.at[here], target, sems.at[3 + i]))
-
-        @pl.when(s == 1)
-        def _(here=here, target=target, i=i):
-            pltpu.make_async_copy(wq_own.at[here], target, sems.at[3 + i]).start()
-
-        @pl.when(s != 1)
-        def _(here=here, target=target, i=i):
-            pltpu.make_async_copy(wq_other.at[here], target, sems.at[3 + i]).start()
-
-    total, length = rows_ref.shape[1], own_ref.shape[1]
-    for i in range(own_ref.shape[0] // total):
-        source = rows_ref.at[s, :, pl.ds(i * length, length)]
-        target = own_ref.at[pl.ds(i * total, total)]
-        copies.append(pltpu.make_async_copy(source, target, sems.at[3 + n + i]))
-        copies[-1].start()
-    for copy in copies:
-        copy.wait()
+        outs[i][above : above + share, :] = of_layer(1, wq_own, wq_other, here, slice(None))
     half = own_ref.shape[0] // 2
-    outs[n - 1][2 * tall + share :, :] = own_ref[:half, :]
-    for i in range(1, n):
-        outs[i][: 2 * tall, :] = outs[0][: 2 * tall, :]
+    outs[n - 1][above + share :, :] = own_ref[:half, :]
 
 
 def line_body(n, tall, *refs):
@@ -663,13 +642,12 @@
         messages = [shape((2 * up_rows + feats // parts, 2 * down_cols))] * (n - 1)
         rest = own_shape.shape[0] // 2
         longer = shape((messages[0].shape[0] + rest, cols))
-        *messages, own = call(
-            functools.partial(share_body, n),
-            messages + [longer, own_shape],
-            [hbm()] * 5,
-            [pltpu.SemaphoreType.DMA((3 + n + feats // cols,))],
-            limit=FIRST_LIMIT,
-        )(enc_up, down_t, *wqs, segment_input[:, 0])
+        share, own = call(
+            share_body, [shape((2 * up_rows, 2 * down_cols)), own_shape], [vm()] * 3
+        )(enc_up, down_t, segment_input[:, 0])
+        messages = call(
+            functools.partial(messages_body, n), messages + [longer], [vm()] * 4
+        )(share, own, *wqs)
         line = scattered(messages)
         *grads, far_grads = call(
             functools.partial(out_grads_body, n),

time: 156 us -> 153 us (0.981)
  waiting for transfers between devices: 82.6 us -> 79.2 us
  local copies, waits for them, and re-layouts: 1.3 us -> 3.5 us
  Pallas kernels: 26.8 us -> 24.7 us
    ppermute x37, waiting for transfers between devices: 73.8 us -> 70.7 us  [xor_move(): return lax.ppermute(value, axis, [(i, i ^ by) for i in range(count)])]
    unnamed x36 -> x34, local copies, waits for them, and re-layouts: 1.15 us -> 3.35 us
    pallas_call x25 -> x26, Pallas kernels: 26.8 us -> 24.7 us  [run(): pl.pallas_call(kernel, out_shape=list(outs) + [shape(x.shape, x.dtype) fo...]
  transfers between devices with their start and end apart: 40 -> 40, of which waited for: 24 -> 23; matrix products, arithmetic and copies ran while one was open for 0% -> 0% of each run, Pallas kernels for 12% -> 11%
where the time goes in v6:
time: 153 us
  waiting for transfers between devices  79.2 us (52%)
  starting transfers between devices  42.8 us (28%)
  Pallas kernels  24.7 us (16%)
  local copies, waits for them, and re-layouts  3.5 us (2%)
    ppermute x37, waiting for transfers between devices, xor_move(): return lax.ppermute(value, axis, [(i, i ^ by) for i in range(count)])  70.7 us
    ppermute x37, starting transfers between devices, xor_move(): return lax.ppermute(value, axis, [(i, i ^ by) for i in range(count)])  40.1 us
    pallas_call x26, Pallas kernels, run(): pl.pallas_call(kernel, out_shape=list(outs) + [shape(x.shape, x.dtype) fo...  24.7 us
    ppermute x1, waiting for transfers between devices, on_device(): next_outer = lax.ppermute(far_inner, 'mp', outer)  8.48 us
    unnamed x34, local copies, waits for them, and re-layouts  3.35 us
  transfers between devices with their start and end apart: 40, of which 23 were waited for; matrix products, arithmetic and copies ran while one was open for 0% of the time, Pallas kernels for 11%

profile of v6, /device:TPU:0, one launch (start us, length us, event | category | flops | bytes accessed | tf_op | source)
XLA Modules:
  0.0 152.6 jit_solution(1929188291389010971)
XLA Ops:
  4.6 3.1 %collective-permute-start.5 = (bf16[544,256]{1,0:T(8,128)(2,1)S(1)}, bf16[544,256]{1,0:T(8,128)(2,1)S(1)}, u32[]{:S(2)}, u32[]{:S(2)}) collective-permute-start(bf16[544,256]{1,0:T(8,128)(2,1)S(1)} %get-tuple-element.76), channel_id=1, source_target_pairs={{0,1},{1,0},{2,3},{3,2},{4,5},{5,4},{6,7},{7,6},{8,9},{9,8},{10,11... | collective-permute-start | bytes 835592 | tf_op jit(solution)/shard_map/ppermute | solution.py:32
  7.7 2.6 %collective-permute-start.3 = (bf16[288,256]{1,0:T(8,128)(2,1)S(1)}, bf16[288,256]{1,0:T(8,128)(2,1)S(1)}, u32[]{:S(2)}, u32[]{:S(2)}) collective-permute-start(bf16[288,256]{1,0:T(8,128)(2,1)S(1)} %get-tuple-element.74), channel_id=1, source_target_pairs={{0,2},{1,3},{2,0},{3,1},{4,6},{5,7},{6,4},{7,5},{8,10},{9,11},{10,... | collective-permute-start | bytes 442376 | tf_op jit(solution)/shard_map/ppermute | solution.py:32
  11.5 6.5 %collective-permute-done.3.refs_1_ = bf16[288,256]{1,0:T(8,128)(2,1)S(1)} collective-permute-done((bf16[288,256]{1,0:T(8,128)(2,1)S(1)}, bf16[288,256]{1,0:T(8,128)(2,1)S(1)}, u32[]{:S(2)}, u32[]{:S(2)}) %collective-permute-start.3) | collective-permute-done | bytes 147488 | tf_op jit(solution)/shard_map/ppermute | solution.py:32
  18.0 5.1 %collective-permute-done.4.refs_2_ = bf16[288,256]{1,0:T(8,128)(2,1)S(1)} collective-permute-done((bf16[288,256]{1,0:T(8,128)(2,1)S(1)}, bf16[288,256]{1,0:T(8,128)(2,1)S(1)}, u32[]{:S(2)}, u32[]{:S(2)}) %collective-permute-start.4) | collective-permute-done | bytes 147488 | tf_op jit(solution)/shard_map/ppermute | solution.py:32
  24.9 1.6 %collective-permute-start.6 = (bf16[3,144,256]{2,1,0:T(8,128)(2,1)S(1)}, bf16[3,144,256]{2,1,0:T(8,128)(2,1)S(1)}, u32[]{:S(2)}, u32[]{:S(2)}) collective-permute-start(bf16[3,144,256]{2,1,0:T(8,128)(2,1)S(1)} %get-tuple-element.78.refs_0_), channel_id=1, source_target_pairs={{0,4},{4,0},{8,12},{12,8},{1,5},{5,1},{9,13},{13,9},{2,6},{6,2},{1... | collective-permute-start | bytes 663560 | tf_op jit(solution)/shard_map/ppermute | solution.py:32
  26.5 1.5 collective-permute-start.7
  28.0 2.9 %collective-permute-done.6.refs_1_ = bf16[3,144,256]{2,1,0:T(8,128)(2,1)S(1)} collective-permute-done((bf16[3,144,256]{2,1,0:T(8,128)(2,1)S(1)}, bf16[3,144,256]{2,1,0:T(8,128)(2,1)S(1)}, u32[]{:S(2)}, u32[]{:S(2)}) %collective-permute-start.6) | collective-permute-done | bytes 221216 | tf_op jit(solution)/shard_map/ppermute | solution.py:32
  30.9 1.5 collective-permute-done.7.refs_3_.refs_4_
  33.5 1.6 %collective-permute-start.10 = (bf16[2,3,144,256]{3,2,1,0:T(8,128)(2,1)S(1)}, bf16[2,3,144,256]{3,2,1,0:T(8,128)(2,1)S(1)}, u32[]{:S(2)}, u32[]{:S(2)}) collective-permute-start(bf16[2,3,144,256]{3,2,1,0:T(8,128)(2,1)S(1)} %get-tuple-element.85), channel_id=1, source_target_pairs={{0,8},{4,12},{8,0},{12,4},{1,9},{5,13},{9,1},{13,5},{2,10},{6,14},... | collective-permute-start | bytes 1327112 | tf_op jit(solution)/shard_map/ppermute | solution.py:32
  35.1 1.5 collective-permute-start.11
  36.6 1.3 collective-permute-start.13
  39.3 8.5 %collective-permute-done.13.refs_10_.refs_7_ = bf16[768,256]{1,0:T(8,128)(2,1)S(1)} collective-permute-done((bf16[768,256]{1,0:T(8,128)(2,1)S(1)}, bf16[768,256]{1,0:T(8,128)(2,1)S(1)}, u32[]{:S(2)}, u32[]{:S(2)}) %collective-permute-start.13) | collective-permute-done | bytes 393248 | tf_op jit(solution)/shard_map/ppermute | solution.py:677
  48.7 3.7 %collective-permute-start.15 = (bf16[512,256]{1,0:T(8,128)(2,1)S(1)}, bf16[512,256]{1,0:T(8,128)(2,1)S(1)}, u32[]{:S(2)}, u32[]{:S(2)}) collective-permute-start(bf16[512,256]{1,0:T(8,128)(2,1)S(1)} %get-tuple-element.92), channel_id=1, source_target_pairs={{0,1},{1,0},{2,3},{3,2},{4,5},{5,4},{6,7},{7,6},{8,9},{9,8},{10,11... | collective-permute-start | bytes 786440 | tf_op jit(solution)/shard_map/ppermute | solution.py:32
  52.4 5.6 %shard_map.147 = (bf16[1024,896]{1,0:T(8,128)(2,1)S(1)}, bf16[4,512,256]{2,1,0:T(8,128)(2,1)S(1)}) custom-call(bf16[1024,896]{1,0:T(8,128)(2,1)S(1)} %bitcast.24, bf16[1024,896]{1,0:T(8,128)(2,1)S(1)} %shard_map.141.refs_11_.refs_1_, bf16[8,3,144,256]{3,2,1,0:T(8,128)(2,1)S(1)} %get-tuple-element.89.refs_2_, ...), custom_call_target="tpu_custom_call" | custom-call | flops 3758096 | bytes 2883 | tf_op jit(solution)/shard_map/pallas_call | solution.py:70
  62.9 1.6 %shard_map.151 = (bf16[256,256]{1,0:T(8,128)(2,1)S(1)}, f32[8,64,512]{2,1,0:T(8,128)S(1)}, bf16[2048,512]{1,0:T(8,128)(2,1)S(1)}, bf16[8,128,1408]{2,1,0:T(8,128)(2,1)S(1)}) custom-call(s32[2,4,4]{2,1,0:T(4,128)S(1)} %bitcast.36, s32[2,4]{1,0:T(2,128)S(1)} %bitcast.39, ...), custom_call_target="tpu_custom_call", output_to_operand_aliasing={{3}: (5, {})} | custom-call | flops 134217 | bytes 3276 | tf_op jit(solution)/shard_map/pallas_call | solution.py:70
  64.8 2.4 %collective-permute-start.18 = (bf16[256,256]{1,0:T(8,128)(2,1)S(1)}, bf16[256,256]{1,0:T(8,128)(2,1)S(1)}, u32[]{:S(2)}, u32[]{:S(2)}) collective-permute-start(bf16[256,256]{1,0:T(8,128)(2,1)S(1)} %get-tuple-element.95.refs_6_), channel_id=1, source_target_pairs={{0,2},{1,3},{2,0},{3,1},{4,6},{5,7},{6,4},{7,5},{8,10},{9,11},{10,... | collective-permute-start | bytes 393224 | tf_op jit(solution)/shard_map/ppermute | solution.py:32
  67.2 2.2 %collective-permute-start.19 = (bf16[256,256]{1,0:T(8,128)(2,1)S(1)}, bf16[256,256]{1,0:T(8,128)(2,1)S(1)}, u32[]{:S(2)}, u32[]{:S(2)}) collective-permute-start(bf16[256,256]{1,0:T(8,128)(2,1)S(1)} %get-tuple-element.95.refs_6_), channel_id=1, source_target_pairs={{0,3},{1,2},{2,1},{3,0},{4,7},{5,6},{6,5},{7,4},{8,11},{9,10},{10,... | collective-permute-start | bytes 393224 | tf_op jit(solution)/shard_map/ppermute | solution.py:32
  69.4 8.3 %collective-permute-done.18.refs_7_ = bf16[256,256]{1,0:T(8,128)(2,1)S(1)} collective-permute-done((bf16[256,256]{1,0:T(8,128)(2,1)S(1)}, bf16[256,256]{1,0:T(8,128)(2,1)S(1)}, u32[]{:S(2)}, u32[]{:S(2)}) %collective-permute-start.18) | collective-permute-done | bytes 131104 | tf_op jit(solution)/shard_map/ppermute | solution.py:32
  79.2 2.6 %collective-permute-start.22 = (bf16[272,256]{1,0:T(8,128)(2,1)S(1)}, bf16[272,256]{1,0:T(8,128)(2,1)S(1)}, u32[]{:S(2)}, u32[]{:S(2)}) collective-permute-start(bf16[272,256]{1,0:T(8,128)(2,1)S(1)} %get-tuple-element.98), channel_id=1, source_target_pairs={{0,2},{1,3},{2,0},{3,1},{4,6},{5,7},{6,4},{7,5},{8,10},{9,11},{10,... | collective-permute-start | bytes 417800 | tf_op jit(solution)/shard_map/ppermute | solution.py:32
  81.9 1.9 %collective-permute-start.23 = (bf16[272,256]{1,0:T(8,128)(2,1)S(1)}, bf16[272,256]{1,0:T(8,128)(2,1)S(1)}, u32[]{:S(2)}, u32[]{:S(2)}) collective-permute-start(bf16[272,256]{1,0:T(8,128)(2,1)S(1)} %get-tuple-element.99), channel_id=1, source_target_pairs={{0,3},{1,2},{2,1},{3,0},{4,7},{5,6},{6,5},{7,4},{8,11},{9,10},{10,... | collective-permute-start | bytes 417800 | tf_op jit(solution)/shard_map/ppermute | solution.py:32
  85.0 7.8 %collective-permute-done.22.refs_2_ = bf16[272,256]{1,0:T(8,128)(2,1)S(1)} collective-permute-done((bf16[272,256]{1,0:T(8,128)(2,1)S(1)}, bf16[272,256]{1,0:T(8,128)(2,1)S(1)}, u32[]{:S(2)}, u32[]{:S(2)}) %collective-permute-start.22) | collective-permute-done | bytes 139296 | tf_op jit(solution)/shard_map/ppermute | solution.py:32
  92.8 1.8 %shard_map.154 = (bf16[272,256]{1,0:T(8,128)(2,1)S(1)}, f32[256,128]{1,0:T(8,128)S(1)}, bf16[256,256]{1,0:T(8,128)(2,1)S(1)}, bf16[8,64,512]{2,1,0:T(8,128)(2,1)S(1)}, bf16[8,64,512]{2,1,0:T(8,128)(2,1)S(1)}) custom-call(s32[2,4]{1,0:T(2,128)S(1)} %bitcast.40, bf16[272,256]{1,0:T(8,128)(2,1)S(1)} %get-tuple-element.97.refs_1_, ...), custom_call_target="tpu_custom_call" | custom-call | flops 201326 | bytes 1449 | tf_op jit(solution)/shard_map/pallas_call | solution.py:70
  94.6 2.4 %collective-permute-start.25 = (bf16[272,256]{1,0:T(8,128)(2,1)S(1)}, bf16[272,256]{1,0:T(8,128)(2,1)S(1)}, u32[]{:S(2)}, u32[]{:S(2)}) collective-permute-start(bf16[272,256]{1,0:T(8,128)(2,1)S(1)} %get-tuple-element.113.refs_8_), channel_id=1, source_target_pairs={{0,2},{1,3},{2,0},{3,1},{4,6},{5,7},{6,4},{7,5},{8,10},{9,11},{10,... | collective-permute-start | bytes 417800 | tf_op jit(solution)/shard_map/ppermute | solution.py:32
  97.0 2.2 %collective-permute-start.26 = (bf16[272,256]{1,0:T(8,128)(2,1)S(1)}, bf16[272,256]{1,0:T(8,128)(2,1)S(1)}, u32[]{:S(2)}, u32[]{:S(2)}) collective-permute-start(bf16[272,256]{1,0:T(8,128)(2,1)S(1)} %get-tuple-element.113.refs_8_), channel_id=1, source_target_pairs={{0,3},{1,2},{2,1},{3,0},{4,7},{5,6},{6,5},{7,4},{8,11},{9,10},{10,... | collective-permute-start | bytes 417800 | tf_op jit(solution)/shard_map/ppermute | solution.py:32
  100.2 2.8 %shard_map.156 = (bf16[896,2048]{1,0:T(8,128)(2,1)S(1)}, bf16[896,256]{1,0:T(8,128)(2,1)S(1)}, bf16[896,256]{1,0:T(8,128)(2,1)S(1)}) custom-call(s32[2,4,4]{2,1,0:T(4,128)S(1)} %bitcast.38, bf16[2048,512]{1,0:T(8,128)(2,1)S(1)} %shard_map.155.refs_1_, bf16[8,128,1408]{2,1,0:T(8,128)(2,1)S(1)} %get-tuple-element.96.refs_4_.refs_2_, ...), custom_call_target="tpu_custom_call" | custom-call | flops 1879048 | bytes 4587 | tf_op jit(solution)/shard_map/pallas_call | solution.py:70
  102.9 3.8 %collective-permute-done.25.refs_9_ = bf16[272,256]{1,0:T(8,128)(2,1)S(1)} collective-permute-done((bf16[272,256]{1,0:T(8,128)(2,1)S(1)}, bf16[272,256]{1,0:T(8,128)(2,1)S(1)}, u32[]{:S(2)}, u32[]{:S(2)}) %collective-permute-start.25) | collective-permute-done | bytes 139296 | tf_op jit(solution)/shard_map/ppermute | solution.py:32
  108.5 2.5 %collective-permute-start.28 = (bf16[256,256]{1,0:T(8,128)(2,1)S(1)}, bf16[256,256]{1,0:T(8,128)(2,1)S(1)}, u32[]{:S(2)}, u32[]{:S(2)}) collective-permute-start(bf16[256,256]{1,0:T(8,128)(2,1)S(1)} %get-tuple-element.117), channel_id=1, source_target_pairs={{0,2},{1,3},{2,0},{3,1},{4,6},{5,7},{6,4},{7,5},{8,10},{9,11},{10,... | collective-permute-start | bytes 393224 | tf_op jit(solution)/shard_map/ppermute | solution.py:32
  113.4 8.0 %collective-permute-done.28.refs_4_ = bf16[256,256]{1,0:T(8,128)(2,1)S(1)} collective-permute-done((bf16[256,256]{1,0:T(8,128)(2,1)S(1)}, bf16[256,256]{1,0:T(8,128)(2,1)S(1)}, u32[]{:S(2)}, u32[]{:S(2)}) %collective-permute-start.28) | collective-permute-done | bytes 131104 | tf_op jit(solution)/shard_map/ppermute | solution.py:32
  128.0 11.4 %collective-permute-done.36 = bf16[896,256]{1,0:T(8,128)(2,1)S(1)} collective-permute-done((bf16[896,256]{1,0:T(8,128)(2,1)S(1)}, bf16[896,256]{1,0:T(8,128)(2,1)S(1)}, u32[]{:S(2)}, u32[]{:S(2)}) %collective-permute-start.36) | collective-permute-done | bytes 458784 | tf_op jit(solution)/shard_map/ppermute | solution.py:32
  140.7 1.5 %collective-permute-start.37 = (bf16[656,256]{1,0:T(8,128)(2,1)S(1)}, bf16[656,256]{1,0:T(8,128)(2,1)S(1)}, u32[]{:S(2)}, u32[]{:S(2)}) collective-permute-start(bf16[656,256]{1,0:T(8,128)(2,1)S(1)} %pad_maximum_fusion.2), channel_id=1, source_target_pairs={{0,8},{4,12},{8,0},{12,4},{1,9},{5,13},{9,1},{13,5},{2,10},{6,14},... | collective-permute-start | bytes 1007624 | tf_op jit(solution)/shard_map/ppermute | solution.py:32
  142.3 6.7 %collective-permute-done.38 = bf16[656,256]{1,0:T(8,128)(2,1)S(1)} collective-permute-done((bf16[656,256]{1,0:T(8,128)(2,1)S(1)}, bf16[656,256]{1,0:T(8,128)(2,1)S(1)}, u32[]{:S(2)}, u32[]{:S(2)}) %collective-permute-start.38) | collective-permute-done | bytes 335904 | tf_op jit(solution)/shard_map/ppermute | solution.py:32
  149.8 1.8 %collective-permute-done.39 = bf16[896,256]{1,0:T(8,128)(2,1)S(1)} collective-permute-done((bf16[896,256]{1,0:T(8,128)(2,1)S(1)}, bf16[896,256]{1,0:T(8,128)(2,1)S(1)}, u32[]{:S(2)}, u32[]{:S(2)}) %collective-permute-start.39) | collective-permute-done | bytes 458784 | tf_op jit(solution)/shard_map/ppermute | solution.py:32
  (127 shorter events, 32.8 us)
Async XLA Ops:
  1.2 9.1 %collective-permute-start.1 = (bf16[1024,512]{1,0:T(8,128)(2,1)}, bf16[1024,512]{1,0:T(8,128)(2,1)S(1)}, u32[]{:S(2)}, u32[]{:S(2)}) collective-permute-start(bf16[1024,512]{1,0:T(8,128)(2,1)} %bitcast.19), channel_id=1, source_target_pairs={{0,16},{16,0},{1,17},{17,1},{2,18},{18,2},{3,19},{19,3},{4,20},{20... | collective-permute-start | bytes 3145736 | tf_op jit(solution)/shard_map/ppermute | solution.py:32
  4.6 18.4 %collective-permute-start.5 = (bf16[544,256]{1,0:T(8,128)(2,1)S(1)}, bf16[544,256]{1,0:T(8,128)(2,1)S(1)}, u32[]{:S(2)}, u32[]{:S(2)}) collective-permute-start(bf16[544,256]{1,0:T(8,128)(2,1)S(1)} %get-tuple-element.76), channel_id=1, source_target_pairs={{0,1},{1,0},{2,3},{3,2},{4,5},{5,4},{6,7},{7,6},{8,9},{9,8},{10,11... | collective-permute-start | bytes 835592 | tf_op jit(solution)/shard_map/ppermute | solution.py:32
  7.7 10.3 %collective-permute-start.3 = (bf16[288,256]{1,0:T(8,128)(2,1)S(1)}, bf16[288,256]{1,0:T(8,128)(2,1)S(1)}, u32[]{:S(2)}, u32[]{:S(2)}) collective-permute-start(bf16[288,256]{1,0:T(8,128)(2,1)S(1)} %get-tuple-element.74), channel_id=1, source_target_pairs={{0,2},{1,3},{2,0},{3,1},{4,6},{5,7},{6,4},{7,5},{8,10},{9,11},{10,... | collective-permute-start | bytes 442376 | tf_op jit(solution)/shard_map/ppermute | solution.py:32
  10.3 12.8 %collective-permute-start.4 = (bf16[288,256]{1,0:T(8,128)(2,1)S(1)}, bf16[288,256]{1,0:T(8,128)(2,1)S(1)}, u32[]{:S(2)}, u32[]{:S(2)}) collective-permute-start(bf16[288,256]{1,0:T(8,128)(2,1)S(1)} %get-tuple-element.75), channel_id=1, source_target_pairs={{0,3},{1,2},{2,1},{3,0},{4,7},{5,6},{6,5},{7,4},{8,11},{9,10},{10,... | collective-permute-start | bytes 442376 | tf_op jit(solution)/shard_map/ppermute | solution.py:32
  23.1 10.2 %collective-permute-start.8 = (bf16[784,256]{1,0:T(8,128)(2,1)S(1)}, bf16[784,256]{1,0:T(8,128)(2,1)S(1)}, u32[]{:S(2)}, u32[]{:S(2)}) collective-permute-start(bf16[784,256]{1,0:T(8,128)(2,1)S(1)} %get-tuple-element.81), channel_id=1, source_target_pairs={{0,1},{1,0},{2,3},{3,2},{4,5},{5,4},{6,7},{7,6},{8,9},{9,8},{10,11... | collective-permute-start | bytes 1204232 | tf_op jit(solution)/shard_map/ppermute | solution.py:32
  24.2 8.2 %collective-permute-start.9 = (bf16[768,256]{1,0:T(8,128)(2,1)S(1)}, bf16[768,256]{1,0:T(8,128)(2,1)S(1)}, u32[]{:S(2)}, u32[]{:S(2)}) collective-permute-start(bf16[768,256]{1,0:T(8,128)(2,1)S(1)} %get-tuple-element.84), channel_id=1, source_target_pairs={{1,2},{2,1},{5,6},{6,5},{9,10},{10,9},{13,14},{14,13},{17,18},{18,... | collective-permute-start | bytes 1179656 | tf_op jit(solution)/shard_map/ppermute | solution.py:668
  24.9 6.0 %collective-permute-start.6 = (bf16[3,144,256]{2,1,0:T(8,128)(2,1)S(1)}, bf16[3,144,256]{2,1,0:T(8,128)(2,1)S(1)}, u32[]{:S(2)}, u32[]{:S(2)}) collective-permute-start(bf16[3,144,256]{2,1,0:T(8,128)(2,1)S(1)} %get-tuple-element.78.refs_0_), channel_id=1, source_target_pairs={{0,4},{4,0},{8,12},{12,8},{1,5},{5,1},{9,13},{13,9},{2,6},{6,2},{1... | collective-permute-start | bytes 663560 | tf_op jit(solution)/shard_map/ppermute | solution.py:32
  33.5 14.3 %collective-permute-start.10 = (bf16[2,3,144,256]{3,2,1,0:T(8,128)(2,1)S(1)}, bf16[2,3,144,256]{3,2,1,0:T(8,128)(2,1)S(1)}, u32[]{:S(2)}, u32[]{:S(2)}) collective-permute-start(bf16[2,3,144,256]{3,2,1,0:T(8,128)(2,1)S(1)} %get-tuple-element.85), channel_id=1, source_target_pairs={{0,8},{4,12},{8,0},{12,4},{1,9},{5,13},{9,1},{13,5},{2,10},{6,14},... | collective-permute-start | bytes 1327112 | tf_op jit(solution)/shard_map/ppermute | solution.py:32
  35.1 12.7 %collective-permute-start.11 = (bf16[2,3,144,256]{3,2,1,0:T(8,128)(2,1)S(1)}, bf16[2,3,144,256]{3,2,1,0:T(8,128)(2,1)S(1)}, u32[]{:S(2)}, u32[]{:S(2)}) collective-permute-start(bf16[2,3,144,256]{3,2,1,0:T(8,128)(2,1)S(1)} %get-tuple-element.86), channel_id=1, source_target_pairs={{0,4},{4,0},{8,12},{12,8},{1,5},{5,1},{9,13},{13,9},{2,6},{6,2},{1... | collective-permute-start | bytes 1327112 | tf_op jit(solution)/shard_map/ppermute | solution.py:32
  36.6 11.2 %collective-permute-start.13 = (bf16[768,256]{1,0:T(8,128)(2,1)S(1)}, bf16[768,256]{1,0:T(8,128)(2,1)S(1)}, u32[]{:S(2)}, u32[]{:S(2)}) collective-permute-start(bf16[768,256]{1,0:T(8,128)(2,1)S(1)} %collective-permute-done.9.refs_8_.refs_6_), channel_id=1, source_target_pairs={{1,0},{2,3},{5,4},{6,7},{9,8},{10,11},{13,12},{14,15},{17,16},{18,... | collective-permute-start | bytes 1179656 | tf_op jit(solution)/shard_map/ppermute | solution.py:677
  37.9 9.9 %collective-permute-start.12 = (bf16[768,256]{1,0:T(8,128)(2,1)S(1)}, bf16[768,256]{1,0:T(8,128)(2,1)S(1)}, u32[]{:S(2)}, u32[]{:S(2)}) collective-permute-start(bf16[768,256]{1,0:T(8,128)(2,1)S(1)} %get-tuple-element.87), channel_id=1, source_target_pairs={{1,2},{2,1},{5,6},{6,5},{9,10},{10,9},{13,14},{14,13},{17,18},{18,... | collective-permute-start | bytes 1179656 | tf_op jit(solution)/shard_map/ppermute | solution.py:678
  48.2 10.7 %collective-permute-start.16 = (bf16[1792,256]{1,0:T(8,128)(2,1)S(1)}, bf16[1792,256]{1,0:T(8,128)(2,1)S(1)}, u32[]{:S(2)}, u32[]{:S(2)}) collective-permute-start(bf16[1792,256]{1,0:T(8,128)(2,1)S(1)} %get-tuple-element.94.refs_1_), channel_id=1, source_target_pairs={{0,16},{16,0},{1,17},{17,1},{2,18},{18,2},{3,19},{19,3},{4,20},{20... | collective-permute-start | bytes 2752520 | tf_op jit(solution)/shard_map/ppermute | solution.py:32
  48.7 10.2 %collective-permute-start.15 = (bf16[512,256]{1,0:T(8,128)(2,1)S(1)}, bf16[512,256]{1,0:T(8,128)(2,1)S(1)}, u32[]{:S(2)}, u32[]{:S(2)}) collective-permute-start(bf16[512,256]{1,0:T(8,128)(2,1)S(1)} %get-tuple-element.92), channel_id=1, source_target_pairs={{0,1},{1,0},{2,3},{3,2},{4,5},{5,4},{6,7},{7,6},{8,9},{9,8},{10,11... | collective-permute-start | bytes 786440 | tf_op jit(solution)/shard_map/ppermute | solution.py:32
  64.6 13.9 %collective-permute-start.21 = (bf16[8,128,1408]{2,1,0:T(8,128)(2,1)S(1)}, bf16[8,128,1408]{2,1,0:T(8,128)(2,1)S(1)}, u32[]{:S(2)}, u32[]{:S(2)}) collective-permute-start(bf16[8,128,1408]{2,1,0:T(8,128)(2,1)S(1)} %get-tuple-element.96.refs_4_.refs_2_), channel_id=1, source_target_pairs={{0,16},{16,0},{1,17},{17,1},{2,18},{18,2},{3,19},{19,3},{4,20},{20... | collective-permute-start | bytes 8650760 | tf_op jit(solution)/shard_map/ppermute | solution.py:32
  64.8 12.9 %collective-permute-start.18 = (bf16[256,256]{1,0:T(8,128)(2,1)S(1)}, bf16[256,256]{1,0:T(8,128)(2,1)S(1)}, u32[]{:S(2)}, u32[]{:S(2)}) collective-permute-start(bf16[256,256]{1,0:T(8,128)(2,1)S(1)} %get-tuple-element.95.refs_6_), channel_id=1, source_target_pairs={{0,2},{1,3},{2,0},{3,1},{4,6},{5,7},{6,4},{7,5},{8,10},{9,11},{10,... | collective-permute-start | bytes 393224 | tf_op jit(solution)/shard_map/ppermute | solution.py:32
  67.2 10.5 %collective-permute-start.19 = (bf16[256,256]{1,0:T(8,128)(2,1)S(1)}, bf16[256,256]{1,0:T(8,128)(2,1)S(1)}, u32[]{:S(2)}, u32[]{:S(2)}) collective-permute-start(bf16[256,256]{1,0:T(8,128)(2,1)S(1)} %get-tuple-element.95.refs_6_), channel_id=1, source_target_pairs={{0,3},{1,2},{2,1},{3,0},{4,7},{5,6},{6,5},{7,4},{8,11},{9,10},{10,... | collective-permute-start | bytes 393224 | tf_op jit(solution)/shard_map/ppermute | solution.py:32
  69.4 9.0 %collective-permute-start.20 = (bf16[256,256]{1,0:T(8,128)(2,1)S(1)}, bf16[256,256]{1,0:T(8,128)(2,1)S(1)}, u32[]{:S(2)}, u32[]{:S(2)}) collective-permute-start(bf16[256,256]{1,0:T(8,128)(2,1)S(1)} %get-tuple-element.95.refs_6_), channel_id=1, source_target_pairs={{0,1},{1,0},{2,3},{3,2},{4,5},{5,4},{6,7},{7,6},{8,9},{9,8},{10,11... | collective-permute-start | bytes 393224 | tf_op jit(solution)/shard_map/ppermute | solution.py:32
  79.2 13.5 %collective-permute-start.22 = (bf16[272,256]{1,0:T(8,128)(2,1)S(1)}, bf16[272,256]{1,0:T(8,128)(2,1)S(1)}, u32[]{:S(2)}, u32[]{:S(2)}) collective-permute-start(bf16[272,256]{1,0:T(8,128)(2,1)S(1)} %get-tuple-element.98), channel_id=1, source_target_pairs={{0,2},{1,3},{2,0},{3,1},{4,6},{5,7},{6,4},{7,5},{8,10},{9,11},{10,... | collective-permute-start | bytes 417800 | tf_op jit(solution)/shard_map/ppermute | solution.py:32
  81.9 10.9 %collective-permute-start.23 = (bf16[272,256]{1,0:T(8,128)(2,1)S(1)}, bf16[272,256]{1,0:T(8,128)(2,1)S(1)}, u32[]{:S(2)}, u32[]{:S(2)}) collective-permute-start(bf16[272,256]{1,0:T(8,128)(2,1)S(1)} %get-tuple-element.99), channel_id=1, source_target_pairs={{0,3},{1,2},{2,1},{3,0},{4,7},{5,6},{6,5},{7,4},{8,11},{9,10},{10,... | collective-permute-start | bytes 417800 | tf_op jit(solution)/shard_map/ppermute | solution.py:32
  83.7 9.1 %collective-permute-start.24 = (bf16[272,256]{1,0:T(8,128)(2,1)S(1)}, bf16[272,256]{1,0:T(8,128)(2,1)S(1)}, u32[]{:S(2)}, u32[]{:S(2)}) collective-permute-start(bf16[272,256]{1,0:T(8,128)(2,1)S(1)} %get-tuple-element.100), channel_id=1, source_target_pairs={{0,1},{1,0},{2,3},{3,2},{4,5},{5,4},{6,7},{7,6},{8,9},{9,8},{10,11... | collective-permute-start | bytes 417800 | tf_op jit(solution)/shard_map/ppermute | solution.py:32
  94.6 12.2 %collective-permute-start.25 = (bf16[272,256]{1,0:T(8,128)(2,1)S(1)}, bf16[272,256]{1,0:T(8,128)(2,1)S(1)}, u32[]{:S(2)}, u32[]{:S(2)}) collective-permute-start(bf16[272,256]{1,0:T(8,128)(2,1)S(1)} %get-tuple-element.113.refs_8_), channel_id=1, source_target_pairs={{0,2},{1,3},{2,0},{3,1},{4,6},{5,7},{6,4},{7,5},{8,10},{9,11},{10,... | collective-permute-start | bytes 417800 | tf_op jit(solution)/shard_map/ppermute | solution.py:32
  97.0 9.8 %collective-permute-start.26 = (bf16[272,256]{1,0:T(8,128)(2,1)S(1)}, bf16[272,256]{1,0:T(8,128)(2,1)S(1)}, u32[]{:S(2)}, u32[]{:S(2)}) collective-permute-start(bf16[272,256]{1,0:T(8,128)(2,1)S(1)} %get-tuple-element.113.refs_8_), channel_id=1, source_target_pairs={{0,3},{1,2},{2,1},{3,0},{4,7},{5,6},{6,5},{7,4},{8,11},{9,10},{10,... | collective-permute-start | bytes 417800 | tf_op jit(solution)/shard_map/ppermute | solution.py:32
  99.2 8.3 %collective-permute-start.27 = (bf16[272,256]{1,0:T(8,128)(2,1)S(1)}, bf16[272,256]{1,0:T(8,128)(2,1)S(1)}, u32[]{:S(2)}, u32[]{:S(2)}) collective-permute-start(bf16[272,256]{1,0:T(8,128)(2,1)S(1)} %get-tuple-element.113.refs_8_), channel_id=1, source_target_pairs={{0,1},{1,0},{2,3},{3,2},{4,5},{5,4},{6,7},{7,6},{8,9},{9,8},{10,11... | collective-permute-start | bytes 417800 | tf_op jit(solution)/shard_map/ppermute | solution.py:32
  108.5 12.9 %collective-permute-start.28 = (bf16[256,256]{1,0:T(8,128)(2,1)S(1)}, bf16[256,256]{1,0:T(8,128)(2,1)S(1)}, u32[]{:S(2)}, u32[]{:S(2)}) collective-permute-start(bf16[256,256]{1,0:T(8,128)(2,1)S(1)} %get-tuple-element.117), channel_id=1, source_target_pairs={{0,2},{1,3},{2,0},{3,1},{4,6},{5,7},{6,4},{7,5},{8,10},{9,11},{10,... | collective-permute-start | bytes 393224 | tf_op jit(solution)/shard_map/ppermute | solution.py:32
  111.0 10.4 %collective-permute-start.29 = (bf16[256,256]{1,0:T(8,128)(2,1)S(1)}, bf16[256,256]{1,0:T(8,128)(2,1)S(1)}, u32[]{:S(2)}, u32[]{:S(2)}) collective-permute-start(bf16[256,256]{1,0:T(8,128)(2,1)S(1)} %get-tuple-element.118), channel_id=1, source_target_pairs={{0,3},{1,2},{2,1},{3,0},{4,7},{5,6},{6,5},{7,4},{8,11},{9,10},{10,... | collective-permute-start | bytes 393224 | tf_op jit(solution)/shard_map/ppermute | solution.py:32
  112.2 10.1 %collective-permute-start.30 = (bf16[256,256]{1,0:T(8,128)(2,1)S(1)}, bf16[256,256]{1,0:T(8,128)(2,1)S(1)}, u32[]{:S(2)}, u32[]{:S(2)}) collective-permute-start(bf16[256,256]{1,0:T(8,128)(2,1)S(1)} %get-tuple-element.119), channel_id=1, source_target_pairs={{0,1},{1,0},{2,3},{3,2},{4,5},{5,4},{6,7},{7,6},{8,9},{9,8},{10,11... | collective-permute-start | bytes 393224 | tf_op jit(solution)/shard_map/ppermute | solution.py:32
  112.3 11.3 %collective-permute-start.32 = (bf16[240,256]{1,0:T(8,128)(2,1)S(1)}, bf16[240,256]{1,0:T(8,128)(2,1)S(1)}, u32[]{:S(2)}, u32[]{:S(2)}) collective-permute-start(bf16[240,256]{1,0:T(8,128)(2,1)S(1)} %get-tuple-element.122.refs_0_), channel_id=1, source_target_pairs={{0,4},{4,0},{8,12},{12,8},{1,5},{5,1},{9,13},{13,9},{2,6},{6,2},{1... | collective-permute-start | bytes 368648 | tf_op jit(solution)/shard_map/ppermute | solution.py:32
  112.9 10.7 %collective-permute-start.33 = (bf16[240,256]{1,0:T(8,128)(2,1)S(1)}, bf16[240,256]{1,0:T(8,128)(2,1)S(1)}, u32[]{:S(2)}, u32[]{:S(2)}) collective-permute-start(bf16[240,256]{1,0:T(8,128)(2,1)S(1)} %get-tuple-element.123.refs_1_), channel_id=1, source_target_pairs={{0,8},{4,12},{8,0},{12,4},{1,9},{5,13},{9,1},{13,5},{2,10},{6,14},... | collective-permute-start | bytes 368648 | tf_op jit(solution)/shard_map/ppermute | solution.py:32
  126.8 12.6 %collective-permute-start.36 = (bf16[896,256]{1,0:T(8,128)(2,1)S(1)}, bf16[896,256]{1,0:T(8,128)(2,1)S(1)}, u32[]{:S(2)}, u32[]{:S(2)}) collective-permute-start(bf16[896,256]{1,0:T(8,128)(2,1)S(1)} %pad_maximum_fusion.1), channel_id=1, source_target_pairs={{0,8},{4,12},{8,0},{12,4},{1,9},{5,13},{9,1},{13,5},{2,10},{6,14},... | collective-permute-start | bytes 1376264 | tf_op jit(solution)/shard_map/ppermute | solution.py:32
  127.4 12.3 %collective-permute-start.35 = (bf16[896,256]{1,0:T(8,128)(2,1)S(1)}, bf16[896,256]{1,0:T(8,128)(2,1)S(1)}, u32[]{:S(2)}, u32[]{:S(2)}) collective-permute-start(bf16[896,256]{1,0:T(8,128)(2,1)S(1)} %pad_maximum_fusion), channel_id=1, source_target_pairs={{0,4},{4,0},{8,12},{12,8},{1,5},{5,1},{9,13},{13,9},{2,6},{6,2},{1... | collective-permute-start | bytes 1376264 | tf_op jit(solution)/shard_map/ppermute | solution.py:32
  140.1 8.9 %collective-permute-start.38 = (bf16[656,256]{1,0:T(8,128)(2,1)S(1)}, bf16[656,256]{1,0:T(8,128)(2,1)S(1)}, u32[]{:S(2)}, u32[]{:S(2)}) collective-permute-start(bf16[656,256]{1,0:T(8,128)(2,1)S(1)} %pad_maximum_fusion.3), channel_id=1, source_target_pairs={{0,4},{4,0},{8,12},{12,8},{1,5},{5,1},{9,13},{13,9},{2,6},{6,2},{1... | collective-permute-start | bytes 1007624 | tf_op jit(solution)/shard_map/ppermute | solution.py:32
  140.7 8.6 %collective-permute-start.37 = (bf16[656,256]{1,0:T(8,128)(2,1)S(1)}, bf16[656,256]{1,0:T(8,128)(2,1)S(1)}, u32[]{:S(2)}, u32[]{:S(2)}) collective-permute-start(bf16[656,256]{1,0:T(8,128)(2,1)S(1)} %pad_maximum_fusion.2), channel_id=1, source_target_pairs={{0,8},{4,12},{8,0},{12,4},{1,9},{5,13},{9,1},{13,5},{2,10},{6,14},... | collective-permute-start | bytes 1007624 | tf_op jit(solution)/shard_map/ppermute | solution.py:32
  (23 other events, 155.0 us)

commit v7 on v6

--- a/solution.py
+++ b/solution.py
@@ -145,16 +145,24 @@
     return jnp.concatenate([value[:, i : i + feats] for i in range(0, cols, feats)], axis=0)
 
 
-def share_body(up_ref, down_ref, rows_ref, out_ref, own_ref):
+def share_body(up_ref, down_ref, rows_ref, out_ref, own_ref, sems):
     s = lax.axis_index("section")
     place = s * lax.axis_size("dp") + lax.axis_index("dp")
+    total, length = rows_ref.shape[1], own_ref.shape[1]
+    copies = []
+    for i in range(own_ref.shape[0] // total):
+        source = rows_ref.at[s, :, pl.ds(i * length, length)]
+        target = own_ref.at[pl.ds(i * total, total)]
+        copies.append(pltpu.make_async_copy(source, target, sems.at[i]))
+        copies[-1].start()
     tall = out_ref.shape[0] // 2
     cols = pl.ds(pl.multiple_of(place * HEAD, HEAD), HEAD)
     out_ref[:tall, :] = up_ref[pl.ds(pl.multiple_of(place * tall, 16), tall), :]
     for side in range(2):
         there = slice(side * HEAD, (side + 1) * HEAD)
         out_ref[tall:, there] = down_ref[side * tall : (side + 1) * tall, cols]
-    own_ref[...] = pack(rows_ref[s], own_ref.shape[1])
+    for copy in copies:
+        copy.wait()
 
 
 def messages_body(n, share_ref, own_ref, wq_own, wq_other, *outs):
@@ -643,7 +651,10 @@
         rest = own_shape.shape[0] // 2
         longer = shape((messages[0].shape[0] + rest, cols))
         share, own = call(
-            share_body, [shape((2 * up_rows, 2 * down_cols)), own_shape], [vm()] * 3
+            share_body,
+            [shape((2 * up_rows, 2 * down_cols)), own_shape],
+            [vm(), vm(), hbm()],
+            [pltpu.SemaphoreType.DMA((feats // cols,))],
         )(enc_up, down_t, segment_input[:, 0])
         messages = call(
             functools.partial(messages_body, n), messages + [longer], [vm()] * 4
@@ -832,7 +843,7 @@
         return call(pieces_body, parts, [vm()] * 2)(kept, swap(sent))
 
     size = enc_width // 2
-    early = size // 2 + 16 if size % 32 == 0 else size // 2
+    early = size // 2 + 32 if size % 64 == 0 else size // 2
     ax, bx, ay, by = pieces_of(kept1, sent1, [early, size - early] * 2)
     if dp == 4:
         ax, ay = over_dp([ax, ay], (1, 2))

time: 153 us -> 153 us (level)
  no operation moved by 1% of the time
where the time goes in v7:
time: 153 us; the launch traced here: 152 us
  waiting for transfers between devices  79.1 us (52%)
  starting transfers between devices  42.8 us (28%)
  Pallas kernels  24.7 us (16%)
  local copies, waits for them, and re-layouts  3.5 us (2%)
    ppermute x37, waiting for transfers between devices, xor_move(): return lax.ppermute(value, axis, [(i, i ^ by) for i in range(count)])  70.6 us
    ppermute x37, starting transfers between devices, xor_move(): return lax.ppermute(value, axis, [(i, i ^ by) for i in range(count)])  40.1 us
    pallas_call x26, Pallas kernels, run(): pl.pallas_call(kernel, out_shape=list(outs) + [shape(x.shape, x.dtype) fo...  24.7 us
    ppermute x1, waiting for transfers between devices, on_device(): next_outer = lax.ppermute(far_inner, 'mp', outer)  8.48 us
    unnamed x34, local copies, waits for them, and re-layouts  3.35 us
  transfers between devices with their start and end apart: 40, of which 23 were waited for; matrix products, arithmetic and copies ran while one was open for 0% of the time, Pallas kernels for 11%

profile of v7, /device:TPU:0, one launch (start us, length us, event | category | flops | bytes accessed | tf_op | source)
XLA Modules:
  0.0 152.4 jit_solution(14896769911888611461)
XLA Ops:
  4.6 3.1 %collective-permute-start.5 = (bf16[544,256]{1,0:T(8,128)(2,1)S(1)}, bf16[544,256]{1,0:T(8,128)(2,1)S(1)}, u32[]{:S(2)}, u32[]{:S(2)}) collective-permute-start(bf16[544,256]{1,0:T(8,128)(2,1)S(1)} %get-tuple-element.76), channel_id=1, source_target_pairs={{0,1},{1,0},{2,3},{3,2},{4,5},{5,4},{6,7},{7,6},{8,9},{9,8},{10,11... | collective-permute-start | bytes 835592 | tf_op jit(solution)/shard_map/ppermute | solution.py:32
  7.7 2.6 %collective-permute-start.3 = (bf16[288,256]{1,0:T(8,128)(2,1)S(1)}, bf16[288,256]{1,0:T(8,128)(2,1)S(1)}, u32[]{:S(2)}, u32[]{:S(2)}) collective-permute-start(bf16[288,256]{1,0:T(8,128)(2,1)S(1)} %get-tuple-element.74), channel_id=1, source_target_pairs={{0,2},{1,3},{2,0},{3,1},{4,6},{5,7},{6,4},{7,5},{8,10},{9,11},{10,... | collective-permute-start | bytes 442376 | tf_op jit(solution)/shard_map/ppermute | solution.py:32
  11.5 6.5 %collective-permute-done.3.refs_1_ = bf16[288,256]{1,0:T(8,128)(2,1)S(1)} collective-permute-done((bf16[288,256]{1,0:T(8,128)(2,1)S(1)}, bf16[288,256]{1,0:T(8,128)(2,1)S(1)}, u32[]{:S(2)}, u32[]{:S(2)}) %collective-permute-start.3) | collective-permute-done | bytes 147488 | tf_op jit(solution)/shard_map/ppermute | solution.py:32
  18.0 5.1 %collective-permute-done.4.refs_2_ = bf16[288,256]{1,0:T(8,128)(2,1)S(1)} collective-permute-done((bf16[288,256]{1,0:T(8,128)(2,1)S(1)}, bf16[288,256]{1,0:T(8,128)(2,1)S(1)}, u32[]{:S(2)}, u32[]{:S(2)}) %collective-permute-start.4) | collective-permute-done | bytes 147488 | tf_op jit(solution)/shard_map/ppermute | solution.py:32
  24.9 1.6 %collective-permute-start.6 = (bf16[3,144,256]{2,1,0:T(8,128)(2,1)S(1)}, bf16[3,144,256]{2,1,0:T(8,128)(2,1)S(1)}, u32[]{:S(2)}, u32[]{:S(2)}) collective-permute-start(bf16[3,144,256]{2,1,0:T(8,128)(2,1)S(1)} %get-tuple-element.78.refs_0_), channel_id=1, source_target_pairs={{0,4},{4,0},{8,12},{12,8},{1,5},{5,1},{9,13},{13,9},{2,6},{6,2},{1... | collective-permute-start | bytes 663560 | tf_op jit(solution)/shard_map/ppermute | solution.py:32
  26.5 1.5 collective-permute-start.7
  28.0 2.9 %collective-permute-done.6.refs_1_ = bf16[3,144,256]{2,1,0:T(8,128)(2,1)S(1)} collective-permute-done((bf16[3,144,256]{2,1,0:T(8,128)(2,1)S(1)}, bf16[3,144,256]{2,1,0:T(8,128)(2,1)S(1)}, u32[]{:S(2)}, u32[]{:S(2)}) %collective-permute-start.6) | collective-permute-done | bytes 221216 | tf_op jit(solution)/shard_map/ppermute | solution.py:32
  30.9 1.5 collective-permute-done.7.refs_3_.refs_4_
  33.6 1.6 %collective-permute-start.10 = (bf16[2,3,144,256]{3,2,1,0:T(8,128)(2,1)S(1)}, bf16[2,3,144,256]{3,2,1,0:T(8,128)(2,1)S(1)}, u32[]{:S(2)}, u32[]{:S(2)}) collective-permute-start(bf16[2,3,144,256]{3,2,1,0:T(8,128)(2,1)S(1)} %get-tuple-element.85), channel_id=1, source_target_pairs={{0,8},{4,12},{8,0},{12,4},{1,9},{5,13},{9,1},{13,5},{2,10},{6,14},... | collective-permute-start | bytes 1327112 | tf_op jit(solution)/shard_map/ppermute | solution.py:32
  35.1 1.5 collective-permute-start.11
  36.6 1.3 collective-permute-start.13
  39.4 8.5 %collective-permute-done.13.refs_10_.refs_7_ = bf16[768,256]{1,0:T(8,128)(2,1)S(1)} collective-permute-done((bf16[768,256]{1,0:T(8,128)(2,1)S(1)}, bf16[768,256]{1,0:T(8,128)(2,1)S(1)}, u32[]{:S(2)}, u32[]{:S(2)}) %collective-permute-start.13) | collective-permute-done | bytes 393248 | tf_op jit(solution)/shard_map/ppermute | solution.py:688
  48.7 3.7 %collective-permute-start.15 = (bf16[512,256]{1,0:T(8,128)(2,1)S(1)}, bf16[512,256]{1,0:T(8,128)(2,1)S(1)}, u32[]{:S(2)}, u32[]{:S(2)}) collective-permute-start(bf16[512,256]{1,0:T(8,128)(2,1)S(1)} %get-tuple-element.92), channel_id=1, source_target_pairs={{0,1},{1,0},{2,3},{3,2},{4,5},{5,4},{6,7},{7,6},{8,9},{9,8},{10,11... | collective-permute-start | bytes 786440 | tf_op jit(solution)/shard_map/ppermute | solution.py:32
  52.4 5.6 %shard_map.147 = (bf16[1024,896]{1,0:T(8,128)(2,1)S(1)}, bf16[4,512,256]{2,1,0:T(8,128)(2,1)S(1)}) custom-call(bf16[1024,896]{1,0:T(8,128)(2,1)S(1)} %bitcast.24, bf16[1024,896]{1,0:T(8,128)(2,1)S(1)} %shard_map.141.refs_11_.refs_1_, bf16[8,3,144,256]{3,2,1,0:T(8,128)(2,1)S(1)} %get-tuple-element.89.refs_2_, ...), custom_call_target="tpu_custom_call" | custom-call | flops 3758096 | bytes 2883 | tf_op jit(solution)/shard_map/pallas_call | solution.py:70
  62.9 1.6 %shard_map.151 = (bf16[256,256]{1,0:T(8,128)(2,1)S(1)}, f32[8,64,512]{2,1,0:T(8,128)S(1)}, bf16[2048,512]{1,0:T(8,128)(2,1)S(1)}, bf16[8,128,1408]{2,1,0:T(8,128)(2,1)S(1)}) custom-call(s32[2,4,4]{2,1,0:T(4,128)S(1)} %bitcast.36, s32[2,4]{1,0:T(2,128)S(1)} %bitcast.39, ...), custom_call_target="tpu_custom_call", output_to_operand_aliasing={{3}: (5, {})} | custom-call | flops 134217 | bytes 3276 | tf_op jit(solution)/shard_map/pallas_call | solution.py:70
  64.8 2.4 %collective-permute-start.18 = (bf16[256,256]{1,0:T(8,128)(2,1)S(1)}, bf16[256,256]{1,0:T(8,128)(2,1)S(1)}, u32[]{:S(2)}, u32[]{:S(2)}) collective-permute-start(bf16[256,256]{1,0:T(8,128)(2,1)S(1)} %get-tuple-element.95.refs_6_), channel_id=1, source_target_pairs={{0,2},{1,3},{2,0},{3,1},{4,6},{5,7},{6,4},{7,5},{8,10},{9,11},{10,... | collective-permute-start | bytes 393224 | tf_op jit(solution)/shard_map/ppermute | solution.py:32
  67.2 2.2 %collective-permute-start.19 = (bf16[256,256]{1,0:T(8,128)(2,1)S(1)}, bf16[256,256]{1,0:T(8,128)(2,1)S(1)}, u32[]{:S(2)}, u32[]{:S(2)}) collective-permute-start(bf16[256,256]{1,0:T(8,128)(2,1)S(1)} %get-tuple-element.95.refs_6_), channel_id=1, source_target_pairs={{0,3},{1,2},{2,1},{3,0},{4,7},{5,6},{6,5},{7,4},{8,11},{9,10},{10,... | collective-permute-start | bytes 393224 | tf_op jit(solution)/shard_map/ppermute | solution.py:32
  69.4 8.3 %collective-permute-done.18.refs_7_ = bf16[256,256]{1,0:T(8,128)(2,1)S(1)} collective-permute-done((bf16[256,256]{1,0:T(8,128)(2,1)S(1)}, bf16[256,256]{1,0:T(8,128)(2,1)S(1)}, u32[]{:S(2)}, u32[]{:S(2)}) %collective-permute-start.18) | collective-permute-done | bytes 131104 | tf_op jit(solution)/shard_map/ppermute | solution.py:32
  79.3 2.6 %collective-permute-start.22 = (bf16[272,256]{1,0:T(8,128)(2,1)S(1)}, bf16[272,256]{1,0:T(8,128)(2,1)S(1)}, u32[]{:S(2)}, u32[]{:S(2)}) collective-permute-start(bf16[272,256]{1,0:T(8,128)(2,1)S(1)} %get-tuple-element.98), channel_id=1, source_target_pairs={{0,2},{1,3},{2,0},{3,1},{4,6},{5,7},{6,4},{7,5},{8,10},{9,11},{10,... | collective-permute-start | bytes 417800 | tf_op jit(solution)/shard_map/ppermute | solution.py:32
  81.9 1.9 %collective-permute-start.23 = (bf16[272,256]{1,0:T(8,128)(2,1)S(1)}, bf16[272,256]{1,0:T(8,128)(2,1)S(1)}, u32[]{:S(2)}, u32[]{:S(2)}) collective-permute-start(bf16[272,256]{1,0:T(8,128)(2,1)S(1)} %get-tuple-element.99), channel_id=1, source_target_pairs={{0,3},{1,2},{2,1},{3,0},{4,7},{5,6},{6,5},{7,4},{8,11},{9,10},{10,... | collective-permute-start | bytes 417800 | tf_op jit(solution)/shard_map/ppermute | solution.py:32
  85.0 7.8 %collective-permute-done.22.refs_2_ = bf16[272,256]{1,0:T(8,128)(2,1)S(1)} collective-permute-done((bf16[272,256]{1,0:T(8,128)(2,1)S(1)}, bf16[272,256]{1,0:T(8,128)(2,1)S(1)}, u32[]{:S(2)}, u32[]{:S(2)}) %collective-permute-start.22) | collective-permute-done | bytes 139296 | tf_op jit(solution)/shard_map/ppermute | solution.py:32
  92.8 1.8 %shard_map.154 = (bf16[272,256]{1,0:T(8,128)(2,1)S(1)}, f32[256,128]{1,0:T(8,128)S(1)}, bf16[256,256]{1,0:T(8,128)(2,1)S(1)}, bf16[8,64,512]{2,1,0:T(8,128)(2,1)S(1)}, bf16[8,64,512]{2,1,0:T(8,128)(2,1)S(1)}) custom-call(s32[2,4]{1,0:T(2,128)S(1)} %bitcast.40, bf16[272,256]{1,0:T(8,128)(2,1)S(1)} %get-tuple-element.97.refs_1_, ...), custom_call_target="tpu_custom_call" | custom-call | flops 201326 | bytes 1449 | tf_op jit(solution)/shard_map/pallas_call | solution.py:70
  94.6 2.4 %collective-permute-start.25 = (bf16[272,256]{1,0:T(8,128)(2,1)S(1)}, bf16[272,256]{1,0:T(8,128)(2,1)S(1)}, u32[]{:S(2)}, u32[]{:S(2)}) collective-permute-start(bf16[272,256]{1,0:T(8,128)(2,1)S(1)} %get-tuple-element.113.refs_8_), channel_id=1, source_target_pairs={{0,2},{1,3},{2,0},{3,1},{4,6},{5,7},{6,4},{7,5},{8,10},{9,11},{10,... | collective-permute-start | bytes 417800 | tf_op jit(solution)/shard_map/ppermute | solution.py:32
  97.0 2.2 %collective-permute-start.26 = (bf16[272,256]{1,0:T(8,128)(2,1)S(1)}, bf16[272,256]{1,0:T(8,128)(2,1)S(1)}, u32[]{:S(2)}, u32[]{:S(2)}) collective-permute-start(bf16[272,256]{1,0:T(8,128)(2,1)S(1)} %get-tuple-element.113.refs_8_), channel_id=1, source_target_pairs={{0,3},{1,2},{2,1},{3,0},{4,7},{5,6},{6,5},{7,4},{8,11},{9,10},{10,... | collective-permute-start | bytes 417800 | tf_op jit(solution)/shard_map/ppermute | solution.py:32
  100.2 2.8 %shard_map.156 = (bf16[896,2048]{1,0:T(8,128)(2,1)S(1)}, bf16[896,256]{1,0:T(8,128)(2,1)S(1)}, bf16[896,256]{1,0:T(8,128)(2,1)S(1)}) custom-call(s32[2,4,4]{2,1,0:T(4,128)S(1)} %bitcast.38, bf16[2048,512]{1,0:T(8,128)(2,1)S(1)} %shard_map.155.refs_1_, bf16[8,128,1408]{2,1,0:T(8,128)(2,1)S(1)} %get-tuple-element.96.refs_4_.refs_2_, ...), custom_call_target="tpu_custom_call" | custom-call | flops 1879048 | bytes 4587 | tf_op jit(solution)/shard_map/pallas_call | solution.py:70
  103.0 3.8 %collective-permute-done.25.refs_9_ = bf16[272,256]{1,0:T(8,128)(2,1)S(1)} collective-permute-done((bf16[272,256]{1,0:T(8,128)(2,1)S(1)}, bf16[272,256]{1,0:T(8,128)(2,1)S(1)}, u32[]{:S(2)}, u32[]{:S(2)}) %collective-permute-start.25) | collective-permute-done | bytes 139296 | tf_op jit(solution)/shard_map/ppermute | solution.py:32
  108.5 2.5 %collective-permute-start.28 = (bf16[256,256]{1,0:T(8,128)(2,1)S(1)}, bf16[256,256]{1,0:T(8,128)(2,1)S(1)}, u32[]{:S(2)}, u32[]{:S(2)}) collective-permute-start(bf16[256,256]{1,0:T(8,128)(2,1)S(1)} %get-tuple-element.117), channel_id=1, source_target_pairs={{0,2},{1,3},{2,0},{3,1},{4,6},{5,7},{6,4},{7,5},{8,10},{9,11},{10,... | collective-permute-start | bytes 393224 | tf_op jit(solution)/shard_map/ppermute | solution.py:32
  113.4 8.0 %collective-permute-done.28.refs_4_ = bf16[256,256]{1,0:T(8,128)(2,1)S(1)} collective-permute-done((bf16[256,256]{1,0:T(8,128)(2,1)S(1)}, bf16[256,256]{1,0:T(8,128)(2,1)S(1)}, u32[]{:S(2)}, u32[]{:S(2)}) %collective-permute-start.28) | collective-permute-done | bytes 131104 | tf_op jit(solution)/shard_map/ppermute | solution.py:32
  128.0 11.4 %collective-permute-done.36 = bf16[896,256]{1,0:T(8,128)(2,1)S(1)} collective-permute-done((bf16[896,256]{1,0:T(8,128)(2,1)S(1)}, bf16[896,256]{1,0:T(8,128)(2,1)S(1)}, u32[]{:S(2)}, u32[]{:S(2)}) %collective-permute-start.36) | collective-permute-done | bytes 458784 | tf_op jit(solution)/shard_map/ppermute | solution.py:32
  140.7 1.6 %collective-permute-start.37 = (bf16[640,256]{1,0:T(8,128)(2,1)S(1)}, bf16[640,256]{1,0:T(8,128)(2,1)S(1)}, u32[]{:S(2)}, u32[]{:S(2)}) collective-permute-start(bf16[640,256]{1,0:T(8,128)(2,1)S(1)} %pad_maximum_fusion.2), channel_id=1, source_target_pairs={{0,8},{4,12},{8,0},{12,4},{1,9},{5,13},{9,1},{13,5},{2,10},{6,14},... | collective-permute-start | bytes 983048 | tf_op jit(solution)/shard_map/ppermute | solution.py:32
  142.3 6.5 %collective-permute-done.38 = bf16[640,256]{1,0:T(8,128)(2,1)S(1)} collective-permute-done((bf16[640,256]{1,0:T(8,128)(2,1)S(1)}, bf16[640,256]{1,0:T(8,128)(2,1)S(1)}, u32[]{:S(2)}, u32[]{:S(2)}) %collective-permute-start.38) | collective-permute-done | bytes 327712 | tf_op jit(solution)/shard_map/ppermute | solution.py:32
  149.6 1.8 %collective-permute-done.39 = bf16[896,256]{1,0:T(8,128)(2,1)S(1)} collective-permute-done((bf16[896,256]{1,0:T(8,128)(2,1)S(1)}, bf16[896,256]{1,0:T(8,128)(2,1)S(1)}, u32[]{:S(2)}, u32[]{:S(2)}) %collective-permute-start.39) | collective-permute-done | bytes 458784 | tf_op jit(solution)/shard_map/ppermute | solution.py:32
  (127 shorter events, 32.7 us)
Async XLA Ops:
  1.2 9.2 %collective-permute-start.1 = (bf16[1024,512]{1,0:T(8,128)(2,1)}, bf16[1024,512]{1,0:T(8,128)(2,1)S(1)}, u32[]{:S(2)}, u32[]{:S(2)}) collective-permute-start(bf16[1024,512]{1,0:T(8,128)(2,1)} %bitcast.19), channel_id=1, source_target_pairs={{0,16},{16,0},{1,17},{17,1},{2,18},{18,2},{3,19},{19,3},{4,20},{20... | collective-permute-start | bytes 3145736 | tf_op jit(solution)/shard_map/ppermute | solution.py:32
  4.6 18.4 %collective-permute-start.5 = (bf16[544,256]{1,0:T(8,128)(2,1)S(1)}, bf16[544,256]{1,0:T(8,128)(2,1)S(1)}, u32[]{:S(2)}, u32[]{:S(2)}) collective-permute-start(bf16[544,256]{1,0:T(8,128)(2,1)S(1)} %get-tuple-element.76), channel_id=1, source_target_pairs={{0,1},{1,0},{2,3},{3,2},{4,5},{5,4},{6,7},{7,6},{8,9},{9,8},{10,11... | collective-permute-start | bytes 835592 | tf_op jit(solution)/shard_map/ppermute | solution.py:32
  7.7 10.3 %collective-permute-start.3 = (bf16[288,256]{1,0:T(8,128)(2,1)S(1)}, bf16[288,256]{1,0:T(8,128)(2,1)S(1)}, u32[]{:S(2)}, u32[]{:S(2)}) collective-permute-start(bf16[288,256]{1,0:T(8,128)(2,1)S(1)} %get-tuple-element.74), channel_id=1, source_target_pairs={{0,2},{1,3},{2,0},{3,1},{4,6},{5,7},{6,4},{7,5},{8,10},{9,11},{10,... | collective-permute-start | bytes 442376 | tf_op jit(solution)/shard_map/ppermute | solution.py:32
  10.3 12.7 %collective-permute-start.4 = (bf16[288,256]{1,0:T(8,128)(2,1)S(1)}, bf16[288,256]{1,0:T(8,128)(2,1)S(1)}, u32[]{:S(2)}, u32[]{:S(2)}) collective-permute-start(bf16[288,256]{1,0:T(8,128)(2,1)S(1)} %get-tuple-element.75), channel_id=1, source_target_pairs={{0,3},{1,2},{2,1},{3,0},{4,7},{5,6},{6,5},{7,4},{8,11},{9,10},{10,... | collective-permute-start | bytes 442376 | tf_op jit(solution)/shard_map/ppermute | solution.py:32
  23.2 10.2 %collective-permute-start.8 = (bf16[784,256]{1,0:T(8,128)(2,1)S(1)}, bf16[784,256]{1,0:T(8,128)(2,1)S(1)}, u32[]{:S(2)}, u32[]{:S(2)}) collective-permute-start(bf16[784,256]{1,0:T(8,128)(2,1)S(1)} %get-tuple-element.81), channel_id=1, source_target_pairs={{0,1},{1,0},{2,3},{3,2},{4,5},{5,4},{6,7},{7,6},{8,9},{9,8},{10,11... | collective-permute-start | bytes 1204232 | tf_op jit(solution)/shard_map/ppermute | solution.py:32
  24.3 8.2 %collective-permute-start.9 = (bf16[768,256]{1,0:T(8,128)(2,1)S(1)}, bf16[768,256]{1,0:T(8,128)(2,1)S(1)}, u32[]{:S(2)}, u32[]{:S(2)}) collective-permute-start(bf16[768,256]{1,0:T(8,128)(2,1)S(1)} %get-tuple-element.84), channel_id=1, source_target_pairs={{1,2},{2,1},{5,6},{6,5},{9,10},{10,9},{13,14},{14,13},{17,18},{18,... | collective-permute-start | bytes 1179656 | tf_op jit(solution)/shard_map/ppermute | solution.py:679
  24.9 6.0 %collective-permute-start.6 = (bf16[3,144,256]{2,1,0:T(8,128)(2,1)S(1)}, bf16[3,144,256]{2,1,0:T(8,128)(2,1)S(1)}, u32[]{:S(2)}, u32[]{:S(2)}) collective-permute-start(bf16[3,144,256]{2,1,0:T(8,128)(2,1)S(1)} %get-tuple-element.78.refs_0_), channel_id=1, source_target_pairs={{0,4},{4,0},{8,12},{12,8},{1,5},{5,1},{9,13},{13,9},{2,6},{6,2},{1... | collective-permute-start | bytes 663560 | tf_op jit(solution)/shard_map/ppermute | solution.py:32
  33.6 14.3 %collective-permute-start.10 = (bf16[2,3,144,256]{3,2,1,0:T(8,128)(2,1)S(1)}, bf16[2,3,144,256]{3,2,1,0:T(8,128)(2,1)S(1)}, u32[]{:S(2)}, u32[]{:S(2)}) collective-permute-start(bf16[2,3,144,256]{3,2,1,0:T(8,128)(2,1)S(1)} %get-tuple-element.85), channel_id=1, source_target_pairs={{0,8},{4,12},{8,0},{12,4},{1,9},{5,13},{9,1},{13,5},{2,10},{6,14},... | collective-permute-start | bytes 1327112 | tf_op jit(solution)/shard_map/ppermute | solution.py:32
  35.1 12.7 %collective-permute-start.11 = (bf16[2,3,144,256]{3,2,1,0:T(8,128)(2,1)S(1)}, bf16[2,3,144,256]{3,2,1,0:T(8,128)(2,1)S(1)}, u32[]{:S(2)}, u32[]{:S(2)}) collective-permute-start(bf16[2,3,144,256]{3,2,1,0:T(8,128)(2,1)S(1)} %get-tuple-element.86), channel_id=1, source_target_pairs={{0,4},{4,0},{8,12},{12,8},{1,5},{5,1},{9,13},{13,9},{2,6},{6,2},{1... | collective-permute-start | bytes 1327112 | tf_op jit(solution)/shard_map/ppermute | solution.py:32
  36.6 11.2 %collective-permute-start.13 = (bf16[768,256]{1,0:T(8,128)(2,1)S(1)}, bf16[768,256]{1,0:T(8,128)(2,1)S(1)}, u32[]{:S(2)}, u32[]{:S(2)}) collective-permute-start(bf16[768,256]{1,0:T(8,128)(2,1)S(1)} %collective-permute-done.9.refs_8_.refs_6_), channel_id=1, source_target_pairs={{1,0},{2,3},{5,4},{6,7},{9,8},{10,11},{13,12},{14,15},{17,16},{18,... | collective-permute-start | bytes 1179656 | tf_op jit(solution)/shard_map/ppermute | solution.py:688
  37.9 9.9 %collective-permute-start.12 = (bf16[768,256]{1,0:T(8,128)(2,1)S(1)}, bf16[768,256]{1,0:T(8,128)(2,1)S(1)}, u32[]{:S(2)}, u32[]{:S(2)}) collective-permute-start(bf16[768,256]{1,0:T(8,128)(2,1)S(1)} %get-tuple-element.87), channel_id=1, source_target_pairs={{1,2},{2,1},{5,6},{6,5},{9,10},{10,9},{13,14},{14,13},{17,18},{18,... | collective-permute-start | bytes 1179656 | tf_op jit(solution)/shard_map/ppermute | solution.py:689
  48.2 10.7 %collective-permute-start.16 = (bf16[1792,256]{1,0:T(8,128)(2,1)S(1)}, bf16[1792,256]{1,0:T(8,128)(2,1)S(1)}, u32[]{:S(2)}, u32[]{:S(2)}) collective-permute-start(bf16[1792,256]{1,0:T(8,128)(2,1)S(1)} %get-tuple-element.94.refs_1_), channel_id=1, source_target_pairs={{0,16},{16,0},{1,17},{17,1},{2,18},{18,2},{3,19},{19,3},{4,20},{20... | collective-permute-start | bytes 2752520 | tf_op jit(solution)/shard_map/ppermute | solution.py:32
  48.7 10.2 %collective-permute-start.15 = (bf16[512,256]{1,0:T(8,128)(2,1)S(1)}, bf16[512,256]{1,0:T(8,128)(2,1)S(1)}, u32[]{:S(2)}, u32[]{:S(2)}) collective-permute-start(bf16[512,256]{1,0:T(8,128)(2,1)S(1)} %get-tuple-element.92), channel_id=1, source_target_pairs={{0,1},{1,0},{2,3},{3,2},{4,5},{5,4},{6,7},{7,6},{8,9},{9,8},{10,11... | collective-permute-start | bytes 786440 | tf_op jit(solution)/shard_map/ppermute | solution.py:32
  64.6 13.9 %collective-permute-start.21 = (bf16[8,128,1408]{2,1,0:T(8,128)(2,1)S(1)}, bf16[8,128,1408]{2,1,0:T(8,128)(2,1)S(1)}, u32[]{:S(2)}, u32[]{:S(2)}) collective-permute-start(bf16[8,128,1408]{2,1,0:T(8,128)(2,1)S(1)} %get-tuple-element.96.refs_4_.refs_2_), channel_id=1, source_target_pairs={{0,16},{16,0},{1,17},{17,1},{2,18},{18,2},{3,19},{19,3},{4,20},{20... | collective-permute-start | bytes 8650760 | tf_op jit(solution)/shard_map/ppermute | solution.py:32
  64.8 12.9 %collective-permute-start.18 = (bf16[256,256]{1,0:T(8,128)(2,1)S(1)}, bf16[256,256]{1,0:T(8,128)(2,1)S(1)}, u32[]{:S(2)}, u32[]{:S(2)}) collective-permute-start(bf16[256,256]{1,0:T(8,128)(2,1)S(1)} %get-tuple-element.95.refs_6_), channel_id=1, source_target_pairs={{0,2},{1,3},{2,0},{3,1},{4,6},{5,7},{6,4},{7,5},{8,10},{9,11},{10,... | collective-permute-start | bytes 393224 | tf_op jit(solution)/shard_map/ppermute | solution.py:32
  67.2 10.5 %collective-permute-start.19 = (bf16[256,256]{1,0:T(8,128)(2,1)S(1)}, bf16[256,256]{1,0:T(8,128)(2,1)S(1)}, u32[]{:S(2)}, u32[]{:S(2)}) collective-permute-start(bf16[256,256]{1,0:T(8,128)(2,1)S(1)} %get-tuple-element.95.refs_6_), channel_id=1, source_target_pairs={{0,3},{1,2},{2,1},{3,0},{4,7},{5,6},{6,5},{7,4},{8,11},{9,10},{10,... | collective-permute-start | bytes 393224 | tf_op jit(solution)/shard_map/ppermute | solution.py:32
  69.4 9.0 %collective-permute-start.20 = (bf16[256,256]{1,0:T(8,128)(2,1)S(1)}, bf16[256,256]{1,0:T(8,128)(2,1)S(1)}, u32[]{:S(2)}, u32[]{:S(2)}) collective-permute-start(bf16[256,256]{1,0:T(8,128)(2,1)S(1)} %get-tuple-element.95.refs_6_), channel_id=1, source_target_pairs={{0,1},{1,0},{2,3},{3,2},{4,5},{5,4},{6,7},{7,6},{8,9},{9,8},{10,11... | collective-permute-start | bytes 393224 | tf_op jit(solution)/shard_map/ppermute | solution.py:32
  79.3 13.5 %collective-permute-start.22 = (bf16[272,256]{1,0:T(8,128)(2,1)S(1)}, bf16[272,256]{1,0:T(8,128)(2,1)S(1)}, u32[]{:S(2)}, u32[]{:S(2)}) collective-permute-start(bf16[272,256]{1,0:T(8,128)(2,1)S(1)} %get-tuple-element.98), channel_id=1, source_target_pairs={{0,2},{1,3},{2,0},{3,1},{4,6},{5,7},{6,4},{7,5},{8,10},{9,11},{10,... | collective-permute-start | bytes 417800 | tf_op jit(solution)/shard_map/ppermute | solution.py:32
  81.9 10.9 %collective-permute-start.23 = (bf16[272,256]{1,0:T(8,128)(2,1)S(1)}, bf16[272,256]{1,0:T(8,128)(2,1)S(1)}, u32[]{:S(2)}, u32[]{:S(2)}) collective-permute-start(bf16[272,256]{1,0:T(8,128)(2,1)S(1)} %get-tuple-element.99), channel_id=1, source_target_pairs={{0,3},{1,2},{2,1},{3,0},{4,7},{5,6},{6,5},{7,4},{8,11},{9,10},{10,... | collective-permute-start | bytes 417800 | tf_op jit(solution)/shard_map/ppermute | solution.py:32
  83.7 9.1 %collective-permute-start.24 = (bf16[272,256]{1,0:T(8,128)(2,1)S(1)}, bf16[272,256]{1,0:T(8,128)(2,1)S(1)}, u32[]{:S(2)}, u32[]{:S(2)}) collective-permute-start(bf16[272,256]{1,0:T(8,128)(2,1)S(1)} %get-tuple-element.100), channel_id=1, source_target_pairs={{0,1},{1,0},{2,3},{3,2},{4,5},{5,4},{6,7},{7,6},{8,9},{9,8},{10,11... | collective-permute-start | bytes 417800 | tf_op jit(solution)/shard_map/ppermute | solution.py:32
  94.6 12.2 %collective-permute-start.25 = (bf16[272,256]{1,0:T(8,128)(2,1)S(1)}, bf16[272,256]{1,0:T(8,128)(2,1)S(1)}, u32[]{:S(2)}, u32[]{:S(2)}) collective-permute-start(bf16[272,256]{1,0:T(8,128)(2,1)S(1)} %get-tuple-element.113.refs_8_), channel_id=1, source_target_pairs={{0,2},{1,3},{2,0},{3,1},{4,6},{5,7},{6,4},{7,5},{8,10},{9,11},{10,... | collective-permute-start | bytes 417800 | tf_op jit(solution)/shard_map/ppermute | solution.py:32
  97.0 9.8 %collective-permute-start.26 = (bf16[272,256]{1,0:T(8,128)(2,1)S(1)}, bf16[272,256]{1,0:T(8,128)(2,1)S(1)}, u32[]{:S(2)}, u32[]{:S(2)}) collective-permute-start(bf16[272,256]{1,0:T(8,128)(2,1)S(1)} %get-tuple-element.113.refs_8_), channel_id=1, source_target_pairs={{0,3},{1,2},{2,1},{3,0},{4,7},{5,6},{6,5},{7,4},{8,11},{9,10},{10,... | collective-permute-start | bytes 417800 | tf_op jit(solution)/shard_map/ppermute | solution.py:32
  99.2 8.3 %collective-permute-start.27 = (bf16[272,256]{1,0:T(8,128)(2,1)S(1)}, bf16[272,256]{1,0:T(8,128)(2,1)S(1)}, u32[]{:S(2)}, u32[]{:S(2)}) collective-permute-start(bf16[272,256]{1,0:T(8,128)(2,1)S(1)} %get-tuple-element.113.refs_8_), channel_id=1, source_target_pairs={{0,1},{1,0},{2,3},{3,2},{4,5},{5,4},{6,7},{7,6},{8,9},{9,8},{10,11... | collective-permute-start | bytes 417800 | tf_op jit(solution)/shard_map/ppermute | solution.py:32
  108.5 12.9 %collective-permute-start.28 = (bf16[256,256]{1,0:T(8,128)(2,1)S(1)}, bf16[256,256]{1,0:T(8,128)(2,1)S(1)}, u32[]{:S(2)}, u32[]{:S(2)}) collective-permute-start(bf16[256,256]{1,0:T(8,128)(2,1)S(1)} %get-tuple-element.117), channel_id=1, source_target_pairs={{0,2},{1,3},{2,0},{3,1},{4,6},{5,7},{6,4},{7,5},{8,10},{9,11},{10,... | collective-permute-start | bytes 393224 | tf_op jit(solution)/shard_map/ppermute | solution.py:32
  111.0 10.4 %collective-permute-start.29 = (bf16[256,256]{1,0:T(8,128)(2,1)S(1)}, bf16[256,256]{1,0:T(8,128)(2,1)S(1)}, u32[]{:S(2)}, u32[]{:S(2)}) collective-permute-start(bf16[256,256]{1,0:T(8,128)(2,1)S(1)} %get-tuple-element.118), channel_id=1, source_target_pairs={{0,3},{1,2},{2,1},{3,0},{4,7},{5,6},{6,5},{7,4},{8,11},{9,10},{10,... | collective-permute-start | bytes 393224 | tf_op jit(solution)/shard_map/ppermute | solution.py:32
  112.2 10.1 %collective-permute-start.30 = (bf16[256,256]{1,0:T(8,128)(2,1)S(1)}, bf16[256,256]{1,0:T(8,128)(2,1)S(1)}, u32[]{:S(2)}, u32[]{:S(2)}) collective-permute-start(bf16[256,256]{1,0:T(8,128)(2,1)S(1)} %get-tuple-element.119), channel_id=1, source_target_pairs={{0,1},{1,0},{2,3},{3,2},{4,5},{5,4},{6,7},{7,6},{8,9},{9,8},{10,11... | collective-permute-start | bytes 393224 | tf_op jit(solution)/shard_map/ppermute | solution.py:32
  112.3 11.3 %collective-permute-start.32 = (bf16[256,256]{1,0:T(8,128)(2,1)S(1)}, bf16[256,256]{1,0:T(8,128)(2,1)S(1)}, u32[]{:S(2)}, u32[]{:S(2)}) collective-permute-start(bf16[256,256]{1,0:T(8,128)(2,1)S(1)} %get-tuple-element.122.refs_0_), channel_id=1, source_target_pairs={{0,4},{4,0},{8,12},{12,8},{1,5},{5,1},{9,13},{13,9},{2,6},{6,2},{1... | collective-permute-start | bytes 393224 | tf_op jit(solution)/shard_map/ppermute | solution.py:32
  112.9 10.7 %collective-permute-start.33 = (bf16[256,256]{1,0:T(8,128)(2,1)S(1)}, bf16[256,256]{1,0:T(8,128)(2,1)S(1)}, u32[]{:S(2)}, u32[]{:S(2)}) collective-permute-start(bf16[256,256]{1,0:T(8,128)(2,1)S(1)} %get-tuple-element.123.refs_1_), channel_id=1, source_target_pairs={{0,8},{4,12},{8,0},{12,4},{1,9},{5,13},{9,1},{13,5},{2,10},{6,14},... | collective-permute-start | bytes 393224 | tf_op jit(solution)/shard_map/ppermute | solution.py:32
  126.8 12.6 %collective-permute-start.36 = (bf16[896,256]{1,0:T(8,128)(2,1)S(1)}, bf16[896,256]{1,0:T(8,128)(2,1)S(1)}, u32[]{:S(2)}, u32[]{:S(2)}) collective-permute-start(bf16[896,256]{1,0:T(8,128)(2,1)S(1)} %pad_maximum_fusion.1), channel_id=1, source_target_pairs={{0,8},{4,12},{8,0},{12,4},{1,9},{5,13},{9,1},{13,5},{2,10},{6,14},... | collective-permute-start | bytes 1376264 | tf_op jit(solution)/shard_map/ppermute | solution.py:32
  127.4 12.3 %collective-permute-start.35 = (bf16[896,256]{1,0:T(8,128)(2,1)S(1)}, bf16[896,256]{1,0:T(8,128)(2,1)S(1)}, u32[]{:S(2)}, u32[]{:S(2)}) collective-permute-start(bf16[896,256]{1,0:T(8,128)(2,1)S(1)} %pad_maximum_fusion), channel_id=1, source_target_pairs={{0,4},{4,0},{8,12},{12,8},{1,5},{5,1},{9,13},{13,9},{2,6},{6,2},{1... | collective-permute-start | bytes 1376264 | tf_op jit(solution)/shard_map/ppermute | solution.py:32
  140.1 8.7 %collective-permute-start.38 = (bf16[640,256]{1,0:T(8,128)(2,1)S(1)}, bf16[640,256]{1,0:T(8,128)(2,1)S(1)}, u32[]{:S(2)}, u32[]{:S(2)}) collective-permute-start(bf16[640,256]{1,0:T(8,128)(2,1)S(1)} %pad_maximum_fusion.3), channel_id=1, source_target_pairs={{0,4},{4,0},{8,12},{12,8},{1,5},{5,1},{9,13},{13,9},{2,6},{6,2},{1... | collective-permute-start | bytes 983048 | tf_op jit(solution)/shard_map/ppermute | solution.py:32
  140.7 8.5 %collective-permute-start.37 = (bf16[640,256]{1,0:T(8,128)(2,1)S(1)}, bf16[640,256]{1,0:T(8,128)(2,1)S(1)}, u32[]{:S(2)}, u32[]{:S(2)}) collective-permute-start(bf16[640,256]{1,0:T(8,128)(2,1)S(1)} %pad_maximum_fusion.2), channel_id=1, source_target_pairs={{0,8},{4,12},{8,0},{12,4},{1,9},{5,13},{9,1},{13,5},{2,10},{6,14},... | collective-permute-start | bytes 983048 | tf_op jit(solution)/shard_map/ppermute | solution.py:32
  (23 other events, 155.2 us)
